TPU v7x, 32 devices: a whole 2x2x4 slice. The times are simulated.
32 devices in a mesh: gx: 4 (over y, core), gy: 8 (over z, x).
Axes of the slice: x: 2, y: 2, z: 4, core: 2. Of those that a mesh axis runs over, the one named last changes fastest.
Arguments:
- query_rows: bfloat16 [4096, 1024], P(('gx', 'gy')), may hold values from -6 to 6
- key_rows: bfloat16 [4096, 1024], P(('gx', 'gy')), may hold values from -6 to 6
- value_rows: bfloat16 [4096, 1024], P(('gx', 'gy')), may hold values from -6 to 6
- out_grad: bfloat16 [4096, 1024], P(('gx', 'gy')), may hold values from -6 to 6
- gate_class: int32 [4096], P(('gx', 'gy')), may hold values from 0 to 31
- gate_table: float32 [32, 20, 8], replicated, may hold values from 0 to 1, as said below
Outputs:
- query_grad: bfloat16 [4096, 1024], P(('gx', 'gy'))
- key_grad: bfloat16 [4096, 1024], P(('gx', 'gy'))
- value_grad: bfloat16 [4096, 1024], P(('gx', 'gy'))
Inputs may be any that keep to these rules, and one draw needn't show every extreme that they name: `gate_class`: row of the gate table for each token. `gate_table`: every entry is positive.
All inputs are finite; a program needn't handle non-finite values.
Results may differ from a plain program's by a relative error of at most 0.0054.
Values may be sent and summed in bfloat16 or wider, within the bound.
No kernel may reach another device: no remote copies, remote signals or barrier semaphores. Data moves between devices by JAX's collectives and lax.ppermute only.
A program may use at most 64 MiB of HBM per device.

v0:
```python
import jax
import jax.numpy as jnp
from jax import lax
from jax.sharding import PartitionSpec as P


def from_partner(block, axis, stride):
    count = lax.axis_size(axis)
    route = []
    for low in range(count):
        high = low | 1 << stride
        if high != low and high < count:
            route += [(low, high), (high, low)]
    return lax.ppermute(block, axis, route)


def level_bits(amount):
    return amount.bit_length() - 1


def gate_values(gate_class, gate_table):
    classes = gate_table.shape[0]
    levels = gate_table.shape[1]
    head_count = gate_table.shape[2]
    picker = (gate_class[:, None] == jnp.arange(classes, dtype=jnp.int32)[None, :]).astype(
        jnp.float32
    )
    flat_table = gate_table.reshape(classes, levels * head_count)
    picked = jnp.dot(
        picker, flat_table, precision=lax.Precision.HIGHEST, preferred_element_type=jnp.float32
    )
    return picked.reshape(gate_class.shape[0], levels, head_count)


def block_weights(gate_rows, amount):
    block_depth = level_bits(amount)
    positions = jnp.arange(amount, dtype=jnp.int32)
    xor_place = jnp.bitwise_xor(positions[:, None], positions[None, :])
    level_map = jnp.zeros((amount, amount), jnp.int32)
    for bit_index in range(block_depth):
        level_map = level_map + (xor_place >= 2**bit_index).astype(jnp.int32)
    causal = positions[None, :] <= positions[:, None]
    weights = jnp.zeros((gate_rows.shape[2], amount, amount), jnp.float32)
    for tree_level in range(block_depth + 1):
        chosen = jnp.logical_and(level_map == tree_level, causal)
        picked = gate_rows[:, tree_level, :].T[:, :, None]
        weights = weights + jnp.where(chosen[None, :, :], picked, jnp.zeros((), jnp.float32))
    return weights


def per_device(query_rows, key_rows, value_rows, out_grad, gate_class, gate_table):
    row_count = query_rows.shape[0]
    head_count = gate_table.shape[2]
    head_size = query_rows.shape[1] // head_count
    inner_bits = level_bits(lax.axis_size("gy"))
    outer_bits = level_bits(lax.axis_size("gx"))
    total_levels = inner_bits + outer_bits
    block_depth = level_bits(row_count)
    inner_index = lax.axis_index("gy")
    outer_index = lax.axis_index("gx")
    flag_list = [inner_index // 2**tree_level % 2 for tree_level in range(inner_bits)]
    flag_list = flag_list + [outer_index // 2**tree_level % 2 for tree_level in range(outer_bits)]
    bit_flags = jnp.stack(flag_list).astype(jnp.float32)
    gate_rows = gate_values(gate_class, gate_table)
    device_gates = (
        gate_rows[:, block_depth + 1 : block_depth + 1 + total_levels, :] * bit_flags[None, :, None]
    )
    query_heads = query_rows.reshape(row_count, head_count, head_size)
    key_heads = key_rows.reshape(row_count, head_count, head_size)
    value_heads = value_rows.reshape(row_count, head_count, head_size)
    grad_heads = out_grad.reshape(row_count, head_count, head_size)
    scores = jnp.einsum("thd,shd->hts", query_heads, key_heads, preferred_element_type=jnp.float32)
    pair_grads = jnp.einsum(
        "the,she->hts", grad_heads, value_heads, preferred_element_type=jnp.float32
    )
    weights = block_weights(gate_rows, row_count)
    weighted_grads = (weights * pair_grads).astype(jnp.bfloat16)
    weighted_scores = (weights * scores).astype(jnp.bfloat16)
    query_total = jnp.einsum(
        "hts,shd->thd", weighted_grads, key_heads, preferred_element_type=jnp.float32
    )
    key_total = jnp.einsum(
        "hts,thd->shd", weighted_grads, query_heads, preferred_element_type=jnp.float32
    )
    value_total = jnp.einsum(
        "hts,the->she", weighted_scores, grad_heads, preferred_element_type=jnp.float32
    )
    group_state = jnp.einsum(
        "thd,the->hde", key_heads, value_heads, preferred_element_type=jnp.float32
    )
    scaled_query = (device_gates[:, :, :, None] * query_heads[:, None, :, :]).astype(jnp.bfloat16)
    level_grads = jnp.einsum(
        "tlhd,the->lhde", scaled_query, grad_heads, preferred_element_type=jnp.float32
    )
    acc_state = group_state
    inner_grads = [level_grads[tree_level] for tree_level in range(inner_bits)]
    state_grad = jnp.zeros_like(group_state)
    rounded_states = []
    for tree_level in range(inner_bits):
        bundle = jnp.stack([acc_state] + inner_grads[tree_level:])
        arrived = from_partner(bundle, "gy", tree_level)
        rounded_states.append(arrived[0].astype(jnp.bfloat16))
        state_grad = state_grad + arrived[1]
        acc_state = acc_state + arrived[0]
        for later in range(tree_level + 1, inner_bits):
            inner_grads[later] = inner_grads[later] + arrived[1 + later - tree_level]
    flat_rows = head_count * head_size
    share_rows = flat_rows // lax.axis_size("gy")
    row_state = acc_state.reshape(flat_rows, head_size)
    state_share = lax.dynamic_slice_in_dim(row_state, inner_index * share_rows, share_rows, 0)
    outer_flat = level_grads[inner_bits:].reshape(outer_bits, flat_rows, head_size)
    grad_share = lax.psum_scatter(outer_flat, "gy", scatter_dimension=1, tiled=True)
    share_grads = [grad_share[tree_level] for tree_level in range(outer_bits)]
    share_total = jnp.zeros_like(state_share)
    state_parts = []
    for tree_level in range(outer_bits):
        bundle = jnp.stack([state_share] + share_grads[tree_level:])
        arrived = from_partner(bundle, "gx", tree_level)
        state_parts.append(arrived[0])
        share_total = share_total + arrived[1]
        state_share = state_share + arrived[0]
        for later in range(tree_level + 1, outer_bits):
            share_grads[later] = share_grads[later] + arrived[1 + later - tree_level]
    part_stack = jnp.stack(state_parts)
    state_rows = lax.all_gather(part_stack.astype(jnp.bfloat16), "gy", axis=1, tiled=True)
    for tree_level in range(outer_bits):
        rounded_states.append(state_rows[tree_level].reshape(head_count, head_size, head_size))
    grad_rows = lax.all_gather(share_total, "gy", axis=0, tiled=True)
    state_grad = state_grad + grad_rows.reshape(head_count, head_size, head_size)
    for tree_level in range(total_levels):
        level_term = jnp.einsum(
            "the,hde->thd",
            grad_heads,
            rounded_states[tree_level],
            preferred_element_type=jnp.float32,
        )
        query_total = query_total + device_gates[:, tree_level, :, None] * level_term
    grad_rounded = state_grad.astype(jnp.bfloat16)
    key_total = key_total + jnp.einsum(
        "the,hde->thd", value_heads, grad_rounded, preferred_element_type=jnp.float32
    )
    value_total = value_total + jnp.einsum(
        "thd,hde->the", key_heads, grad_rounded, preferred_element_type=jnp.float32
    )
    width = head_count * head_size
    return (
        query_total.reshape(row_count, width).astype(jnp.bfloat16),
        key_total.reshape(row_count, width).astype(jnp.bfloat16),
        value_total.reshape(row_count, width).astype(jnp.bfloat16),
    )


def solution(mesh):
    return jax.shard_map(
        per_device,
        mesh=mesh,
        in_specs=(
            P(("gx", "gy"), None),
            P(("gx", "gy"), None),
            P(("gx", "gy"), None),
            P(("gx", "gy"), None),
            P(("gx", "gy")),
            P(),
        ),
        out_specs=(P(("gx", "gy"), None), P(("gx", "gy"), None), P(("gx", "gy"), None)),
        check_vma=False,
    )
```

profile of v0, /device:TPU:0, one launch (start us, length us, event | category | flops | bytes accessed | tf_op | source)
XLA Modules:
  0.0 248.3 jit_solution(2690352279597091223)
XLA Ops:
  7.3 1.0 copy.60
  9.7 0.8 copy-done.1
  11.1 3.0 %collective-permute-start = (f32[4,8,128,128]{3,2,1,0:T(8,128)S(1)}, f32[4,8,128,128]{3,2,1,0:T(8,128)S(1)}, u32[]{:S(2)}, u32[]{:S(2)}) collective-permute-start(f32[4,8,128,128]{3,2,1,0:T(8,128)S(1)} %pad_maximum_fusion), channel_id=1, source_target_pairs={{0,1},{1,0},{2,3},{3,2},{4,5},{5,4},{6,7},{7,6},{8,9},{9,8},{10,11... | collective-permute-start | bytes 6291464 | tf_op jit(solution)/shard_map/ppermute | solution.py:14
  14.1 45.6 %collective-permute-done = f32[4,8,128,128]{3,2,1,0:T(8,128)S(1)} collective-permute-done((f32[4,8,128,128]{3,2,1,0:T(8,128)S(1)}, f32[4,8,128,128]{3,2,1,0:T(8,128)S(1)}, u32[]{:S(2)}, u32[]{:S(2)}) %collective-permute-start) | collective-permute-done | bytes 2097184 | tf_op jit(solution)/shard_map/ppermute | solution.py:14
  59.9 1.3 pad_maximum_fusion.1
  61.2 1.8 collective-permute-start.1
  63.0 1.0 slice.170
  67.4 38.1 %collective-permute-done.1 = f32[3,8,128,128]{3,2,1,0:T(8,128)} collective-permute-done((f32[3,8,128,128]{3,2,1,0:T(8,128)}, f32[3,8,128,128]{3,2,1,0:T(8,128)}, u32[]{:S(2)}, u32[]{:S(2)}) %collective-permute-start.1) | collective-permute-done | bytes 1572896 | tf_op jit(solution)/shard_map/ppermute | solution.py:14
  105.5 1.1 slice_add_fusion.2
  106.6 1.1 fusion.69
  107.8 1.1 pad_maximum_fusion.2
  108.9 2.5 %collective-permute-start.2 = (f32[2,8,128,128]{3,2,1,0:T(8,128)}, f32[2,8,128,128]{3,2,1,0:T(8,128)}, u32[]{:S(2)}, u32[]{:S(2)}) collective-permute-start(f32[2,8,128,128]{3,2,1,0:T(8,128)} %pad_maximum_fusion.2), channel_id=1, source_target_pairs={{0,4},{4,0},{1,5},{5,1},{2,6},{6,2},{3,7},{7,3},{8,12},{12,8},{9,1... | collective-permute-start | bytes 3145736 | tf_op jit(solution)/shard_map/ppermute | solution.py:14
  111.6 2.2 fusion.14
  113.8 1.2 convolution_bitcast_fusion.10
  115.0 1.1 convolution_bitcast_fusion.2
  116.0 2.9 %convolution_bitcast_fusion.1 = f32[128,8,128]{0,2,1:T(8,128)} fusion(f32[8,128]{1,0:T(8,128)} %bitcast.281, f32[8,128]{1,0:T(8,128)} %bitcast.283, f32[8,128]{1,0:T(8,128)} %bitcast.285, f32[8,128]{1,0:T(8,128)} %bitcast.287, f32[8,128]{1,0:T(8,128)} %bitcast.289, f32[8,128]{1,0:T(8,128)} %bitcast.291, f32[8,128]{1,0:T(8,128)} %bitcast.293, ...), kind=kOutput, calls=%fused_computation.5 | convolution fusion | flops 69337088 | bytes 1474560 | tf_op jit(solution)/shard_map/hts,the->she/dot_general | solution.py:85
  119.0 41.4 %collective-permute-done.2 = f32[2,8,128,128]{3,2,1,0:T(8,128)} collective-permute-done((f32[2,8,128,128]{3,2,1,0:T(8,128)}, f32[2,8,128,128]{3,2,1,0:T(8,128)}, u32[]{:S(2)}, u32[]{:S(2)}) %collective-permute-start.2) | collective-permute-done | bytes 1048608 | tf_op jit(solution)/shard_map/ppermute | solution.py:14
  160.3 1.3 fusion.25
  161.7 0.8 copy-done.10
  162.5 1.0 pad_maximum_fusion.3
  163.5 1.3 fusion.7
  165.0 0.9 fusion.80
  165.9 1.2 collective-permute-start.4
  167.1 1.3 fusion.8
  168.5 3.4 %collective-permute-done.4 = f32[2,128,128]{2,1,0:T(8,128)S(1)} collective-permute-done((f32[2,128,128]{2,1,0:T(8,128)S(1)}, f32[2,128,128]{2,1,0:T(8,128)S(1)}, u32[]{:S(2)}, u32[]{:S(2)}) %collective-permute-start.4) | collective-permute-done | bytes 131104 | tf_op jit(solution)/shard_map/ppermute | solution.py:14
  171.9 31.6 %all_gather.6 = bf16[2,1024,128]{2,1,0:T(8,128)(2,1)S(1)} all-gather(bf16[2,128,128]{2,1,0:T(8,128)(2,1)S(1)} %pad_maximum_fusion.5), channel_id=1, replica_groups=mesh['gx'=4,'gy'=8] {'gy'}, dimensions={1}, use_global_device_ids=true | all-gather | bytes 589824 | tf_op jit(solution)/shard_map/all_gather | solution.py:125
  204.8 0.9 copy.49
  205.7 0.9 slice_add_fusion.5
  206.6 31.2 %all-gather = f32[1,1024,128]{2,1,0:T(8,128)S(1)} all-gather(f32[1,128,128]{2,1,0:T(8,128)S(1)} %slice_add_fusion.5), channel_id=2, replica_groups=mesh['gx'=4,'gy'=8] {'gy'}, dimensions={1}, use_global_device_ids=true | all-gather | bytes 589824 | tf_op jit(solution)/shard_map/all_gather | solution.py:128
  237.8 1.3 fusion.20
  239.4 0.9 copy.50
  240.6 0.9 copy.51
  (79 shorter events, 7.8 us)
Async XLA Ops:
  7.2 1.9 copy-start
  7.2 1.6 copy-start.14
  7.2 1.6 copy-start.22
  7.2 155.3 %reduce-scatter.2.cloned.1.call-start = ((), (), s32[]{:S(2)}) async-start(), calls=%async_computation.1 | async-start | bytes 1179648 | tf_op jit(solution)/shard_map/reduce_scatter | solution.py:112
  9.5 1.0 copy-start.1
  9.5 1.0 copy-start.5
  11.1 48.6 %collective-permute-start = (f32[4,8,128,128]{3,2,1,0:T(8,128)S(1)}, f32[4,8,128,128]{3,2,1,0:T(8,128)S(1)}, u32[]{:S(2)}, u32[]{:S(2)}) collective-permute-start(f32[4,8,128,128]{3,2,1,0:T(8,128)S(1)} %pad_maximum_fusion), channel_id=1, source_target_pairs={{0,1},{1,0},{2,3},{3,2},{4,5},{5,4},{6,7},{7,6},{8,9},{9,8},{10,11... | collective-permute-start | bytes 6291464 | tf_op jit(solution)/shard_map/ppermute | solution.py:14
  61.2 44.3 %collective-permute-start.1 = (f32[3,8,128,128]{3,2,1,0:T(8,128)}, f32[3,8,128,128]{3,2,1,0:T(8,128)}, u32[]{:S(2)}, u32[]{:S(2)}) collective-permute-start(f32[3,8,128,128]{3,2,1,0:T(8,128)} %pad_maximum_fusion.1), channel_id=1, source_target_pairs={{0,2},{2,0},{1,3},{3,1},{4,6},{6,4},{5,7},{7,5},{8,10},{10,8},{9,1... | collective-permute-start | bytes 4718600 | tf_op jit(solution)/shard_map/ppermute | solution.py:14
  107.7 3.8 %copy-start.6 = (bf16[128,1024]{1,0:T(8,128)(2,1)S(1)}, bf16[128,1024]{1,0:T(8,128)(2,1)}, u32[]{:S(2)}) copy-start(bf16[128,1024]{1,0:T(8,128)(2,1)} %param.8) | copy-start | bytes 786436
  107.7 3.8 %copy-start.15 = (pred[128,128]{1,0:T(8,128)(4,1)S(1)}, pred[128,128]{1,0:T(8,128)(4,1)}, u32[]{:S(2)}) copy-start(pred[128,128]{1,0:T(8,128)(4,1)} %get-tuple-element.26) | copy-start | bytes 49156
  107.7 3.8 %copy-start.16 = (pred[128,128]{1,0:T(8,128)(4,1)S(1)}, pred[128,128]{1,0:T(8,128)(4,1)}, u32[]{:S(2)}) copy-start(pred[128,128]{1,0:T(8,128)(4,1)} %get-tuple-element.27) | copy-start | bytes 49156
  107.7 3.8 %copy-start.17 = (pred[128,128]{1,0:T(8,128)(4,1)S(1)}, pred[128,128]{1,0:T(8,128)(4,1)}, u32[]{:S(2)}) copy-start(pred[128,128]{1,0:T(8,128)(4,1)} %get-tuple-element.28) | copy-start | bytes 49156
  107.8 3.8 %copy-start.18 = (pred[128,128]{1,0:T(8,128)(4,1)S(1)}, pred[128,128]{1,0:T(8,128)(4,1)}, u32[]{:S(2)}) copy-start(pred[128,128]{1,0:T(8,128)(4,1)} %get-tuple-element.29) | copy-start | bytes 49156
  107.8 3.8 %copy-start.19 = (pred[128,128]{1,0:T(8,128)(4,1)S(1)}, pred[128,128]{1,0:T(8,128)(4,1)}, u32[]{:S(2)}) copy-start(pred[128,128]{1,0:T(8,128)(4,1)} %get-tuple-element.30) | copy-start | bytes 49156
  107.8 3.8 %copy-start.20 = (pred[128,128]{1,0:T(8,128)(4,1)S(1)}, pred[128,128]{1,0:T(8,128)(4,1)}, u32[]{:S(2)}) copy-start(pred[128,128]{1,0:T(8,128)(4,1)} %get-tuple-element.31) | copy-start | bytes 49156
  108.9 51.4 %collective-permute-start.2 = (f32[2,8,128,128]{3,2,1,0:T(8,128)}, f32[2,8,128,128]{3,2,1,0:T(8,128)}, u32[]{:S(2)}, u32[]{:S(2)}) collective-permute-start(f32[2,8,128,128]{3,2,1,0:T(8,128)} %pad_maximum_fusion.2), channel_id=1, source_target_pairs={{0,4},{4,0},{1,5},{5,1},{2,6},{6,2},{3,7},{7,3},{8,12},{12,8},{9,1... | collective-permute-start | bytes 3145736 | tf_op jit(solution)/shard_map/ppermute | solution.py:14
  111.6 2.2 copy-start.2
  111.6 3.4 %copy-start.8 = (bf16[128,1024]{1,0:T(8,128)(2,1)S(1)}, bf16[128,1024]{1,0:T(8,128)(2,1)}, u32[]{:S(2)}) copy-start(bf16[128,1024]{1,0:T(8,128)(2,1)} %param.6) | copy-start | bytes 786436
  113.8 2.2 copy-start.9
  161.6 0.8 copy-start.10
  162.5 2.5 %copy-start.12 = (f32[2,128,128]{2,1,0:T(8,128)S(1)}, f32[2,128,128]{2,1,0:T(8,128)}, u32[]{:S(2)}) copy-start(f32[2,128,128]{2,1,0:T(8,128)} %reduce-scatter.2.cloned.1.call-done) | copy-start | bytes 393220
  163.5 1.5 collective-permute-start.3
  165.0 6.9 %copy-start.13 = (f32[3,128,128]{2,1,0:T(8,128)}, f32[3,128,128]{2,1,0:T(8,128)S(1)}, u32[]{:S(2)}) copy-start(f32[3,128,128]{2,1,0:T(8,128)S(1)} %collective-permute-done.3) | copy-start | bytes 589828
  165.9 5.9 %collective-permute-start.4 = (f32[2,128,128]{2,1,0:T(8,128)S(1)}, f32[2,128,128]{2,1,0:T(8,128)S(1)}, u32[]{:S(2)}, u32[]{:S(2)}) collective-permute-start(f32[2,128,128]{2,1,0:T(8,128)S(1)} %pad_maximum_fusion.4), channel_id=1, source_target_pairs={{0,16},{16,0},{8,24},{24,8},{1,17},{17,1},{9,25},{25,9},{2,18},{18... | collective-permute-start | bytes 393224 | tf_op jit(solution)/shard_map/ppermute | solution.py:14
  203.5 1.0 copy-start.4
  203.5 1.0 copy-start.21
  205.7 33.4 %copy-start.3 = (f32[128,8,128]{0,2,1:T(8,128)S(1)}, f32[128,8,128]{0,2,1:T(8,128)}, u32[]{:S(2)}) copy-start(f32[128,8,128]{0,2,1:T(8,128)} %convolution_bitcast_fusion.2) | copy-start | bytes 1572868
  205.7 33.4 %copy-start.7 = (bf16[128,1024]{1,0:T(8,128)(2,1)S(1)}, bf16[128,1024]{1,0:T(8,128)(2,1)}, u32[]{:S(2)}) copy-start(bf16[128,1024]{1,0:T(8,128)(2,1)} %param.8) | copy-start | bytes 786436
  239.1 1.2 copy-start.11
Sparse Core Ops, SparseCore 0:
  64.2 97.4 reduce-scatter.1
where the time goes:
time: 249 us; the launch traced here: 248 us
  waiting for transfers between devices  129 us (52%)
  blocking collectives  62.8 us (25%)
  between operations  14.5 us (6%)
  other arithmetic  12.8 us (5%)
  matrix products  12.5 us (5%)
  starting transfers between devices  8.66 us (3%)
  local copies, waits for them, and re-layouts  8.49 us (3%)
    ppermute x5, waiting for transfers between devices, from_partner(): return lax.ppermute(block, axis, route)  129 us
    all_gather x1, blocking collectives, per_device(): lax.all_gather(part_stack.astype(jnp.bfloat16), 'gy', axis=1, tiled=True)  31.6 us
    all_gather x1, blocking collectives, per_device(): grad_rows = lax.all_gather(share_total, 'gy', axis=0, tiled=True)  31.2 us
    ppermute x5, starting transfers between devices, from_partner(): return lax.ppermute(block, axis, route)  8.62 us
    unnamed x50, local copies, waits for them, and re-layouts  5.69 us
  transfers between devices with their start and end apart: 6, of which 5 were waited for; matrix products, arithmetic and copies ran while one was open for 8% of the time, Pallas kernels for 0%

commit v1 on v0

v1 whole, which is shorter than its diff:
```python
import jax
import jax.numpy as jnp
from jax import lax
from jax.sharding import PartitionSpec as P

NEAR = 3


def level_bits(amount):
    return amount.bit_length() - 1


def trade(block, axis, offset):
    count = lax.axis_size(axis)
    return lax.ppermute(block, axis, [(place, place ^ offset) for place in range(count)])


def gate_values(gate_class, gate_table):
    classes, levels, head_count = gate_table.shape
    picker = (gate_class[:, None] == jnp.arange(classes, dtype=jnp.int32)[None, :]).astype(
        jnp.float32
    )
    picked = jnp.dot(
        picker,
        gate_table.reshape(classes, levels * head_count),
        precision=lax.Precision.HIGHEST,
        preferred_element_type=jnp.float32,
    )
    return picked.reshape(gate_class.shape[0], levels, head_count)


def block_weights(gate_rows, amount):
    block_depth = level_bits(amount)
    positions = jnp.arange(amount, dtype=jnp.int32)
    xor_place = jnp.bitwise_xor(positions[:, None], positions[None, :])
    level_map = jnp.zeros((amount, amount), jnp.int32)
    for bit_index in range(block_depth):
        level_map = level_map + (xor_place >= 2**bit_index).astype(jnp.int32)
    causal = positions[None, :] <= positions[:, None]
    weights = jnp.zeros((gate_rows.shape[2], amount, amount), jnp.float32)
    for tree_level in range(block_depth + 1):
        chosen = jnp.logical_and(level_map == tree_level, causal)
        picked = gate_rows[:, tree_level, :].T[:, :, None]
        weights = weights + jnp.where(chosen[None, :, :], picked, jnp.zeros((), jnp.float32))
    return weights


def per_device(query_rows, key_rows, value_rows, out_grad, gate_class, gate_table):
    row_count = query_rows.shape[0]
    head_count = gate_table.shape[2]
    head_size = query_rows.shape[1] // head_count
    inner_bits = level_bits(lax.axis_size("gy"))
    outer_bits = level_bits(lax.axis_size("gx"))
    total_levels = inner_bits + outer_bits
    block_depth = level_bits(row_count)
    inner_index = lax.axis_index("gy")
    outer_index = lax.axis_index("gx")
    block_index = (outer_index << inner_bits) | inner_index
    flags = [((block_index >> level) & 1) == 1 for level in range(total_levels)]

    def swap(block, bit):
        if bit < inner_bits:
            return trade(block, "gy", 1 << bit)
        return trade(block, "gx", 1 << (bit - inner_bits))

    def wide(values):
        return values.astype(jnp.float32)

    def narrow(values):
        return values.astype(jnp.bfloat16)

    gate_rows = gate_values(gate_class, gate_table)
    level_gates = gate_rows[:, block_depth + 1 : block_depth + 1 + total_levels, :]
    shape_three = (row_count, head_count, head_size)
    query_heads = query_rows.reshape(shape_three)
    key_heads = key_rows.reshape(shape_three)
    value_heads = value_rows.reshape(shape_three)
    grad_heads = out_grad.reshape(shape_three)

    def payload(level):
        scaled = narrow(level_gates[:, level, :, None] * wide(query_heads))
        left = jnp.where(flags[level], scaled, key_heads)
        right = jnp.where(flags[level], grad_heads, value_heads)
        return narrow(
            jnp.einsum("thd,the->hde", left, right, preferred_element_type=jnp.float32)
        )

    quarter = head_count // 4
    half = head_count // 2
    cell = (head_size, head_size)
    z_place = (inner_index >> 1) & 3
    x_place = inner_index & 1

    upper = jnp.stack([payload(level) for level in range(NEAR, total_levels)], axis=1)
    upper = upper.reshape((4, quarter, total_levels - NEAR) + cell)

    def upper_part(place):
        return lax.dynamic_index_in_dim(upper, place, 0, keepdims=False)

    came = [trade(upper_part(z_place ^ offset), "gy", offset << 1) for offset in (3, 2, 1)]
    part = wide(upper_part(z_place)) + wide(came[0]) + wide(came[1]) + wide(came[2])
    parts = [part[:, place] for place in range(total_levels - NEAR)]
    done_parts = []
    for level in range(NEAR, total_levels):
        seen = wide(swap(narrow(jnp.stack(parts, axis=1)), level))
        done_parts.append(seen[:, 0])
        parts = [parts[place] + seen[:, place] for place in range(1, len(parts))]
    shares = jnp.stack(done_parts, axis=1)
    shares = narrow(shares + wide(swap(narrow(shares), 0)))
    pieces = [shares] + [trade(shares, "gy", offset << 1) for offset in (1, 2, 3)]
    near_pair = [
        jnp.where(z_place & 1 == 1, pieces[1], pieces[0]),
        jnp.where(z_place & 1 == 1, pieces[0], pieces[1]),
    ]
    far_pair = [
        jnp.where(z_place & 1 == 1, pieces[3], pieces[2]),
        jnp.where(z_place & 1 == 1, pieces[2], pieces[3]),
    ]
    far_side = z_place & 2 == 2
    ordered = [
        jnp.where(far_side, far_pair[0], near_pair[0]),
        jnp.where(far_side, far_pair[1], near_pair[1]),
        jnp.where(far_side, near_pair[0], far_pair[0]),
        jnp.where(far_side, near_pair[1], far_pair[1]),
    ]
    upper_done = jnp.concatenate(ordered, axis=0)

    low_two = payload(2).reshape((2, half) + cell)
    low_one = payload(1)
    two_other = lax.dynamic_index_in_dim(low_two, 1 - x_place, 0, keepdims=False)
    two_own = lax.dynamic_index_in_dim(low_two, x_place, 0, keepdims=False)
    seen = wide(swap(jnp.concatenate([low_one, two_other], axis=0), 0))
    one_sum = wide(low_one) + seen[:head_count]
    two_sum = wide(two_own) + seen[head_count:]
    arrived = swap(jnp.concatenate([narrow(one_sum), narrow(two_sum)], axis=0), 1)
    one_done = arrived[:head_count]
    two_sum = two_sum + wide(arrived[head_count:])
    two_half = swap(narrow(two_sum), 2)
    two_rest = swap(two_half, 0)
    two_done = jnp.concatenate(
        [
            jnp.where(x_place == 0, two_half, two_rest),
            jnp.where(x_place == 0, two_rest, two_half),
        ],
        axis=0,
    )
    zero_done = swap(payload(0), 0)
    states = [zero_done, one_done, two_done]
    states = states + [upper_done[:, place] for place in range(total_levels - NEAR)]

    scores = jnp.einsum("thd,shd->hts", query_heads, key_heads, preferred_element_type=jnp.float32)
    pair_grads = jnp.einsum(
        "the,she->hts", grad_heads, value_heads, preferred_element_type=jnp.float32
    )
    weights = block_weights(gate_rows, row_count)
    weighted_grads = narrow(weights * pair_grads)
    weighted_scores = narrow(weights * scores)
    query_total = jnp.einsum(
        "hts,shd->thd", weighted_grads, key_heads, preferred_element_type=jnp.float32
    )
    key_total = jnp.einsum(
        "hts,thd->shd", weighted_grads, query_heads, preferred_element_type=jnp.float32
    )
    value_total = jnp.einsum(
        "hts,the->she", weighted_scores, grad_heads, preferred_element_type=jnp.float32
    )
    state_grad = jnp.zeros((head_count,) + cell, jnp.float32)
    for level in range(total_levels):
        level_term = jnp.einsum(
            "the,hde->thd", grad_heads, states[level], preferred_element_type=jnp.float32
        )
        gate_here = jnp.where(flags[level], level_gates[:, level, :], 0.0)
        query_total = query_total + gate_here[:, :, None] * level_term
        state_grad = state_grad + jnp.where(flags[level], 0.0, wide(states[level]))
    grad_rounded = narrow(state_grad)
    key_total = key_total + jnp.einsum(
        "the,hde->thd", value_heads, grad_rounded, preferred_element_type=jnp.float32
    )
    value_total = value_total + jnp.einsum(
        "thd,hde->the", key_heads, grad_rounded, preferred_element_type=jnp.float32
    )
    width = head_count * head_size
    return (
        narrow(query_total.reshape(row_count, width)),
        narrow(key_total.reshape(row_count, width)),
        narrow(value_total.reshape(row_count, width)),
    )


def solution(mesh):
    rows = P(("gx", "gy"), None)
    return jax.shard_map(
        per_device,
        mesh=mesh,
        in_specs=(rows, rows, rows, rows, P(("gx", "gy")), P()),
        out_specs=(rows, rows, rows),
        check_vma=False,
    )
```

time: 249 us -> 73.5 us (0.30)
  waiting for transfers between devices: 129 us -> 35.2 us
  blocking collectives: 62.8 us -> 0 us
  between operations: 14.5 us -> 1.01 us
  other arithmetic: 12.8 us -> 4.72 us
  starting transfers between devices: 8.66 us -> 15.9 us
  matrix products: 12.5 us -> 9.78 us
    ppermute x5 -> x14, waiting for transfers between devices: 129 us -> 35.2 us  [trade(): lax.ppermute(block, axis, [(place, place ^ offset) for place in range(cou...]
    all_gather x2 -> x0, blocking collectives: 62.8 us -> none  [the longest x1 31.6 us: per_device(): lax.all_gather(part_stack.astype(jnp.bfloat16), 'gy', axis=1, tiled=True)]
    ppermute x5 -> x14, starting transfers between devices: 8.62 us -> 15.9 us  [trade(): lax.ppermute(block, axis, [(place, place ^ offset) for place in range(cou...]
    another operation x9 -> x0, other arithmetic: 5.71 us -> none  [the longest x5 3.77 us: per_device(): bundle = jnp.stack([acc_state] + inner_grads[tree_level:])]
    add x5 -> x0, other arithmetic: 3.49 us -> none  [the longest x1 1.31 us: per_device(): acc_state = acc_state + arrived[0]]
    dot_general x8 -> x11, matrix products: 4.57 us -> 5.1 us  [the longest x5 2.2 us: payload(): jnp.einsum('thd,the->hde', left, right, preferred_element_type=jnp.float32)]
    unnamed x50 -> x19, local copies, waits for them, and re-layouts: 5.69 us -> 5.84 us
  transfers between devices with their start and end apart: 6 -> 14, of which waited for: 5 -> 10; matrix products, arithmetic and copies ran while one was open for 8% -> 14% of each run, Pallas kernels for 0% -> 0%
where the time goes in v1:
time: 73.5 us; the launch traced here: 73.1 us
  waiting for transfers between devices  35.2 us (48%)
  starting transfers between devices  15.9 us (22%)
  matrix products  9.78 us (13%)
  local copies, waits for them, and re-layouts  6.58 us (9%)
  other arithmetic  4.72 us (6%)
  between operations  1.01 us (1%)
    ppermute x14, waiting for transfers between devices, trade(): lax.ppermute(block, axis, [(place, place ^ offset) for place in range(cou...  35.2 us
    ppermute x14, starting transfers between devices, trade(): lax.ppermute(block, axis, [(place, place ^ offset) for place in range(cou...  15.9 us
    unnamed x19, local copies, waits for them, and re-layouts  5.84 us
    dot_general x1, matrix products, per_device(): jnp.einsum('hts,the->she', weighted_scores, grad_heads, preferred_element...  2.26 us
    dot_general x5, matrix products, payload(): jnp.einsum('thd,the->hde', left, right, preferred_element_type=jnp.float32)  2.2 us
    dot_general x5, matrix products, per_device(): jnp.einsum('the,hde->thd', grad_heads, states[level], preferred_element_t...  2.06 us
    convert_element_type x8, other arithmetic, narrow(): return values.astype(jnp.bfloat16)  1.55 us
  transfers between devices with their start and end apart: 14, of which 10 were waited for; matrix products, arithmetic and copies ran while one was open for 14% of the time, Pallas kernels for 0%

profile of v1, /device:TPU:0, one launch (start us, length us, event | category | flops | bytes accessed | tf_op | source)
XLA Modules:
  0.0 73.1 jit_solution(10747772646287897652)
XLA Ops:
  0.7 0.9 %copy-done = f32[32,20,8]{0,2,1:T(8,128)S(1)} copy-done((f32[32,20,8]{0,2,1:T(8,128)S(1)}, f32[32,20,8]{0,2,1:T(8,128)}, u32[]{:S(2)}) %copy-start) | copy-done | bytes 20504
  1.5 0.8 %fusion.78 = f32[128,20,8]{0,1,2:T(8,128)S(1)} fusion(f32[20,8,32]{2,1,0:T(8,128)S(1)} %bitcast.153, s32[128]{0:T(128)} %param.10), kind=kOutput, calls=%fused_computation.129 | convolution fusion | flops 7868416 | bytes 102912 | tf_op jit(solution)/shard_map/dot_general | solution.py:23
  2.6 0.8 %copy-done.5 = bf16[128,1024]{1,0:T(8,128)(2,1)S(1)} copy-done((bf16[128,1024]{1,0:T(8,128)(2,1)S(1)}, bf16[128,1024]{1,0:T(8,128)(2,1)}, u32[]{:S(2)}) %copy-start.5) | copy-done | bytes 262168
  3.5 0.8 %copy-done.6 = bf16[128,1024]{1,0:T(8,128)(2,1)S(1)} copy-done((bf16[128,1024]{1,0:T(8,128)(2,1)S(1)}, bf16[128,1024]{1,0:T(8,128)(2,1)}, u32[]{:S(2)}) %copy-start.6) | copy-done | bytes 262168
  4.5 0.8 %copy-done.7 = bf16[128,1024]{1,0:T(8,128)(2,1)S(1)} copy-done((bf16[128,1024]{1,0:T(8,128)(2,1)S(1)}, bf16[128,1024]{1,0:T(8,128)(2,1)}, u32[]{:S(2)}) %copy-start.7) | copy-done | bytes 262168
  6.1 0.8 %pad_maximum_fusion.1 = bf16[12,128,128]{2,1,0:T(8,128)(2,1)} fusion(bf16[4,128,128]{2,1,0:T(8,128)(2,1)S(1)} %dynamic-slice_bitcast_fusion, bf16[8,128,128]{2,1,0:T(8,128)(2,1)S(1)} %convolution_convert_fusion.3), kind=kLoop, calls=%fused_computation.57 | loop fusion | flops 196608 | bytes 786432 | tf_op jit(solution)/shard_map/concatenate | solution.py:132
  6.9 2.9 %collective-permute-start.1 = (bf16[12,128,128]{2,1,0:T(8,128)(2,1)}, bf16[12,128,128]{2,1,0:T(8,128)(2,1)}, u32[]{:S(2)}, u32[]{:S(2)}) collective-permute-start(bf16[12,128,128]{2,1,0:T(8,128)(2,1)} %pad_maximum_fusion.1), channel_id=1, source_target_pairs={{0,1},{1,0},{2,3},{3,2},{4,5},{5,4},{6,7},{7,6},{8,9},{9,8},{10,11... | collective-permute-start | bytes 1179656 | tf_op jit(solution)/shard_map/ppermute | solution.py:15
  10.5 0.8 %fusion.74 = (bf16[2,2,128,128]{3,2,0,1:T(8,128)(2,1)}, bf16[2,2,128,128]{3,2,0,1:T(8,128)(2,1)}, bf16[2,2,128,128]{3,2,0,1:T(8,128)(2,1)S(1)}) fusion(s32[]{:T(128)S(6)} %select_n.270, bf16[4,2,1,128,128]{4,3,1,2,0:T(8,128)(2,1)S(1)} %bitcast.184, bf16[4,2,1,128,128]{4,3,1,2,0:T(8,128)(2,1)S(1)} %bitcast.186, s32[]{:T(128)S(6)} %select_n.271, s32[]{:T(128)S(6)} %select_n.272), kind=kLoop, calls=%fused_computation.113 | loop fusion | flops 196608 | bytes 917516 | tf_op jit(solution)/shard_map/jit(dynamic_index_in_dim)/squeeze | solution.py:98
  11.2 3.6 %collective-permute-start.5 = (bf16[2,2,128,128]{3,2,0,1:T(8,128)(2,1)}, bf16[2,2,128,128]{3,2,0,1:T(8,128)(2,1)S(1)}, u32[]{:S(2)}, u32[]{:S(2)}) collective-permute-start(bf16[2,2,128,128]{3,2,0,1:T(8,128)(2,1)} %get-tuple-element.15), channel_id=1, source_target_pairs={{0,6},{1,7},{2,4},{3,5},{4,2},{5,3},{6,0},{7,1},{8,14},{9,15},{10,... | collective-permute-start | bytes 393224 | tf_op jit(solution)/shard_map/ppermute | solution.py:15
  14.8 0.8 %collective-permute-start.7 = (bf16[2,2,128,128]{3,2,0,1:T(8,128)(2,1)S(1)}, bf16[2,2,128,128]{3,2,0,1:T(8,128)(2,1)S(1)}, u32[]{:S(2)}, u32[]{:S(2)}) collective-permute-start(bf16[2,2,128,128]{3,2,0,1:T(8,128)(2,1)S(1)} %get-tuple-element.17), channel_id=1, source_target_pairs={{0,2},{1,3},{2,0},{3,1},{4,6},{5,7},{6,4},{7,5},{8,10},{9,11},{10,... | collective-permute-start | bytes 393224 | tf_op jit(solution)/shard_map/ppermute | solution.py:15
  15.6 1.0 %convolution_convert_fusion.4 = bf16[8,128,128]{2,1,0:T(8,128)(2,1)} fusion(bf16[128,8,128]{0,2,1:T(8,128)(2,1)S(1)} %bitcast.170, bf16[128,8,128]{0,2,1:T(8,128)(2,1)S(1)} %bitcast.192, bf16[128,8,128]{0,2,1:T(8,128)(2,1)S(1)} %bitcast.158, bf16[128,8,128]{0,2,1:T(8,128)(2,1)S(1)} %bitcast.178, f32[128,8]{0,1:T(8,128)S(1)} %bitcast.204, pred[]{:T(512)S(6)} %eq.128), kind=kOutput, calls=%fused_computation.29 | convolution fusion | flops 34340864 | bytes 1314817 | tf_op jit(solution)/shard_map/thd,the->hde/dot_general | solution.py:85
  17.3 2.3 %convolution_bitcast_fusion.1 = f32[128,8,128]{0,2,1:T(8,128)} fusion(bf16[128,8,128]{0,2,1:T(8,128)(2,1)S(1)} %bitcast.159, bf16[128,8,128]{0,2,1:T(8,128)(2,1)S(1)} %bitcast.193, bf16[128,8,128]{0,2,1:T(8,128)(2,1)S(1)} %bitcast.171, f32[8,128]{1,0:T(8,128)S(1)} %bitcast.208, f32[8,128]{1,0:T(8,128)S(1)} %bitcast.210, f32[8,128]{1,0:T(8,128)S(1)} %bitcast.212, ...), kind=kOutput, calls=%fused_computation.1 | convolution fusion | flops 69337088 | bytes 1474560 | tf_op jit(solution)/shard_map/hts,the->she/dot_general | solution.py:164
  19.5 1.4 %fusion.13 = bf16[8,128,128]{2,1,0:T(8,128)(2,1)S(1)} fusion(bf16[128,8,128]{0,2,1:T(8,128)(2,1)S(1)} %bitcast.160, bf16[128,8,128]{0,2,1:T(8,128)(2,1)S(1)} %bitcast.179, f32[8,128]{1,0:T(8,128)S(1)} %bitcast.209, f32[8,128]{1,0:T(8,128)S(1)} %bitcast.211, f32[8,128]{1,0:T(8,128)S(1)} %bitcast.213, f32[8,128]{1,0:T(8,128)S(1)} %bitcast.215, ...), kind=kOutput, calls=%fused_computation.30 | convolution fusion | flops 35782656 | bytes 950272 | tf_op jit(solution)/shard_map/the,she->hts/dot_general | solution.py:152
  21.5 4.3 %collective-permute-done.6 = bf16[2,2,128,128]{3,2,0,1:T(8,128)(2,1)S(1)} collective-permute-done((bf16[2,2,128,128]{3,2,0,1:T(8,128)(2,1)}, bf16[2,2,128,128]{3,2,0,1:T(8,128)(2,1)S(1)}, u32[]{:S(2)}, u32[]{:S(2)}) %collective-permute-start.6) | collective-permute-done | bytes 131104 | tf_op jit(solution)/shard_map/ppermute | solution.py:15
  26.0 1.3 %collective-permute-done.8 = bf16[2,2,128,128]{3,2,0,1:T(8,128)(2,1)S(1)} collective-permute-done((bf16[2,2,128,128]{3,2,0,1:T(8,128)(2,1)S(1)}, bf16[2,2,128,128]{3,2,0,1:T(8,128)(2,1)S(1)}, u32[]{:S(2)}, u32[]{:S(2)}) %collective-permute-start.8) | collective-permute-done | bytes 131104 | tf_op jit(solution)/shard_map/ppermute | solution.py:15
  27.4 1.6 %collective-permute-start.9 = (bf16[2,1,128,128]{3,2,0,1:T(8,128)(2,1)S(1)}, bf16[2,1,128,128]{3,2,0,1:T(8,128)(2,1)S(1)}, u32[]{:S(2)}, u32[]{:S(2)}) collective-permute-start(bf16[2,1,128,128]{3,2,0,1:T(8,128)(2,1)S(1)} %fusion.77), channel_id=1, source_target_pairs={{0,16},{8,24},{16,0},{24,8},{1,17},{9,25},{17,1},{25,9},{2,18},{10... | collective-permute-start | bytes 196616 | tf_op jit(solution)/shard_map/ppermute | solution.py:15
  29.0 2.7 %collective-permute-done.9 = bf16[2,1,128,128]{3,2,0,1:T(8,128)(2,1)S(1)} collective-permute-done((bf16[2,1,128,128]{3,2,0,1:T(8,128)(2,1)S(1)}, bf16[2,1,128,128]{3,2,0,1:T(8,128)(2,1)S(1)}, u32[]{:S(2)}, u32[]{:S(2)}) %collective-permute-start.9) | collective-permute-done | bytes 65568 | tf_op jit(solution)/shard_map/ppermute | solution.py:15
  32.3 1.1 %convert_element_type.452 = f32[12,128,128]{2,1,0:T(8,128)S(1)} convert(bf16[12,128,128]{2,1,0:T(8,128)(2,1)} %collective-permute-done.1) | non-fusion elementwise | flops 196608 | bytes 1179648 | tf_op jit(solution)/shard_map/convert_element_type | solution.py:67
  33.5 3.3 %collective-permute-done.10 = bf16[2,2,128,128]{3,2,0,1:T(8,128)(2,1)S(1)} collective-permute-done((bf16[2,2,128,128]{3,2,0,1:T(8,128)(2,1)S(1)}, bf16[2,2,128,128]{3,2,0,1:T(8,128)(2,1)S(1)}, u32[]{:S(2)}, u32[]{:S(2)}) %collective-permute-start.10) | collective-permute-done | bytes 131104 | tf_op jit(solution)/shard_map/ppermute | solution.py:15
  36.8 2.6 %collective-permute-start.11 = (bf16[2,2,128,128]{3,2,0,1:T(8,128)(2,1)S(1)}, bf16[2,2,128,128]{3,2,0,1:T(8,128)(2,1)S(1)}, u32[]{:S(2)}, u32[]{:S(2)}) collective-permute-start(bf16[2,2,128,128]{3,2,0,1:T(8,128)(2,1)S(1)} %add_convert_fusion.1), channel_id=1, source_target_pairs={{0,6},{1,7},{2,4},{3,5},{4,2},{5,3},{6,0},{7,1},{8,14},{9,15},{10,... | collective-permute-start | bytes 393224 | tf_op jit(solution)/shard_map/ppermute | solution.py:15
  39.4 1.9 %collective-permute-start.13 = (bf16[2,2,128,128]{3,2,0,1:T(8,128)(2,1)S(1)}, bf16[2,2,128,128]{3,2,0,1:T(8,128)(2,1)S(1)}, u32[]{:S(2)}, u32[]{:S(2)}) collective-permute-start(bf16[2,2,128,128]{3,2,0,1:T(8,128)(2,1)S(1)} %add_convert_fusion.1), channel_id=1, source_target_pairs={{0,2},{1,3},{2,0},{3,1},{4,6},{5,7},{6,4},{7,5},{8,10},{9,11},{10,... | collective-permute-start | bytes 393224 | tf_op jit(solution)/shard_map/ppermute | solution.py:15
  41.6 3.5 %collective-permute-done.11 = bf16[2,2,128,128]{3,2,0,1:T(8,128)(2,1)S(1)} collective-permute-done((bf16[2,2,128,128]{3,2,0,1:T(8,128)(2,1)S(1)}, bf16[2,2,128,128]{3,2,0,1:T(8,128)(2,1)S(1)}, u32[]{:S(2)}, u32[]{:S(2)}) %collective-permute-start.11) | collective-permute-done | bytes 131104 | tf_op jit(solution)/shard_map/ppermute | solution.py:15
  45.1 3.9 %collective-permute-done.12 = bf16[2,2,128,128]{3,2,0,1:T(8,128)(2,1)S(1)} collective-permute-done((bf16[2,2,128,128]{3,2,0,1:T(8,128)(2,1)S(1)}, bf16[2,2,128,128]{3,2,0,1:T(8,128)(2,1)S(1)}, u32[]{:S(2)}, u32[]{:S(2)}) %collective-permute-start.12) | collective-permute-done | bytes 131104 | tf_op jit(solution)/shard_map/ppermute | solution.py:15
  50.0 6.0 %collective-permute-done.2 = bf16[12,128,128]{2,1,0:T(8,128)(2,1)S(1)} collective-permute-done((bf16[12,128,128]{2,1,0:T(8,128)(2,1)S(1)}, bf16[12,128,128]{2,1,0:T(8,128)(2,1)S(1)}, u32[]{:S(2)}, u32[]{:S(2)}) %collective-permute-start.2) | collective-permute-done | bytes 393248 | tf_op jit(solution)/shard_map/ppermute | solution.py:15
  56.0 0.8 %collective-permute-start.3 = (bf16[4,128,128]{2,1,0:T(8,128)(2,1)S(1)}, bf16[4,128,128]{2,1,0:T(8,128)(2,1)S(1)}, u32[]{:S(2)}, u32[]{:S(2)}) collective-permute-start(bf16[4,128,128]{2,1,0:T(8,128)(2,1)S(1)} %add_convert_fusion.2), channel_id=1, source_target_pairs={{0,4},{1,5},{2,6},{3,7},{4,0},{5,1},{6,2},{7,3},{8,12},{9,13},{10,... | collective-permute-start | bytes 393224 | tf_op jit(solution)/shard_map/ppermute | solution.py:15
  57.0 6.4 %collective-permute-done.3 = bf16[4,128,128]{2,1,0:T(8,128)(2,1)S(1)} collective-permute-done((bf16[4,128,128]{2,1,0:T(8,128)(2,1)S(1)}, bf16[4,128,128]{2,1,0:T(8,128)(2,1)S(1)}, u32[]{:S(2)}, u32[]{:S(2)}) %collective-permute-start.3) | collective-permute-done | bytes 131104 | tf_op jit(solution)/shard_map/ppermute | solution.py:15
  64.0 1.2 %fusion.2 = f32[128,8,128]{0,2,1:T(8,128)S(1)} fusion(f32[128,8,128]{0,2,1:T(8,128)S(1)} %fusion.11, f32[128,8,128]{0,2,1:T(8,128)S(1)} %convolution_bitcast_fusion.9, bf16[8,128,128]{2,1,0:T(8,128)(2,1)} %collective-permute-done, bf16[128,8,128]{0,2,1:T(8,128)(2,1)S(1)} %bitcast.164, f32[128,8]{0,1:T(8,128)S(1)} %broadcast_select_fusion.14), kind=kOutput, calls=%fused_computation.12 | convolution fusion | flops 33947648 | bytes 2101248 | tf_op jit(solution)/shard_map/the,hde->thd/dot_general | solution.py:169
  65.2 3.2 %collective-permute-done.4 = bf16[4,128,128]{2,1,0:T(8,128)(2,1)S(1)} collective-permute-done((bf16[4,128,128]{2,1,0:T(8,128)(2,1)S(1)}, bf16[4,128,128]{2,1,0:T(8,128)(2,1)S(1)}, u32[]{:S(2)}, u32[]{:S(2)}) %collective-permute-start.4) | collective-permute-done | bytes 131104 | tf_op jit(solution)/shard_map/ppermute | solution.py:15
  68.4 1.3 %add_convert_fusion = bf16[8,128,128]{2,1,0:T(8,128)(2,1)S(1)} fusion(bf16[8,128,128]{2,1,0:T(8,128)(2,1)} %collective-permute-done, bf16[12,128,128]{2,1,0:T(8,128)(2,1)S(1)} %collective-permute-done.2, pred[]{:T(512)S(6)} %eq.135, pred[]{:T(512)S(6)} %eq.132, pred[]{:T(512)S(6)} %eq.130, pred[]{:T(512)S(6)} %eq.129, pred[]{:T(512)S(6)} %eq.128, ...), kind=kLoop, calls=%fused_computation.55 | loop fusion | flops 2097152 | bytes 1572869 | tf_op jit(solution)/shard_map/convert_element_type | solution.py:70
  70.0 0.8 %copy.91 = bf16[128,1024]{1,0:T(8,128)(2,1)} copy(bf16[128,1024]{0,1:T(8,128)(2,1)S(1)} %bitcast.183) | data formatting | bytes 524288
  71.2 0.8 %copy.90 = bf16[128,1024]{1,0:T(8,128)(2,1)} copy(bf16[128,1024]{0,1:T(8,128)(2,1)S(1)} %bitcast.182) | data formatting | bytes 524288
  72.3 0.8 %copy.89 = bf16[128,1024]{1,0:T(8,128)(2,1)} copy(bf16[128,1024]{0,1:T(8,128)(2,1)S(1)} %bitcast.181) | data formatting | bytes 524288
  (65 shorter events, 7.0 us)
Async XLA Ops:
  0.6 0.9 %copy-start = (f32[32,20,8]{0,2,1:T(8,128)S(1)}, f32[32,20,8]{0,2,1:T(8,128)}, u32[]{:S(2)}) copy-start(f32[32,20,8]{0,2,1:T(8,128)} %param.11) | copy-start | bytes 61444
  0.6 1.8 %copy-start.4 = (bf16[128,1024]{1,0:T(8,128)(2,1)S(1)}, bf16[128,1024]{1,0:T(8,128)(2,1)}, u32[]{:S(2)}) copy-start(bf16[128,1024]{1,0:T(8,128)(2,1)} %param.9) | copy-start | bytes 786436
  2.4 1.0 %copy-start.5 = (bf16[128,1024]{1,0:T(8,128)(2,1)S(1)}, bf16[128,1024]{1,0:T(8,128)(2,1)}, u32[]{:S(2)}) copy-start(bf16[128,1024]{1,0:T(8,128)(2,1)} %param.7) | copy-start | bytes 786436
  3.4 0.9 %copy-start.6 = (bf16[128,1024]{1,0:T(8,128)(2,1)S(1)}, bf16[128,1024]{1,0:T(8,128)(2,1)}, u32[]{:S(2)}) copy-start(bf16[128,1024]{1,0:T(8,128)(2,1)} %param.8) | copy-start | bytes 786436
  4.3 0.9 %copy-start.7 = (bf16[128,1024]{1,0:T(8,128)(2,1)S(1)}, bf16[128,1024]{1,0:T(8,128)(2,1)}, u32[]{:S(2)}) copy-start(bf16[128,1024]{1,0:T(8,128)(2,1)} %param.6) | copy-start | bytes 786436
  5.3 14.2 %copy-start.1 = (bf16[128,1024]{0,1:T(8,128)(2,1)}, bf16[128,1024]{0,1:T(8,128)(2,1)S(1)}, u32[]{:S(2)}) copy-start(bf16[128,1024]{0,1:T(8,128)(2,1)S(1)} %copy.104) | copy-start | bytes 786436
  6.9 25.5 %collective-permute-start.1 = (bf16[12,128,128]{2,1,0:T(8,128)(2,1)}, bf16[12,128,128]{2,1,0:T(8,128)(2,1)}, u32[]{:S(2)}, u32[]{:S(2)}) collective-permute-start(bf16[12,128,128]{2,1,0:T(8,128)(2,1)} %pad_maximum_fusion.1), channel_id=1, source_target_pairs={{0,1},{1,0},{2,3},{3,2},{4,5},{5,4},{6,7},{7,6},{8,9},{9,8},{10,11... | collective-permute-start | bytes 1179656 | tf_op jit(solution)/shard_map/ppermute | solution.py:15
  11.2 10.3 %collective-permute-start.5 = (bf16[2,2,128,128]{3,2,0,1:T(8,128)(2,1)}, bf16[2,2,128,128]{3,2,0,1:T(8,128)(2,1)S(1)}, u32[]{:S(2)}, u32[]{:S(2)}) collective-permute-start(bf16[2,2,128,128]{3,2,0,1:T(8,128)(2,1)} %get-tuple-element.15), channel_id=1, source_target_pairs={{0,6},{1,7},{2,4},{3,5},{4,2},{5,3},{6,0},{7,1},{8,14},{9,15},{10,... | collective-permute-start | bytes 393224 | tf_op jit(solution)/shard_map/ppermute | solution.py:15
  14.8 11.0 %collective-permute-start.6 = (bf16[2,2,128,128]{3,2,0,1:T(8,128)(2,1)}, bf16[2,2,128,128]{3,2,0,1:T(8,128)(2,1)S(1)}, u32[]{:S(2)}, u32[]{:S(2)}) collective-permute-start(bf16[2,2,128,128]{3,2,0,1:T(8,128)(2,1)} %get-tuple-element.16), channel_id=1, source_target_pairs={{0,4},{1,5},{2,6},{3,7},{4,0},{5,1},{6,2},{7,3},{8,12},{9,13},{10,... | collective-permute-start | bytes 393224 | tf_op jit(solution)/shard_map/ppermute | solution.py:15
  14.8 11.0 %collective-permute-start.7 = (bf16[2,2,128,128]{3,2,0,1:T(8,128)(2,1)S(1)}, bf16[2,2,128,128]{3,2,0,1:T(8,128)(2,1)S(1)}, u32[]{:S(2)}, u32[]{:S(2)}) collective-permute-start(bf16[2,2,128,128]{3,2,0,1:T(8,128)(2,1)S(1)} %get-tuple-element.17), channel_id=1, source_target_pairs={{0,2},{1,3},{2,0},{3,1},{4,6},{5,7},{6,4},{7,5},{8,10},{9,11},{10,... | collective-permute-start | bytes 393224 | tf_op jit(solution)/shard_map/ppermute | solution.py:15
  16.6 47.4 %collective-permute-start = (bf16[8,128,128]{2,1,0:T(8,128)(2,1)}, bf16[8,128,128]{2,1,0:T(8,128)(2,1)}, u32[]{:S(2)}, u32[]{:S(2)}) collective-permute-start(bf16[8,128,128]{2,1,0:T(8,128)(2,1)} %convolution_convert_fusion.4), channel_id=1, source_target_pairs={{0,1},{1,0},{2,3},{3,2},{4,5},{5,4},{6,7},{7,6},{8,9},{9,8},{10,11... | collective-permute-start | bytes 786440 | tf_op jit(solution)/shard_map/ppermute | solution.py:15
  25.9 1.4 %collective-permute-start.8 = (bf16[2,2,128,128]{3,2,0,1:T(8,128)(2,1)S(1)}, bf16[2,2,128,128]{3,2,0,1:T(8,128)(2,1)S(1)}, u32[]{:S(2)}, u32[]{:S(2)}) collective-permute-start(bf16[2,2,128,128]{3,2,0,1:T(8,128)(2,1)S(1)} %get-tuple-element.9), channel_id=1, source_target_pairs={{0,8},{8,0},{16,24},{24,16},{1,9},{9,1},{17,25},{25,17},{2,10},{10... | collective-permute-start | bytes 393224 | tf_op jit(solution)/shard_map/ppermute | solution.py:15
  27.4 4.3 %collective-permute-start.9 = (bf16[2,1,128,128]{3,2,0,1:T(8,128)(2,1)S(1)}, bf16[2,1,128,128]{3,2,0,1:T(8,128)(2,1)S(1)}, u32[]{:S(2)}, u32[]{:S(2)}) collective-permute-start(bf16[2,1,128,128]{3,2,0,1:T(8,128)(2,1)S(1)} %fusion.77), channel_id=1, source_target_pairs={{0,16},{8,24},{16,0},{24,8},{1,17},{9,25},{17,1},{25,9},{2,18},{10... | collective-permute-start | bytes 196616 | tf_op jit(solution)/shard_map/ppermute | solution.py:15
  31.7 5.0 %collective-permute-start.10 = (bf16[2,2,128,128]{3,2,0,1:T(8,128)(2,1)S(1)}, bf16[2,2,128,128]{3,2,0,1:T(8,128)(2,1)S(1)}, u32[]{:S(2)}, u32[]{:S(2)}) collective-permute-start(bf16[2,2,128,128]{3,2,0,1:T(8,128)(2,1)S(1)} %fusion.67), channel_id=1, source_target_pairs={{0,1},{1,0},{2,3},{3,2},{4,5},{5,4},{6,7},{7,6},{8,9},{9,8},{10,11... | collective-permute-start | bytes 393224 | tf_op jit(solution)/shard_map/ppermute | solution.py:15
  36.8 8.3 %collective-permute-start.11 = (bf16[2,2,128,128]{3,2,0,1:T(8,128)(2,1)S(1)}, bf16[2,2,128,128]{3,2,0,1:T(8,128)(2,1)S(1)}, u32[]{:S(2)}, u32[]{:S(2)}) collective-permute-start(bf16[2,2,128,128]{3,2,0,1:T(8,128)(2,1)S(1)} %add_convert_fusion.1), channel_id=1, source_target_pairs={{0,6},{1,7},{2,4},{3,5},{4,2},{5,3},{6,0},{7,1},{8,14},{9,15},{10,... | collective-permute-start | bytes 393224 | tf_op jit(solution)/shard_map/ppermute | solution.py:15
  39.4 9.6 %collective-permute-start.12 = (bf16[2,2,128,128]{3,2,0,1:T(8,128)(2,1)S(1)}, bf16[2,2,128,128]{3,2,0,1:T(8,128)(2,1)S(1)}, u32[]{:S(2)}, u32[]{:S(2)}) collective-permute-start(bf16[2,2,128,128]{3,2,0,1:T(8,128)(2,1)S(1)} %add_convert_fusion.1), channel_id=1, source_target_pairs={{0,4},{1,5},{2,6},{3,7},{4,0},{5,1},{6,2},{7,3},{8,12},{9,13},{10,... | collective-permute-start | bytes 393224 | tf_op jit(solution)/shard_map/ppermute | solution.py:15
  39.4 10.0 %collective-permute-start.13 = (bf16[2,2,128,128]{3,2,0,1:T(8,128)(2,1)S(1)}, bf16[2,2,128,128]{3,2,0,1:T(8,128)(2,1)S(1)}, u32[]{:S(2)}, u32[]{:S(2)}) collective-permute-start(bf16[2,2,128,128]{3,2,0,1:T(8,128)(2,1)S(1)} %add_convert_fusion.1), channel_id=1, source_target_pairs={{0,2},{1,3},{2,0},{3,1},{4,6},{5,7},{6,4},{7,5},{8,10},{9,11},{10,... | collective-permute-start | bytes 393224 | tf_op jit(solution)/shard_map/ppermute | solution.py:15
  41.3 14.6 %collective-permute-start.2 = (bf16[12,128,128]{2,1,0:T(8,128)(2,1)S(1)}, bf16[12,128,128]{2,1,0:T(8,128)(2,1)S(1)}, u32[]{:S(2)}, u32[]{:S(2)}) collective-permute-start(bf16[12,128,128]{2,1,0:T(8,128)(2,1)S(1)} %pad_maximum_fusion.2), channel_id=1, source_target_pairs={{0,2},{1,3},{2,0},{3,1},{4,6},{5,7},{6,4},{7,5},{8,10},{9,11},{10,... | collective-permute-start | bytes 1179656 | tf_op jit(solution)/shard_map/ppermute | solution.py:15
  56.0 7.4 %collective-permute-start.3 = (bf16[4,128,128]{2,1,0:T(8,128)(2,1)S(1)}, bf16[4,128,128]{2,1,0:T(8,128)(2,1)S(1)}, u32[]{:S(2)}, u32[]{:S(2)}) collective-permute-start(bf16[4,128,128]{2,1,0:T(8,128)(2,1)S(1)} %add_convert_fusion.2), channel_id=1, source_target_pairs={{0,4},{1,5},{2,6},{3,7},{4,0},{5,1},{6,2},{7,3},{8,12},{9,13},{10,... | collective-permute-start | bytes 393224 | tf_op jit(solution)/shard_map/ppermute | solution.py:15
  63.4 5.0 %collective-permute-start.4 = (bf16[4,128,128]{2,1,0:T(8,128)(2,1)S(1)}, bf16[4,128,128]{2,1,0:T(8,128)(2,1)S(1)}, u32[]{:S(2)}, u32[]{:S(2)}) collective-permute-start(bf16[4,128,128]{2,1,0:T(8,128)(2,1)S(1)} %collective-permute-done.3), channel_id=1, source_target_pairs={{0,1},{1,0},{2,3},{3,2},{4,5},{5,4},{6,7},{7,6},{8,9},{9,8},{10,11... | collective-permute-start | bytes 393224 | tf_op jit(solution)/shard_map/ppermute | solution.py:15
  68.4 1.3 %copy-start.3 = (f32[128,8,128]{0,2,1:T(8,128)S(1)}, f32[128,8,128]{0,2,1:T(8,128)}, u32[]{:S(2)}) copy-start(f32[128,8,128]{0,2,1:T(8,128)} %convolution_bitcast_fusion.1) | copy-start | bytes 1572868
  70.0 1.0 %copy-start.2 = (bf16[128,1024]{0,1:T(8,128)(2,1)S(1)}, bf16[128,1024]{0,1:T(8,128)(2,1)}, u32[]{:S(2)}) copy-start(bf16[128,1024]{0,1:T(8,128)(2,1)} %copy-done.1) | copy-start | bytes 786436

commit v2 on v1

v2 whole, which is shorter than its diff:
```python
import functools

import jax
import jax.numpy as jnp
from jax import lax
from jax.experimental import pallas as pl
from jax.experimental.pallas import tpu as pltpu
from jax.sharding import PartitionSpec as P

NEAR = 3
VMEM_BYTES = 48 * 1024 * 1024


def level_bits(amount):
    return amount.bit_length() - 1


def wide(values):
    return values.astype(jnp.float32)


def narrow(values):
    return values.astype(jnp.bfloat16)


def product(left, right, left_dim, right_dim):
    return lax.dot_general(
        left,
        right,
        (((left_dim,), (right_dim,)), ((), ())),
        preferred_element_type=jnp.float32,
    )


def gate_lanes(class_ref, table_ref, first, last):
    classes = table_ref.shape[2]
    tokens = class_ref.shape[1]
    rows = (last - first) * table_ref.shape[1]
    numbers = lax.broadcasted_iota(jnp.int32, (classes, tokens), 0)
    picker = (numbers == class_ref[...]).astype(jnp.float32)
    table = table_ref[first:last].reshape(rows, classes)
    return jnp.dot(
        table, picker, precision=lax.Precision.HIGHEST, preferred_element_type=jnp.float32
    )


def payload_kernel(
    levels, offset, head_size, flag_ref, class_ref, table_ref, q_ref, k_ref, v_ref, g_ref, out_ref
):
    head_count = table_ref.shape[1]
    gates = gate_lanes(class_ref, table_ref, offset + levels[0], offset + levels[-1] + 1)
    for head in range(head_count):
        columns = pl.ds(head * head_size, head_size)
        query_turned = wide(q_ref[:, columns].T)
        key_turned = wide(k_ref[:, columns].T)
        grad_here = g_ref[:, columns]
        value_here = v_ref[:, columns]
        for place, level in enumerate(levels):
            row = place * head_count + head
            flag = flag_ref[level] == 1
            left = jnp.where(flag, gates[row : row + 1, :] * query_turned, key_turned)
            right = jnp.where(flag, wide(grad_here), wide(value_here))
            out_ref[place, head] = narrow(product(narrow(left), narrow(right), 1, 0))


def local_kernel(
    block_depth, head_size, class_ref, table_ref, q_ref, k_ref, v_ref, g_ref, qo_ref, ko_ref, vo_ref
):
    head_count = table_ref.shape[1]
    tokens = q_ref.shape[0]
    gates = gate_lanes(class_ref, table_ref, 0, block_depth + 1)
    source = lax.broadcasted_iota(jnp.int32, (tokens, tokens), 0)
    target = lax.broadcasted_iota(jnp.int32, (tokens, tokens), 1)
    apart = jnp.bitwise_xor(source, target)
    causal = source <= target
    for head in range(head_count):
        columns = pl.ds(head * head_size, head_size)
        query_here = q_ref[:, columns]
        key_here = k_ref[:, columns]
        value_here = v_ref[:, columns]
        grad_here = g_ref[:, columns]
        weight = jnp.broadcast_to(gates[head : head + 1, :], (tokens, tokens))
        for level in range(1, block_depth + 1):
            row = level * head_count + head
            weight = jnp.where(apart >= 2 ** (level - 1), gates[row : row + 1, :], weight)
        weight = jnp.where(causal, weight, 0.0)
        weighted_scores = narrow(weight * product(key_here, query_here, 1, 1))
        weighted_grads = narrow(weight * product(value_here, grad_here, 1, 1))
        qo_ref[:, columns] = product(weighted_grads, key_here, 0, 0)
        ko_ref[:, columns] = product(weighted_grads, query_here, 1, 0)
        vo_ref[:, columns] = product(weighted_scores, grad_here, 1, 0)


def gate_columns(class_ref, table_ref, first, last):
    return gate_lanes(class_ref, table_ref, first, last).T


def final_kernel(
    offset,
    head_size,
    total,
    inner,
    flag_ref,
    class_ref,
    table_ref,
    k_ref,
    v_ref,
    g_ref,
    ql_ref,
    kl_ref,
    vl_ref,
    zero_ref,
    one_ref,
    two_own_ref,
    two_other_ref,
    piece0_ref,
    piece1_ref,
    piece2_ref,
    piece3_ref,
    split_own_ref,
    split_other_ref,
    qo_ref,
    ko_ref,
    vo_ref,
    held_ref,
):
    head_count = table_ref.shape[1]
    half = head_count // 2
    quarter = head_count // 4
    eighth = head_count // 8
    gates = gate_columns(class_ref, table_ref, offset, offset + total)
    x_place = flag_ref[0]
    z_place = flag_ref[1] + 2 * flag_ref[2]
    core = flag_ref[inner]
    held_ref[0] = zero_ref[...]
    held_ref[1] = one_ref[...]
    held_ref[2, pl.ds(x_place * half, half)] = two_own_ref[...]
    held_ref[2, pl.ds((1 - x_place) * half, half)] = two_other_ref[...]
    pieces = (piece0_ref, piece1_ref, piece2_ref, piece3_ref)
    split = inner + 1
    for level in range(NEAR, split):
        for offs in range(4):
            first = jnp.bitwise_xor(z_place, offs) * quarter
            held_ref[level, pl.ds(first, quarter)] = pieces[offs][level - NEAR]
    for level in range(split, total):
        for offs in range(4):
            first = jnp.bitwise_xor(z_place, offs) * eighth
            rows = pl.ds(offs * eighth, eighth)
            held_ref[level, pl.ds(core * half + first, eighth)] = split_own_ref[level - split, rows]
            held_ref[level, pl.ds((1 - core) * half + first, eighth)] = split_other_ref[
                level - split, rows
            ]
    for head in range(head_count):
        columns = pl.ds(head * head_size, head_size)
        grad_here = g_ref[:, columns]
        query_total = ql_ref[:, columns]
        state_grad = jnp.zeros((head_size, head_size), jnp.float32)
        for level in range(total):
            state = held_ref[level, head]
            term = product(grad_here, state, 1, 1)
            row = level * head_count + head
            on = wide(flag_ref[level])
            query_total = query_total + (gates[:, row : row + 1] * on) * term
            state_grad = state_grad + wide(state) * (1.0 - on)
        grad_rounded = narrow(state_grad)
        qo_ref[:, columns] = narrow(query_total)
        ko_ref[:, columns] = narrow(
            kl_ref[:, columns] + product(v_ref[:, columns], grad_rounded, 1, 1)
        )
        vo_ref[:, columns] = narrow(
            vl_ref[:, columns] + product(k_ref[:, columns], grad_rounded, 1, 0)
        )


def per_device(query_rows, key_rows, value_rows, out_grad, gate_class, gate_table):
    row_count, width = query_rows.shape
    head_count = gate_table.shape[2]
    head_size = width // head_count
    inner_bits = level_bits(lax.axis_size("gy"))
    outer_bits = level_bits(lax.axis_size("gx"))
    total = inner_bits + outer_bits
    block_depth = level_bits(row_count)
    offset = block_depth + 1
    inner_index = lax.axis_index("gy")
    outer_index = lax.axis_index("gx")
    block_index = (outer_index << inner_bits) | inner_index
    flag_bits = (block_index >> jnp.arange(total, dtype=jnp.int32)) & 1
    inner_size = lax.axis_size("gy")
    device_count = inner_size * lax.axis_size("gx")

    def swap(block, *bits):
        mask = sum(1 << bit for bit in bits)
        if mask < inner_size:
            return lax.ppermute(block, "gy", [(i, i ^ mask) for i in range(inner_size)])
        if mask % inner_size == 0:
            mask = mask // inner_size
            size = lax.axis_size("gx")
            return lax.ppermute(block, "gx", [(i, i ^ mask) for i in range(size)])
        return lax.ppermute(block, ("gx", "gy"), [(i, i ^ mask) for i in range(device_count)])

    class_lanes = gate_class.reshape(1, row_count)
    table = jnp.transpose(gate_table, (1, 2, 0))
    smem = pl.BlockSpec(memory_space=pltpu.SMEM)
    vmem = pl.BlockSpec(memory_space=pltpu.VMEM)
    cell = (head_size, head_size)
    params = pltpu.CompilerParams(vmem_limit_bytes=VMEM_BYTES)

    def payloads(levels):
        flops = 2 * len(levels) * row_count * width * head_size
        return pl.pallas_call(
            functools.partial(payload_kernel, levels, offset, head_size),
            out_shape=jax.ShapeDtypeStruct((len(levels), head_count) + cell, jnp.bfloat16),
            in_specs=[smem] + [vmem] * 6,
            out_specs=vmem,
            compiler_params=params,
            cost_estimate=pl.CostEstimate(
                flops=flops, bytes_accessed=10 * row_count * width, transcendentals=0
            ),
        )(flag_bits, class_lanes, table, query_rows, key_rows, value_rows, out_grad)

    quarter = head_count // 4
    half = head_count // 2
    eighth = head_count // 8
    z_place = (inner_index >> 1) & 3
    x_place = inner_index & 1
    core = outer_index & 1
    split = inner_bits + 1
    whole_levels = split - NEAR
    split_levels = total - split

    upper = payloads(tuple(range(NEAR, total)))
    lead = upper[:whole_levels]
    late = upper[whole_levels:].reshape((split_levels, 2, half) + cell)
    late_other = lax.dynamic_index_in_dim(late, 1 - core, 1, keepdims=False)
    late_own = lax.dynamic_index_in_dim(late, core, 1, keepdims=False)
    sent = jnp.concatenate([upper[whole_levels - 1], late_other.reshape((-1,) + cell)], axis=0)
    seen = swap(sent, inner_bits)
    late_sum = narrow(wide(late_own) + wide(seen[head_count:].reshape((split_levels, half) + cell)))
    full = jnp.concatenate([lead[: whole_levels - 1], seen[None, :head_count]], axis=0)
    full = full.reshape((whole_levels, 4, quarter) + cell)
    late_sum = late_sum.reshape((split_levels, 4, eighth) + cell)

    def z_share(place):
        first = lax.dynamic_index_in_dim(full, place, 1, keepdims=False)
        second = lax.dynamic_index_in_dim(late_sum, place, 1, keepdims=False)
        return jnp.concatenate([first.reshape((-1,) + cell), second.reshape((-1,) + cell)], axis=0)

    came = [
        swap(z_share(z_place ^ offs), *[bit + 1 for bit in range(2) if offs >> bit & 1])
        for offs in (3, 2, 1)
    ]
    part = wide(z_share(z_place)) + wide(came[0]) + wide(came[1]) + wide(came[2])
    cut = whole_levels * quarter
    whole_part = part[:cut].reshape((whole_levels, quarter) + cell)
    split_part = part[cut:].reshape((split_levels, eighth) + cell)
    parts = {level: whole_part[level - NEAR] for level in range(NEAR, split)}
    parts.update({level: split_part[level - split] for level in range(split, total)})

    def flat(levels):
        return narrow(jnp.concatenate([parts[level] for level in levels], axis=0))

    for bit in range(NEAR, total - 1):
        if bit == inner_bits:
            continue
        going = [level for level in range(bit, total) if level != inner_bits or bit < inner_bits]
        seen_part = wide(swap(flat(going), bit))
        row = 0
        for level in going:
            size = parts[level].shape[0]
            got = seen_part[row : row + size]
            parts[level] = got if level == bit else parts[level] + got
            row += size
    top = total - 1
    below = list(range(NEAR, top))
    top_sent = flat([top])
    below_sent = flat(below)
    top_near = swap(top_sent, top)
    top_far = swap(top_sent, 0, top)
    below_far = swap(below_sent, 0)
    below_done = narrow(wide(below_sent) + wide(below_far))
    top_done = narrow(wide(top_near) + wide(top_far))
    shares = jnp.concatenate([below_done, top_done], axis=0)
    pieces = [shares] + [
        swap(shares, *[bit + 1 for bit in range(2) if offs >> bit & 1]) for offs in (1, 2, 3)
    ]
    split_own = jnp.stack(
        [piece[cut:].reshape((split_levels, eighth) + cell) for piece in pieces], axis=1
    ).reshape((split_levels, half) + cell)
    split_other = swap(split_own, inner_bits)
    whole_pieces = [piece[:cut].reshape((whole_levels, quarter) + cell) for piece in pieces]

    lower = payloads(tuple(range(NEAR)))
    low_two = lower[2].reshape((2, half) + cell)
    two_other = lax.dynamic_index_in_dim(low_two, 1 - x_place, 0, keepdims=False)
    two_own = lax.dynamic_index_in_dim(low_two, x_place, 0, keepdims=False)
    two_sum = wide(two_own) + wide(swap(two_other, 0))
    near_seen = swap(lower[:2], 0)
    zero_done = near_seen[0]
    one_done = swap(narrow(wide(lower[1]) + wide(near_seen[1])), 1)
    two_sum = two_sum + wide(swap(narrow(two_sum), 1))
    two_half = swap(narrow(two_sum), 2)
    two_rest = swap(two_half, 0)

    big = jax.ShapeDtypeStruct((row_count, width), jnp.float32)
    query_local, key_local, value_local = pl.pallas_call(
        functools.partial(local_kernel, block_depth, head_size),
        out_shape=(big, big, big),
        in_specs=[vmem] * 6,
        out_specs=(vmem, vmem, vmem),
        compiler_params=params,
        cost_estimate=pl.CostEstimate(
            flops=10 * row_count * width * row_count,
            bytes_accessed=20 * row_count * width,
            transcendentals=0,
        ),
    )(class_lanes, table, query_rows, key_rows, value_rows, out_grad)

    small = jax.ShapeDtypeStruct((row_count, width), jnp.bfloat16)
    return pl.pallas_call(
        functools.partial(final_kernel, offset, head_size, total, inner_bits),
        out_shape=(small, small, small),
        in_specs=[smem] + [vmem] * 18,
        out_specs=(vmem, vmem, vmem),
        scratch_shapes=[pltpu.VMEM((total, head_count) + cell, jnp.bfloat16)],
        compiler_params=params,
        cost_estimate=pl.CostEstimate(
            flops=(2 * total + 4) * row_count * width * head_size,
            bytes_accessed=24 * row_count * width,
            transcendentals=0,
        ),
    )(
        flag_bits,
        class_lanes,
        table,
        key_rows,
        value_rows,
        out_grad,
        query_local,
        key_local,
        value_local,
        zero_done,
        one_done,
        two_half,
        two_rest,
        *whole_pieces,
        split_own,
        split_other,
    )


def solution(mesh):
    rows = P(("gx", "gy"), None)
    return jax.shard_map(
        per_device,
        mesh=mesh,
        in_specs=(rows, rows, rows, rows, P(("gx", "gy")), P()),
        out_specs=(rows, rows, rows),
        check_vma=False,
    )
```

time: 73.5 us -> 58 us (0.79)
  waiting for transfers between devices: 35.2 us -> 14.7 us
  matrix products: 9.78 us -> 0 us
  starting transfers between devices: 15.9 us -> 24.3 us
  Pallas kernels: 0 us -> 7.1 us
  other arithmetic: 4.72 us -> 2.26 us
  local copies, waits for them, and re-layouts: 6.58 us -> 8.33 us
    ppermute x14 -> x17, waiting for transfers between devices: 35.2 us -> 14.7 us  [the longest x13 12 us: swap(): return lax.ppermute(block, 'gy', [(i, i ^ mask) for i in range(inner_size)])]
    dot_general x17 -> x0, matrix products: 9.78 us -> none  [the longest x1 2.26 us: per_device(): jnp.einsum('hts,the->she', weighted_scores, grad_heads, preferred_element...]
    ppermute x14 -> x17, starting transfers between devices: 15.9 us -> 24.3 us  [the longest x13 20.9 us: swap(): return lax.ppermute(block, 'gy', [(i, i ^ mask) for i in range(inner_size)])]
    pallas_call x0 -> x4, Pallas kernels: none -> 7.1 us  [the longest x1 2.81 us: per_device(): pl.pallas_call(functools.partial(final_kernel, offset, head_size, total,...]
    slice x2 -> x5, local copies, waits for them, and re-layouts: 0.05 us -> 1.84 us  [the longest x1 0.97 us: per_device(): seen[None, :head_count]]
    convert_element_type x3 -> x0, other arithmetic: 1.09 us -> none  [wide(): return values.astype(jnp.float32)]
    squeeze x0 -> x2, local copies, waits for them, and re-layouts: none -> 1 us  [the longest x1 0.97 us: per_device(): zero_done = near_seen[0]]
    concatenate x3 -> x5, other arithmetic: 0.89 us -> 0.08 us  [the longest x1 0.04 us: per_device(): jnp.concatenate([upper[whole_levels - 1], late_other.reshape((-1,) + cell...]
  transfers between devices with their start and end apart: 14 -> 17, of which waited for: 10 -> 8; matrix products, arithmetic and copies ran while one was open for 14% -> 9% of each run, Pallas kernels for 0% -> 5%
where the time goes in v2:
time: 58 us; the launch traced here: 57.6 us
  starting transfers between devices  24.3 us (42%)
  waiting for transfers between devices  14.7 us (25%)
  local copies, waits for them, and re-layouts  8.33 us (14%)
  Pallas kernels  7.1 us (12%)
  other arithmetic  2.26 us (4%)
  between operations  0.94 us (2%)
    ppermute x13, starting transfers between devices, swap(): return lax.ppermute(block, 'gy', [(i, i ^ mask) for i in range(inner_size)])  20.9 us
    ppermute x13, waiting for transfers between devices, swap(): return lax.ppermute(block, 'gy', [(i, i ^ mask) for i in range(inner_size)])  12 us
    unnamed x22, local copies, waits for them, and re-layouts  5.36 us
    pallas_call x1, Pallas kernels, per_device(): pl.pallas_call(functools.partial(final_kernel, offset, head_size, total,...  2.81 us
    ppermute x1, starting transfers between devices, swap(): lax.ppermute(block, ('gx', 'gy'), [(i, i ^ mask) for i in range(device_co...  2.76 us
    ppermute x3, waiting for transfers between devices, swap(): return lax.ppermute(block, 'gx', [(i, i ^ mask) for i in range(size)])  2.72 us
    pallas_call x2, Pallas kernels, payloads(): pl.pallas_call(functools.partial(payload_kernel, levels, offset, head_siz...  2.26 us
    convert_element_type x6, other arithmetic, narrow(): return values.astype(jnp.bfloat16)  2.1 us
  transfers between devices with their start and end apart: 17, of which 8 were waited for; matrix products, arithmetic and copies ran while one was open for 9% of the time, Pallas kernels for 5%

profile of v2, /device:TPU:0, one launch (start us, length us, event | category | flops | bytes accessed | tf_op | source)
XLA Modules:
  0.0 57.6 jit_solution(9531196433660182352)
XLA Ops:
  1.3 0.9 %copy-done = bf16[128,1024]{1,0:T(8,128)(2,1)S(1)} copy-done((bf16[128,1024]{1,0:T(8,128)(2,1)S(1)}, bf16[128,1024]{1,0:T(8,128)(2,1)}, u32[]{:S(2)}) %copy-start) | copy-done | bytes 262168
  2.3 0.9 %copy-done.2 = bf16[128,1024]{1,0:T(8,128)(2,1)S(1)} copy-done((bf16[128,1024]{1,0:T(8,128)(2,1)S(1)}, bf16[128,1024]{1,0:T(8,128)(2,1)}, u32[]{:S(2)}) %copy-start.2) | copy-done | bytes 262168
  3.2 0.9 %copy-done.4 = bf16[128,1024]{1,0:T(8,128)(2,1)S(1)} copy-done((bf16[128,1024]{1,0:T(8,128)(2,1)S(1)}, bf16[128,1024]{1,0:T(8,128)(2,1)}, u32[]{:S(2)}) %copy-start.4) | copy-done | bytes 262168
  4.2 0.9 %copy-done.6 = bf16[128,1024]{1,0:T(8,128)(2,1)S(1)} copy-done((bf16[128,1024]{1,0:T(8,128)(2,1)S(1)}, bf16[128,1024]{1,0:T(8,128)(2,1)}, u32[]{:S(2)}) %copy-start.6) | copy-done | bytes 262168
  5.1 0.9 %copy-done.8 = f32[32,20,8]{0,2,1:T(8,128)S(1)} copy-done((f32[32,20,8]{0,2,1:T(8,128)S(1)}, f32[32,20,8]{0,2,1:T(8,128)}, u32[]{:S(2)}) %copy-start.8) | copy-done | bytes 20504
  6.0 1.2 %shard_map.86 = bf16[3,8,128,128]{3,2,1,0:T(8,128)(2,1)S(1)} custom-call(s32[5]{0:T(128)S(1)} %shift-right-arithmetic_and_fusion.flag_ref, s32[1,128]{1,0:T(1,128)S(1)} %bitcast.57, f32[20,8,32]{2,1,0:T(8,128)S(1)} %bitcast.52, bf16[128,1024]{1,0:T(8,128)(2,1)S(1)} %copy-done.6, bf16[128,1024]{1,0:T(8,128)(2,1)S(1)} %copy-done, ...), custom_call_target="tpu_custom_call" | custom-call | flops 100663296 | bytes 1310720 | tf_op jit(solution)/shard_map/pallas_call | solution.py:210
  7.3 3.0 %collective-permute-start.2 = (bf16[4,128,128]{2,1,0:T(8,128)(2,1)S(1)}, bf16[4,128,128]{2,1,0:T(8,128)(2,1)S(1)}, u32[]{:S(2)}, u32[]{:S(2)}) collective-permute-start(bf16[4,128,128]{2,1,0:T(8,128)(2,1)S(1)} %dynamic-slice_bitcast_fusion.1), channel_id=1, source_target_pairs={{0,1},{1,0},{2,3},{3,2},{4,5},{5,4},{6,7},{7,6},{8,9},{9,8},{10,11... | collective-permute-start | bytes 393224 | tf_op jit(solution)/shard_map/ppermute | solution.py:194
  10.3 1.1 %shard_map.87 = bf16[2,8,128,128]{3,2,1,0:T(8,128)(2,1)S(1)} custom-call(s32[5]{0:T(128)S(1)} %shift-right-arithmetic_and_fusion.flag_ref, s32[1,128]{1,0:T(1,128)S(1)} %bitcast.58, f32[20,8,32]{2,1,0:T(8,128)S(1)} %bitcast.53, bf16[128,1024]{1,0:T(8,128)(2,1)S(1)} %copy-done.7, bf16[128,1024]{1,0:T(8,128)(2,1)S(1)} %copy-done.1, ...), custom_call_target="tpu_custom_call" | custom-call | flops 67108864 | bytes 1310720 | tf_op jit(solution)/shard_map/pallas_call | solution.py:210
  11.6 2.2 %collective-permute-done.2 = bf16[4,128,128]{2,1,0:T(8,128)(2,1)S(1)} collective-permute-done((bf16[4,128,128]{2,1,0:T(8,128)(2,1)S(1)}, bf16[4,128,128]{2,1,0:T(8,128)(2,1)S(1)}, u32[]{:S(2)}, u32[]{:S(2)}) %collective-permute-start.2) | collective-permute-done | bytes 131104 | tf_op jit(solution)/shard_map/ppermute | solution.py:194
  13.8 1.9 %collective-permute-start.3 = (bf16[4,128,128]{2,1,0:T(8,128)(2,1)S(1)}, bf16[4,128,128]{2,1,0:T(8,128)(2,1)S(1)}, u32[]{:S(2)}, u32[]{:S(2)}) collective-permute-start(bf16[4,128,128]{2,1,0:T(8,128)(2,1)S(1)} %fusion.2), channel_id=1, source_target_pairs={{0,2},{1,3},{2,0},{3,1},{4,6},{5,7},{6,4},{7,5},{8,10},{9,11},{10,... | collective-permute-start | bytes 393224 | tf_op jit(solution)/shard_map/ppermute | solution.py:194
  15.7 0.8 %slice.70 = bf16[2,8,128,128]{3,2,1,0:T(8,128)(2,1)} slice(bf16[3,8,128,128]{3,2,1,0:T(8,128)(2,1)S(1)} %shard_map.86), slice={[0:2], [0:8], [0:128], [0:128]} | slice | bytes 1048576 | tf_op jit(solution)/shard_map/slice | solution.py:297
  16.6 1.5 %collective-permute-start = (bf16[2,8,128,128]{3,2,1,0:T(8,128)(2,1)}, bf16[2,8,128,128]{3,2,1,0:T(8,128)(2,1)}, u32[]{:S(2)}, u32[]{:S(2)}) collective-permute-start(bf16[2,8,128,128]{3,2,1,0:T(8,128)(2,1)} %slice.70), channel_id=1, source_target_pairs={{0,1},{1,0},{2,3},{3,2},{4,5},{5,4},{6,7},{7,6},{8,9},{9,8},{10,11... | collective-permute-start | bytes 1572872 | tf_op jit(solution)/shard_map/ppermute | solution.py:194
  18.9 2.9 %collective-permute-start.4 = (bf16[4,128,128]{2,1,0:T(8,128)(2,1)S(1)}, bf16[4,128,128]{2,1,0:T(8,128)(2,1)S(1)}, u32[]{:S(2)}, u32[]{:S(2)}) collective-permute-start(bf16[4,128,128]{2,1,0:T(8,128)(2,1)S(1)} %add_convert_fusion.1), channel_id=1, source_target_pairs={{0,4},{1,5},{2,6},{3,7},{4,0},{5,1},{6,2},{7,3},{8,12},{9,13},{10,... | collective-permute-start | bytes 393224 | tf_op jit(solution)/shard_map/ppermute | solution.py:194
  21.8 1.0 %slice.77 = bf16[8,128,128]{2,1,0:T(8,128)(2,1)S(1)} slice(bf16[12,128,128]{2,1,0:T(8,128)(2,1)} %collective-permute-done.6), slice={[0:8], [0:128], [0:128]} | slice | bytes 524288 | tf_op jit(solution)/shard_map/slice | solution.py:239
  22.8 0.9 %fusion.1 = bf16[4,128,128]{2,1,0:T(8,128)(2,1)S(1)} fusion(bf16[12,128,128]{2,1,0:T(8,128)(2,1)} %collective-permute-done.6, bf16[1,2,4,128,128]{4,3,2,1,0:T(8,128)(2,1)S(1)} %bitcast.66, s32[]{:T(128)S(6)} %select_n.36), kind=kLoop, calls=%fused_computation.6 | loop fusion | flops 262144 | bytes 393220 | tf_op jit(solution)/shard_map/convert_element_type | solution.py:23
  23.8 1.4 %collective-permute-start.7 = (bf16[3,128,128]{2,1,0:T(8,128)(2,1)S(1)}, bf16[3,128,128]{2,1,0:T(8,128)(2,1)S(1)}, u32[]{:S(2)}, u32[]{:S(2)}) collective-permute-start(bf16[3,128,128]{2,1,0:T(8,128)(2,1)S(1)} %pad_maximum_fusion.1), channel_id=1, source_target_pairs={{0,6},{1,7},{2,4},{3,5},{4,2},{5,3},{6,0},{7,1},{8,14},{9,15},{10,... | collective-permute-start | bytes 294920 | tf_op jit(solution)/shard_map/ppermute | solution.py:194
  25.3 1.8 %collective-permute-start.8 = (bf16[3,128,128]{2,1,0:T(8,128)(2,1)S(1)}, bf16[3,128,128]{2,1,0:T(8,128)(2,1)S(1)}, u32[]{:S(2)}, u32[]{:S(2)}) collective-permute-start(bf16[3,128,128]{2,1,0:T(8,128)(2,1)S(1)} %pad_maximum_fusion.2), channel_id=1, source_target_pairs={{0,4},{1,5},{2,6},{3,7},{4,0},{5,1},{6,2},{7,3},{8,12},{9,13},{10,... | collective-permute-start | bytes 294920 | tf_op jit(solution)/shard_map/ppermute | solution.py:194
  27.0 1.4 %collective-permute-start.9 = (bf16[3,128,128]{2,1,0:T(8,128)(2,1)S(1)}, bf16[3,128,128]{2,1,0:T(8,128)(2,1)S(1)}, u32[]{:S(2)}, u32[]{:S(2)}) collective-permute-start(bf16[3,128,128]{2,1,0:T(8,128)(2,1)S(1)} %pad_maximum_fusion.3), channel_id=1, source_target_pairs={{0,2},{1,3},{2,0},{3,1},{4,6},{5,7},{6,4},{7,5},{8,10},{9,11},{10,... | collective-permute-start | bytes 294920 | tf_op jit(solution)/shard_map/ppermute | solution.py:194
  28.4 2.0 %shard_map.85 = (f32[128,1024]{1,0:T(8,128)S(1)}, f32[128,1024]{1,0:T(8,128)S(1)}, f32[128,1024]{1,0:T(8,128)S(1)}) custom-call(s32[1,128]{1,0:T(1,128)S(1)} %bitcast.59, f32[20,8,32]{2,1,0:T(8,128)S(1)} %bitcast.54, bf16[128,1024]{1,0:T(8,128)(2,1)S(1)} %copy-done.7, bf16[128,1024]{1,0:T(8,128)(2,1)S(1)} %copy-done.1, bf16[128,1024]{1,0:T(8,128)(2,1)S(1)} %copy-done.3, ...), custom_call_target="tpu_custom_call" | custom-call | flops 167772160 | bytes 2621440 | tf_op jit(solution)/shard_map/pallas_call | solution.py:305
  30.5 1.6 %collective-permute-start.5 = (bf16[4,128,128]{2,1,0:T(8,128)(2,1)S(1)}, bf16[4,128,128]{2,1,0:T(8,128)(2,1)S(1)}, u32[]{:S(2)}, u32[]{:S(2)}) collective-permute-start(bf16[4,128,128]{2,1,0:T(8,128)(2,1)S(1)} %collective-permute-done.4.two_own_ref), channel_id=1, source_target_pairs={{0,1},{1,0},{2,3},{3,2},{4,5},{5,4},{6,7},{7,6},{8,9},{9,8},{10,11... | collective-permute-start | bytes 393224 | tf_op jit(solution)/shard_map/ppermute | solution.py:194
  32.0 2.6 %collective-permute-done.8 = bf16[3,128,128]{2,1,0:T(8,128)(2,1)S(1)} collective-permute-done((bf16[3,128,128]{2,1,0:T(8,128)(2,1)S(1)}, bf16[3,128,128]{2,1,0:T(8,128)(2,1)S(1)}, u32[]{:S(2)}, u32[]{:S(2)}) %collective-permute-start.8) | collective-permute-done | bytes 98336 | tf_op jit(solution)/shard_map/ppermute | solution.py:194
  34.8 2.8 %collective-permute-start.12 = (bf16[1,128,128]{2,1,0:T(8,128)(2,1)S(1)}, bf16[1,128,128]{2,1,0:T(8,128)(2,1)S(1)}, u32[]{:S(2)}, u32[]{:S(2)}) collective-permute-start(bf16[1,128,128]{2,1,0:T(8,128)(2,1)S(1)} %slice.80), channel_id=1, source_target_pairs={{0,17},{1,16},{2,19},{3,18},{4,21},{5,20},{6,23},{7,22},{8,25},{9,... | collective-permute-start | bytes 98312 | tf_op jit(solution)/shard_map/ppermute | solution.py:199
  38.3 1.0 %fusion = bf16[8,128,128]{2,1,0:T(8,128)(2,1)S(1)} fusion(bf16[2,8,128,128]{3,2,1,0:T(8,128)(2,1)} %collective-permute-done, bf16[3,8,128,128]{3,2,1,0:T(8,128)(2,1)S(1)} %shard_map.86), kind=kLoop, calls=%fused_computation.2 | loop fusion | flops 524288 | bytes 786432 | tf_op jit(solution)/shard_map/convert_element_type | solution.py:23
  40.0 1.4 %collective-permute-done.11 = bf16[1,128,128]{2,1,0:T(8,128)(2,1)S(1)} collective-permute-done((bf16[1,128,128]{2,1,0:T(8,128)(2,1)S(1)}, bf16[1,128,128]{2,1,0:T(8,128)(2,1)S(1)}, u32[]{:S(2)}, u32[]{:S(2)}) %collective-permute-start.11) | collective-permute-done | bytes 32800 | tf_op jit(solution)/shard_map/ppermute | solution.py:198
  41.4 0.8 %collective-permute-done.10 = bf16[2,128,128]{2,1,0:T(8,128)(2,1)S(1)} collective-permute-done((bf16[2,128,128]{2,1,0:T(8,128)(2,1)S(1)}, bf16[2,128,128]{2,1,0:T(8,128)(2,1)S(1)}, u32[]{:S(2)}, u32[]{:S(2)}) %collective-permute-start.10) | collective-permute-done | bytes 65568 | tf_op jit(solution)/shard_map/ppermute | solution.py:194
  42.3 3.2 %collective-permute-start.15 = (bf16[3,128,128]{2,1,0:T(8,128)(2,1)S(1)}, bf16[3,128,128]{2,1,0:T(8,128)(2,1)S(1)}, u32[]{:S(2)}, u32[]{:S(2)}) collective-permute-start(bf16[3,128,128]{2,1,0:T(8,128)(2,1)S(1)} %pad_maximum_fusion.4), channel_id=1, source_target_pairs={{0,6},{1,7},{2,4},{3,5},{4,2},{5,3},{6,0},{7,1},{8,14},{9,15},{10,... | collective-permute-start | bytes 294920 | tf_op jit(solution)/shard_map/ppermute | solution.py:194
  45.5 1.0 %slice_bitcast_fusion.1.zero_ref = bf16[8,128,128]{2,1,0:T(8,128)(2,1)S(1)} fusion(bf16[2,8,128,128]{3,2,1,0:T(8,128)(2,1)} %collective-permute-done), kind=kLoop, calls=%fused_computation.4 | loop fusion | bytes 524288 | tf_op jit(solution)/shard_map/squeeze | solution.py:298
  46.6 1.2 %collective-permute-start.13 = (bf16[3,128,128]{2,1,0:T(8,128)(2,1)S(1)}, bf16[3,128,128]{2,1,0:T(8,128)(2,1)S(1)}, u32[]{:S(2)}, u32[]{:S(2)}) collective-permute-start(bf16[3,128,128]{2,1,0:T(8,128)(2,1)S(1)} %pad_maximum_fusion.4), channel_id=1, source_target_pairs={{0,2},{1,3},{2,0},{3,1},{4,6},{5,7},{6,4},{7,5},{8,10},{9,11},{10,... | collective-permute-start | bytes 294920 | tf_op jit(solution)/shard_map/ppermute | solution.py:194
  47.8 3.7 %collective-permute-done.15 = bf16[3,128,128]{2,1,0:T(8,128)(2,1)S(1)} collective-permute-done((bf16[3,128,128]{2,1,0:T(8,128)(2,1)S(1)}, bf16[3,128,128]{2,1,0:T(8,128)(2,1)S(1)}, u32[]{:S(2)}, u32[]{:S(2)}) %collective-permute-start.15) | collective-permute-done | bytes 98336 | tf_op jit(solution)/shard_map/ppermute | solution.py:194
  51.5 1.9 %collective-permute-done.14 = bf16[3,128,128]{2,1,0:T(8,128)(2,1)S(1)} collective-permute-done((bf16[3,128,128]{2,1,0:T(8,128)(2,1)S(1)}, bf16[3,128,128]{2,1,0:T(8,128)(2,1)S(1)}, u32[]{:S(2)}, u32[]{:S(2)}) %collective-permute-start.14) | collective-permute-done | bytes 98336 | tf_op jit(solution)/shard_map/ppermute | solution.py:194
  53.6 1.3 %collective-permute-done.16.split_other_ref = bf16[1,4,128,128]{3,2,1,0:T(8,128)(2,1)S(1)} collective-permute-done((bf16[1,4,128,128]{3,2,1,0:T(8,128)(2,1)S(1)}, bf16[1,4,128,128]{3,2,1,0:T(8,128)(2,1)S(1)}, u32[]{:S(2)}, u32[]{:S(2)}) %collective-permute-start.16) | collective-permute-done | bytes 131104 | tf_op jit(solution)/shard_map/ppermute | solution.py:198
  54.8 2.8 %shard_map.88 = (bf16[128,1024]{1,0:T(8,128)(2,1)}, bf16[128,1024]{1,0:T(8,128)(2,1)}, bf16[128,1024]{1,0:T(8,128)(2,1)}) custom-call(s32[5]{0:T(128)S(1)} %shift-right-arithmetic_and_fusion.flag_ref, s32[1,128]{1,0:T(1,128)S(1)} %bitcast.60, f32[20,8,32]{2,1,0:T(8,128)S(1)} %bitcast.55, bf16[128,1024]{1,0:T(8,128)(2,1)S(1)} %copy-done.1, ...), custom_call_target="tpu_custom_call" | custom-call | flops 234881024 | bytes 3145728 | tf_op jit(solution)/shard_map/pallas_call | solution.py:319
  (59 shorter events, 3.6 us)
Async XLA Ops:
  0.7 0.7 %copy-start.10 = (s32[128]{0:T(128)S(1)}, s32[128]{0:T(128)}, u32[]{:S(2)}) copy-start(s32[128]{0:T(128)} %param.10) | copy-start | bytes 1540
  1.3 0.9 %copy-start = (bf16[128,1024]{1,0:T(8,128)(2,1)S(1)}, bf16[128,1024]{1,0:T(8,128)(2,1)}, u32[]{:S(2)}) copy-start(bf16[128,1024]{1,0:T(8,128)(2,1)} %k_ref.7) | copy-start | bytes 786436
  2.3 0.9 %copy-start.2 = (bf16[128,1024]{1,0:T(8,128)(2,1)S(1)}, bf16[128,1024]{1,0:T(8,128)(2,1)}, u32[]{:S(2)}) copy-start(bf16[128,1024]{1,0:T(8,128)(2,1)} %v_ref.7) | copy-start | bytes 786436
  3.2 0.9 %copy-start.4 = (bf16[128,1024]{1,0:T(8,128)(2,1)S(1)}, bf16[128,1024]{1,0:T(8,128)(2,1)}, u32[]{:S(2)}) copy-start(bf16[128,1024]{1,0:T(8,128)(2,1)} %g_ref.7) | copy-start | bytes 786436
  4.2 0.9 %copy-start.6 = (bf16[128,1024]{1,0:T(8,128)(2,1)S(1)}, bf16[128,1024]{1,0:T(8,128)(2,1)}, u32[]{:S(2)}) copy-start(bf16[128,1024]{1,0:T(8,128)(2,1)} %q_ref.5) | copy-start | bytes 786436
  5.1 0.9 %copy-start.8 = (f32[32,20,8]{0,2,1:T(8,128)S(1)}, f32[32,20,8]{0,2,1:T(8,128)}, u32[]{:S(2)}) copy-start(f32[32,20,8]{0,2,1:T(8,128)} %param.11) | copy-start | bytes 61444
  6.0 4.3 %copy-start.7 = (bf16[128,1024]{1,0:T(8,128)(2,1)S(1)}, bf16[128,1024]{1,0:T(8,128)(2,1)}, u32[]{:S(2)}) copy-start(bf16[128,1024]{1,0:T(8,128)(2,1)} %q_ref.5) | copy-start | bytes 786436
  6.0 4.3 %copy-start.9 = (f32[32,20,8]{0,2,1:T(8,128)S(1)}, f32[32,20,8]{0,2,1:T(8,128)}, u32[]{:S(2)}) copy-start(f32[32,20,8]{0,2,1:T(8,128)} %param.11) | copy-start | bytes 61444
  7.2 3.1 %copy-start.3 = (bf16[128,1024]{1,0:T(8,128)(2,1)S(1)}, bf16[128,1024]{1,0:T(8,128)(2,1)}, u32[]{:S(2)}) copy-start(bf16[128,1024]{1,0:T(8,128)(2,1)} %v_ref.7) | copy-start | bytes 786436
  7.2 3.1 %copy-start.5 = (bf16[128,1024]{1,0:T(8,128)(2,1)S(1)}, bf16[128,1024]{1,0:T(8,128)(2,1)}, u32[]{:S(2)}) copy-start(bf16[128,1024]{1,0:T(8,128)(2,1)} %g_ref.7) | copy-start | bytes 786436
  7.2 3.1 %copy-start.1 = (bf16[128,1024]{1,0:T(8,128)(2,1)S(1)}, bf16[128,1024]{1,0:T(8,128)(2,1)}, u32[]{:S(2)}) copy-start(bf16[128,1024]{1,0:T(8,128)(2,1)} %k_ref.7) | copy-start | bytes 786436
  7.3 6.5 %collective-permute-start.2 = (bf16[4,128,128]{2,1,0:T(8,128)(2,1)S(1)}, bf16[4,128,128]{2,1,0:T(8,128)(2,1)S(1)}, u32[]{:S(2)}, u32[]{:S(2)}) collective-permute-start(bf16[4,128,128]{2,1,0:T(8,128)(2,1)S(1)} %dynamic-slice_bitcast_fusion.1), channel_id=1, source_target_pairs={{0,1},{1,0},{2,3},{3,2},{4,5},{5,4},{6,7},{7,6},{8,9},{9,8},{10,11... | collective-permute-start | bytes 393224 | tf_op jit(solution)/shard_map/ppermute | solution.py:194
  11.5 10.3 %collective-permute-start.6 = (bf16[12,128,128]{2,1,0:T(8,128)(2,1)S(1)}, bf16[12,128,128]{2,1,0:T(8,128)(2,1)}, u32[]{:S(2)}, u32[]{:S(2)}) collective-permute-start(bf16[12,128,128]{2,1,0:T(8,128)(2,1)S(1)} %pad_maximum_fusion), channel_id=1, source_target_pairs={{0,8},{8,0},{16,24},{24,16},{1,9},{9,1},{17,25},{25,17},{2,10},{10... | collective-permute-start | bytes 1179656 | tf_op jit(solution)/shard_map/ppermute | solution.py:198
  13.8 5.0 %collective-permute-start.3 = (bf16[4,128,128]{2,1,0:T(8,128)(2,1)S(1)}, bf16[4,128,128]{2,1,0:T(8,128)(2,1)S(1)}, u32[]{:S(2)}, u32[]{:S(2)}) collective-permute-start(bf16[4,128,128]{2,1,0:T(8,128)(2,1)S(1)} %fusion.2), channel_id=1, source_target_pairs={{0,2},{1,3},{2,0},{3,1},{4,6},{5,7},{6,4},{7,5},{8,10},{9,11},{10,... | collective-permute-start | bytes 393224 | tf_op jit(solution)/shard_map/ppermute | solution.py:194
  16.6 21.8 %collective-permute-start = (bf16[2,8,128,128]{3,2,1,0:T(8,128)(2,1)}, bf16[2,8,128,128]{3,2,1,0:T(8,128)(2,1)}, u32[]{:S(2)}, u32[]{:S(2)}) collective-permute-start(bf16[2,8,128,128]{3,2,1,0:T(8,128)(2,1)} %slice.70), channel_id=1, source_target_pairs={{0,1},{1,0},{2,3},{3,2},{4,5},{5,4},{6,7},{7,6},{8,9},{9,8},{10,11... | collective-permute-start | bytes 1572872 | tf_op jit(solution)/shard_map/ppermute | solution.py:194
  18.9 11.6 %collective-permute-start.4 = (bf16[4,128,128]{2,1,0:T(8,128)(2,1)S(1)}, bf16[4,128,128]{2,1,0:T(8,128)(2,1)S(1)}, u32[]{:S(2)}, u32[]{:S(2)}) collective-permute-start(bf16[4,128,128]{2,1,0:T(8,128)(2,1)S(1)} %add_convert_fusion.1), channel_id=1, source_target_pairs={{0,4},{1,5},{2,6},{3,7},{4,0},{5,1},{6,2},{7,3},{8,12},{9,13},{10,... | collective-permute-start | bytes 393224 | tf_op jit(solution)/shard_map/ppermute | solution.py:194
  23.8 8.2 %collective-permute-start.7 = (bf16[3,128,128]{2,1,0:T(8,128)(2,1)S(1)}, bf16[3,128,128]{2,1,0:T(8,128)(2,1)S(1)}, u32[]{:S(2)}, u32[]{:S(2)}) collective-permute-start(bf16[3,128,128]{2,1,0:T(8,128)(2,1)S(1)} %pad_maximum_fusion.1), channel_id=1, source_target_pairs={{0,6},{1,7},{2,4},{3,5},{4,2},{5,3},{6,0},{7,1},{8,14},{9,15},{10,... | collective-permute-start | bytes 294920 | tf_op jit(solution)/shard_map/ppermute | solution.py:194
  25.3 9.4 %collective-permute-start.8 = (bf16[3,128,128]{2,1,0:T(8,128)(2,1)S(1)}, bf16[3,128,128]{2,1,0:T(8,128)(2,1)S(1)}, u32[]{:S(2)}, u32[]{:S(2)}) collective-permute-start(bf16[3,128,128]{2,1,0:T(8,128)(2,1)S(1)} %pad_maximum_fusion.2), channel_id=1, source_target_pairs={{0,4},{1,5},{2,6},{3,7},{4,0},{5,1},{6,2},{7,3},{8,12},{9,13},{10,... | collective-permute-start | bytes 294920 | tf_op jit(solution)/shard_map/ppermute | solution.py:194
  27.0 7.7 %collective-permute-start.9 = (bf16[3,128,128]{2,1,0:T(8,128)(2,1)S(1)}, bf16[3,128,128]{2,1,0:T(8,128)(2,1)S(1)}, u32[]{:S(2)}, u32[]{:S(2)}) collective-permute-start(bf16[3,128,128]{2,1,0:T(8,128)(2,1)S(1)} %pad_maximum_fusion.3), channel_id=1, source_target_pairs={{0,2},{1,3},{2,0},{3,1},{4,6},{5,7},{6,4},{7,5},{8,10},{9,11},{10,... | collective-permute-start | bytes 294920 | tf_op jit(solution)/shard_map/ppermute | solution.py:194
  30.5 23.1 %collective-permute-start.5 = (bf16[4,128,128]{2,1,0:T(8,128)(2,1)S(1)}, bf16[4,128,128]{2,1,0:T(8,128)(2,1)S(1)}, u32[]{:S(2)}, u32[]{:S(2)}) collective-permute-start(bf16[4,128,128]{2,1,0:T(8,128)(2,1)S(1)} %collective-permute-done.4.two_own_ref), channel_id=1, source_target_pairs={{0,1},{1,0},{2,3},{3,2},{4,5},{5,4},{6,7},{7,6},{8,9},{9,8},{10,11... | collective-permute-start | bytes 393224 | tf_op jit(solution)/shard_map/ppermute | solution.py:194
  34.8 5.2 %collective-permute-start.12 = (bf16[1,128,128]{2,1,0:T(8,128)(2,1)S(1)}, bf16[1,128,128]{2,1,0:T(8,128)(2,1)S(1)}, u32[]{:S(2)}, u32[]{:S(2)}) collective-permute-start(bf16[1,128,128]{2,1,0:T(8,128)(2,1)S(1)} %slice.80), channel_id=1, source_target_pairs={{0,17},{1,16},{2,19},{3,18},{4,21},{5,20},{6,23},{7,22},{8,25},{9,... | collective-permute-start | bytes 98312 | tf_op jit(solution)/shard_map/ppermute | solution.py:199
  37.5 3.9 %collective-permute-start.11 = (bf16[1,128,128]{2,1,0:T(8,128)(2,1)S(1)}, bf16[1,128,128]{2,1,0:T(8,128)(2,1)S(1)}, u32[]{:S(2)}, u32[]{:S(2)}) collective-permute-start(bf16[1,128,128]{2,1,0:T(8,128)(2,1)S(1)} %slice.80), channel_id=1, source_target_pairs={{0,16},{8,24},{16,0},{24,8},{1,17},{9,25},{17,1},{25,9},{2,18},{10... | collective-permute-start | bytes 98312 | tf_op jit(solution)/shard_map/ppermute | solution.py:198
  38.0 4.3 %collective-permute-start.10 = (bf16[2,128,128]{2,1,0:T(8,128)(2,1)S(1)}, bf16[2,128,128]{2,1,0:T(8,128)(2,1)S(1)}, u32[]{:S(2)}, u32[]{:S(2)}) collective-permute-start(bf16[2,128,128]{2,1,0:T(8,128)(2,1)S(1)} %slice.79), channel_id=1, source_target_pairs={{0,1},{1,0},{2,3},{3,2},{4,5},{5,4},{6,7},{7,6},{8,9},{9,8},{10,11... | collective-permute-start | bytes 196616 | tf_op jit(solution)/shard_map/ppermute | solution.py:194
  39.3 14.2 %collective-permute-start.1 = (bf16[8,128,128]{2,1,0:T(8,128)(2,1)S(1)}, bf16[8,128,128]{2,1,0:T(8,128)(2,1)S(1)}, u32[]{:S(2)}, u32[]{:S(2)}) collective-permute-start(bf16[8,128,128]{2,1,0:T(8,128)(2,1)S(1)} %fusion), channel_id=1, source_target_pairs={{0,2},{1,3},{2,0},{3,1},{4,6},{5,7},{6,4},{7,5},{8,10},{9,11},{10,... | collective-permute-start | bytes 786440 | tf_op jit(solution)/shard_map/ppermute | solution.py:194
  42.3 9.2 %collective-permute-start.15 = (bf16[3,128,128]{2,1,0:T(8,128)(2,1)S(1)}, bf16[3,128,128]{2,1,0:T(8,128)(2,1)S(1)}, u32[]{:S(2)}, u32[]{:S(2)}) collective-permute-start(bf16[3,128,128]{2,1,0:T(8,128)(2,1)S(1)} %pad_maximum_fusion.4), channel_id=1, source_target_pairs={{0,6},{1,7},{2,4},{3,5},{4,2},{5,3},{6,0},{7,1},{8,14},{9,15},{10,... | collective-permute-start | bytes 294920 | tf_op jit(solution)/shard_map/ppermute | solution.py:194
  46.5 6.9 %collective-permute-start.14 = (bf16[3,128,128]{2,1,0:T(8,128)(2,1)S(1)}, bf16[3,128,128]{2,1,0:T(8,128)(2,1)S(1)}, u32[]{:S(2)}, u32[]{:S(2)}) collective-permute-start(bf16[3,128,128]{2,1,0:T(8,128)(2,1)S(1)} %pad_maximum_fusion.4), channel_id=1, source_target_pairs={{0,4},{1,5},{2,6},{3,7},{4,0},{5,1},{6,2},{7,3},{8,12},{9,13},{10,... | collective-permute-start | bytes 294920 | tf_op jit(solution)/shard_map/ppermute | solution.py:194
  46.6 6.8 %collective-permute-start.13 = (bf16[3,128,128]{2,1,0:T(8,128)(2,1)S(1)}, bf16[3,128,128]{2,1,0:T(8,128)(2,1)S(1)}, u32[]{:S(2)}, u32[]{:S(2)}) collective-permute-start(bf16[3,128,128]{2,1,0:T(8,128)(2,1)S(1)} %pad_maximum_fusion.4), channel_id=1, source_target_pairs={{0,2},{1,3},{2,0},{3,1},{4,6},{5,7},{6,4},{7,5},{8,10},{9,11},{10,... | collective-permute-start | bytes 294920 | tf_op jit(solution)/shard_map/ppermute | solution.py:194
  53.4 1.4 %collective-permute-start.16 = (bf16[1,4,128,128]{3,2,1,0:T(8,128)(2,1)S(1)}, bf16[1,4,128,128]{3,2,1,0:T(8,128)(2,1)S(1)}, u32[]{:S(2)}, u32[]{:S(2)}) collective-permute-start(bf16[1,4,128,128]{3,2,1,0:T(8,128)(2,1)S(1)} %maximum_bitcast_fusion.split_own_ref), channel_id=1, source_target_pairs={{0,8},{8,0},{16,24},{24,16},{1,9},{9,1},{17,25},{25,17},{2,10},{10... | collective-permute-start | bytes 393224 | tf_op jit(solution)/shard_map/ppermute | solution.py:198

commit v3 on v2

v3 whole, which is shorter than its diff:
```python
import functools

import jax
import jax.numpy as jnp
from jax import lax
from jax.experimental import pallas as pl
from jax.experimental.pallas import tpu as pltpu
from jax.sharding import PartitionSpec as P

NEAR = 3
VMEM_BYTES = 16 * 1024 * 1024


def level_bits(amount):
    return amount.bit_length() - 1


def wide(values):
    return values.astype(jnp.float32)


def narrow(values):
    return values.astype(jnp.bfloat16)


def product(left, right, left_dim, right_dim):
    return lax.dot_general(
        left,
        right,
        (((left_dim,), (right_dim,)), ((), ())),
        preferred_element_type=jnp.float32,
    )


def gate_lanes(class_ref, table_ref, first, last):
    classes = table_ref.shape[2]
    tokens = class_ref.shape[1]
    rows = (last - first) * table_ref.shape[1]
    numbers = lax.broadcasted_iota(jnp.int32, (classes, tokens), 0)
    picker = (numbers == class_ref[...]).astype(jnp.float32)
    table = table_ref[first:last].reshape(rows, classes)
    return jnp.dot(
        table, picker, precision=lax.Precision.HIGHEST, preferred_element_type=jnp.float32
    )


def payload_cell(flags, gates, rows, level_places, q_ref, k_ref, v_ref, g_ref, columns, store):
    query_turned = wide(q_ref[:, columns].T)
    key_turned = wide(k_ref[:, columns].T)
    grad_here = wide(g_ref[:, columns])
    value_here = wide(v_ref[:, columns])
    for place in level_places:
        row = rows[place]
        flag = flags[place] == 1
        left = jnp.where(flag, gates[row : row + 1, :] * query_turned, key_turned)
        right = jnp.where(flag, grad_here, value_here)
        store(place, narrow(product(narrow(left), narrow(right), 1, 0)))


def upper_kernel(
    levels,
    split,
    offset,
    head_size,
    flag_ref,
    class_hbm,
    table_hbm,
    q_hbm,
    k_hbm,
    v_hbm,
    g_hbm,
    sent_ref,
    keep_ref,
    *rest,
):
    lead_refs = rest[:-7]
    class_ref, table_ref, q_ref, k_ref, v_ref, g_ref, arrived = rest[-7:]
    moves = [
        pltpu.make_async_copy(source, target, arrived.at[place])
        for place, (source, target) in enumerate(
            (
                (class_hbm, class_ref),
                (table_hbm, table_ref),
                (q_hbm, q_ref),
                (k_hbm, k_ref),
                (g_hbm, g_ref),
                (v_hbm, v_ref),
            )
        )
    ]
    for move in moves:
        move.start()
    moves[0].wait()
    moves[1].wait()
    head_count = table_ref.shape[1]
    half = head_count // 2
    core = flag_ref[split - 1]
    gates = gate_lanes(class_ref, table_ref, offset + levels[0], offset + levels[-1] + 1)
    for move in moves[2:]:
        move.wait()
    flags = [flag_ref[level] for level in levels]
    for head in range(head_count):
        rows = [place * head_count + head for place in range(len(levels))]

        def store(place, value):
            level = levels[place]
            if level < split - 1:
                lead_refs[0][level - levels[0], head] = value
            elif level == split - 1:
                sent_ref[head] = value
            else:
                row = (level - split) * half + head % half

                @pl.when(core == head // half)
                def _():
                    keep_ref[row] = value

                @pl.when(core != head // half)
                def _():
                    sent_ref[head_count + row] = value

        columns = pl.ds(head * head_size, head_size)
        payload_cell(
            flags, gates, rows, range(len(levels)), q_ref, k_ref, v_ref, g_ref, columns, store
        )


def share_kernel(head_count, places, flag_ref, seen_ref, keep_ref, *refs):
    lead_refs = refs[:-4]
    out_refs = refs[-4:]
    quarter = head_count // 4
    eighth = head_count // 8
    z_place = flag_ref[1] + 2 * flag_ref[2]
    for offs in range(4):
        place = jnp.bitwise_xor(z_place, offs)
        row = 0
        for lead in range(places[0] - 1):
            out_refs[offs][row : row + quarter] = lead_refs[0][lead, pl.ds(place * quarter, quarter)]
            row += quarter
        out_refs[offs][row : row + quarter] = seen_ref[pl.ds(place * quarter, quarter)]
        row += quarter
        for late in range(places[1]):
            first = late * (head_count // 2) + place * eighth
            total = wide(keep_ref[pl.ds(first, eighth)])
            total = total + wide(seen_ref[pl.ds(head_count + first, eighth)])
            out_refs[offs][row : row + eighth] = narrow(total)
            row += eighth


def lower_kernel(
    offset,
    head_size,
    flag_ref,
    class_ref,
    table_ref,
    q_ref,
    k_ref,
    v_ref,
    g_ref,
    after_ref,
    two_own_ref,
    two_other_ref,
    near_ref,
):
    head_count = table_ref.shape[1]
    half = head_count // 2
    x_place = flag_ref[0]
    gates = gate_lanes(class_ref, table_ref, offset, offset + NEAR)
    flags = [flag_ref[level] for level in range(NEAR)]
    for head in range(head_count):
        rows = [place * head_count + head for place in range(NEAR)]

        def store(place, value):
            if place < 2:
                near_ref[place, head] = value
                return

            @pl.when(x_place == head // half)
            def _():
                two_own_ref[head % half] = value

            @pl.when(x_place != head // half)
            def _():
                two_other_ref[head % half] = value

        columns = pl.ds(head * head_size, head_size)
        payload_cell(flags, gates, rows, range(NEAR), q_ref, k_ref, v_ref, g_ref, columns, store)


def four_sum_kernel(top_rows, own_ref, *refs):
    came_refs = refs[:-2]
    below_ref, top_ref = refs[-2:]
    total = wide(own_ref[...])
    for came_ref in came_refs:
        total = total + wide(came_ref[...])
    rows = total.shape[0] - top_rows
    below_ref[...] = narrow(total[:rows])
    top_ref[...] = narrow(total[rows:])


def pair_sum_kernel(below_ref, far_ref, near_top_ref, far_top_ref, out_ref):
    rows = below_ref.shape[0]
    out_ref[:rows] = narrow(wide(below_ref[...]) + wide(far_ref[...]))
    out_ref[rows:] = narrow(wide(near_top_ref[...]) + wide(far_top_ref[...]))


def gather_kernel(cut, piece0_ref, piece1_ref, piece2_ref, piece3_ref, out_ref):
    for offs, piece_ref in enumerate((piece0_ref, piece1_ref, piece2_ref, piece3_ref)):
        split_levels = out_ref.shape[0]
        eighth = out_ref.shape[1] // 4
        for level in range(split_levels):
            first = cut + level * eighth
            out_ref[level, offs * eighth : (offs + 1) * eighth] = piece_ref[first : first + eighth]


def near_sum_kernel(near_ref, seen_ref, one_ref):
    one_ref[...] = narrow(wide(near_ref[1]) + wide(seen_ref[1]))


def local_kernel(
    block_depth, head_size, class_ref, table_ref, q_ref, k_ref, v_ref, g_ref, qo_ref, ko_ref, vo_ref
):
    head_count = table_ref.shape[1]
    tokens = q_ref.shape[0]
    gates = gate_lanes(class_ref, table_ref, 0, block_depth + 1)
    source = lax.broadcasted_iota(jnp.int32, (tokens, tokens), 0)
    target = lax.broadcasted_iota(jnp.int32, (tokens, tokens), 1)
    apart = jnp.bitwise_xor(source, target)
    causal = source <= target
    for head in range(head_count):
        columns = pl.ds(head * head_size, head_size)
        query_here = q_ref[:, columns]
        key_here = k_ref[:, columns]
        value_here = v_ref[:, columns]
        grad_here = g_ref[:, columns]
        weight = jnp.broadcast_to(gates[head : head + 1, :], (tokens, tokens))
        for level in range(1, block_depth + 1):
            row = level * head_count + head
            weight = jnp.where(apart >= 2 ** (level - 1), gates[row : row + 1, :], weight)
        weight = jnp.where(causal, weight, 0.0)
        weighted_scores = narrow(weight * product(key_here, query_here, 1, 1))
        weighted_grads = narrow(weight * product(value_here, grad_here, 1, 1))
        qo_ref[:, columns] = product(weighted_grads, key_here, 0, 0)
        ko_ref[:, columns] = product(weighted_grads, query_here, 1, 0)
        vo_ref[:, columns] = product(weighted_scores, grad_here, 1, 0)


def gate_columns(class_ref, table_ref, first, last):
    return gate_lanes(class_ref, table_ref, first, last).T


def final_kernel(
    offset,
    head_size,
    total,
    inner,
    flag_ref,
    class_ref,
    table_ref,
    k_ref,
    v_ref,
    g_ref,
    ql_ref,
    kl_ref,
    vl_ref,
    near_ref,
    one_ref,
    two_own_ref,
    two_other_ref,
    piece0_ref,
    piece1_ref,
    piece2_ref,
    piece3_ref,
    split_own_ref,
    split_other_ref,
    qo_ref,
    ko_ref,
    vo_ref,
    held_ref,
):
    head_count = table_ref.shape[1]
    half = head_count // 2
    quarter = head_count // 4
    eighth = head_count // 8
    gates = gate_columns(class_ref, table_ref, offset, offset + total)
    x_place = flag_ref[0]
    z_place = flag_ref[1] + 2 * flag_ref[2]
    core = flag_ref[inner]
    held_ref[0] = near_ref[0]
    held_ref[1] = one_ref[...]
    held_ref[2, pl.ds(x_place * half, half)] = two_own_ref[...]
    held_ref[2, pl.ds((1 - x_place) * half, half)] = two_other_ref[...]
    pieces = (piece0_ref, piece1_ref, piece2_ref, piece3_ref)
    split = inner + 1
    for level in range(NEAR, split):
        for offs in range(4):
            first = jnp.bitwise_xor(z_place, offs) * quarter
            row = (level - NEAR) * quarter
            held_ref[level, pl.ds(first, quarter)] = pieces[offs][row : row + quarter]
    for level in range(split, total):
        for offs in range(4):
            first = jnp.bitwise_xor(z_place, offs) * eighth
            rows = pl.ds(offs * eighth, eighth)
            held_ref[level, pl.ds(core * half + first, eighth)] = split_own_ref[level - split, rows]
            held_ref[level, pl.ds((1 - core) * half + first, eighth)] = split_other_ref[
                level - split, rows
            ]
    for head in range(head_count):
        columns = pl.ds(head * head_size, head_size)
        grad_here = g_ref[:, columns]
        query_total = ql_ref[:, columns]
        state_grad = jnp.zeros((head_size, head_size), jnp.float32)
        for level in range(total):
            state = held_ref[level, head]
            term = product(grad_here, state, 1, 1)
            row = level * head_count + head
            on = wide(flag_ref[level])
            query_total = query_total + (gates[:, row : row + 1] * on) * term
            state_grad = state_grad + wide(state) * (1.0 - on)
        grad_rounded = narrow(state_grad)
        qo_ref[:, columns] = narrow(query_total)
        ko_ref[:, columns] = narrow(
            kl_ref[:, columns] + product(v_ref[:, columns], grad_rounded, 1, 1)
        )
        vo_ref[:, columns] = narrow(
            vl_ref[:, columns] + product(k_ref[:, columns], grad_rounded, 1, 0)
        )


def per_device(query_rows, key_rows, value_rows, out_grad, gate_class, gate_table):
    row_count, width = query_rows.shape
    head_count = gate_table.shape[2]
    head_size = width // head_count
    inner_bits = level_bits(lax.axis_size("gy"))
    outer_bits = level_bits(lax.axis_size("gx"))
    total = inner_bits + outer_bits
    block_depth = level_bits(row_count)
    offset = block_depth + 1
    inner_index = lax.axis_index("gy")
    outer_index = lax.axis_index("gx")
    block_index = (outer_index << inner_bits) | inner_index
    flag_bits = (block_index >> jnp.arange(total, dtype=jnp.int32)) & 1
    inner_size = lax.axis_size("gy")
    device_count = inner_size * lax.axis_size("gx")

    def swap(block, *bits):
        mask = sum(1 << bit for bit in bits)
        if mask < inner_size:
            return lax.ppermute(block, "gy", [(i, i ^ mask) for i in range(inner_size)])
        if mask % inner_size == 0:
            mask = mask // inner_size
            size = lax.axis_size("gx")
            return lax.ppermute(block, "gx", [(i, i ^ mask) for i in range(size)])
        return lax.ppermute(block, ("gx", "gy"), [(i, i ^ mask) for i in range(device_count)])

    class_lanes = gate_class.reshape(1, row_count)
    table = jnp.transpose(gate_table, (1, 2, 0))
    smem = pl.BlockSpec(memory_space=pltpu.SMEM)
    vmem = pl.BlockSpec(memory_space=pltpu.VMEM)
    hbm = pl.BlockSpec(memory_space=pltpu.HBM)
    anywhere = pl.BlockSpec(memory_space=pl.ANY)
    cell = (head_size, head_size)
    params = pltpu.CompilerParams(vmem_limit_bytes=VMEM_BYTES)

    def cells(*lead):
        return jax.ShapeDtypeStruct(lead + cell, jnp.bfloat16)

    def call(kernel, in_specs, outs, operands, flops=0, scratch=()):
        moved = sum(operand.size * operand.dtype.itemsize for operand in operands)
        return pl.pallas_call(
            kernel,
            out_shape=outs,
            in_specs=in_specs,
            out_specs=jax.tree.map(lambda _: vmem, outs),
            scratch_shapes=scratch,
            compiler_params=params,
            cost_estimate=pl.CostEstimate(flops=flops, bytes_accessed=moved, transcendentals=0),
        )(*operands)

    quarter = head_count // 4
    half = head_count // 2
    eighth = head_count // 8
    split = inner_bits + 1
    whole_levels = split - NEAR
    split_levels = total - split
    cut = whole_levels * quarter
    share_rows = cut + split_levels * eighth
    block = pltpu.VMEM((row_count, width), jnp.bfloat16)

    levels = tuple(range(NEAR, total))
    outs = (cells(head_count + split_levels * half), cells(split_levels * half))
    if whole_levels > 1:
        outs = outs + (cells(whole_levels - 1, head_count),)
    sent, keep, *lead = call(
        functools.partial(upper_kernel, levels, split, offset, head_size),
        [smem] + [hbm] * 6,
        outs,
        (flag_bits, class_lanes, table, query_rows, key_rows, value_rows, out_grad),
        flops=2 * len(levels) * row_count * width * head_size,
        scratch=[
            pltpu.VMEM(class_lanes.shape, jnp.int32),
            pltpu.VMEM(table.shape, jnp.float32),
            block,
            block,
            block,
            block,
            pltpu.SemaphoreType.DMA((6,)),
        ],
    )
    seen = swap(sent, inner_bits)
    own_share, *shares_out = call(
        functools.partial(share_kernel, head_count, (whole_levels, split_levels)),
        [smem] + [vmem] * (2 + len(lead)),
        (cells(share_rows),) * 4,
        (flag_bits, seen, keep, *lead),
    )

    def z_bits(offs):
        return [bit + 1 for bit in range(2) if offs >> bit & 1]

    came = [swap(shares_out[offs - 1], *z_bits(offs)) for offs in (3, 2, 1)]
    top = total - 1
    below, top_sent = call(
        functools.partial(four_sum_kernel, eighth),
        [vmem] * 4,
        (cells(share_rows - eighth), cells(eighth)),
        (own_share, *came),
    )
    middle = [bit for bit in range(NEAR, top) if bit != inner_bits]
    if middle:
        part = wide(jnp.concatenate([below, top_sent], axis=0))
        parts = {
            level: part[(level - NEAR) * quarter : (level - NEAR + 1) * quarter]
            for level in range(NEAR, split)
        }
        for level in range(split, total):
            row = cut + (level - split) * eighth
            parts[level] = part[row : row + eighth]
        for bit in middle:
            going = range(bit, total)
            block_sent = narrow(jnp.concatenate([parts[level] for level in going], axis=0))
            seen_part = wide(swap(block_sent, bit))
            row = 0
            for level in going:
                size = parts[level].shape[0]
                got = seen_part[row : row + size]
                parts[level] = got if level == bit else parts[level] + got
                row += size
        below = narrow(jnp.concatenate([parts[level] for level in range(NEAR, top)], axis=0))
        top_sent = narrow(parts[top])
    shares = call(
        pair_sum_kernel,
        [vmem] * 4,
        cells(share_rows),
        (below, swap(below, 0), swap(top_sent, top), swap(top_sent, 0, top)),
    )
    pieces = [shares] + [swap(shares, *z_bits(offs)) for offs in (1, 2, 3)]
    split_own = call(
        functools.partial(gather_kernel, cut), [vmem] * 4, cells(split_levels, half), pieces
    )
    split_other = swap(split_own, inner_bits)

    two_own, two_other, near = call(
        functools.partial(lower_kernel, offset, head_size),
        [smem] + [vmem] * 6 + [anywhere],
        (cells(half), cells(half), cells(2, head_count)),
        (flag_bits, class_lanes, table, query_rows, key_rows, value_rows, out_grad, own_share),
        flops=2 * NEAR * row_count * width * head_size,
    )
    two_sum = narrow(wide(two_own) + wide(swap(two_other, 0)))
    near_seen = swap(near, 0)
    one_sum = call(near_sum_kernel, [vmem] * 2, cells(head_count), (near, near_seen))
    one_done = swap(one_sum, 1)
    two_sum = narrow(wide(two_sum) + wide(swap(two_sum, 1)))
    two_half = swap(two_sum, 2)
    two_rest = swap(two_half, 0)

    big = jax.ShapeDtypeStruct((row_count, width), jnp.float32)
    query_local, key_local, value_local = call(
        functools.partial(local_kernel, block_depth, head_size),
        [vmem] * 6,
        (big, big, big),
        (class_lanes, table, query_rows, key_rows, value_rows, out_grad),
        flops=10 * row_count * width * row_count,
    )

    small = jax.ShapeDtypeStruct((row_count, width), jnp.bfloat16)
    return call(
        functools.partial(final_kernel, offset, head_size, total, inner_bits),
        [smem] + [vmem] * 18,
        (small, small, small),
        (
            flag_bits,
            class_lanes,
            table,
            key_rows,
            value_rows,
            out_grad,
            query_local,
            key_local,
            value_local,
            near_seen,
            one_done,
            two_half,
            two_rest,
            *pieces,
            split_own,
            split_other,
        ),
        flops=(2 * total + 4) * row_count * width * head_size,
        scratch=[pltpu.VMEM((total, head_count) + cell, jnp.bfloat16)],
    )


def solution(mesh):
    rows = P(("gx", "gy"), None)
    return jax.shard_map(
        per_device,
        mesh=mesh,
        in_specs=(rows, rows, rows, rows, P(("gx", "gy")), P()),
        out_specs=(rows, rows, rows),
        check_vma=False,
    )
```

time: 58 us -> 61.7 us (1.064)
  waiting for transfers between devices: 14.7 us -> 21.1 us
  Pallas kernels: 7.1 us -> 10.8 us
  local copies, waits for them, and re-layouts: 8.33 us -> 5.75 us
  other arithmetic: 2.26 us -> 0.08 us
  starting transfers between devices: 24.3 us -> 23 us
    ppermute x13, waiting for transfers between devices: 12 us -> 19.8 us  [swap(): return lax.ppermute(block, 'gy', [(i, i ^ mask) for i in range(inner_size)])]
    pallas_call x4 -> x9, Pallas kernels: 7.1 us -> 10.8 us  [call(): pl.pallas_call(kernel, out_shape=outs, in_specs=in_specs, out_specs=jax.t...]
    convert_element_type x6 -> x2, other arithmetic: 2.1 us -> 0.08 us  [narrow(): return values.astype(jnp.bfloat16)]
    slice x5 -> x0, local copies, waits for them, and re-layouts: 1.84 us -> none  [the longest x1 0.97 us: per_device(): seen[None, :head_count]]
    ppermute x13, starting transfers between devices: 20.9 us -> 19.3 us  [swap(): return lax.ppermute(block, 'gy', [(i, i ^ mask) for i in range(inner_size)])]
    ppermute x3, waiting for transfers between devices: 2.72 us -> 1.35 us  [swap(): return lax.ppermute(block, 'gx', [(i, i ^ mask) for i in range(size)])]
    squeeze x3 -> x0, local copies, waits for them, and re-layouts: 1.02 us -> none  [the longest x1 0.97 us: per_device(): zero_done = near_seen[0]]
  transfers between devices with their start and end apart: 17 -> 17, of which waited for: 8 -> 8; matrix products, arithmetic and copies ran while one was open for 9% -> 0% of each run, Pallas kernels for 5% -> 4%
where the time goes in v3:
time: 61.7 us; the launch traced here: 61.4 us
  starting transfers between devices  23 us (37%)
  waiting for transfers between devices  21.1 us (34%)
  Pallas kernels  10.8 us (18%)
  local copies, waits for them, and re-layouts  5.75 us (9%)
  between operations  0.77 us (1%)
    ppermute x13, waiting for transfers between devices, swap(): return lax.ppermute(block, 'gy', [(i, i ^ mask) for i in range(inner_size)])  19.8 us
    ppermute x13, starting transfers between devices, swap(): return lax.ppermute(block, 'gy', [(i, i ^ mask) for i in range(inner_size)])  19.3 us
    pallas_call x9, Pallas kernels, call(): pl.pallas_call(kernel, out_shape=outs, in_specs=in_specs, out_specs=jax.t...  10.8 us
    unnamed x22, local copies, waits for them, and re-layouts  5.75 us
    ppermute x1, starting transfers between devices, swap(): lax.ppermute(block, ('gx', 'gy'), [(i, i ^ mask) for i in range(device_co...  2.53 us
    ppermute x3, waiting for transfers between devices, swap(): return lax.ppermute(block, 'gx', [(i, i ^ mask) for i in range(size)])  1.35 us
  transfers between devices with their start and end apart: 17, of which 8 were waited for; matrix products, arithmetic and copies ran while one was open for 0% of the time, Pallas kernels for 4%

profile of v3, /device:TPU:0, one launch (start us, length us, event | category | flops | bytes accessed | tf_op | source)
XLA Modules:
  0.0 61.4 jit_solution(6823524646344669188)
XLA Ops:
  0.7 0.6 %copy-done.10 = s32[128]{0:T(128)S(1)} copy-done((s32[128]{0:T(128)S(1)}, s32[128]{0:T(128)}, u32[]{:S(2)}) %copy-start.10) | copy-done | bytes 536
  1.3 0.9 %copy-done = bf16[128,1024]{1,0:T(8,128)(2,1)S(1)} copy-done((bf16[128,1024]{1,0:T(8,128)(2,1)S(1)}, bf16[128,1024]{1,0:T(8,128)(2,1)}, u32[]{:S(2)}) %copy-start) | copy-done | bytes 262168
  2.3 0.9 %copy-done.2 = bf16[128,1024]{1,0:T(8,128)(2,1)S(1)} copy-done((bf16[128,1024]{1,0:T(8,128)(2,1)S(1)}, bf16[128,1024]{1,0:T(8,128)(2,1)}, u32[]{:S(2)}) %copy-start.2) | copy-done | bytes 262168
  3.2 0.9 %copy-done.4 = bf16[128,1024]{1,0:T(8,128)(2,1)S(1)} copy-done((bf16[128,1024]{1,0:T(8,128)(2,1)S(1)}, bf16[128,1024]{1,0:T(8,128)(2,1)}, u32[]{:S(2)}) %copy-start.4) | copy-done | bytes 262168
  4.2 0.9 %copy-done.6 = bf16[128,1024]{1,0:T(8,128)(2,1)S(1)} copy-done((bf16[128,1024]{1,0:T(8,128)(2,1)S(1)}, bf16[128,1024]{1,0:T(8,128)(2,1)}, u32[]{:S(2)}) %copy-start.6) | copy-done | bytes 262168
  5.1 0.9 %copy-done.8 = f32[32,20,8]{0,2,1:T(8,128)S(1)} copy-done((f32[32,20,8]{0,2,1:T(8,128)S(1)}, f32[32,20,8]{0,2,1:T(8,128)}, u32[]{:S(2)}) %copy-start.8) | copy-done | bytes 20504
  6.0 2.7 %shard_map.86 = (bf16[12,128,128]{2,1,0:T(8,128)(2,1)S(1)}, bf16[4,128,128]{2,1,0:T(8,128)(2,1)S(1)}) custom-call(s32[5]{0:T(128)S(1)} %shift-right-arithmetic_and_fusion.flag_ref, s32[1,128]{1,0:T(1,128)S(1)} %bitcast.6, f32[20,8,32]{2,1,0:T(8,128)S(1)} %bitcast.2, bf16[128,1024]{1,0:T(8,128)(2,1)S(1)} %copy-done.6, bf16[128,1024]{1,0:T(8,128)(2,1)S(1)} %copy-done, ...), custom_call_target="tpu_custom_call" | custom-call | flops 67108864 | bytes 1069588 | tf_op jit(solution)/shard_map/pallas_call | solution.py:370
  8.7 0.5 collective-permute-start
  9.2 1.3 %collective-permute-done.seen_ref = bf16[12,128,128]{2,1,0:T(8,128)(2,1)S(1)} collective-permute-done((bf16[12,128,128]{2,1,0:T(8,128)(2,1)S(1)}, bf16[12,128,128]{2,1,0:T(8,128)(2,1)S(1)}, u32[]{:S(2)}, u32[]{:S(2)}) %collective-permute-start) | collective-permute-done | bytes 393248 | tf_op jit(solution)/shard_map/ppermute | solution.py:353
  10.6 0.6 shard_map.87
  11.6 2.5 %shard_map.88 = (bf16[4,128,128]{2,1,0:T(8,128)(2,1)S(1)}, bf16[4,128,128]{2,1,0:T(8,128)(2,1)S(1)}, bf16[2,8,128,128]{3,2,1,0:T(8,128)(2,1)S(1)}) custom-call(s32[5]{0:T(128)S(1)} %shift-right-arithmetic_and_fusion.flag_ref, s32[1,128]{1,0:T(1,128)S(1)} %bitcast.7, f32[20,8,32]{2,1,0:T(8,128)S(1)} %bitcast.3, bf16[128,1024]{1,0:T(8,128)(2,1)S(1)} %copy-done.7, ...), custom_call_target="tpu_custom_call" | custom-call | flops 100663296 | bytes 1167892 | tf_op jit(solution)/shard_map/pallas_call | solution.py:370
  14.1 2.9 %collective-permute-start.3 = (bf16[4,128,128]{2,1,0:T(8,128)(2,1)S(1)}, bf16[4,128,128]{2,1,0:T(8,128)(2,1)S(1)}, u32[]{:S(2)}, u32[]{:S(2)}) collective-permute-start(bf16[4,128,128]{2,1,0:T(8,128)(2,1)S(1)} %get-tuple-element.25), channel_id=1, source_target_pairs={{0,1},{1,0},{2,3},{3,2},{4,5},{5,4},{6,7},{7,6},{8,9},{9,8},{10,11... | collective-permute-start | bytes 393224 | tf_op jit(solution)/shard_map/ppermute | solution.py:349
  17.1 4.2 %collective-permute-done.3 = bf16[4,128,128]{2,1,0:T(8,128)(2,1)S(1)} collective-permute-done((bf16[4,128,128]{2,1,0:T(8,128)(2,1)S(1)}, bf16[4,128,128]{2,1,0:T(8,128)(2,1)S(1)}, u32[]{:S(2)}, u32[]{:S(2)}) %collective-permute-start.3) | collective-permute-done | bytes 131104 | tf_op jit(solution)/shard_map/ppermute | solution.py:349
  21.4 2.2 %collective-permute-start.4 = (bf16[4,128,128]{2,1,0:T(8,128)(2,1)S(1)}, bf16[4,128,128]{2,1,0:T(8,128)(2,1)S(1)}, u32[]{:S(2)}, u32[]{:S(2)}) collective-permute-start(bf16[4,128,128]{2,1,0:T(8,128)(2,1)S(1)} %add_convert_fusion.1), channel_id=1, source_target_pairs={{0,2},{1,3},{2,0},{3,1},{4,6},{5,7},{6,4},{7,5},{8,10},{9,11},{10,... | collective-permute-start | bytes 393224 | tf_op jit(solution)/shard_map/ppermute | solution.py:349
  23.6 2.5 %collective-permute-start.7 = (bf16[3,128,128]{2,1,0:T(8,128)(2,1)S(1)}, bf16[3,128,128]{2,1,0:T(8,128)(2,1)S(1)}, u32[]{:S(2)}, u32[]{:S(2)}) collective-permute-start(bf16[3,128,128]{2,1,0:T(8,128)(2,1)S(1)} %get-tuple-element.26), channel_id=1, source_target_pairs={{0,6},{1,7},{2,4},{3,5},{4,2},{5,3},{6,0},{7,1},{8,14},{9,15},{10,... | collective-permute-start | bytes 294920 | tf_op jit(solution)/shard_map/ppermute | solution.py:349
  26.2 1.8 %collective-permute-start.9 = (bf16[3,128,128]{2,1,0:T(8,128)(2,1)S(1)}, bf16[3,128,128]{2,1,0:T(8,128)(2,1)S(1)}, u32[]{:S(2)}, u32[]{:S(2)}) collective-permute-start(bf16[3,128,128]{2,1,0:T(8,128)(2,1)S(1)} %get-tuple-element.28), channel_id=1, source_target_pairs={{0,2},{1,3},{2,0},{3,1},{4,6},{5,7},{6,4},{7,5},{8,10},{9,11},{10,... | collective-permute-start | bytes 294920 | tf_op jit(solution)/shard_map/ppermute | solution.py:349
  27.9 4.3 %collective-permute-done.7.refs_0_ = bf16[3,128,128]{2,1,0:T(8,128)(2,1)S(1)} collective-permute-done((bf16[3,128,128]{2,1,0:T(8,128)(2,1)S(1)}, bf16[3,128,128]{2,1,0:T(8,128)(2,1)S(1)}, u32[]{:S(2)}, u32[]{:S(2)}) %collective-permute-start.7) | collective-permute-done | bytes 98336 | tf_op jit(solution)/shard_map/ppermute | solution.py:349
  32.3 1.6 %collective-permute-done.8.refs_1_ = bf16[3,128,128]{2,1,0:T(8,128)(2,1)S(1)} collective-permute-done((bf16[3,128,128]{2,1,0:T(8,128)(2,1)S(1)}, bf16[3,128,128]{2,1,0:T(8,128)(2,1)S(1)}, u32[]{:S(2)}, u32[]{:S(2)}) %collective-permute-start.8) | collective-permute-done | bytes 98336 | tf_op jit(solution)/shard_map/ppermute | solution.py:349
  33.9 2.5 %collective-permute-start.12 = (bf16[1,128,128]{2,1,0:T(8,128)(2,1)S(1)}, bf16[1,128,128]{2,1,0:T(8,128)(2,1)S(1)}, u32[]{:S(2)}, u32[]{:S(2)}) collective-permute-start(bf16[1,128,128]{2,1,0:T(8,128)(2,1)S(1)} %get-tuple-element.30), channel_id=1, source_target_pairs={{0,17},{1,16},{2,19},{3,18},{4,21},{5,20},{6,23},{7,22},{8,25},{9,... | collective-permute-start | bytes 98312 | tf_op jit(solution)/shard_map/ppermute | solution.py:354
  36.5 0.5 collective-permute-start.11
  37.0 0.5 collective-permute-start.10
  37.5 1.0 %collective-permute-start.5 = (bf16[4,128,128]{2,1,0:T(8,128)(2,1)S(1)}, bf16[4,128,128]{2,1,0:T(8,128)(2,1)S(1)}, u32[]{:S(2)}, u32[]{:S(2)}) collective-permute-start(bf16[4,128,128]{2,1,0:T(8,128)(2,1)S(1)} %add_convert_fusion), channel_id=1, source_target_pairs={{0,4},{1,5},{2,6},{3,7},{4,0},{5,1},{6,2},{7,3},{8,12},{9,13},{10,... | collective-permute-start | bytes 393224 | tf_op jit(solution)/shard_map/ppermute | solution.py:349
  38.6 2.3 %collective-permute-start.2 = (bf16[8,128,128]{2,1,0:T(8,128)(2,1)S(1)}, bf16[8,128,128]{2,1,0:T(8,128)(2,1)S(1)}, u32[]{:S(2)}, u32[]{:S(2)}) collective-permute-start(bf16[8,128,128]{2,1,0:T(8,128)(2,1)S(1)} %shard_map.89), channel_id=1, source_target_pairs={{0,2},{1,3},{2,0},{3,1},{4,6},{5,7},{6,4},{7,5},{8,10},{9,11},{10,... | collective-permute-start | bytes 786440 | tf_op jit(solution)/shard_map/ppermute | solution.py:349
  40.9 0.3 collective-permute-done.10.far_ref
  41.3 2.6 %collective-permute-start.15 = (bf16[3,128,128]{2,1,0:T(8,128)(2,1)S(1)}, bf16[3,128,128]{2,1,0:T(8,128)(2,1)S(1)}, u32[]{:S(2)}, u32[]{:S(2)}) collective-permute-start(bf16[3,128,128]{2,1,0:T(8,128)(2,1)S(1)} %shard_map.91.piece0_ref), channel_id=1, source_target_pairs={{0,6},{1,7},{2,4},{3,5},{4,2},{5,3},{6,0},{7,1},{8,14},{9,15},{10,... | collective-permute-start | bytes 294920 | tf_op jit(solution)/shard_map/ppermute | solution.py:349
  43.9 1.8 %collective-permute-start.13 = (bf16[3,128,128]{2,1,0:T(8,128)(2,1)S(1)}, bf16[3,128,128]{2,1,0:T(8,128)(2,1)S(1)}, u32[]{:S(2)}, u32[]{:S(2)}) collective-permute-start(bf16[3,128,128]{2,1,0:T(8,128)(2,1)S(1)} %shard_map.91.piece0_ref), channel_id=1, source_target_pairs={{0,2},{1,3},{2,0},{3,1},{4,6},{5,7},{6,4},{7,5},{8,10},{9,11},{10,... | collective-permute-start | bytes 294920 | tf_op jit(solution)/shard_map/ppermute | solution.py:349
  45.7 5.8 %collective-permute-done.15.piece3_ref = bf16[3,128,128]{2,1,0:T(8,128)(2,1)S(1)} collective-permute-done((bf16[3,128,128]{2,1,0:T(8,128)(2,1)S(1)}, bf16[3,128,128]{2,1,0:T(8,128)(2,1)S(1)}, u32[]{:S(2)}, u32[]{:S(2)}) %collective-permute-start.15) | collective-permute-done | bytes 98336 | tf_op jit(solution)/shard_map/ppermute | solution.py:349
  51.6 1.0 %collective-permute-done.13.piece1_ref = bf16[3,128,128]{2,1,0:T(8,128)(2,1)S(1)} collective-permute-done((bf16[3,128,128]{2,1,0:T(8,128)(2,1)S(1)}, bf16[3,128,128]{2,1,0:T(8,128)(2,1)S(1)}, u32[]{:S(2)}, u32[]{:S(2)}) %collective-permute-start.13) | collective-permute-done | bytes 98336 | tf_op jit(solution)/shard_map/ppermute | solution.py:349
  52.7 1.5 %collective-permute-start.6 = (bf16[4,128,128]{2,1,0:T(8,128)(2,1)S(1)}, bf16[4,128,128]{2,1,0:T(8,128)(2,1)S(1)}, u32[]{:S(2)}, u32[]{:S(2)}) collective-permute-start(bf16[4,128,128]{2,1,0:T(8,128)(2,1)S(1)} %collective-permute-done.5.two_own_ref), channel_id=1, source_target_pairs={{0,1},{1,0},{2,3},{3,2},{4,5},{5,4},{6,7},{7,6},{8,9},{9,8},{10,11... | collective-permute-start | bytes 393224 | tf_op jit(solution)/shard_map/ppermute | solution.py:349
  54.2 2.0 %shard_map.85 = (f32[128,1024]{1,0:T(8,128)S(1)}, f32[128,1024]{1,0:T(8,128)S(1)}, f32[128,1024]{1,0:T(8,128)S(1)}) custom-call(s32[1,128]{1,0:T(1,128)S(1)} %bitcast.8, f32[20,8,32]{2,1,0:T(8,128)S(1)} %bitcast.4, bf16[128,1024]{1,0:T(8,128)(2,1)S(1)} %copy-done.7, bf16[128,1024]{1,0:T(8,128)(2,1)S(1)} %copy-done.1, bf16[128,1024]{1,0:T(8,128)(2,1)S(1)} %copy-done.3, ...), custom_call_target="tpu_custom_call" | custom-call | flops 167772160 | bytes 1069568 | tf_op jit(solution)/shard_map/pallas_call | solution.py:370
  56.2 2.4 %collective-permute-done.6.two_other_ref = bf16[4,128,128]{2,1,0:T(8,128)(2,1)S(1)} collective-permute-done((bf16[4,128,128]{2,1,0:T(8,128)(2,1)S(1)}, bf16[4,128,128]{2,1,0:T(8,128)(2,1)S(1)}, u32[]{:S(2)}, u32[]{:S(2)}) %collective-permute-start.6) | collective-permute-done | bytes 131104 | tf_op jit(solution)/shard_map/ppermute | solution.py:349
  58.6 2.8 %shard_map.93 = (bf16[128,1024]{1,0:T(8,128)(2,1)}, bf16[128,1024]{1,0:T(8,128)(2,1)}, bf16[128,1024]{1,0:T(8,128)(2,1)}) custom-call(s32[5]{0:T(128)S(1)} %shift-right-arithmetic_and_fusion.flag_ref, s32[1,128]{1,0:T(1,128)S(1)} %bitcast.9, f32[20,8,32]{2,1,0:T(8,128)S(1)} %bitcast.5, bf16[128,1024]{1,0:T(8,128)(2,1)S(1)} %copy-done.1, ...), custom_call_target="tpu_custom_call" | custom-call | flops 234881024 | bytes 4084244 | tf_op jit(solution)/shard_map/pallas_call | solution.py:370
  (36 shorter events, 1.0 us)
Async XLA Ops:
  0.6 0.7 %copy-start.10 = (s32[128]{0:T(128)S(1)}, s32[128]{0:T(128)}, u32[]{:S(2)}) copy-start(s32[128]{0:T(128)} %param.10) | copy-start | bytes 1540
  1.3 0.9 %copy-start = (bf16[128,1024]{1,0:T(8,128)(2,1)S(1)}, bf16[128,1024]{1,0:T(8,128)(2,1)}, u32[]{:S(2)}) copy-start(bf16[128,1024]{1,0:T(8,128)(2,1)} %k_ref.5) | copy-start | bytes 786436
  2.3 0.9 %copy-start.2 = (bf16[128,1024]{1,0:T(8,128)(2,1)S(1)}, bf16[128,1024]{1,0:T(8,128)(2,1)}, u32[]{:S(2)}) copy-start(bf16[128,1024]{1,0:T(8,128)(2,1)} %v_ref.5) | copy-start | bytes 786436
  3.2 0.9 %copy-start.4 = (bf16[128,1024]{1,0:T(8,128)(2,1)S(1)}, bf16[128,1024]{1,0:T(8,128)(2,1)}, u32[]{:S(2)}) copy-start(bf16[128,1024]{1,0:T(8,128)(2,1)} %g_ref.5) | copy-start | bytes 786436
  4.2 0.9 %copy-start.6 = (bf16[128,1024]{1,0:T(8,128)(2,1)S(1)}, bf16[128,1024]{1,0:T(8,128)(2,1)}, u32[]{:S(2)}) copy-start(bf16[128,1024]{1,0:T(8,128)(2,1)} %q_ref.3) | copy-start | bytes 786436
  5.1 0.9 %copy-start.8 = (f32[32,20,8]{0,2,1:T(8,128)S(1)}, f32[32,20,8]{0,2,1:T(8,128)}, u32[]{:S(2)}) copy-start(f32[32,20,8]{0,2,1:T(8,128)} %param.11) | copy-start | bytes 61444
  6.0 5.2 %copy-start.5 = (bf16[128,1024]{1,0:T(8,128)(2,1)S(1)}, bf16[128,1024]{1,0:T(8,128)(2,1)}, u32[]{:S(2)}) copy-start(bf16[128,1024]{1,0:T(8,128)(2,1)} %g_ref.5) | copy-start | bytes 786436
  6.0 5.2 %copy-start.7 = (bf16[128,1024]{1,0:T(8,128)(2,1)S(1)}, bf16[128,1024]{1,0:T(8,128)(2,1)}, u32[]{:S(2)}) copy-start(bf16[128,1024]{1,0:T(8,128)(2,1)} %q_ref.3) | copy-start | bytes 786436
  6.0 5.2 %copy-start.9 = (f32[32,20,8]{0,2,1:T(8,128)S(1)}, f32[32,20,8]{0,2,1:T(8,128)}, u32[]{:S(2)}) copy-start(f32[32,20,8]{0,2,1:T(8,128)} %param.11) | copy-start | bytes 61444
  8.7 1.9 %collective-permute-start = (bf16[12,128,128]{2,1,0:T(8,128)(2,1)S(1)}, bf16[12,128,128]{2,1,0:T(8,128)(2,1)S(1)}, u32[]{:S(2)}, u32[]{:S(2)}) collective-permute-start(bf16[12,128,128]{2,1,0:T(8,128)(2,1)S(1)} %get-tuple-element.20), channel_id=1, source_target_pairs={{0,8},{8,0},{16,24},{24,16},{1,9},{9,1},{17,25},{25,17},{2,10},{10... | collective-permute-start | bytes 1179656 | tf_op jit(solution)/shard_map/ppermute | solution.py:353
  10.6 0.9 %copy-start.1 = (bf16[128,1024]{1,0:T(8,128)(2,1)S(1)}, bf16[128,1024]{1,0:T(8,128)(2,1)}, u32[]{:S(2)}) copy-start(bf16[128,1024]{1,0:T(8,128)(2,1)} %k_ref.5) | copy-start | bytes 786436
  10.6 1.0 %copy-start.3 = (bf16[128,1024]{1,0:T(8,128)(2,1)S(1)}, bf16[128,1024]{1,0:T(8,128)(2,1)}, u32[]{:S(2)}) copy-start(bf16[128,1024]{1,0:T(8,128)(2,1)} %v_ref.5) | copy-start | bytes 786436
  14.1 7.2 %collective-permute-start.3 = (bf16[4,128,128]{2,1,0:T(8,128)(2,1)S(1)}, bf16[4,128,128]{2,1,0:T(8,128)(2,1)S(1)}, u32[]{:S(2)}, u32[]{:S(2)}) collective-permute-start(bf16[4,128,128]{2,1,0:T(8,128)(2,1)S(1)} %get-tuple-element.25), channel_id=1, source_target_pairs={{0,1},{1,0},{2,3},{3,2},{4,5},{5,4},{6,7},{7,6},{8,9},{9,8},{10,11... | collective-permute-start | bytes 393224 | tf_op jit(solution)/shard_map/ppermute | solution.py:349
  17.0 21.5 %collective-permute-start.1 = (bf16[2,8,128,128]{3,2,1,0:T(8,128)(2,1)S(1)}, bf16[2,8,128,128]{3,2,1,0:T(8,128)(2,1)S(1)}, u32[]{:S(2)}, u32[]{:S(2)}) collective-permute-start(bf16[2,8,128,128]{3,2,1,0:T(8,128)(2,1)S(1)} %get-tuple-element.23.near_ref), channel_id=1, source_target_pairs={{0,1},{1,0},{2,3},{3,2},{4,5},{5,4},{6,7},{7,6},{8,9},{9,8},{10,11... | collective-permute-start | bytes 1572872 | tf_op jit(solution)/shard_map/ppermute | solution.py:349
  21.4 16.1 %collective-permute-start.4 = (bf16[4,128,128]{2,1,0:T(8,128)(2,1)S(1)}, bf16[4,128,128]{2,1,0:T(8,128)(2,1)S(1)}, u32[]{:S(2)}, u32[]{:S(2)}) collective-permute-start(bf16[4,128,128]{2,1,0:T(8,128)(2,1)S(1)} %add_convert_fusion.1), channel_id=1, source_target_pairs={{0,2},{1,3},{2,0},{3,1},{4,6},{5,7},{6,4},{7,5},{8,10},{9,11},{10,... | collective-permute-start | bytes 393224 | tf_op jit(solution)/shard_map/ppermute | solution.py:349
  23.6 8.7 %collective-permute-start.7 = (bf16[3,128,128]{2,1,0:T(8,128)(2,1)S(1)}, bf16[3,128,128]{2,1,0:T(8,128)(2,1)S(1)}, u32[]{:S(2)}, u32[]{:S(2)}) collective-permute-start(bf16[3,128,128]{2,1,0:T(8,128)(2,1)S(1)} %get-tuple-element.26), channel_id=1, source_target_pairs={{0,6},{1,7},{2,4},{3,5},{4,2},{5,3},{6,0},{7,1},{8,14},{9,15},{10,... | collective-permute-start | bytes 294920 | tf_op jit(solution)/shard_map/ppermute | solution.py:349
  26.0 7.9 %collective-permute-start.8 = (bf16[3,128,128]{2,1,0:T(8,128)(2,1)S(1)}, bf16[3,128,128]{2,1,0:T(8,128)(2,1)S(1)}, u32[]{:S(2)}, u32[]{:S(2)}) collective-permute-start(bf16[3,128,128]{2,1,0:T(8,128)(2,1)S(1)} %get-tuple-element.27), channel_id=1, source_target_pairs={{0,4},{1,5},{2,6},{3,7},{4,0},{5,1},{6,2},{7,3},{8,12},{9,13},{10,... | collective-permute-start | bytes 294920 | tf_op jit(solution)/shard_map/ppermute | solution.py:349
  26.2 7.7 %collective-permute-start.9 = (bf16[3,128,128]{2,1,0:T(8,128)(2,1)S(1)}, bf16[3,128,128]{2,1,0:T(8,128)(2,1)S(1)}, u32[]{:S(2)}, u32[]{:S(2)}) collective-permute-start(bf16[3,128,128]{2,1,0:T(8,128)(2,1)S(1)} %get-tuple-element.28), channel_id=1, source_target_pairs={{0,2},{1,3},{2,0},{3,1},{4,6},{5,7},{6,4},{7,5},{8,10},{9,11},{10,... | collective-permute-start | bytes 294920 | tf_op jit(solution)/shard_map/ppermute | solution.py:349
  33.9 7.0 %collective-permute-start.12 = (bf16[1,128,128]{2,1,0:T(8,128)(2,1)S(1)}, bf16[1,128,128]{2,1,0:T(8,128)(2,1)S(1)}, u32[]{:S(2)}, u32[]{:S(2)}) collective-permute-start(bf16[1,128,128]{2,1,0:T(8,128)(2,1)S(1)} %get-tuple-element.30), channel_id=1, source_target_pairs={{0,17},{1,16},{2,19},{3,18},{4,21},{5,20},{6,23},{7,22},{8,25},{9,... | collective-permute-start | bytes 98312 | tf_op jit(solution)/shard_map/ppermute | solution.py:354
  36.5 4.4 %collective-permute-start.11 = (bf16[1,128,128]{2,1,0:T(8,128)(2,1)S(1)}, bf16[1,128,128]{2,1,0:T(8,128)(2,1)S(1)}, u32[]{:S(2)}, u32[]{:S(2)}) collective-permute-start(bf16[1,128,128]{2,1,0:T(8,128)(2,1)S(1)} %get-tuple-element.30), channel_id=1, source_target_pairs={{0,16},{8,24},{16,0},{24,8},{1,17},{9,25},{17,1},{25,9},{2,18},{10... | collective-permute-start | bytes 98312 | tf_op jit(solution)/shard_map/ppermute | solution.py:353
  37.0 4.3 %collective-permute-start.10 = (bf16[2,128,128]{2,1,0:T(8,128)(2,1)S(1)}, bf16[2,128,128]{2,1,0:T(8,128)(2,1)S(1)}, u32[]{:S(2)}, u32[]{:S(2)}) collective-permute-start(bf16[2,128,128]{2,1,0:T(8,128)(2,1)S(1)} %get-tuple-element.29.below_ref), channel_id=1, source_target_pairs={{0,1},{1,0},{2,3},{3,2},{4,5},{5,4},{6,7},{7,6},{8,9},{9,8},{10,11... | collective-permute-start | bytes 196616 | tf_op jit(solution)/shard_map/ppermute | solution.py:349
  37.5 15.2 %collective-permute-start.5 = (bf16[4,128,128]{2,1,0:T(8,128)(2,1)S(1)}, bf16[4,128,128]{2,1,0:T(8,128)(2,1)S(1)}, u32[]{:S(2)}, u32[]{:S(2)}) collective-permute-start(bf16[4,128,128]{2,1,0:T(8,128)(2,1)S(1)} %add_convert_fusion), channel_id=1, source_target_pairs={{0,4},{1,5},{2,6},{3,7},{4,0},{5,1},{6,2},{7,3},{8,12},{9,13},{10,... | collective-permute-start | bytes 393224 | tf_op jit(solution)/shard_map/ppermute | solution.py:349
  38.6 20.0 %collective-permute-start.2 = (bf16[8,128,128]{2,1,0:T(8,128)(2,1)S(1)}, bf16[8,128,128]{2,1,0:T(8,128)(2,1)S(1)}, u32[]{:S(2)}, u32[]{:S(2)}) collective-permute-start(bf16[8,128,128]{2,1,0:T(8,128)(2,1)S(1)} %shard_map.89), channel_id=1, source_target_pairs={{0,2},{1,3},{2,0},{3,1},{4,6},{5,7},{6,4},{7,5},{8,10},{9,11},{10,... | collective-permute-start | bytes 786440 | tf_op jit(solution)/shard_map/ppermute | solution.py:349
  41.3 10.3 %collective-permute-start.15 = (bf16[3,128,128]{2,1,0:T(8,128)(2,1)S(1)}, bf16[3,128,128]{2,1,0:T(8,128)(2,1)S(1)}, u32[]{:S(2)}, u32[]{:S(2)}) collective-permute-start(bf16[3,128,128]{2,1,0:T(8,128)(2,1)S(1)} %shard_map.91.piece0_ref), channel_id=1, source_target_pairs={{0,6},{1,7},{2,4},{3,5},{4,2},{5,3},{6,0},{7,1},{8,14},{9,15},{10,... | collective-permute-start | bytes 294920 | tf_op jit(solution)/shard_map/ppermute | solution.py:349
  43.9 7.7 %collective-permute-start.14 = (bf16[3,128,128]{2,1,0:T(8,128)(2,1)S(1)}, bf16[3,128,128]{2,1,0:T(8,128)(2,1)S(1)}, u32[]{:S(2)}, u32[]{:S(2)}) collective-permute-start(bf16[3,128,128]{2,1,0:T(8,128)(2,1)S(1)} %shard_map.91.piece0_ref), channel_id=1, source_target_pairs={{0,4},{1,5},{2,6},{3,7},{4,0},{5,1},{6,2},{7,3},{8,12},{9,13},{10,... | collective-permute-start | bytes 294920 | tf_op jit(solution)/shard_map/ppermute | solution.py:349
  43.9 8.7 %collective-permute-start.13 = (bf16[3,128,128]{2,1,0:T(8,128)(2,1)S(1)}, bf16[3,128,128]{2,1,0:T(8,128)(2,1)S(1)}, u32[]{:S(2)}, u32[]{:S(2)}) collective-permute-start(bf16[3,128,128]{2,1,0:T(8,128)(2,1)S(1)} %shard_map.91.piece0_ref), channel_id=1, source_target_pairs={{0,2},{1,3},{2,0},{3,1},{4,6},{5,7},{6,4},{7,5},{8,10},{9,11},{10,... | collective-permute-start | bytes 294920 | tf_op jit(solution)/shard_map/ppermute | solution.py:349
  52.6 3.6 %collective-permute-start.16 = (bf16[1,4,128,128]{3,2,1,0:T(8,128)(2,1)S(1)}, bf16[1,4,128,128]{3,2,1,0:T(8,128)(2,1)S(1)}, u32[]{:S(2)}, u32[]{:S(2)}) collective-permute-start(bf16[1,4,128,128]{3,2,1,0:T(8,128)(2,1)S(1)} %shard_map.92.split_own_ref), channel_id=1, source_target_pairs={{0,8},{8,0},{16,24},{24,16},{1,9},{9,1},{17,25},{25,17},{2,10},{10... | collective-permute-start | bytes 393224 | tf_op jit(solution)/shard_map/ppermute | solution.py:353
  52.7 5.9 %collective-permute-start.6 = (bf16[4,128,128]{2,1,0:T(8,128)(2,1)S(1)}, bf16[4,128,128]{2,1,0:T(8,128)(2,1)S(1)}, u32[]{:S(2)}, u32[]{:S(2)}) collective-permute-start(bf16[4,128,128]{2,1,0:T(8,128)(2,1)S(1)} %collective-permute-done.5.two_own_ref), channel_id=1, source_target_pairs={{0,1},{1,0},{2,3},{3,2},{4,5},{5,4},{6,7},{7,6},{8,9},{9,8},{10,11... | collective-permute-start | bytes 393224 | tf_op jit(solution)/shard_map/ppermute | solution.py:349

commit v4 on v3

--- a/solution.py
+++ b/solution.py
@@ -9,6 +9,7 @@
 
 NEAR = 3
 VMEM_BYTES = 16 * 1024 * 1024
+FIRST_BYTES = 16 * 1024 * 1024
 
 
 def level_bits(amount):
@@ -73,8 +74,8 @@
     keep_ref,
     *rest,
 ):
-    lead_refs = rest[:-7]
-    class_ref, table_ref, q_ref, k_ref, v_ref, g_ref, arrived = rest[-7:]
+    lead_refs = rest[:-8]
+    class_ref, table_ref, q_ref, k_ref, v_ref, g_ref, late_ref, arrived = rest[-8:]
     moves = [
         pltpu.make_async_copy(source, target, arrived.at[place])
         for place, (source, target) in enumerate(
@@ -109,23 +110,21 @@
             elif level == split - 1:
                 sent_ref[head] = value
             else:
-                row = (level - split) * half + head % half
-
-                @pl.when(core == head // half)
-                def _():
-                    keep_ref[row] = value
-
-                @pl.when(core != head // half)
-                def _():
-                    sent_ref[head_count + row] = value
+                late_ref[level - split, head] = value
 
         columns = pl.ds(head * head_size, head_size)
         payload_cell(
             flags, gates, rows, range(len(levels)), q_ref, k_ref, v_ref, g_ref, columns, store
         )
-
-
-def share_kernel(head_count, places, flag_ref, seen_ref, keep_ref, *refs):
+    for place in range(levels[-1] + 1 - split):
+        row = place * half
+        keep_ref[row : row + half] = late_ref[place, pl.ds(core * half, half)]
+        sent_ref[head_count + row : head_count + row + half] = late_ref[
+            place, pl.ds((1 - core) * half, half)
+        ]
+
+
+def share_kernel(head_count, places, flag_ref, seen_ref, keep_ref, after_ref, *refs):
     lead_refs = refs[:-4]
     out_refs = refs[-4:]
     quarter = head_count // 4
@@ -159,8 +158,9 @@
     g_ref,
     after_ref,
     two_own_ref,
-    two_other_ref,
-    near_ref,
+    sent_ref,
+    zero_ref,
+    two_ref,
 ):
     head_count = table_ref.shape[1]
     half = head_count // 2
@@ -171,23 +171,20 @@
         rows = [place * head_count + head for place in range(NEAR)]
 
         def store(place, value):
-            if place < 2:
-                near_ref[place, head] = value
-                return
-
-            @pl.when(x_place == head // half)
-            def _():
-                two_own_ref[head % half] = value
-
-            @pl.when(x_place != head // half)
-            def _():
-                two_other_ref[head % half] = value
+            if place == 0:
+                zero_ref[head] = value
+            elif place == 1:
+                sent_ref[half + head] = value
+            else:
+                two_ref[head] = value
 
         columns = pl.ds(head * head_size, head_size)
         payload_cell(flags, gates, rows, range(NEAR), q_ref, k_ref, v_ref, g_ref, columns, store)
-
-
-def four_sum_kernel(top_rows, own_ref, *refs):
+    two_own_ref[...] = two_ref[pl.ds(x_place * half, half)]
+    sent_ref[:half] = two_ref[pl.ds((1 - x_place) * half, half)]
+
+
+def four_sum_kernel(top_rows, own_ref, after_ref, *refs):
     came_refs = refs[:-2]
     below_ref, top_ref = refs[-2:]
     total = wide(own_ref[...])
@@ -213,12 +210,27 @@
             out_ref[level, offs * eighth : (offs + 1) * eighth] = piece_ref[first : first + eighth]
 
 
-def near_sum_kernel(near_ref, seen_ref, one_ref):
-    one_ref[...] = narrow(wide(near_ref[1]) + wide(seen_ref[1]))
+def lower_sum_kernel(own_ref, sent_ref, seen_ref, after_ref, two_ref, one_ref):
+    half = own_ref.shape[0]
+    two_ref[...] = narrow(wide(own_ref[...]) + wide(seen_ref[:half]))
+    one_ref[...] = narrow(wide(sent_ref[half:]) + wide(seen_ref[half:]))
 
 
 def local_kernel(
-    block_depth, head_size, class_ref, table_ref, q_ref, k_ref, v_ref, g_ref, qo_ref, ko_ref, vo_ref
+    block_depth,
+    head_size,
+    class_ref,
+    table_ref,
+    q_ref,
+    k_ref,
+    v_ref,
+    g_ref,
+    after_ref,
+    held_ref,
+    qo_ref,
+    ko_ref,
+    vo_ref,
+    held_out_ref,
 ):
     head_count = table_ref.shape[1]
     tokens = q_ref.shape[0]
@@ -263,7 +275,7 @@
     ql_ref,
     kl_ref,
     vl_ref,
-    near_ref,
+    zero_ref,
     one_ref,
     two_own_ref,
     two_other_ref,
@@ -286,7 +298,7 @@
     x_place = flag_ref[0]
     z_place = flag_ref[1] + 2 * flag_ref[2]
     core = flag_ref[inner]
-    held_ref[0] = near_ref[0]
+    held_ref[0] = zero_ref[...]
     held_ref[1] = one_ref[...]
     held_ref[2, pl.ds(x_place * half, half)] = two_own_ref[...]
     held_ref[2, pl.ds((1 - x_place) * half, half)] = two_other_ref[...]
@@ -360,20 +372,20 @@
     hbm = pl.BlockSpec(memory_space=pltpu.HBM)
     anywhere = pl.BlockSpec(memory_space=pl.ANY)
     cell = (head_size, head_size)
-    params = pltpu.CompilerParams(vmem_limit_bytes=VMEM_BYTES)
 
     def cells(*lead):
         return jax.ShapeDtypeStruct(lead + cell, jnp.bfloat16)
 
-    def call(kernel, in_specs, outs, operands, flops=0, scratch=()):
+    def call(kernel, in_specs, outs, operands, flops=0, scratch=(), grant=VMEM_BYTES, out_specs=None, aliases=None):
         moved = sum(operand.size * operand.dtype.itemsize for operand in operands)
         return pl.pallas_call(
             kernel,
             out_shape=outs,
             in_specs=in_specs,
-            out_specs=jax.tree.map(lambda _: vmem, outs),
+            out_specs=out_specs or jax.tree.map(lambda _: vmem, outs),
+            input_output_aliases=aliases or {},
             scratch_shapes=scratch,
-            compiler_params=params,
+            compiler_params=pltpu.CompilerParams(vmem_limit_bytes=grant),
             cost_estimate=pl.CostEstimate(flops=flops, bytes_accessed=moved, transcendentals=0),
         )(*operands)
 
@@ -388,6 +400,7 @@
     block = pltpu.VMEM((row_count, width), jnp.bfloat16)
 
     levels = tuple(range(NEAR, total))
+    first_reads = (class_lanes, table, query_rows, key_rows, value_rows, out_grad)
     outs = (cells(head_count + split_levels * half), cells(split_levels * half))
     if whole_levels > 1:
         outs = outs + (cells(whole_levels - 1, head_count),)
@@ -395,7 +408,7 @@
         functools.partial(upper_kernel, levels, split, offset, head_size),
         [smem] + [hbm] * 6,
         outs,
-        (flag_bits, class_lanes, table, query_rows, key_rows, value_rows, out_grad),
+        (flag_bits, *[pltpu.with_memory_space_constraint(held, pltpu.HBM) for held in first_reads]),
         flops=2 * len(levels) * row_count * width * head_size,
         scratch=[
             pltpu.VMEM(class_lanes.shape, jnp.int32),
@@ -404,15 +417,35 @@
             block,
             block,
             block,
+            pltpu.VMEM((split_levels, head_count) + cell, jnp.bfloat16),
             pltpu.SemaphoreType.DMA((6,)),
         ],
+        grant=FIRST_BYTES,
     )
     seen = swap(sent, inner_bits)
+    two_own, lower_sent, zero = call(
+        functools.partial(lower_kernel, offset, head_size),
+        [smem] + [vmem] * 6 + [anywhere],
+        (cells(half), cells(half + head_count), cells(head_count)),
+        (flag_bits, class_lanes, table, query_rows, key_rows, value_rows, out_grad, keep),
+        flops=2 * NEAR * row_count * width * head_size,
+        scratch=[pltpu.VMEM((head_count,) + cell, jnp.bfloat16)],
+    )
     own_share, *shares_out = call(
         functools.partial(share_kernel, head_count, (whole_levels, split_levels)),
-        [smem] + [vmem] * (2 + len(lead)),
+        [smem] + [vmem] * 2 + [anywhere] + [vmem] * len(lead),
         (cells(share_rows),) * 4,
-        (flag_bits, seen, keep, *lead),
+        (flag_bits, seen, keep, two_own, *lead),
+    )
+    big = jax.ShapeDtypeStruct((row_count, width), jnp.float32)
+    query_local, key_local, value_local, zero = call(
+        functools.partial(local_kernel, block_depth, head_size),
+        [vmem] * 6 + [anywhere] * 2,
+        (big, big, big, cells(head_count)),
+        (class_lanes, table, query_rows, key_rows, value_rows, out_grad, own_share, zero),
+        out_specs=(vmem, vmem, vmem, anywhere),
+        aliases={7: 3},
+        flops=10 * row_count * width * row_count,
     )
 
     def z_bits(offs):
@@ -422,9 +455,9 @@
     top = total - 1
     below, top_sent = call(
         functools.partial(four_sum_kernel, eighth),
-        [vmem] * 4,
+        [vmem, anywhere] + [vmem] * 3,
         (cells(share_rows - eighth), cells(eighth)),
-        (own_share, *came),
+        (own_share, query_local, *came),
     )
     middle = [bit for bit in range(NEAR, top) if bit != inner_bits]
     if middle:
@@ -460,29 +493,17 @@
     )
     split_other = swap(split_own, inner_bits)
 
-    two_own, two_other, near = call(
-        functools.partial(lower_kernel, offset, head_size),
-        [smem] + [vmem] * 6 + [anywhere],
-        (cells(half), cells(half), cells(2, head_count)),
-        (flag_bits, class_lanes, table, query_rows, key_rows, value_rows, out_grad, own_share),
-        flops=2 * NEAR * row_count * width * head_size,
-    )
-    two_sum = narrow(wide(two_own) + wide(swap(two_other, 0)))
-    near_seen = swap(near, 0)
-    one_sum = call(near_sum_kernel, [vmem] * 2, cells(head_count), (near, near_seen))
-    one_done = swap(one_sum, 1)
+    two_sum, one_sum = call(
+        lower_sum_kernel,
+        [vmem] * 3 + [anywhere],
+        (cells(half), cells(head_count)),
+        (two_own, lower_sent, swap(lower_sent, 0), query_local),
+    )
     two_sum = narrow(wide(two_sum) + wide(swap(two_sum, 1)))
     two_half = swap(two_sum, 2)
     two_rest = swap(two_half, 0)
-
-    big = jax.ShapeDtypeStruct((row_count, width), jnp.float32)
-    query_local, key_local, value_local = call(
-        functools.partial(local_kernel, block_depth, head_size),
-        [vmem] * 6,
-        (big, big, big),
-        (class_lanes, table, query_rows, key_rows, value_rows, out_grad),
-        flops=10 * row_count * width * row_count,
-    )
+    one_done = swap(one_sum, 1)
+    zero_done = swap(zero, 0)
 
     small = jax.ShapeDtypeStruct((row_count, width), jnp.bfloat16)
     return call(
@@ -499,7 +520,7 @@
             query_local,
             key_local,
             value_local,
-            near_seen,
+            zero_done,
             one_done,
             two_half,
             two_rest,

time: 61.7 us -> 53.2 us (0.86)
  local copies, waits for them, and re-layouts: 5.75 us -> 0.14 us
  Pallas kernels: 10.8 us -> 9.08 us
  starting transfers between devices: 23 us -> 21.3 us
    unnamed x22 -> x12, local copies, waits for them, and re-layouts: 5.75 us -> 0.14 us
    ppermute x1, waiting for transfers between devices: 0.01 us -> 2.05 us  [swap(): lax.ppermute(block, ('gx', 'gy'), [(i, i ^ mask) for i in range(device_co...]
    ppermute x13, starting transfers between devices: 19.3 us -> 17.7 us  [swap(): return lax.ppermute(block, 'gy', [(i, i ^ mask) for i in range(inner_size)])]
    pallas_call x9, Pallas kernels: 10.8 us -> 9.08 us  [call(): pl.pallas_call(kernel, out_shape=outs, in_specs=in_specs, out_specs=out_s...]
    ppermute x3, waiting for transfers between devices: 1.35 us -> 0.5 us  [swap(): return lax.ppermute(block, 'gx', [(i, i ^ mask) for i in range(size)])]
  transfers between devices with their start and end apart: 17 -> 17, of which waited for: 8 -> 9; matrix products, arithmetic and copies ran while one was open for 0% -> 0% of each run, Pallas kernels for 4% -> 8%
where the time goes in v4:
time: 53.2 us; the launch traced here: 53 us
  waiting for transfers between devices  21.7 us (41%)
  starting transfers between devices  21.3 us (40%)
  Pallas kernels  9.08 us (17%)
  between operations  0.78 us (1%)
    ppermute x13, waiting for transfers between devices, swap(): return lax.ppermute(block, 'gy', [(i, i ^ mask) for i in range(inner_size)])  19.1 us
    ppermute x13, starting transfers between devices, swap(): return lax.ppermute(block, 'gy', [(i, i ^ mask) for i in range(inner_size)])  17.7 us
    pallas_call x9, Pallas kernels, call(): pl.pallas_call(kernel, out_shape=outs, in_specs=in_specs, out_specs=out_s...  9.08 us
    ppermute x1, starting transfers between devices, swap(): lax.ppermute(block, ('gx', 'gy'), [(i, i ^ mask) for i in range(device_co...  2.55 us
    ppermute x1, waiting for transfers between devices, swap(): lax.ppermute(block, ('gx', 'gy'), [(i, i ^ mask) for i in range(device_co...  2.05 us
    ppermute x3, starting transfers between devices, swap(): return lax.ppermute(block, 'gx', [(i, i ^ mask) for i in range(size)])  1.09 us
  transfers between devices with their start and end apart: 17, of which 9 were waited for; matrix products, arithmetic and copies ran while one was open for 0% of the time, Pallas kernels for 8%

profile of v4, /device:TPU:0, one launch (start us, length us, event | category | flops | bytes accessed | tf_op | source)
XLA Modules:
  0.0 53.0 jit_solution(5286360369565583501)
XLA Ops:
  0.7 2.3 %shard_map.85 = (bf16[12,128,128]{2,1,0:T(8,128)(2,1)S(1)}, bf16[4,128,128]{2,1,0:T(8,128)(2,1)S(1)}) custom-call(s32[5]{0:T(128)S(1)} %shift-right-arithmetic_and_fusion.flag_ref, s32[1,128]{1,0:T(1,128)} %bitcast.6, f32[20,8,32]{2,1,0:T(8,128)} %bitcast.2, bf16[128,1024]{1,0:T(8,128)(2,1)} %q_ref.3, bf16[128,1024]{1,0:T(8,128)(2,1)} %k_ref.5, ...), custom_call_target="tpu_custom_call" | custom-call | flops 67108864 | bytes 1069588 | tf_op jit(solution)/shard_map/pallas_call | solution.py:381
  3.0 0.5 collective-permute-start
  3.5 0.1 copy-done.5
  3.6 1.2 %shard_map.86 = (bf16[4,128,128]{2,1,0:T(8,128)(2,1)S(1)}, bf16[12,128,128]{2,1,0:T(8,128)(2,1)S(1)}, bf16[8,128,128]{2,1,0:T(8,128)(2,1)S(1)}) custom-call(s32[5]{0:T(128)S(1)} %shift-right-arithmetic_and_fusion.flag_ref, s32[1,128]{1,0:T(1,128)S(1)} %bitcast.7, f32[20,8,32]{2,1,0:T(8,128)S(1)} %bitcast.3, bf16[128,1024]{1,0:T(8,128)(2,1)S(1)} %copy-done.3, ...), custom_call_target="tpu_custom_call" | custom-call | flops 100663296 | bytes 1200660 | tf_op jit(solution)/shard_map/pallas_call | solution.py:381
  4.8 3.0 %collective-permute-start.2 = (bf16[12,128,128]{2,1,0:T(8,128)(2,1)S(1)}, bf16[12,128,128]{2,1,0:T(8,128)(2,1)S(1)}, u32[]{:S(2)}, u32[]{:S(2)}) collective-permute-start(bf16[12,128,128]{2,1,0:T(8,128)(2,1)S(1)} %get-tuple-element.29.sent_ref), channel_id=1, source_target_pairs={{0,1},{1,0},{2,3},{3,2},{4,5},{5,4},{6,7},{7,6},{8,9},{9,8},{10,11... | collective-permute-start | bytes 1179656 | tf_op jit(solution)/shard_map/ppermute | solution.py:361
  7.8 0.6 %shard_map.87 = (bf16[3,128,128]{2,1,0:T(8,128)(2,1)S(1)}, bf16[3,128,128]{2,1,0:T(8,128)(2,1)S(1)}, bf16[3,128,128]{2,1,0:T(8,128)(2,1)S(1)}, bf16[3,128,128]{2,1,0:T(8,128)(2,1)S(1)}) custom-call(s32[5]{0:T(128)S(1)} %shift-right-arithmetic_and_fusion.flag_ref, bf16[12,128,128]{2,1,0:T(8,128)(2,1)S(1)} %collective-permute-done.seen_ref, ...), custom_call_target="tpu_custom_call" | custom-call | bytes 655380 | tf_op jit(solution)/shard_map/pallas_call | solution.py:381
  8.4 3.7 %collective-permute-start.7 = (bf16[3,128,128]{2,1,0:T(8,128)(2,1)S(1)}, bf16[3,128,128]{2,1,0:T(8,128)(2,1)S(1)}, u32[]{:S(2)}, u32[]{:S(2)}) collective-permute-start(bf16[3,128,128]{2,1,0:T(8,128)(2,1)S(1)} %get-tuple-element.32), channel_id=1, source_target_pairs={{0,6},{1,7},{2,4},{3,5},{4,2},{5,3},{6,0},{7,1},{8,14},{9,15},{10,... | collective-permute-start | bytes 294920 | tf_op jit(solution)/shard_map/ppermute | solution.py:361
  12.1 0.8 %collective-permute-start.9 = (bf16[3,128,128]{2,1,0:T(8,128)(2,1)S(1)}, bf16[3,128,128]{2,1,0:T(8,128)(2,1)S(1)}, u32[]{:S(2)}, u32[]{:S(2)}) collective-permute-start(bf16[3,128,128]{2,1,0:T(8,128)(2,1)S(1)} %get-tuple-element.34), channel_id=1, source_target_pairs={{0,2},{1,3},{2,0},{3,1},{4,6},{5,7},{6,4},{7,5},{8,10},{9,11},{10,... | collective-permute-start | bytes 294920 | tf_op jit(solution)/shard_map/ppermute | solution.py:361
  12.9 2.0 %shard_map.88 = (f32[128,1024]{1,0:T(8,128)S(1)}, f32[128,1024]{1,0:T(8,128)S(1)}, f32[128,1024]{1,0:T(8,128)S(1)}, bf16[8,128,128]{2,1,0:T(8,128)(2,1)S(1)}) custom-call(s32[1,128]{1,0:T(1,128)S(1)} %bitcast.8, f32[20,8,32]{2,1,0:T(8,128)S(1)} %bitcast.4, bf16[128,1024]{1,0:T(8,128)(2,1)S(1)} %copy-done.3, ...), custom_call_target="tpu_custom_call", output_to_operand_aliasing={{3}: (7, {})} | custom-call | flops 167772160 | bytes 1430016 | tf_op jit(solution)/shard_map/pallas_call | solution.py:381
  14.9 2.2 %collective-permute-done.2.seen_ref = bf16[12,128,128]{2,1,0:T(8,128)(2,1)S(1)} collective-permute-done((bf16[12,128,128]{2,1,0:T(8,128)(2,1)S(1)}, bf16[12,128,128]{2,1,0:T(8,128)(2,1)S(1)}, u32[]{:S(2)}, u32[]{:S(2)}) %collective-permute-start.2) | collective-permute-done | bytes 393248 | tf_op jit(solution)/shard_map/ppermute | solution.py:361
  17.1 0.1 shard_map.89
  17.2 1.9 %collective-permute-start.4 = (bf16[4,128,128]{2,1,0:T(8,128)(2,1)S(1)}, bf16[4,128,128]{2,1,0:T(8,128)(2,1)S(1)}, u32[]{:S(2)}, u32[]{:S(2)}) collective-permute-start(bf16[4,128,128]{2,1,0:T(8,128)(2,1)S(1)} %get-tuple-element.31), channel_id=1, source_target_pairs={{0,2},{1,3},{2,0},{3,1},{4,6},{5,7},{6,4},{7,5},{8,10},{9,11},{10,... | collective-permute-start | bytes 393224 | tf_op jit(solution)/shard_map/ppermute | solution.py:361
  19.1 1.2 %collective-permute-done.8.refs_1_ = bf16[3,128,128]{2,1,0:T(8,128)(2,1)S(1)} collective-permute-done((bf16[3,128,128]{2,1,0:T(8,128)(2,1)S(1)}, bf16[3,128,128]{2,1,0:T(8,128)(2,1)S(1)}, u32[]{:S(2)}, u32[]{:S(2)}) %collective-permute-start.8) | collective-permute-done | bytes 98336 | tf_op jit(solution)/shard_map/ppermute | solution.py:361
  20.3 0.1 shard_map.90
  20.4 0.5 collective-permute-start.10
  20.9 2.6 %collective-permute-start.12 = (bf16[1,128,128]{2,1,0:T(8,128)(2,1)S(1)}, bf16[1,128,128]{2,1,0:T(8,128)(2,1)S(1)}, u32[]{:S(2)}, u32[]{:S(2)}) collective-permute-start(bf16[1,128,128]{2,1,0:T(8,128)(2,1)S(1)} %get-tuple-element.36), channel_id=1, source_target_pairs={{0,17},{1,16},{2,19},{3,18},{4,21},{5,20},{6,23},{7,22},{8,25},{9,... | collective-permute-start | bytes 98312 | tf_op jit(solution)/shard_map/ppermute | solution.py:366
  23.4 0.5 collective-permute-start.11
  23.9 0.4 collective-permute-start.1
  24.4 2.0 %collective-permute-done.12.far_top_ref = bf16[1,128,128]{2,1,0:T(8,128)(2,1)S(1)} collective-permute-done((bf16[1,128,128]{2,1,0:T(8,128)(2,1)S(1)}, bf16[1,128,128]{2,1,0:T(8,128)(2,1)S(1)}, u32[]{:S(2)}, u32[]{:S(2)}) %collective-permute-start.12) | collective-permute-done | bytes 32800 | tf_op jit(solution)/shard_map/ppermute | solution.py:366
  26.4 0.6 %collective-permute-start.3 = (bf16[8,128,128]{2,1,0:T(8,128)(2,1)S(1)}, bf16[8,128,128]{2,1,0:T(8,128)(2,1)S(1)}, u32[]{:S(2)}, u32[]{:S(2)}) collective-permute-start(bf16[8,128,128]{2,1,0:T(8,128)(2,1)S(1)} %get-tuple-element.30), channel_id=1, source_target_pairs={{0,2},{1,3},{2,0},{3,1},{4,6},{5,7},{6,4},{7,5},{8,10},{9,11},{10,... | collective-permute-start | bytes 786440 | tf_op jit(solution)/shard_map/ppermute | solution.py:361
  27.0 0.3 collective-permute-done.11.near_top_ref
  27.4 2.6 %collective-permute-start.15 = (bf16[3,128,128]{2,1,0:T(8,128)(2,1)S(1)}, bf16[3,128,128]{2,1,0:T(8,128)(2,1)S(1)}, u32[]{:S(2)}, u32[]{:S(2)}) collective-permute-start(bf16[3,128,128]{2,1,0:T(8,128)(2,1)S(1)} %shard_map.91.piece0_ref), channel_id=1, source_target_pairs={{0,6},{1,7},{2,4},{3,5},{4,2},{5,3},{6,0},{7,1},{8,14},{9,15},{10,... | collective-permute-start | bytes 294920 | tf_op jit(solution)/shard_map/ppermute | solution.py:361
  30.1 0.2 collective-permute-start.5
  30.3 2.8 %collective-permute-start.14 = (bf16[3,128,128]{2,1,0:T(8,128)(2,1)S(1)}, bf16[3,128,128]{2,1,0:T(8,128)(2,1)S(1)}, u32[]{:S(2)}, u32[]{:S(2)}) collective-permute-start(bf16[3,128,128]{2,1,0:T(8,128)(2,1)S(1)} %shard_map.91.piece0_ref), channel_id=1, source_target_pairs={{0,4},{1,5},{2,6},{3,7},{4,0},{5,1},{6,2},{7,3},{8,12},{9,13},{10,... | collective-permute-start | bytes 294920 | tf_op jit(solution)/shard_map/ppermute | solution.py:361
  33.1 5.9 %collective-permute-done.15.piece3_ref = bf16[3,128,128]{2,1,0:T(8,128)(2,1)S(1)} collective-permute-done((bf16[3,128,128]{2,1,0:T(8,128)(2,1)S(1)}, bf16[3,128,128]{2,1,0:T(8,128)(2,1)S(1)}, u32[]{:S(2)}, u32[]{:S(2)}) %collective-permute-start.15) | collective-permute-done | bytes 98336 | tf_op jit(solution)/shard_map/ppermute | solution.py:361
  39.0 4.2 %collective-permute-done.14.piece2_ref = bf16[3,128,128]{2,1,0:T(8,128)(2,1)S(1)} collective-permute-done((bf16[3,128,128]{2,1,0:T(8,128)(2,1)S(1)}, bf16[3,128,128]{2,1,0:T(8,128)(2,1)S(1)}, u32[]{:S(2)}, u32[]{:S(2)}) %collective-permute-start.14) | collective-permute-done | bytes 98336 | tf_op jit(solution)/shard_map/ppermute | solution.py:361
  43.2 1.0 %collective-permute-done.13.piece1_ref = bf16[3,128,128]{2,1,0:T(8,128)(2,1)S(1)} collective-permute-done((bf16[3,128,128]{2,1,0:T(8,128)(2,1)S(1)}, bf16[3,128,128]{2,1,0:T(8,128)(2,1)S(1)}, u32[]{:S(2)}, u32[]{:S(2)}) %collective-permute-start.13) | collective-permute-done | bytes 98336 | tf_op jit(solution)/shard_map/ppermute | solution.py:361
  44.2 0.1 collective-permute-start.16
  44.3 1.1 %collective-permute-start.6 = (bf16[4,128,128]{2,1,0:T(8,128)(2,1)S(1)}, bf16[4,128,128]{2,1,0:T(8,128)(2,1)S(1)}, u32[]{:S(2)}, u32[]{:S(2)}) collective-permute-start(bf16[4,128,128]{2,1,0:T(8,128)(2,1)S(1)} %collective-permute-done.5.two_own_ref), channel_id=1, source_target_pairs={{0,1},{1,0},{2,3},{3,2},{4,5},{5,4},{6,7},{7,6},{8,9},{9,8},{10,11... | collective-permute-start | bytes 393224 | tf_op jit(solution)/shard_map/ppermute | solution.py:361
  45.4 0.2 collective-permute-done.16.split_other_ref
  45.6 4.6 %collective-permute-done.6.two_other_ref = bf16[4,128,128]{2,1,0:T(8,128)(2,1)S(1)} collective-permute-done((bf16[4,128,128]{2,1,0:T(8,128)(2,1)S(1)}, bf16[4,128,128]{2,1,0:T(8,128)(2,1)S(1)}, u32[]{:S(2)}, u32[]{:S(2)}) %collective-permute-start.6) | collective-permute-done | bytes 131104 | tf_op jit(solution)/shard_map/ppermute | solution.py:361
  50.2 2.8 %shard_map.93 = (bf16[128,1024]{1,0:T(8,128)(2,1)}, bf16[128,1024]{1,0:T(8,128)(2,1)}, bf16[128,1024]{1,0:T(8,128)(2,1)}) custom-call(s32[5]{0:T(128)S(1)} %shift-right-arithmetic_and_fusion.flag_ref, s32[1,128]{1,0:T(1,128)S(1)} %bitcast.9, f32[20,8,32]{2,1,0:T(8,128)S(1)} %bitcast.5, bf16[128,1024]{1,0:T(8,128)(2,1)S(1)} %copy-done, ...), custom_call_target="tpu_custom_call" | custom-call | flops 234881024 | bytes 3822100 | tf_op jit(solution)/shard_map/pallas_call | solution.py:381
  (25 shorter events, 0.1 us)
Async XLA Ops:
  0.6 2.9 %copy-start = (bf16[128,1024]{1,0:T(8,128)(2,1)S(1)}, bf16[128,1024]{1,0:T(8,128)(2,1)}, u32[]{:S(2)}) copy-start(bf16[128,1024]{1,0:T(8,128)(2,1)} %k_ref.5) | copy-start | bytes 786436
  0.7 2.9 %copy-start.1 = (bf16[128,1024]{1,0:T(8,128)(2,1)S(1)}, bf16[128,1024]{1,0:T(8,128)(2,1)}, u32[]{:S(2)}) copy-start(bf16[128,1024]{1,0:T(8,128)(2,1)} %v_ref.5) | copy-start | bytes 786436
  0.7 2.9 %copy-start.2 = (bf16[128,1024]{1,0:T(8,128)(2,1)S(1)}, bf16[128,1024]{1,0:T(8,128)(2,1)}, u32[]{:S(2)}) copy-start(bf16[128,1024]{1,0:T(8,128)(2,1)} %g_ref.5) | copy-start | bytes 786436
  0.7 2.8 %copy-start.3 = (bf16[128,1024]{1,0:T(8,128)(2,1)S(1)}, bf16[128,1024]{1,0:T(8,128)(2,1)}, u32[]{:S(2)}) copy-start(bf16[128,1024]{1,0:T(8,128)(2,1)} %q_ref.3) | copy-start | bytes 786436
  0.7 2.8 %copy-start.4 = (f32[32,20,8]{0,2,1:T(8,128)S(1)}, f32[32,20,8]{0,2,1:T(8,128)}, u32[]{:S(2)}) copy-start(f32[32,20,8]{0,2,1:T(8,128)} %param.11) | copy-start | bytes 61444
  3.0 0.7 %copy-start.5 = (s32[128]{0:T(128)S(1)}, s32[128]{0:T(128)}, u32[]{:S(2)}) copy-start(s32[128]{0:T(128)} %param.10) | copy-start | bytes 1540
  3.0 4.8 %collective-permute-start = (bf16[12,128,128]{2,1,0:T(8,128)(2,1)S(1)}, bf16[12,128,128]{2,1,0:T(8,128)(2,1)S(1)}, u32[]{:S(2)}, u32[]{:S(2)}) collective-permute-start(bf16[12,128,128]{2,1,0:T(8,128)(2,1)S(1)} %get-tuple-element.20), channel_id=1, source_target_pairs={{0,8},{8,0},{16,24},{24,16},{1,9},{9,1},{17,25},{25,17},{2,10},{10... | collective-permute-start | bytes 1179656 | tf_op jit(solution)/shard_map/ppermute | solution.py:365
  4.8 12.2 %collective-permute-start.2 = (bf16[12,128,128]{2,1,0:T(8,128)(2,1)S(1)}, bf16[12,128,128]{2,1,0:T(8,128)(2,1)S(1)}, u32[]{:S(2)}, u32[]{:S(2)}) collective-permute-start(bf16[12,128,128]{2,1,0:T(8,128)(2,1)S(1)} %get-tuple-element.29.sent_ref), channel_id=1, source_target_pairs={{0,1},{1,0},{2,3},{3,2},{4,5},{5,4},{6,7},{7,6},{8,9},{9,8},{10,11... | collective-permute-start | bytes 1179656 | tf_op jit(solution)/shard_map/ppermute | solution.py:361
  8.4 10.6 %collective-permute-start.7 = (bf16[3,128,128]{2,1,0:T(8,128)(2,1)S(1)}, bf16[3,128,128]{2,1,0:T(8,128)(2,1)S(1)}, u32[]{:S(2)}, u32[]{:S(2)}) collective-permute-start(bf16[3,128,128]{2,1,0:T(8,128)(2,1)S(1)} %get-tuple-element.32), channel_id=1, source_target_pairs={{0,6},{1,7},{2,4},{3,5},{4,2},{5,3},{6,0},{7,1},{8,14},{9,15},{10,... | collective-permute-start | bytes 294920 | tf_op jit(solution)/shard_map/ppermute | solution.py:361
  12.1 8.2 %collective-permute-start.8 = (bf16[3,128,128]{2,1,0:T(8,128)(2,1)S(1)}, bf16[3,128,128]{2,1,0:T(8,128)(2,1)S(1)}, u32[]{:S(2)}, u32[]{:S(2)}) collective-permute-start(bf16[3,128,128]{2,1,0:T(8,128)(2,1)S(1)} %get-tuple-element.33), channel_id=1, source_target_pairs={{0,4},{1,5},{2,6},{3,7},{4,0},{5,1},{6,2},{7,3},{8,12},{9,13},{10,... | collective-permute-start | bytes 294920 | tf_op jit(solution)/shard_map/ppermute | solution.py:361
  12.1 8.2 %collective-permute-start.9 = (bf16[3,128,128]{2,1,0:T(8,128)(2,1)S(1)}, bf16[3,128,128]{2,1,0:T(8,128)(2,1)S(1)}, u32[]{:S(2)}, u32[]{:S(2)}) collective-permute-start(bf16[3,128,128]{2,1,0:T(8,128)(2,1)S(1)} %get-tuple-element.34), channel_id=1, source_target_pairs={{0,2},{1,3},{2,0},{3,1},{4,6},{5,7},{6,4},{7,5},{8,10},{9,11},{10,... | collective-permute-start | bytes 294920 | tf_op jit(solution)/shard_map/ppermute | solution.py:361
  17.2 12.8 %collective-permute-start.4 = (bf16[4,128,128]{2,1,0:T(8,128)(2,1)S(1)}, bf16[4,128,128]{2,1,0:T(8,128)(2,1)S(1)}, u32[]{:S(2)}, u32[]{:S(2)}) collective-permute-start(bf16[4,128,128]{2,1,0:T(8,128)(2,1)S(1)} %get-tuple-element.31), channel_id=1, source_target_pairs={{0,2},{1,3},{2,0},{3,1},{4,6},{5,7},{6,4},{7,5},{8,10},{9,11},{10,... | collective-permute-start | bytes 393224 | tf_op jit(solution)/shard_map/ppermute | solution.py:361
  20.4 7.0 %collective-permute-start.10 = (bf16[2,128,128]{2,1,0:T(8,128)(2,1)S(1)}, bf16[2,128,128]{2,1,0:T(8,128)(2,1)S(1)}, u32[]{:S(2)}, u32[]{:S(2)}) collective-permute-start(bf16[2,128,128]{2,1,0:T(8,128)(2,1)S(1)} %get-tuple-element.35.below_ref), channel_id=1, source_target_pairs={{0,1},{1,0},{2,3},{3,2},{4,5},{5,4},{6,7},{7,6},{8,9},{9,8},{10,11... | collective-permute-start | bytes 196616 | tf_op jit(solution)/shard_map/ppermute | solution.py:361
  20.9 5.5 %collective-permute-start.12 = (bf16[1,128,128]{2,1,0:T(8,128)(2,1)S(1)}, bf16[1,128,128]{2,1,0:T(8,128)(2,1)S(1)}, u32[]{:S(2)}, u32[]{:S(2)}) collective-permute-start(bf16[1,128,128]{2,1,0:T(8,128)(2,1)S(1)} %get-tuple-element.36), channel_id=1, source_target_pairs={{0,17},{1,16},{2,19},{3,18},{4,21},{5,20},{6,23},{7,22},{8,25},{9,... | collective-permute-start | bytes 98312 | tf_op jit(solution)/shard_map/ppermute | solution.py:366
  23.4 3.9 %collective-permute-start.11 = (bf16[1,128,128]{2,1,0:T(8,128)(2,1)S(1)}, bf16[1,128,128]{2,1,0:T(8,128)(2,1)S(1)}, u32[]{:S(2)}, u32[]{:S(2)}) collective-permute-start(bf16[1,128,128]{2,1,0:T(8,128)(2,1)S(1)} %get-tuple-element.36), channel_id=1, source_target_pairs={{0,16},{8,24},{16,0},{24,8},{1,17},{9,25},{17,1},{25,9},{2,18},{10... | collective-permute-start | bytes 98312 | tf_op jit(solution)/shard_map/ppermute | solution.py:365
  23.9 21.5 %collective-permute-start.1 = (bf16[8,128,128]{2,1,0:T(8,128)(2,1)S(1)}, bf16[8,128,128]{2,1,0:T(8,128)(2,1)S(1)}, u32[]{:S(2)}, u32[]{:S(2)}) collective-permute-start(bf16[8,128,128]{2,1,0:T(8,128)(2,1)S(1)} %get-tuple-element.28), channel_id=1, source_target_pairs={{0,1},{1,0},{2,3},{3,2},{4,5},{5,4},{6,7},{7,6},{8,9},{9,8},{10,11... | collective-permute-start | bytes 786440 | tf_op jit(solution)/shard_map/ppermute | solution.py:361
  26.4 19.0 %collective-permute-start.3 = (bf16[8,128,128]{2,1,0:T(8,128)(2,1)S(1)}, bf16[8,128,128]{2,1,0:T(8,128)(2,1)S(1)}, u32[]{:S(2)}, u32[]{:S(2)}) collective-permute-start(bf16[8,128,128]{2,1,0:T(8,128)(2,1)S(1)} %get-tuple-element.30), channel_id=1, source_target_pairs={{0,2},{1,3},{2,0},{3,1},{4,6},{5,7},{6,4},{7,5},{8,10},{9,11},{10,... | collective-permute-start | bytes 786440 | tf_op jit(solution)/shard_map/ppermute | solution.py:361
  27.4 11.6 %collective-permute-start.15 = (bf16[3,128,128]{2,1,0:T(8,128)(2,1)S(1)}, bf16[3,128,128]{2,1,0:T(8,128)(2,1)S(1)}, u32[]{:S(2)}, u32[]{:S(2)}) collective-permute-start(bf16[3,128,128]{2,1,0:T(8,128)(2,1)S(1)} %shard_map.91.piece0_ref), channel_id=1, source_target_pairs={{0,6},{1,7},{2,4},{3,5},{4,2},{5,3},{6,0},{7,1},{8,14},{9,15},{10,... | collective-permute-start | bytes 294920 | tf_op jit(solution)/shard_map/ppermute | solution.py:361
  30.1 14.2 %collective-permute-start.5 = (bf16[4,128,128]{2,1,0:T(8,128)(2,1)S(1)}, bf16[4,128,128]{2,1,0:T(8,128)(2,1)S(1)}, u32[]{:S(2)}, u32[]{:S(2)}) collective-permute-start(bf16[4,128,128]{2,1,0:T(8,128)(2,1)S(1)} %add_convert_fusion), channel_id=1, source_target_pairs={{0,4},{1,5},{2,6},{3,7},{4,0},{5,1},{6,2},{7,3},{8,12},{9,13},{10,... | collective-permute-start | bytes 393224 | tf_op jit(solution)/shard_map/ppermute | solution.py:361
  30.3 13.0 %collective-permute-start.14 = (bf16[3,128,128]{2,1,0:T(8,128)(2,1)S(1)}, bf16[3,128,128]{2,1,0:T(8,128)(2,1)S(1)}, u32[]{:S(2)}, u32[]{:S(2)}) collective-permute-start(bf16[3,128,128]{2,1,0:T(8,128)(2,1)S(1)} %shard_map.91.piece0_ref), channel_id=1, source_target_pairs={{0,4},{1,5},{2,6},{3,7},{4,0},{5,1},{6,2},{7,3},{8,12},{9,13},{10,... | collective-permute-start | bytes 294920 | tf_op jit(solution)/shard_map/ppermute | solution.py:361
  39.0 5.2 %collective-permute-start.13 = (bf16[3,128,128]{2,1,0:T(8,128)(2,1)S(1)}, bf16[3,128,128]{2,1,0:T(8,128)(2,1)S(1)}, u32[]{:S(2)}, u32[]{:S(2)}) collective-permute-start(bf16[3,128,128]{2,1,0:T(8,128)(2,1)S(1)} %shard_map.91.piece0_ref), channel_id=1, source_target_pairs={{0,2},{1,3},{2,0},{3,1},{4,6},{5,7},{6,4},{7,5},{8,10},{9,11},{10,... | collective-permute-start | bytes 294920 | tf_op jit(solution)/shard_map/ppermute | solution.py:361
  44.2 1.4 %collective-permute-start.16 = (bf16[1,4,128,128]{3,2,1,0:T(8,128)(2,1)S(1)}, bf16[1,4,128,128]{3,2,1,0:T(8,128)(2,1)S(1)}, u32[]{:S(2)}, u32[]{:S(2)}) collective-permute-start(bf16[1,4,128,128]{3,2,1,0:T(8,128)(2,1)S(1)} %shard_map.92.split_own_ref), channel_id=1, source_target_pairs={{0,8},{8,0},{16,24},{24,16},{1,9},{9,1},{17,25},{25,17},{2,10},{10... | collective-permute-start | bytes 393224 | tf_op jit(solution)/shard_map/ppermute | solution.py:365
  44.3 5.9 %collective-permute-start.6 = (bf16[4,128,128]{2,1,0:T(8,128)(2,1)S(1)}, bf16[4,128,128]{2,1,0:T(8,128)(2,1)S(1)}, u32[]{:S(2)}, u32[]{:S(2)}) collective-permute-start(bf16[4,128,128]{2,1,0:T(8,128)(2,1)S(1)} %collective-permute-done.5.two_own_ref), channel_id=1, source_target_pairs={{0,1},{1,0},{2,3},{3,2},{4,5},{5,4},{6,7},{7,6},{8,9},{9,8},{10,11... | collective-permute-start | bytes 393224 | tf_op jit(solution)/shard_map/ppermute | solution.py:361

commit v5 on v4

--- a/solution.py
+++ b/solution.py
@@ -158,8 +158,8 @@
     g_ref,
     after_ref,
     two_own_ref,
-    sent_ref,
-    zero_ref,
+    two_other_ref,
+    near_ref,
     two_ref,
 ):
     head_count = table_ref.shape[1]
@@ -171,17 +171,15 @@
         rows = [place * head_count + head for place in range(NEAR)]
 
         def store(place, value):
-            if place == 0:
-                zero_ref[head] = value
-            elif place == 1:
-                sent_ref[half + head] = value
+            if place < 2:
+                near_ref[place, head] = value
             else:
                 two_ref[head] = value
 
         columns = pl.ds(head * head_size, head_size)
         payload_cell(flags, gates, rows, range(NEAR), q_ref, k_ref, v_ref, g_ref, columns, store)
     two_own_ref[...] = two_ref[pl.ds(x_place * half, half)]
-    sent_ref[:half] = two_ref[pl.ds((1 - x_place) * half, half)]
+    two_other_ref[...] = two_ref[pl.ds((1 - x_place) * half, half)]
 
 
 def four_sum_kernel(top_rows, own_ref, after_ref, *refs):
@@ -210,10 +208,12 @@
             out_ref[level, offs * eighth : (offs + 1) * eighth] = piece_ref[first : first + eighth]
 
 
-def lower_sum_kernel(own_ref, sent_ref, seen_ref, after_ref, two_ref, one_ref):
-    half = own_ref.shape[0]
-    two_ref[...] = narrow(wide(own_ref[...]) + wide(seen_ref[:half]))
-    one_ref[...] = narrow(wide(sent_ref[half:]) + wide(seen_ref[half:]))
+def two_sum_kernel(own_ref, seen_ref, after_ref, out_ref):
+    out_ref[...] = narrow(wide(own_ref[...]) + wide(seen_ref[...]))
+
+
+def near_sum_kernel(near_ref, seen_ref, one_ref):
+    one_ref[...] = narrow(wide(near_ref[1]) + wide(seen_ref[1]))
 
 
 def local_kernel(
@@ -226,11 +226,9 @@
     v_ref,
     g_ref,
     after_ref,
-    held_ref,
     qo_ref,
     ko_ref,
     vo_ref,
-    held_out_ref,
 ):
     head_count = table_ref.shape[1]
     tokens = q_ref.shape[0]
@@ -275,7 +273,7 @@
     ql_ref,
     kl_ref,
     vl_ref,
-    zero_ref,
+    near_ref,
     one_ref,
     two_own_ref,
     two_other_ref,
@@ -298,7 +296,7 @@
     x_place = flag_ref[0]
     z_place = flag_ref[1] + 2 * flag_ref[2]
     core = flag_ref[inner]
-    held_ref[0] = zero_ref[...]
+    held_ref[0] = near_ref[0]
     held_ref[1] = one_ref[...]
     held_ref[2, pl.ds(x_place * half, half)] = two_own_ref[...]
     held_ref[2, pl.ds((1 - x_place) * half, half)] = two_other_ref[...]
@@ -376,14 +374,13 @@
     def cells(*lead):
         return jax.ShapeDtypeStruct(lead + cell, jnp.bfloat16)
 
-    def call(kernel, in_specs, outs, operands, flops=0, scratch=(), grant=VMEM_BYTES, out_specs=None, aliases=None):
+    def call(kernel, in_specs, outs, operands, flops=0, scratch=(), grant=VMEM_BYTES):
         moved = sum(operand.size * operand.dtype.itemsize for operand in operands)
         return pl.pallas_call(
             kernel,
             out_shape=outs,
             in_specs=in_specs,
-            out_specs=out_specs or jax.tree.map(lambda _: vmem, outs),
-            input_output_aliases=aliases or {},
+            out_specs=jax.tree.map(lambda _: vmem, outs),
             scratch_shapes=scratch,
             compiler_params=pltpu.CompilerParams(vmem_limit_bytes=grant),
             cost_estimate=pl.CostEstimate(flops=flops, bytes_accessed=moved, transcendentals=0),
@@ -423,10 +420,10 @@
         grant=FIRST_BYTES,
     )
     seen = swap(sent, inner_bits)
-    two_own, lower_sent, zero = call(
+    two_own, two_other, near = call(
         functools.partial(lower_kernel, offset, head_size),
         [smem] + [vmem] * 6 + [anywhere],
-        (cells(half), cells(half + head_count), cells(head_count)),
+        (cells(half), cells(half), cells(2, head_count)),
         (flag_bits, class_lanes, table, query_rows, key_rows, value_rows, out_grad, keep),
         flops=2 * NEAR * row_count * width * head_size,
         scratch=[pltpu.VMEM((head_count,) + cell, jnp.bfloat16)],
@@ -438,13 +435,11 @@
         (flag_bits, seen, keep, two_own, *lead),
     )
     big = jax.ShapeDtypeStruct((row_count, width), jnp.float32)
-    query_local, key_local, value_local, zero = call(
+    query_local, key_local, value_local = call(
         functools.partial(local_kernel, block_depth, head_size),
-        [vmem] * 6 + [anywhere] * 2,
-        (big, big, big, cells(head_count)),
-        (class_lanes, table, query_rows, key_rows, value_rows, out_grad, own_share, zero),
-        out_specs=(vmem, vmem, vmem, anywhere),
-        aliases={7: 3},
+        [vmem] * 6 + [anywhere],
+        (big, big, big),
+        (class_lanes, table, query_rows, key_rows, value_rows, out_grad, own_share),
         flops=10 * row_count * width * row_count,
     )
 
@@ -481,29 +476,30 @@
                 row += size
         below = narrow(jnp.concatenate([parts[level] for level in range(NEAR, top)], axis=0))
         top_sent = narrow(parts[top])
+    two_sum = call(
+        two_sum_kernel,
+        [vmem] * 2 + [anywhere],
+        cells(half),
+        (two_own, swap(two_other, 0), query_local),
+    )
+    two_sum = call(
+        two_sum_kernel, [vmem] * 2 + [anywhere], cells(half), (two_sum, swap(two_sum, 1), two_sum)
+    )
+    two_half = swap(two_sum, 2)
     shares = call(
         pair_sum_kernel,
         [vmem] * 4,
         cells(share_rows),
         (below, swap(below, 0), swap(top_sent, top), swap(top_sent, 0, top)),
     )
+    two_rest = swap(two_half, 0)
+    near_seen = swap(near, 0)
+    one_done = swap(call(near_sum_kernel, [vmem] * 2, cells(head_count), (near, near_seen)), 1)
     pieces = [shares] + [swap(shares, *z_bits(offs)) for offs in (1, 2, 3)]
     split_own = call(
         functools.partial(gather_kernel, cut), [vmem] * 4, cells(split_levels, half), pieces
     )
     split_other = swap(split_own, inner_bits)
-
-    two_sum, one_sum = call(
-        lower_sum_kernel,
-        [vmem] * 3 + [anywhere],
-        (cells(half), cells(head_count)),
-        (two_own, lower_sent, swap(lower_sent, 0), query_local),
-    )
-    two_sum = narrow(wide(two_sum) + wide(swap(two_sum, 1)))
-    two_half = swap(two_sum, 2)
-    two_rest = swap(two_half, 0)
-    one_done = swap(one_sum, 1)
-    zero_done = swap(zero, 0)
 
     small = jax.ShapeDtypeStruct((row_count, width), jnp.bfloat16)
     return call(
@@ -520,7 +516,7 @@
             query_local,
             key_local,
             value_local,
-            zero_done,
+            near_seen,
             one_done,
             two_half,
             two_rest,

time: 53.2 us -> 54.3 us (1.021)
  starting transfers between devices: 21.3 us -> 23.1 us
  waiting for transfers between devices: 21.7 us -> 21.1 us
    ppermute x13, starting transfers between devices: 17.7 us -> 20.5 us  [swap(): return lax.ppermute(block, 'gy', [(i, i ^ mask) for i in range(inner_size)])]
    ppermute x1, waiting for transfers between devices: 2.05 us -> 0.01 us  [swap(): lax.ppermute(block, ('gx', 'gy'), [(i, i ^ mask) for i in range(device_co...]
    ppermute x13, waiting for transfers between devices: 19.1 us -> 20.9 us  [swap(): return lax.ppermute(block, 'gy', [(i, i ^ mask) for i in range(inner_size)])]
    ppermute x1, starting transfers between devices: 2.55 us -> 1.49 us  [swap(): lax.ppermute(block, ('gx', 'gy'), [(i, i ^ mask) for i in range(device_co...]
    pallas_call x9 -> x11, Pallas kernels: 9.08 us -> 9.12 us  [call(): pl.pallas_call(kernel, out_shape=outs, in_specs=in_specs, out_specs=jax.t...]
  transfers between devices with their start and end apart: 17 -> 17, of which waited for: 9 -> 5; matrix products, arithmetic and copies ran while one was open for 0% -> 0% of each run, Pallas kernels for 8% -> 7%
where the time goes in v5:
time: 54.3 us; the launch traced here: 54.2 us
  starting transfers between devices  23.1 us (43%)
  waiting for transfers between devices  21.1 us (39%)
  Pallas kernels  9.12 us (17%)
  between operations  0.79 us (1%)
    ppermute x13, waiting for transfers between devices, swap(): return lax.ppermute(block, 'gy', [(i, i ^ mask) for i in range(inner_size)])  20.9 us
    ppermute x13, starting transfers between devices, swap(): return lax.ppermute(block, 'gy', [(i, i ^ mask) for i in range(inner_size)])  20.5 us
    pallas_call x11, Pallas kernels, call(): pl.pallas_call(kernel, out_shape=outs, in_specs=in_specs, out_specs=jax.t...  9.12 us
    ppermute x1, starting transfers between devices, swap(): lax.ppermute(block, ('gx', 'gy'), [(i, i ^ mask) for i in range(device_co...  1.49 us
    ppermute x3, starting transfers between devices, swap(): return lax.ppermute(block, 'gx', [(i, i ^ mask) for i in range(size)])  1.09 us
  transfers between devices with their start and end apart: 17, of which 5 were waited for; matrix products, arithmetic and copies ran while one was open for 0% of the time, Pallas kernels for 7%

profile of v5, /device:TPU:0, one launch (start us, length us, event | category | flops | bytes accessed | tf_op | source)
XLA Modules:
  0.0 54.2 jit_solution(1886325952002763557)
XLA Ops:
  0.7 0.0 copy-start.1
  0.7 0.0 copy-start.2
  0.7 2.3 %shard_map.85 = (bf16[12,128,128]{2,1,0:T(8,128)(2,1)S(1)}, bf16[4,128,128]{2,1,0:T(8,128)(2,1)S(1)}) custom-call(s32[5]{0:T(128)S(1)} %shift-right-arithmetic_and_fusion.flag_ref, s32[1,128]{1,0:T(1,128)} %bitcast.6, f32[20,8,32]{2,1,0:T(8,128)} %bitcast.2, bf16[128,1024]{1,0:T(8,128)(2,1)} %q_ref.3, bf16[128,1024]{1,0:T(8,128)(2,1)} %k_ref.5, ...), custom_call_target="tpu_custom_call" | custom-call | flops 67108864 | bytes 1069588 | tf_op jit(solution)/shard_map/pallas_call | solution.py:379
  3.0 0.0 copy-start.5
  3.0 0.5 collective-permute-start
  3.5 0.1 copy-done.5
  3.6 1.2 %shard_map.86 = (bf16[4,128,128]{2,1,0:T(8,128)(2,1)S(1)}, bf16[4,128,128]{2,1,0:T(8,128)(2,1)S(1)}, bf16[2,8,128,128]{3,2,1,0:T(8,128)(2,1)S(1)}) custom-call(s32[5]{0:T(128)S(1)} %shift-right-arithmetic_and_fusion.flag_ref, s32[1,128]{1,0:T(1,128)S(1)} %bitcast.7, f32[20,8,32]{2,1,0:T(8,128)S(1)} %bitcast.3, bf16[128,1024]{1,0:T(8,128)(2,1)S(1)} %copy-done.3, ...), custom_call_target="tpu_custom_call" | custom-call | flops 100663296 | bytes 1200660 | tf_op jit(solution)/shard_map/pallas_call | solution.py:379
  4.8 3.0 %collective-permute-start.1 = (bf16[2,8,128,128]{3,2,1,0:T(8,128)(2,1)S(1)}, bf16[2,8,128,128]{3,2,1,0:T(8,128)(2,1)S(1)}, u32[]{:S(2)}, u32[]{:S(2)}) collective-permute-start(bf16[2,8,128,128]{3,2,1,0:T(8,128)(2,1)S(1)} %get-tuple-element.24.near_ref), channel_id=1, source_target_pairs={{0,1},{1,0},{2,3},{3,2},{4,5},{5,4},{6,7},{7,6},{8,9},{9,8},{10,11... | collective-permute-start | bytes 1572872 | tf_op jit(solution)/shard_map/ppermute | solution.py:359
  7.8 0.1 collective-permute-start.3
  7.9 0.6 %shard_map.87 = (bf16[3,128,128]{2,1,0:T(8,128)(2,1)S(1)}, bf16[3,128,128]{2,1,0:T(8,128)(2,1)S(1)}, bf16[3,128,128]{2,1,0:T(8,128)(2,1)S(1)}, bf16[3,128,128]{2,1,0:T(8,128)(2,1)S(1)}) custom-call(s32[5]{0:T(128)S(1)} %shift-right-arithmetic_and_fusion.flag_ref, bf16[12,128,128]{2,1,0:T(8,128)(2,1)S(1)} %collective-permute-done.seen_ref, ...), custom_call_target="tpu_custom_call" | custom-call | bytes 655380 | tf_op jit(solution)/shard_map/pallas_call | solution.py:379
  8.5 4.1 %collective-permute-start.7 = (bf16[3,128,128]{2,1,0:T(8,128)(2,1)S(1)}, bf16[3,128,128]{2,1,0:T(8,128)(2,1)S(1)}, u32[]{:S(2)}, u32[]{:S(2)}) collective-permute-start(bf16[3,128,128]{2,1,0:T(8,128)(2,1)S(1)} %get-tuple-element.26), channel_id=1, source_target_pairs={{0,6},{1,7},{2,4},{3,5},{4,2},{5,3},{6,0},{7,1},{8,14},{9,15},{10,... | collective-permute-start | bytes 294920 | tf_op jit(solution)/shard_map/ppermute | solution.py:359
  12.6 0.6 %collective-permute-start.9 = (bf16[3,128,128]{2,1,0:T(8,128)(2,1)S(1)}, bf16[3,128,128]{2,1,0:T(8,128)(2,1)S(1)}, u32[]{:S(2)}, u32[]{:S(2)}) collective-permute-start(bf16[3,128,128]{2,1,0:T(8,128)(2,1)S(1)} %get-tuple-element.28), channel_id=1, source_target_pairs={{0,2},{1,3},{2,0},{3,1},{4,6},{5,7},{6,4},{7,5},{8,10},{9,11},{10,... | collective-permute-start | bytes 294920 | tf_op jit(solution)/shard_map/ppermute | solution.py:359
  13.3 2.0 %shard_map.88 = (f32[128,1024]{1,0:T(8,128)S(1)}, f32[128,1024]{1,0:T(8,128)S(1)}, f32[128,1024]{1,0:T(8,128)S(1)}) custom-call(s32[1,128]{1,0:T(1,128)S(1)} %bitcast.8, f32[20,8,32]{2,1,0:T(8,128)S(1)} %bitcast.4, bf16[128,1024]{1,0:T(8,128)(2,1)S(1)} %copy-done.3, bf16[128,1024]{1,0:T(8,128)(2,1)S(1)} %copy-done, bf16[128,1024]{1,0:T(8,128)(2,1)S(1)} %copy-done.1, ...), custom_call_target="tpu_custom_call" | custom-call | flops 167772160 | bytes 1167872 | tf_op jit(solution)/shard_map/pallas_call | solution.py:379
  15.3 7.4 %collective-permute-done.3.seen_ref = bf16[4,128,128]{2,1,0:T(8,128)(2,1)S(1)} collective-permute-done((bf16[4,128,128]{2,1,0:T(8,128)(2,1)S(1)}, bf16[4,128,128]{2,1,0:T(8,128)(2,1)S(1)}, u32[]{:S(2)}, u32[]{:S(2)}) %collective-permute-start.3) | collective-permute-done | bytes 131104 | tf_op jit(solution)/shard_map/ppermute | solution.py:359
  22.7 1.9 %collective-permute-start.4 = (bf16[4,128,128]{2,1,0:T(8,128)(2,1)S(1)}, bf16[4,128,128]{2,1,0:T(8,128)(2,1)S(1)}, u32[]{:S(2)}, u32[]{:S(2)}) collective-permute-start(bf16[4,128,128]{2,1,0:T(8,128)(2,1)S(1)} %shard_map.90.own_ref.after_ref), channel_id=1, source_target_pairs={{0,2},{1,3},{2,0},{3,1},{4,6},{5,7},{6,4},{7,5},{8,10},{9,11},{10,... | collective-permute-start | bytes 393224 | tf_op jit(solution)/shard_map/ppermute | solution.py:359
  24.6 0.1 shard_map.92
  24.7 1.6 %collective-permute-start.10 = (bf16[2,128,128]{2,1,0:T(8,128)(2,1)S(1)}, bf16[2,128,128]{2,1,0:T(8,128)(2,1)S(1)}, u32[]{:S(2)}, u32[]{:S(2)}) collective-permute-start(bf16[2,128,128]{2,1,0:T(8,128)(2,1)S(1)} %get-tuple-element.29.below_ref), channel_id=1, source_target_pairs={{0,1},{1,0},{2,3},{3,2},{4,5},{5,4},{6,7},{7,6},{8,9},{9,8},{10,11... | collective-permute-start | bytes 196616 | tf_op jit(solution)/shard_map/ppermute | solution.py:359
  26.3 1.5 %collective-permute-start.12 = (bf16[1,128,128]{2,1,0:T(8,128)(2,1)S(1)}, bf16[1,128,128]{2,1,0:T(8,128)(2,1)S(1)}, u32[]{:S(2)}, u32[]{:S(2)}) collective-permute-start(bf16[1,128,128]{2,1,0:T(8,128)(2,1)S(1)} %get-tuple-element.30), channel_id=1, source_target_pairs={{0,17},{1,16},{2,19},{3,18},{4,21},{5,20},{6,23},{7,22},{8,25},{9,... | collective-permute-start | bytes 98312 | tf_op jit(solution)/shard_map/ppermute | solution.py:364
  27.7 0.5 collective-permute-start.11
  28.3 0.1 shard_map.89
  28.3 0.3 collective-permute-start.2
  28.6 2.9 %collective-permute-start.5 = (bf16[4,128,128]{2,1,0:T(8,128)(2,1)S(1)}, bf16[4,128,128]{2,1,0:T(8,128)(2,1)S(1)}, u32[]{:S(2)}, u32[]{:S(2)}) collective-permute-start(bf16[4,128,128]{2,1,0:T(8,128)(2,1)S(1)} %shard_map.91), channel_id=1, source_target_pairs={{0,4},{1,5},{2,6},{3,7},{4,0},{5,1},{6,2},{7,3},{8,12},{9,13},{10,... | collective-permute-start | bytes 393224 | tf_op jit(solution)/shard_map/ppermute | solution.py:359
  31.5 0.1 collective-permute-done.11.near_top_ref
  31.7 2.5 %collective-permute-start.15 = (bf16[3,128,128]{2,1,0:T(8,128)(2,1)S(1)}, bf16[3,128,128]{2,1,0:T(8,128)(2,1)S(1)}, u32[]{:S(2)}, u32[]{:S(2)}) collective-permute-start(bf16[3,128,128]{2,1,0:T(8,128)(2,1)S(1)} %shard_map.93.piece0_ref), channel_id=1, source_target_pairs={{0,6},{1,7},{2,4},{3,5},{4,2},{5,3},{6,0},{7,1},{8,14},{9,15},{10,... | collective-permute-start | bytes 294920 | tf_op jit(solution)/shard_map/ppermute | solution.py:359
  34.2 0.5 collective-permute-start.14
  34.7 1.5 %collective-permute-start.13 = (bf16[3,128,128]{2,1,0:T(8,128)(2,1)S(1)}, bf16[3,128,128]{2,1,0:T(8,128)(2,1)S(1)}, u32[]{:S(2)}, u32[]{:S(2)}) collective-permute-start(bf16[3,128,128]{2,1,0:T(8,128)(2,1)S(1)} %shard_map.93.piece0_ref), channel_id=1, source_target_pairs={{0,2},{1,3},{2,0},{3,1},{4,6},{5,7},{6,4},{7,5},{8,10},{9,11},{10,... | collective-permute-start | bytes 294920 | tf_op jit(solution)/shard_map/ppermute | solution.py:359
  36.2 7.5 %collective-permute-done.15.piece3_ref = bf16[3,128,128]{2,1,0:T(8,128)(2,1)S(1)} collective-permute-done((bf16[3,128,128]{2,1,0:T(8,128)(2,1)S(1)}, bf16[3,128,128]{2,1,0:T(8,128)(2,1)S(1)}, u32[]{:S(2)}, u32[]{:S(2)}) %collective-permute-start.15) | collective-permute-done | bytes 98336 | tf_op jit(solution)/shard_map/ppermute | solution.py:359
  43.6 1.7 %collective-permute-done.14.piece2_ref = bf16[3,128,128]{2,1,0:T(8,128)(2,1)S(1)} collective-permute-done((bf16[3,128,128]{2,1,0:T(8,128)(2,1)S(1)}, bf16[3,128,128]{2,1,0:T(8,128)(2,1)S(1)}, u32[]{:S(2)}, u32[]{:S(2)}) %collective-permute-start.14) | collective-permute-done | bytes 98336 | tf_op jit(solution)/shard_map/ppermute | solution.py:359
  45.3 0.1 collective-permute-start.16
  45.4 1.6 %collective-permute-start.6 = (bf16[4,128,128]{2,1,0:T(8,128)(2,1)S(1)}, bf16[4,128,128]{2,1,0:T(8,128)(2,1)S(1)}, u32[]{:S(2)}, u32[]{:S(2)}) collective-permute-start(bf16[4,128,128]{2,1,0:T(8,128)(2,1)S(1)} %collective-permute-done.5.two_own_ref), channel_id=1, source_target_pairs={{0,1},{1,0},{2,3},{3,2},{4,5},{5,4},{6,7},{7,6},{8,9},{9,8},{10,11... | collective-permute-start | bytes 393224 | tf_op jit(solution)/shard_map/ppermute | solution.py:359
  47.0 4.3 %collective-permute-done.6.two_other_ref = bf16[4,128,128]{2,1,0:T(8,128)(2,1)S(1)} collective-permute-done((bf16[4,128,128]{2,1,0:T(8,128)(2,1)S(1)}, bf16[4,128,128]{2,1,0:T(8,128)(2,1)S(1)}, u32[]{:S(2)}, u32[]{:S(2)}) %collective-permute-start.6) | collective-permute-done | bytes 131104 | tf_op jit(solution)/shard_map/ppermute | solution.py:359
  51.3 2.8 %shard_map.95 = (bf16[128,1024]{1,0:T(8,128)(2,1)}, bf16[128,1024]{1,0:T(8,128)(2,1)}, bf16[128,1024]{1,0:T(8,128)(2,1)}) custom-call(s32[5]{0:T(128)S(1)} %shift-right-arithmetic_and_fusion.flag_ref, s32[1,128]{1,0:T(1,128)S(1)} %bitcast.9, f32[20,8,32]{2,1,0:T(8,128)S(1)} %bitcast.5, bf16[128,1024]{1,0:T(8,128)(2,1)S(1)} %copy-done, ...), custom_call_target="tpu_custom_call" | custom-call | flops 234881024 | bytes 4084244 | tf_op jit(solution)/shard_map/pallas_call | solution.py:379
  (26 shorter events, 0.2 us)
Async XLA Ops:
  0.6 2.9 %copy-start = (bf16[128,1024]{1,0:T(8,128)(2,1)S(1)}, bf16[128,1024]{1,0:T(8,128)(2,1)}, u32[]{:S(2)}) copy-start(bf16[128,1024]{1,0:T(8,128)(2,1)} %k_ref.5) | copy-start | bytes 786436
  0.7 2.9 %copy-start.1 = (bf16[128,1024]{1,0:T(8,128)(2,1)S(1)}, bf16[128,1024]{1,0:T(8,128)(2,1)}, u32[]{:S(2)}) copy-start(bf16[128,1024]{1,0:T(8,128)(2,1)} %v_ref.5) | copy-start | bytes 786436
  0.7 2.9 %copy-start.2 = (bf16[128,1024]{1,0:T(8,128)(2,1)S(1)}, bf16[128,1024]{1,0:T(8,128)(2,1)}, u32[]{:S(2)}) copy-start(bf16[128,1024]{1,0:T(8,128)(2,1)} %g_ref.5) | copy-start | bytes 786436
  0.7 2.8 %copy-start.3 = (bf16[128,1024]{1,0:T(8,128)(2,1)S(1)}, bf16[128,1024]{1,0:T(8,128)(2,1)}, u32[]{:S(2)}) copy-start(bf16[128,1024]{1,0:T(8,128)(2,1)} %q_ref.3) | copy-start | bytes 786436
  0.7 2.8 %copy-start.4 = (f32[32,20,8]{0,2,1:T(8,128)S(1)}, f32[32,20,8]{0,2,1:T(8,128)}, u32[]{:S(2)}) copy-start(f32[32,20,8]{0,2,1:T(8,128)} %param.11) | copy-start | bytes 61444
  3.0 0.7 %copy-start.5 = (s32[128]{0:T(128)S(1)}, s32[128]{0:T(128)}, u32[]{:S(2)}) copy-start(s32[128]{0:T(128)} %param.10) | copy-start | bytes 1540
  3.0 4.9 %collective-permute-start = (bf16[12,128,128]{2,1,0:T(8,128)(2,1)S(1)}, bf16[12,128,128]{2,1,0:T(8,128)(2,1)S(1)}, u32[]{:S(2)}, u32[]{:S(2)}) collective-permute-start(bf16[12,128,128]{2,1,0:T(8,128)(2,1)S(1)} %get-tuple-element.17), channel_id=1, source_target_pairs={{0,8},{8,0},{16,24},{24,16},{1,9},{9,1},{17,25},{25,17},{2,10},{10... | collective-permute-start | bytes 1179656 | tf_op jit(solution)/shard_map/ppermute | solution.py:363
  4.8 23.4 %collective-permute-start.1 = (bf16[2,8,128,128]{3,2,1,0:T(8,128)(2,1)S(1)}, bf16[2,8,128,128]{3,2,1,0:T(8,128)(2,1)S(1)}, u32[]{:S(2)}, u32[]{:S(2)}) collective-permute-start(bf16[2,8,128,128]{3,2,1,0:T(8,128)(2,1)S(1)} %get-tuple-element.24.near_ref), channel_id=1, source_target_pairs={{0,1},{1,0},{2,3},{3,2},{4,5},{5,4},{6,7},{7,6},{8,9},{9,8},{10,11... | collective-permute-start | bytes 1572872 | tf_op jit(solution)/shard_map/ppermute | solution.py:359
  7.8 14.9 %collective-permute-start.3 = (bf16[4,128,128]{2,1,0:T(8,128)(2,1)S(1)}, bf16[4,128,128]{2,1,0:T(8,128)(2,1)S(1)}, u32[]{:S(2)}, u32[]{:S(2)}) collective-permute-start(bf16[4,128,128]{2,1,0:T(8,128)(2,1)S(1)} %get-tuple-element.25), channel_id=1, source_target_pairs={{0,1},{1,0},{2,3},{3,2},{4,5},{5,4},{6,7},{7,6},{8,9},{9,8},{10,11... | collective-permute-start | bytes 393224 | tf_op jit(solution)/shard_map/ppermute | solution.py:359
  8.5 16.1 %collective-permute-start.7 = (bf16[3,128,128]{2,1,0:T(8,128)(2,1)S(1)}, bf16[3,128,128]{2,1,0:T(8,128)(2,1)S(1)}, u32[]{:S(2)}, u32[]{:S(2)}) collective-permute-start(bf16[3,128,128]{2,1,0:T(8,128)(2,1)S(1)} %get-tuple-element.26), channel_id=1, source_target_pairs={{0,6},{1,7},{2,4},{3,5},{4,2},{5,3},{6,0},{7,1},{8,14},{9,15},{10,... | collective-permute-start | bytes 294920 | tf_op jit(solution)/shard_map/ppermute | solution.py:359
  12.6 12.0 %collective-permute-start.8 = (bf16[3,128,128]{2,1,0:T(8,128)(2,1)S(1)}, bf16[3,128,128]{2,1,0:T(8,128)(2,1)S(1)}, u32[]{:S(2)}, u32[]{:S(2)}) collective-permute-start(bf16[3,128,128]{2,1,0:T(8,128)(2,1)S(1)} %get-tuple-element.27), channel_id=1, source_target_pairs={{0,4},{1,5},{2,6},{3,7},{4,0},{5,1},{6,2},{7,3},{8,12},{9,13},{10,... | collective-permute-start | bytes 294920 | tf_op jit(solution)/shard_map/ppermute | solution.py:359
  12.6 12.0 %collective-permute-start.9 = (bf16[3,128,128]{2,1,0:T(8,128)(2,1)S(1)}, bf16[3,128,128]{2,1,0:T(8,128)(2,1)S(1)}, u32[]{:S(2)}, u32[]{:S(2)}) collective-permute-start(bf16[3,128,128]{2,1,0:T(8,128)(2,1)S(1)} %get-tuple-element.28), channel_id=1, source_target_pairs={{0,2},{1,3},{2,0},{3,1},{4,6},{5,7},{6,4},{7,5},{8,10},{9,11},{10,... | collective-permute-start | bytes 294920 | tf_op jit(solution)/shard_map/ppermute | solution.py:359
  22.7 5.9 %collective-permute-start.4 = (bf16[4,128,128]{2,1,0:T(8,128)(2,1)S(1)}, bf16[4,128,128]{2,1,0:T(8,128)(2,1)S(1)}, u32[]{:S(2)}, u32[]{:S(2)}) collective-permute-start(bf16[4,128,128]{2,1,0:T(8,128)(2,1)S(1)} %shard_map.90.own_ref.after_ref), channel_id=1, source_target_pairs={{0,2},{1,3},{2,0},{3,1},{4,6},{5,7},{6,4},{7,5},{8,10},{9,11},{10,... | collective-permute-start | bytes 393224 | tf_op jit(solution)/shard_map/ppermute | solution.py:359
  24.7 7.0 %collective-permute-start.10 = (bf16[2,128,128]{2,1,0:T(8,128)(2,1)S(1)}, bf16[2,128,128]{2,1,0:T(8,128)(2,1)S(1)}, u32[]{:S(2)}, u32[]{:S(2)}) collective-permute-start(bf16[2,128,128]{2,1,0:T(8,128)(2,1)S(1)} %get-tuple-element.29.below_ref), channel_id=1, source_target_pairs={{0,1},{1,0},{2,3},{3,2},{4,5},{5,4},{6,7},{7,6},{8,9},{9,8},{10,11... | collective-permute-start | bytes 196616 | tf_op jit(solution)/shard_map/ppermute | solution.py:359
  26.3 5.3 %collective-permute-start.12 = (bf16[1,128,128]{2,1,0:T(8,128)(2,1)S(1)}, bf16[1,128,128]{2,1,0:T(8,128)(2,1)S(1)}, u32[]{:S(2)}, u32[]{:S(2)}) collective-permute-start(bf16[1,128,128]{2,1,0:T(8,128)(2,1)S(1)} %get-tuple-element.30), channel_id=1, source_target_pairs={{0,17},{1,16},{2,19},{3,18},{4,21},{5,20},{6,23},{7,22},{8,25},{9,... | collective-permute-start | bytes 98312 | tf_op jit(solution)/shard_map/ppermute | solution.py:364
  27.7 3.9 %collective-permute-start.11 = (bf16[1,128,128]{2,1,0:T(8,128)(2,1)S(1)}, bf16[1,128,128]{2,1,0:T(8,128)(2,1)S(1)}, u32[]{:S(2)}, u32[]{:S(2)}) collective-permute-start(bf16[1,128,128]{2,1,0:T(8,128)(2,1)S(1)} %get-tuple-element.30), channel_id=1, source_target_pairs={{0,16},{8,24},{16,0},{24,8},{1,17},{9,25},{17,1},{25,9},{2,18},{10... | collective-permute-start | bytes 98312 | tf_op jit(solution)/shard_map/ppermute | solution.py:363
  28.3 18.7 %collective-permute-start.2 = (bf16[8,128,128]{2,1,0:T(8,128)(2,1)S(1)}, bf16[8,128,128]{2,1,0:T(8,128)(2,1)S(1)}, u32[]{:S(2)}, u32[]{:S(2)}) collective-permute-start(bf16[8,128,128]{2,1,0:T(8,128)(2,1)S(1)} %shard_map.89), channel_id=1, source_target_pairs={{0,2},{1,3},{2,0},{3,1},{4,6},{5,7},{6,4},{7,5},{8,10},{9,11},{10,... | collective-permute-start | bytes 786440 | tf_op jit(solution)/shard_map/ppermute | solution.py:359
  28.6 16.8 %collective-permute-start.5 = (bf16[4,128,128]{2,1,0:T(8,128)(2,1)S(1)}, bf16[4,128,128]{2,1,0:T(8,128)(2,1)S(1)}, u32[]{:S(2)}, u32[]{:S(2)}) collective-permute-start(bf16[4,128,128]{2,1,0:T(8,128)(2,1)S(1)} %shard_map.91), channel_id=1, source_target_pairs={{0,4},{1,5},{2,6},{3,7},{4,0},{5,1},{6,2},{7,3},{8,12},{9,13},{10,... | collective-permute-start | bytes 393224 | tf_op jit(solution)/shard_map/ppermute | solution.py:359
  31.7 11.9 %collective-permute-start.15 = (bf16[3,128,128]{2,1,0:T(8,128)(2,1)S(1)}, bf16[3,128,128]{2,1,0:T(8,128)(2,1)S(1)}, u32[]{:S(2)}, u32[]{:S(2)}) collective-permute-start(bf16[3,128,128]{2,1,0:T(8,128)(2,1)S(1)} %shard_map.93.piece0_ref), channel_id=1, source_target_pairs={{0,6},{1,7},{2,4},{3,5},{4,2},{5,3},{6,0},{7,1},{8,14},{9,15},{10,... | collective-permute-start | bytes 294920 | tf_op jit(solution)/shard_map/ppermute | solution.py:359
  34.2 11.1 %collective-permute-start.14 = (bf16[3,128,128]{2,1,0:T(8,128)(2,1)S(1)}, bf16[3,128,128]{2,1,0:T(8,128)(2,1)S(1)}, u32[]{:S(2)}, u32[]{:S(2)}) collective-permute-start(bf16[3,128,128]{2,1,0:T(8,128)(2,1)S(1)} %shard_map.93.piece0_ref), channel_id=1, source_target_pairs={{0,4},{1,5},{2,6},{3,7},{4,0},{5,1},{6,2},{7,3},{8,12},{9,13},{10,... | collective-permute-start | bytes 294920 | tf_op jit(solution)/shard_map/ppermute | solution.py:359
  34.7 10.6 %collective-permute-start.13 = (bf16[3,128,128]{2,1,0:T(8,128)(2,1)S(1)}, bf16[3,128,128]{2,1,0:T(8,128)(2,1)S(1)}, u32[]{:S(2)}, u32[]{:S(2)}) collective-permute-start(bf16[3,128,128]{2,1,0:T(8,128)(2,1)S(1)} %shard_map.93.piece0_ref), channel_id=1, source_target_pairs={{0,2},{1,3},{2,0},{3,1},{4,6},{5,7},{6,4},{7,5},{8,10},{9,11},{10,... | collective-permute-start | bytes 294920 | tf_op jit(solution)/shard_map/ppermute | solution.py:359
  45.3 1.7 %collective-permute-start.16 = (bf16[1,4,128,128]{3,2,1,0:T(8,128)(2,1)S(1)}, bf16[1,4,128,128]{3,2,1,0:T(8,128)(2,1)S(1)}, u32[]{:S(2)}, u32[]{:S(2)}) collective-permute-start(bf16[1,4,128,128]{3,2,1,0:T(8,128)(2,1)S(1)} %shard_map.94.split_own_ref), channel_id=1, source_target_pairs={{0,8},{8,0},{16,24},{24,16},{1,9},{9,1},{17,25},{25,17},{2,10},{10... | collective-permute-start | bytes 393224 | tf_op jit(solution)/shard_map/ppermute | solution.py:363
  45.4 5.9 %collective-permute-start.6 = (bf16[4,128,128]{2,1,0:T(8,128)(2,1)S(1)}, bf16[4,128,128]{2,1,0:T(8,128)(2,1)S(1)}, u32[]{:S(2)}, u32[]{:S(2)}) collective-permute-start(bf16[4,128,128]{2,1,0:T(8,128)(2,1)S(1)} %collective-permute-done.5.two_own_ref), channel_id=1, source_target_pairs={{0,1},{1,0},{2,3},{3,2},{4,5},{5,4},{6,7},{7,6},{8,9},{9,8},{10,11... | collective-permute-start | bytes 393224 | tf_op jit(solution)/shard_map/ppermute | solution.py:359

commit v6 on v5

--- a/solution.py
+++ b/solution.py
@@ -159,7 +159,8 @@
     after_ref,
     two_own_ref,
     two_other_ref,
-    near_ref,
+    zero_ref,
+    one_ref,
     two_ref,
 ):
     head_count = table_ref.shape[1]
@@ -171,10 +172,7 @@
         rows = [place * head_count + head for place in range(NEAR)]
 
         def store(place, value):
-            if place < 2:
-                near_ref[place, head] = value
-            else:
-                two_ref[head] = value
+            (zero_ref, one_ref, two_ref)[place][head] = value
 
         columns = pl.ds(head * head_size, head_size)
         payload_cell(flags, gates, rows, range(NEAR), q_ref, k_ref, v_ref, g_ref, columns, store)
@@ -193,13 +191,14 @@
     top_ref[...] = narrow(total[rows:])
 
 
-def pair_sum_kernel(below_ref, far_ref, near_top_ref, far_top_ref, out_ref):
+def pair_sum_kernel(below_ref, far_ref, near_top_ref, far_top_ref, *refs):
+    out_ref = refs[-1]
     rows = below_ref.shape[0]
     out_ref[:rows] = narrow(wide(below_ref[...]) + wide(far_ref[...]))
     out_ref[rows:] = narrow(wide(near_top_ref[...]) + wide(far_top_ref[...]))
 
 
-def gather_kernel(cut, piece0_ref, piece1_ref, piece2_ref, piece3_ref, out_ref):
+def gather_kernel(cut, piece0_ref, piece1_ref, piece2_ref, piece3_ref, after_ref, out_ref):
     for offs, piece_ref in enumerate((piece0_ref, piece1_ref, piece2_ref, piece3_ref)):
         split_levels = out_ref.shape[0]
         eighth = out_ref.shape[1] // 4
@@ -210,10 +209,6 @@
 
 def two_sum_kernel(own_ref, seen_ref, after_ref, out_ref):
     out_ref[...] = narrow(wide(own_ref[...]) + wide(seen_ref[...]))
-
-
-def near_sum_kernel(near_ref, seen_ref, one_ref):
-    one_ref[...] = narrow(wide(near_ref[1]) + wide(seen_ref[1]))
 
 
 def local_kernel(
@@ -273,7 +268,7 @@
     ql_ref,
     kl_ref,
     vl_ref,
-    near_ref,
+    zero_ref,
     one_ref,
     two_own_ref,
     two_other_ref,
@@ -296,7 +291,7 @@
     x_place = flag_ref[0]
     z_place = flag_ref[1] + 2 * flag_ref[2]
     core = flag_ref[inner]
-    held_ref[0] = near_ref[0]
+    held_ref[0] = zero_ref[...]
     held_ref[1] = one_ref[...]
     held_ref[2, pl.ds(x_place * half, half)] = two_own_ref[...]
     held_ref[2, pl.ds((1 - x_place) * half, half)] = two_other_ref[...]
@@ -374,17 +369,28 @@
     def cells(*lead):
         return jax.ShapeDtypeStruct(lead + cell, jnp.bfloat16)
 
-    def call(kernel, in_specs, outs, operands, flops=0, scratch=(), grant=VMEM_BYTES):
+    def call(kernel, in_specs, outs, operands, flops=0, scratch=(), grant=VMEM_BYTES, carry=()):
         moved = sum(operand.size * operand.dtype.itemsize for operand in operands)
-        return pl.pallas_call(
+        outs = tuple(outs) if isinstance(outs, (tuple, list)) else (outs,)
+        count, taken = len(outs), len(operands)
+        if carry:
+            inner = kernel
+            held = len(carry)
+
+            def kernel(*refs):
+                inner(*refs[:taken], *refs[taken + held : taken + held + count], *refs[taken + 2 * held + count :])
+
+        results = pl.pallas_call(
             kernel,
-            out_shape=outs,
-            in_specs=in_specs,
-            out_specs=jax.tree.map(lambda _: vmem, outs),
+            out_shape=outs + tuple(jax.ShapeDtypeStruct(item.shape, item.dtype) for item in carry),
+            in_specs=in_specs + [anywhere] * len(carry),
+            out_specs=(vmem,) * count + (anywhere,) * len(carry),
+            input_output_aliases={taken + place: count + place for place in range(len(carry))},
             scratch_shapes=scratch,
             compiler_params=pltpu.CompilerParams(vmem_limit_bytes=grant),
             cost_estimate=pl.CostEstimate(flops=flops, bytes_accessed=moved, transcendentals=0),
-        )(*operands)
+        )(*operands, *carry)
+        return results if len(results) > 1 else results[0]
 
     quarter = head_count // 4
     half = head_count // 2
@@ -420,19 +426,20 @@
         grant=FIRST_BYTES,
     )
     seen = swap(sent, inner_bits)
-    two_own, two_other, near = call(
+    two_own, two_other, zero, one = call(
         functools.partial(lower_kernel, offset, head_size),
         [smem] + [vmem] * 6 + [anywhere],
-        (cells(half), cells(half), cells(2, head_count)),
+        (cells(half), cells(half), cells(head_count), cells(head_count)),
         (flag_bits, class_lanes, table, query_rows, key_rows, value_rows, out_grad, keep),
         flops=2 * NEAR * row_count * width * head_size,
         scratch=[pltpu.VMEM((head_count,) + cell, jnp.bfloat16)],
     )
-    own_share, *shares_out = call(
+    own_share, *shares_out, zero = call(
         functools.partial(share_kernel, head_count, (whole_levels, split_levels)),
         [smem] + [vmem] * 2 + [anywhere] + [vmem] * len(lead),
         (cells(share_rows),) * 4,
         (flag_bits, seen, keep, two_own, *lead),
+        carry=(zero,),
     )
     big = jax.ShapeDtypeStruct((row_count, width), jnp.float32)
     query_local, key_local, value_local = call(
@@ -485,19 +492,25 @@
     two_sum = call(
         two_sum_kernel, [vmem] * 2 + [anywhere], cells(half), (two_sum, swap(two_sum, 1), two_sum)
     )
+    one_sum = call(
+        two_sum_kernel, [vmem] * 2 + [anywhere], cells(head_count), (one, swap(one, 0), query_local)
+    )
+    one_done = swap(one_sum, 1)
+    zero_done = swap(zero, 0)
     two_half = swap(two_sum, 2)
+    two_rest = swap(two_half, 0)
     shares = call(
         pair_sum_kernel,
-        [vmem] * 4,
+        [vmem] * 4 + [anywhere] * 3,
         cells(share_rows),
-        (below, swap(below, 0), swap(top_sent, top), swap(top_sent, 0, top)),
-    )
-    two_rest = swap(two_half, 0)
-    near_seen = swap(near, 0)
-    one_done = swap(call(near_sum_kernel, [vmem] * 2, cells(head_count), (near, near_seen)), 1)
+        (below, swap(below, 0), swap(top_sent, top), swap(top_sent, 0, top), two_sum, one_sum, zero_done),
+    )
     pieces = [shares] + [swap(shares, *z_bits(offs)) for offs in (1, 2, 3)]
     split_own = call(
-        functools.partial(gather_kernel, cut), [vmem] * 4, cells(split_levels, half), pieces
+        functools.partial(gather_kernel, cut),
+        [vmem] * 4 + [anywhere],
+        cells(split_levels, half),
+        (*pieces, two_half),
     )
     split_other = swap(split_own, inner_bits)
 
@@ -516,7 +529,7 @@
             query_local,
             key_local,
             value_local,
-            near_seen,
+            zero_done,
             one_done,
             two_half,
             two_rest,

time: 54.3 us -> 47.2 us (0.87)
  waiting for transfers between devices: 21.1 us -> 13.5 us
    ppermute x13 -> x14, waiting for transfers between devices: 20.9 us -> 11.3 us  [swap(): return lax.ppermute(block, 'gy', [(i, i ^ mask) for i in range(inner_size)])]
    ppermute x3, waiting for transfers between devices: 0.13 us -> 1.32 us  [swap(): return lax.ppermute(block, 'gx', [(i, i ^ mask) for i in range(size)])]
    ppermute x1, waiting for transfers between devices: 0.01 us -> 0.96 us  [swap(): lax.ppermute(block, ('gx', 'gy'), [(i, i ^ mask) for i in range(device_co...]
    ppermute x13 -> x14, starting transfers between devices: 20.5 us -> 20.4 us  [swap(): return lax.ppermute(block, 'gy', [(i, i ^ mask) for i in range(inner_size)])]
  transfers between devices with their start and end apart: 17 -> 18, of which waited for: 5 -> 7; matrix products, arithmetic and copies ran while one was open for 0% -> 0% of each run, Pallas kernels for 7% -> 9%
where the time goes in v6:
time: 47.2 us; the launch traced here: 47 us
  starting transfers between devices  23.4 us (50%)
  waiting for transfers between devices  13.5 us (29%)
  Pallas kernels  9.12 us (19%)
  between operations  0.82 us (2%)
    ppermute x14, starting transfers between devices, swap(): return lax.ppermute(block, 'gy', [(i, i ^ mask) for i in range(inner_size)])  20.4 us
    ppermute x14, waiting for transfers between devices, swap(): return lax.ppermute(block, 'gy', [(i, i ^ mask) for i in range(inner_size)])  11.3 us
    pallas_call x11, Pallas kernels, call(): pl.pallas_call(kernel, out_shape=outs + tuple((jax.ShapeDtypeStruct(item....  9.12 us
    ppermute x1, starting transfers between devices, swap(): lax.ppermute(block, ('gx', 'gy'), [(i, i ^ mask) for i in range(device_co...  1.93 us
    ppermute x3, waiting for transfers between devices, swap(): return lax.ppermute(block, 'gx', [(i, i ^ mask) for i in range(size)])  1.32 us
    ppermute x3, starting transfers between devices, swap(): return lax.ppermute(block, 'gx', [(i, i ^ mask) for i in range(size)])  1.09 us
    ppermute x1, waiting for transfers between devices, swap(): lax.ppermute(block, ('gx', 'gy'), [(i, i ^ mask) for i in range(device_co...  0.96 us
  transfers between devices with their start and end apart: 18, of which 7 were waited for; matrix products, arithmetic and copies ran while one was open for 0% of the time, Pallas kernels for 9%

profile of v6, /device:TPU:0, one launch (start us, length us, event | category | flops | bytes accessed | tf_op | source)
XLA Modules:
  0.0 47.0 jit_solution(14729286433709919748)
XLA Ops:
  0.6 0.0 copy-start
  0.7 0.0 copy-start.2
  0.7 2.3 %shard_map.85 = (bf16[12,128,128]{2,1,0:T(8,128)(2,1)S(1)}, bf16[4,128,128]{2,1,0:T(8,128)(2,1)S(1)}) custom-call(s32[5]{0:T(128)S(1)} %shift-right-arithmetic_and_fusion.flag_ref.refs_0_, s32[1,128]{1,0:T(1,128)} %bitcast.6, f32[20,8,32]{2,1,0:T(8,128)} %bitcast.2, bf16[128,1024]{1,0:T(8,128)(2,1)} %q_ref.3, bf16[128,1024]{1,0:T(8,128)(2,1)} %k_ref.5, ...), custom_call_target="tpu_custom_call" | custom-call | flops 67108864 | bytes 1069588 | tf_op jit(solution)/shard_map/pallas_call | solution.py:383
  3.0 0.5 %collective-permute-start = (bf16[12,128,128]{2,1,0:T(8,128)(2,1)S(1)}, bf16[12,128,128]{2,1,0:T(8,128)(2,1)S(1)}, u32[]{:S(2)}, u32[]{:S(2)}) collective-permute-start(bf16[12,128,128]{2,1,0:T(8,128)(2,1)S(1)} %get-tuple-element.19), channel_id=1, source_target_pairs={{0,8},{8,0},{16,24},{24,16},{1,9},{9,1},{17,25},{25,17},{2,10},{10... | collective-permute-start | bytes 1179656 | tf_op jit(solution)/shard_map/ppermute | solution.py:358
  3.5 0.1 copy-done.5
  3.6 1.2 %shard_map.86 = (bf16[4,128,128]{2,1,0:T(8,128)(2,1)S(1)}, bf16[4,128,128]{2,1,0:T(8,128)(2,1)S(1)}, bf16[8,128,128]{2,1,0:T(8,128)(2,1)S(1)}, bf16[8,128,128]{2,1,0:T(8,128)(2,1)S(1)}) custom-call(s32[5]{0:T(128)S(1)} %shift-right-arithmetic_and_fusion.flag_ref.refs_0_, s32[1,128]{1,0:T(1,128)S(1)} %bitcast.7, f32[20,8,32]{2,1,0:T(8,128)S(1)} %bitcast.3, ...), custom_call_target="tpu_custom_call" | custom-call | flops 100663296 | bytes 1200660 | tf_op jit(solution)/shard_map/pallas_call | solution.py:383
  4.8 3.0 %collective-permute-start.4 = (bf16[4,128,128]{2,1,0:T(8,128)(2,1)S(1)}, bf16[4,128,128]{2,1,0:T(8,128)(2,1)S(1)}, u32[]{:S(2)}, u32[]{:S(2)}) collective-permute-start(bf16[4,128,128]{2,1,0:T(8,128)(2,1)S(1)} %get-tuple-element.29), channel_id=1, source_target_pairs={{0,1},{1,0},{2,3},{3,2},{4,5},{5,4},{6,7},{7,6},{8,9},{9,8},{10,11... | collective-permute-start | bytes 393224 | tf_op jit(solution)/shard_map/ppermute | solution.py:354
  7.8 0.1 collective-permute-start.2
  7.9 0.6 %shard_map.87 = (bf16[3,128,128]{2,1,0:T(8,128)(2,1)S(1)}, bf16[3,128,128]{2,1,0:T(8,128)(2,1)S(1)}, bf16[3,128,128]{2,1,0:T(8,128)(2,1)S(1)}, bf16[3,128,128]{2,1,0:T(8,128)(2,1)S(1)}, bf16[8,128,128]{2,1,0:T(8,128)(2,1)S(1)}) custom-call(s32[5]{0:T(128)S(1)} %shift-right-arithmetic_and_fusion.flag_ref.refs_0_, ...), custom_call_target="tpu_custom_call", output_to_operand_aliasing={{4}: (4, {})} | custom-call | bytes 655380 | tf_op jit(solution)/shard_map/pallas_call | solution.py:383
  8.5 4.1 %collective-permute-start.8 = (bf16[3,128,128]{2,1,0:T(8,128)(2,1)S(1)}, bf16[3,128,128]{2,1,0:T(8,128)(2,1)S(1)}, u32[]{:S(2)}, u32[]{:S(2)}) collective-permute-start(bf16[3,128,128]{2,1,0:T(8,128)(2,1)S(1)} %get-tuple-element.30), channel_id=1, source_target_pairs={{0,6},{1,7},{2,4},{3,5},{4,2},{5,3},{6,0},{7,1},{8,14},{9,15},{10,... | collective-permute-start | bytes 294920 | tf_op jit(solution)/shard_map/ppermute | solution.py:354
  12.6 1.5 %collective-permute-start.1 = (bf16[8,128,128]{2,1,0:T(8,128)(2,1)S(1)}, bf16[8,128,128]{2,1,0:T(8,128)(2,1)S(1)}, u32[]{:S(2)}, u32[]{:S(2)}) collective-permute-start(bf16[8,128,128]{2,1,0:T(8,128)(2,1)S(1)} %get-tuple-element.27), channel_id=1, source_target_pairs={{0,1},{1,0},{2,3},{3,2},{4,5},{5,4},{6,7},{7,6},{8,9},{9,8},{10,11... | collective-permute-start | bytes 786440 | tf_op jit(solution)/shard_map/ppermute | solution.py:354
  14.1 2.0 %shard_map.88 = (f32[128,1024]{1,0:T(8,128)S(1)}, f32[128,1024]{1,0:T(8,128)S(1)}, f32[128,1024]{1,0:T(8,128)S(1)}) custom-call(s32[1,128]{1,0:T(1,128)S(1)} %bitcast.8, f32[20,8,32]{2,1,0:T(8,128)S(1)} %bitcast.4, bf16[128,1024]{1,0:T(8,128)(2,1)S(1)} %copy-done.3, bf16[128,1024]{1,0:T(8,128)(2,1)S(1)} %copy-done, bf16[128,1024]{1,0:T(8,128)(2,1)S(1)} %copy-done.1, ...), custom_call_target="tpu_custom_call" | custom-call | flops 167772160 | bytes 1167872 | tf_op jit(solution)/shard_map/pallas_call | solution.py:383
  16.2 0.8 %collective-permute-start.10 = (bf16[3,128,128]{2,1,0:T(8,128)(2,1)S(1)}, bf16[3,128,128]{2,1,0:T(8,128)(2,1)S(1)}, u32[]{:S(2)}, u32[]{:S(2)}) collective-permute-start(bf16[3,128,128]{2,1,0:T(8,128)(2,1)S(1)} %get-tuple-element.32), channel_id=1, source_target_pairs={{0,2},{1,3},{2,0},{3,1},{4,6},{5,7},{6,4},{7,5},{8,10},{9,11},{10,... | collective-permute-start | bytes 294920 | tf_op jit(solution)/shard_map/ppermute | solution.py:354
  17.1 2.6 %collective-permute-start.5 = (bf16[4,128,128]{2,1,0:T(8,128)(2,1)S(1)}, bf16[4,128,128]{2,1,0:T(8,128)(2,1)S(1)}, u32[]{:S(2)}, u32[]{:S(2)}) collective-permute-start(bf16[4,128,128]{2,1,0:T(8,128)(2,1)S(1)} %shard_map.90.own_ref.after_ref), channel_id=1, source_target_pairs={{0,2},{1,3},{2,0},{3,1},{4,6},{5,7},{6,4},{7,5},{8,10},{9,11},{10,... | collective-permute-start | bytes 393224 | tf_op jit(solution)/shard_map/ppermute | solution.py:354
  19.7 0.9 %collective-permute-done.9.refs_1_ = bf16[3,128,128]{2,1,0:T(8,128)(2,1)S(1)} collective-permute-done((bf16[3,128,128]{2,1,0:T(8,128)(2,1)S(1)}, bf16[3,128,128]{2,1,0:T(8,128)(2,1)S(1)}, u32[]{:S(2)}, u32[]{:S(2)}) %collective-permute-start.9) | collective-permute-done | bytes 98336 | tf_op jit(solution)/shard_map/ppermute | solution.py:354
  20.6 2.2 %collective-permute-done.10.refs_2_ = bf16[3,128,128]{2,1,0:T(8,128)(2,1)S(1)} collective-permute-done((bf16[3,128,128]{2,1,0:T(8,128)(2,1)S(1)}, bf16[3,128,128]{2,1,0:T(8,128)(2,1)S(1)}, u32[]{:S(2)}, u32[]{:S(2)}) %collective-permute-start.10) | collective-permute-done | bytes 98336 | tf_op jit(solution)/shard_map/ppermute | solution.py:354
  22.7 0.1 shard_map.92
  22.8 1.1 %collective-permute-start.11 = (bf16[2,128,128]{2,1,0:T(8,128)(2,1)S(1)}, bf16[2,128,128]{2,1,0:T(8,128)(2,1)S(1)}, u32[]{:S(2)}, u32[]{:S(2)}) collective-permute-start(bf16[2,128,128]{2,1,0:T(8,128)(2,1)S(1)} %get-tuple-element.33.below_ref), channel_id=1, source_target_pairs={{0,1},{1,0},{2,3},{3,2},{4,5},{5,4},{6,7},{7,6},{8,9},{9,8},{10,11... | collective-permute-start | bytes 196616 | tf_op jit(solution)/shard_map/ppermute | solution.py:354
  23.9 1.9 %collective-permute-start.13 = (bf16[1,128,128]{2,1,0:T(8,128)(2,1)S(1)}, bf16[1,128,128]{2,1,0:T(8,128)(2,1)S(1)}, u32[]{:S(2)}, u32[]{:S(2)}) collective-permute-start(bf16[1,128,128]{2,1,0:T(8,128)(2,1)S(1)} %get-tuple-element.34), channel_id=1, source_target_pairs={{0,17},{1,16},{2,19},{3,18},{4,21},{5,20},{6,23},{7,22},{8,25},{9,... | collective-permute-start | bytes 98312 | tf_op jit(solution)/shard_map/ppermute | solution.py:359
  25.8 0.5 %collective-permute-start.12 = (bf16[1,128,128]{2,1,0:T(8,128)(2,1)S(1)}, bf16[1,128,128]{2,1,0:T(8,128)(2,1)S(1)}, u32[]{:S(2)}, u32[]{:S(2)}) collective-permute-start(bf16[1,128,128]{2,1,0:T(8,128)(2,1)S(1)} %get-tuple-element.34), channel_id=1, source_target_pairs={{0,16},{8,24},{16,0},{24,8},{1,17},{9,25},{17,1},{25,9},{2,18},{10... | collective-permute-start | bytes 98312 | tf_op jit(solution)/shard_map/ppermute | solution.py:358
  26.4 1.3 %collective-permute-start.6 = (bf16[4,128,128]{2,1,0:T(8,128)(2,1)S(1)}, bf16[4,128,128]{2,1,0:T(8,128)(2,1)S(1)}, u32[]{:S(2)}, u32[]{:S(2)}) collective-permute-start(bf16[4,128,128]{2,1,0:T(8,128)(2,1)S(1)} %shard_map.91.refs_0_), channel_id=1, source_target_pairs={{0,4},{1,5},{2,6},{3,7},{4,0},{5,1},{6,2},{7,3},{8,12},{9,13},{10,... | collective-permute-start | bytes 393224 | tf_op jit(solution)/shard_map/ppermute | solution.py:354
  27.7 0.1 shard_map.89.refs_1_
  27.8 1.0 %collective-permute-done.13.far_top_ref = bf16[1,128,128]{2,1,0:T(8,128)(2,1)S(1)} collective-permute-done((bf16[1,128,128]{2,1,0:T(8,128)(2,1)S(1)}, bf16[1,128,128]{2,1,0:T(8,128)(2,1)S(1)}, u32[]{:S(2)}, u32[]{:S(2)}) %collective-permute-start.13) | collective-permute-done | bytes 32800 | tf_op jit(solution)/shard_map/ppermute | solution.py:359
  28.7 1.4 %collective-permute-start.3 = (bf16[8,128,128]{2,1,0:T(8,128)(2,1)S(1)}, bf16[8,128,128]{2,1,0:T(8,128)(2,1)S(1)}, u32[]{:S(2)}, u32[]{:S(2)}) collective-permute-start(bf16[8,128,128]{2,1,0:T(8,128)(2,1)S(1)} %shard_map.89.refs_1_), channel_id=1, source_target_pairs={{0,2},{1,3},{2,0},{3,1},{4,6},{5,7},{6,4},{7,5},{8,10},{9,11},{10,... | collective-permute-start | bytes 786440 | tf_op jit(solution)/shard_map/ppermute | solution.py:354
  30.1 2.6 %collective-permute-start.16 = (bf16[3,128,128]{2,1,0:T(8,128)(2,1)S(1)}, bf16[3,128,128]{2,1,0:T(8,128)(2,1)S(1)}, u32[]{:S(2)}, u32[]{:S(2)}) collective-permute-start(bf16[3,128,128]{2,1,0:T(8,128)(2,1)S(1)} %shard_map.93.piece0_ref), channel_id=1, source_target_pairs={{0,6},{1,7},{2,4},{3,5},{4,2},{5,3},{6,0},{7,1},{8,14},{9,15},{10,... | collective-permute-start | bytes 294920 | tf_op jit(solution)/shard_map/ppermute | solution.py:354
  32.8 1.8 %collective-permute-start.14 = (bf16[3,128,128]{2,1,0:T(8,128)(2,1)S(1)}, bf16[3,128,128]{2,1,0:T(8,128)(2,1)S(1)}, u32[]{:S(2)}, u32[]{:S(2)}) collective-permute-start(bf16[3,128,128]{2,1,0:T(8,128)(2,1)S(1)} %shard_map.93.piece0_ref), channel_id=1, source_target_pairs={{0,2},{1,3},{2,0},{3,1},{4,6},{5,7},{6,4},{7,5},{8,10},{9,11},{10,... | collective-permute-start | bytes 294920 | tf_op jit(solution)/shard_map/ppermute | solution.py:354
  34.6 2.1 %collective-permute-done.6.after_ref.two_own_ref = bf16[4,128,128]{2,1,0:T(8,128)(2,1)S(1)} collective-permute-done((bf16[4,128,128]{2,1,0:T(8,128)(2,1)S(1)}, bf16[4,128,128]{2,1,0:T(8,128)(2,1)S(1)}, u32[]{:S(2)}, u32[]{:S(2)}) %collective-permute-start.6) | collective-permute-done | bytes 131104 | tf_op jit(solution)/shard_map/ppermute | solution.py:354
  36.7 4.2 %collective-permute-done.16.piece3_ref = bf16[3,128,128]{2,1,0:T(8,128)(2,1)S(1)} collective-permute-done((bf16[3,128,128]{2,1,0:T(8,128)(2,1)S(1)}, bf16[3,128,128]{2,1,0:T(8,128)(2,1)S(1)}, u32[]{:S(2)}, u32[]{:S(2)}) %collective-permute-start.16) | collective-permute-done | bytes 98336 | tf_op jit(solution)/shard_map/ppermute | solution.py:354
  40.8 1.9 %collective-permute-done.14.piece1_ref = bf16[3,128,128]{2,1,0:T(8,128)(2,1)S(1)} collective-permute-done((bf16[3,128,128]{2,1,0:T(8,128)(2,1)S(1)}, bf16[3,128,128]{2,1,0:T(8,128)(2,1)S(1)}, u32[]{:S(2)}, u32[]{:S(2)}) %collective-permute-start.14) | collective-permute-done | bytes 98336 | tf_op jit(solution)/shard_map/ppermute | solution.py:354
  42.8 0.1 collective-permute-start.17
  42.9 1.3 %collective-permute-done.17.split_other_ref = bf16[1,4,128,128]{3,2,1,0:T(8,128)(2,1)S(1)} collective-permute-done((bf16[1,4,128,128]{3,2,1,0:T(8,128)(2,1)S(1)}, bf16[1,4,128,128]{3,2,1,0:T(8,128)(2,1)S(1)}, u32[]{:S(2)}, u32[]{:S(2)}) %collective-permute-start.17) | collective-permute-done | bytes 131104 | tf_op jit(solution)/shard_map/ppermute | solution.py:358
  44.2 2.8 %shard_map.95 = (bf16[128,1024]{1,0:T(8,128)(2,1)}, bf16[128,1024]{1,0:T(8,128)(2,1)}, bf16[128,1024]{1,0:T(8,128)(2,1)}) custom-call(s32[5]{0:T(128)S(1)} %shift-right-arithmetic_and_fusion.flag_ref.refs_0_, s32[1,128]{1,0:T(1,128)S(1)} %bitcast.9, f32[20,8,32]{2,1,0:T(8,128)S(1)} %bitcast.5, bf16[128,1024]{1,0:T(8,128)(2,1)S(1)} %copy-done, ...), custom_call_target="tpu_custom_call" | custom-call | flops 234881024 | bytes 3822100 | tf_op jit(solution)/shard_map/pallas_call | solution.py:383
  (28 shorter events, 0.2 us)
Async XLA Ops:
  0.6 2.9 %copy-start = (bf16[128,1024]{1,0:T(8,128)(2,1)S(1)}, bf16[128,1024]{1,0:T(8,128)(2,1)}, u32[]{:S(2)}) copy-start(bf16[128,1024]{1,0:T(8,128)(2,1)} %k_ref.5) | copy-start | bytes 786436
  0.7 2.9 %copy-start.1 = (bf16[128,1024]{1,0:T(8,128)(2,1)S(1)}, bf16[128,1024]{1,0:T(8,128)(2,1)}, u32[]{:S(2)}) copy-start(bf16[128,1024]{1,0:T(8,128)(2,1)} %v_ref.5) | copy-start | bytes 786436
  0.7 2.9 %copy-start.2 = (bf16[128,1024]{1,0:T(8,128)(2,1)S(1)}, bf16[128,1024]{1,0:T(8,128)(2,1)}, u32[]{:S(2)}) copy-start(bf16[128,1024]{1,0:T(8,128)(2,1)} %g_ref.5) | copy-start | bytes 786436
  0.7 2.8 %copy-start.3 = (bf16[128,1024]{1,0:T(8,128)(2,1)S(1)}, bf16[128,1024]{1,0:T(8,128)(2,1)}, u32[]{:S(2)}) copy-start(bf16[128,1024]{1,0:T(8,128)(2,1)} %q_ref.3) | copy-start | bytes 786436
  0.7 2.8 %copy-start.4 = (f32[32,20,8]{0,2,1:T(8,128)S(1)}, f32[32,20,8]{0,2,1:T(8,128)}, u32[]{:S(2)}) copy-start(f32[32,20,8]{0,2,1:T(8,128)} %param.11) | copy-start | bytes 61444
  3.0 0.7 %copy-start.5 = (s32[128]{0:T(128)S(1)}, s32[128]{0:T(128)}, u32[]{:S(2)}) copy-start(s32[128]{0:T(128)} %param.10) | copy-start | bytes 1540
  3.0 4.9 %collective-permute-start = (bf16[12,128,128]{2,1,0:T(8,128)(2,1)S(1)}, bf16[12,128,128]{2,1,0:T(8,128)(2,1)S(1)}, u32[]{:S(2)}, u32[]{:S(2)}) collective-permute-start(bf16[12,128,128]{2,1,0:T(8,128)(2,1)S(1)} %get-tuple-element.19), channel_id=1, source_target_pairs={{0,8},{8,0},{16,24},{24,16},{1,9},{9,1},{17,25},{25,17},{2,10},{10... | collective-permute-start | bytes 1179656 | tf_op jit(solution)/shard_map/ppermute | solution.py:358
  4.8 11.3 %collective-permute-start.4 = (bf16[4,128,128]{2,1,0:T(8,128)(2,1)S(1)}, bf16[4,128,128]{2,1,0:T(8,128)(2,1)S(1)}, u32[]{:S(2)}, u32[]{:S(2)}) collective-permute-start(bf16[4,128,128]{2,1,0:T(8,128)(2,1)S(1)} %get-tuple-element.29), channel_id=1, source_target_pairs={{0,1},{1,0},{2,3},{3,2},{4,5},{5,4},{6,7},{7,6},{8,9},{9,8},{10,11... | collective-permute-start | bytes 393224 | tf_op jit(solution)/shard_map/ppermute | solution.py:354
  7.8 18.6 %collective-permute-start.2 = (bf16[8,128,128]{2,1,0:T(8,128)(2,1)S(1)}, bf16[8,128,128]{2,1,0:T(8,128)(2,1)S(1)}, u32[]{:S(2)}, u32[]{:S(2)}) collective-permute-start(bf16[8,128,128]{2,1,0:T(8,128)(2,1)S(1)} %get-tuple-element.28.own_ref), channel_id=1, source_target_pairs={{0,1},{1,0},{2,3},{3,2},{4,5},{5,4},{6,7},{7,6},{8,9},{9,8},{10,11... | collective-permute-start | bytes 786440 | tf_op jit(solution)/shard_map/ppermute | solution.py:354
  8.5 8.5 %collective-permute-start.8 = (bf16[3,128,128]{2,1,0:T(8,128)(2,1)S(1)}, bf16[3,128,128]{2,1,0:T(8,128)(2,1)S(1)}, u32[]{:S(2)}, u32[]{:S(2)}) collective-permute-start(bf16[3,128,128]{2,1,0:T(8,128)(2,1)S(1)} %get-tuple-element.30), channel_id=1, source_target_pairs={{0,6},{1,7},{2,4},{3,5},{4,2},{5,3},{6,0},{7,1},{8,14},{9,15},{10,... | collective-permute-start | bytes 294920 | tf_op jit(solution)/shard_map/ppermute | solution.py:354
  12.6 17.5 %collective-permute-start.1 = (bf16[8,128,128]{2,1,0:T(8,128)(2,1)S(1)}, bf16[8,128,128]{2,1,0:T(8,128)(2,1)S(1)}, u32[]{:S(2)}, u32[]{:S(2)}) collective-permute-start(bf16[8,128,128]{2,1,0:T(8,128)(2,1)S(1)} %get-tuple-element.27), channel_id=1, source_target_pairs={{0,1},{1,0},{2,3},{3,2},{4,5},{5,4},{6,7},{7,6},{8,9},{9,8},{10,11... | collective-permute-start | bytes 786440 | tf_op jit(solution)/shard_map/ppermute | solution.py:354
  14.1 6.5 %collective-permute-start.9 = (bf16[3,128,128]{2,1,0:T(8,128)(2,1)S(1)}, bf16[3,128,128]{2,1,0:T(8,128)(2,1)S(1)}, u32[]{:S(2)}, u32[]{:S(2)}) collective-permute-start(bf16[3,128,128]{2,1,0:T(8,128)(2,1)S(1)} %get-tuple-element.31), channel_id=1, source_target_pairs={{0,4},{1,5},{2,6},{3,7},{4,0},{5,1},{6,2},{7,3},{8,12},{9,13},{10,... | collective-permute-start | bytes 294920 | tf_op jit(solution)/shard_map/ppermute | solution.py:354
  16.2 6.6 %collective-permute-start.10 = (bf16[3,128,128]{2,1,0:T(8,128)(2,1)S(1)}, bf16[3,128,128]{2,1,0:T(8,128)(2,1)S(1)}, u32[]{:S(2)}, u32[]{:S(2)}) collective-permute-start(bf16[3,128,128]{2,1,0:T(8,128)(2,1)S(1)} %get-tuple-element.32), channel_id=1, source_target_pairs={{0,2},{1,3},{2,0},{3,1},{4,6},{5,7},{6,4},{7,5},{8,10},{9,11},{10,... | collective-permute-start | bytes 294920 | tf_op jit(solution)/shard_map/ppermute | solution.py:354
  17.1 8.8 %collective-permute-start.5 = (bf16[4,128,128]{2,1,0:T(8,128)(2,1)S(1)}, bf16[4,128,128]{2,1,0:T(8,128)(2,1)S(1)}, u32[]{:S(2)}, u32[]{:S(2)}) collective-permute-start(bf16[4,128,128]{2,1,0:T(8,128)(2,1)S(1)} %shard_map.90.own_ref.after_ref), channel_id=1, source_target_pairs={{0,2},{1,3},{2,0},{3,1},{4,6},{5,7},{6,4},{7,5},{8,10},{9,11},{10,... | collective-permute-start | bytes 393224 | tf_op jit(solution)/shard_map/ppermute | solution.py:354
  22.8 7.3 %collective-permute-start.11 = (bf16[2,128,128]{2,1,0:T(8,128)(2,1)S(1)}, bf16[2,128,128]{2,1,0:T(8,128)(2,1)S(1)}, u32[]{:S(2)}, u32[]{:S(2)}) collective-permute-start(bf16[2,128,128]{2,1,0:T(8,128)(2,1)S(1)} %get-tuple-element.33.below_ref), channel_id=1, source_target_pairs={{0,1},{1,0},{2,3},{3,2},{4,5},{5,4},{6,7},{7,6},{8,9},{9,8},{10,11... | collective-permute-start | bytes 196616 | tf_op jit(solution)/shard_map/ppermute | solution.py:354
  23.9 4.8 %collective-permute-start.13 = (bf16[1,128,128]{2,1,0:T(8,128)(2,1)S(1)}, bf16[1,128,128]{2,1,0:T(8,128)(2,1)S(1)}, u32[]{:S(2)}, u32[]{:S(2)}) collective-permute-start(bf16[1,128,128]{2,1,0:T(8,128)(2,1)S(1)} %get-tuple-element.34), channel_id=1, source_target_pairs={{0,17},{1,16},{2,19},{3,18},{4,21},{5,20},{6,23},{7,22},{8,25},{9,... | collective-permute-start | bytes 98312 | tf_op jit(solution)/shard_map/ppermute | solution.py:359
  25.8 4.2 %collective-permute-start.12 = (bf16[1,128,128]{2,1,0:T(8,128)(2,1)S(1)}, bf16[1,128,128]{2,1,0:T(8,128)(2,1)S(1)}, u32[]{:S(2)}, u32[]{:S(2)}) collective-permute-start(bf16[1,128,128]{2,1,0:T(8,128)(2,1)S(1)} %get-tuple-element.34), channel_id=1, source_target_pairs={{0,16},{8,24},{16,0},{24,8},{1,17},{9,25},{17,1},{25,9},{2,18},{10... | collective-permute-start | bytes 98312 | tf_op jit(solution)/shard_map/ppermute | solution.py:358
  26.4 10.3 %collective-permute-start.6 = (bf16[4,128,128]{2,1,0:T(8,128)(2,1)S(1)}, bf16[4,128,128]{2,1,0:T(8,128)(2,1)S(1)}, u32[]{:S(2)}, u32[]{:S(2)}) collective-permute-start(bf16[4,128,128]{2,1,0:T(8,128)(2,1)S(1)} %shard_map.91.refs_0_), channel_id=1, source_target_pairs={{0,4},{1,5},{2,6},{3,7},{4,0},{5,1},{6,2},{7,3},{8,12},{9,13},{10,... | collective-permute-start | bytes 393224 | tf_op jit(solution)/shard_map/ppermute | solution.py:354
  28.7 14.1 %collective-permute-start.3 = (bf16[8,128,128]{2,1,0:T(8,128)(2,1)S(1)}, bf16[8,128,128]{2,1,0:T(8,128)(2,1)S(1)}, u32[]{:S(2)}, u32[]{:S(2)}) collective-permute-start(bf16[8,128,128]{2,1,0:T(8,128)(2,1)S(1)} %shard_map.89.refs_1_), channel_id=1, source_target_pairs={{0,2},{1,3},{2,0},{3,1},{4,6},{5,7},{6,4},{7,5},{8,10},{9,11},{10,... | collective-permute-start | bytes 786440 | tf_op jit(solution)/shard_map/ppermute | solution.py:354
  30.1 10.7 %collective-permute-start.16 = (bf16[3,128,128]{2,1,0:T(8,128)(2,1)S(1)}, bf16[3,128,128]{2,1,0:T(8,128)(2,1)S(1)}, u32[]{:S(2)}, u32[]{:S(2)}) collective-permute-start(bf16[3,128,128]{2,1,0:T(8,128)(2,1)S(1)} %shard_map.93.piece0_ref), channel_id=1, source_target_pairs={{0,6},{1,7},{2,4},{3,5},{4,2},{5,3},{6,0},{7,1},{8,14},{9,15},{10,... | collective-permute-start | bytes 294920 | tf_op jit(solution)/shard_map/ppermute | solution.py:354
  32.8 8.1 %collective-permute-start.15 = (bf16[3,128,128]{2,1,0:T(8,128)(2,1)S(1)}, bf16[3,128,128]{2,1,0:T(8,128)(2,1)S(1)}, u32[]{:S(2)}, u32[]{:S(2)}) collective-permute-start(bf16[3,128,128]{2,1,0:T(8,128)(2,1)S(1)} %shard_map.93.piece0_ref), channel_id=1, source_target_pairs={{0,4},{1,5},{2,6},{3,7},{4,0},{5,1},{6,2},{7,3},{8,12},{9,13},{10,... | collective-permute-start | bytes 294920 | tf_op jit(solution)/shard_map/ppermute | solution.py:354
  32.8 10.0 %collective-permute-start.14 = (bf16[3,128,128]{2,1,0:T(8,128)(2,1)S(1)}, bf16[3,128,128]{2,1,0:T(8,128)(2,1)S(1)}, u32[]{:S(2)}, u32[]{:S(2)}) collective-permute-start(bf16[3,128,128]{2,1,0:T(8,128)(2,1)S(1)} %shard_map.93.piece0_ref), channel_id=1, source_target_pairs={{0,2},{1,3},{2,0},{3,1},{4,6},{5,7},{6,4},{7,5},{8,10},{9,11},{10,... | collective-permute-start | bytes 294920 | tf_op jit(solution)/shard_map/ppermute | solution.py:354
  36.7 6.2 %collective-permute-start.7 = (bf16[4,128,128]{2,1,0:T(8,128)(2,1)S(1)}, bf16[4,128,128]{2,1,0:T(8,128)(2,1)S(1)}, u32[]{:S(2)}, u32[]{:S(2)}) collective-permute-start(bf16[4,128,128]{2,1,0:T(8,128)(2,1)S(1)} %collective-permute-done.6.after_ref.two_own_ref), channel_id=1, source_target_pairs={{0,1},{1,0},{2,3},{3,2},{4,5},{5,4},{6,7},{7,6},{8,9},{9,8},{10,11... | collective-permute-start | bytes 393224 | tf_op jit(solution)/shard_map/ppermute | solution.py:354
  42.8 1.4 %collective-permute-start.17 = (bf16[1,4,128,128]{3,2,1,0:T(8,128)(2,1)S(1)}, bf16[1,4,128,128]{3,2,1,0:T(8,128)(2,1)S(1)}, u32[]{:S(2)}, u32[]{:S(2)}) collective-permute-start(bf16[1,4,128,128]{3,2,1,0:T(8,128)(2,1)S(1)} %shard_map.94.split_own_ref), channel_id=1, source_target_pairs={{0,8},{8,0},{16,24},{24,16},{1,9},{9,1},{17,25},{25,17},{2,10},{10... | collective-permute-start | bytes 393224 | tf_op jit(solution)/shard_map/ppermute | solution.py:358

commit v7 on v6

--- a/solution.py
+++ b/solution.py
@@ -214,6 +214,8 @@
 def local_kernel(
     block_depth,
     head_size,
+    total,
+    flag_ref,
     class_ref,
     table_ref,
     q_ref,
@@ -224,10 +226,17 @@
     qo_ref,
     ko_ref,
     vo_ref,
+    gate_ref,
 ):
     head_count = table_ref.shape[1]
     tokens = q_ref.shape[0]
-    gates = gate_lanes(class_ref, table_ref, 0, block_depth + 1)
+    offset = block_depth + 1
+    gates = gate_lanes(class_ref, table_ref, 0, offset + total)
+    for level in range(total):
+        first = (offset + level) * head_count
+        row = level * head_count
+        on = wide(flag_ref[level])
+        gate_ref[:, row : row + head_count] = (gates[first : first + head_count] * on).T
     source = lax.broadcasted_iota(jnp.int32, (tokens, tokens), 0)
     target = lax.broadcasted_iota(jnp.int32, (tokens, tokens), 1)
     apart = jnp.bitwise_xor(source, target)
@@ -250,18 +259,13 @@
         vo_ref[:, columns] = product(weighted_scores, grad_here, 1, 0)
 
 
-def gate_columns(class_ref, table_ref, first, last):
-    return gate_lanes(class_ref, table_ref, first, last).T
-
-
 def final_kernel(
-    offset,
+    head_count,
     head_size,
     total,
     inner,
     flag_ref,
-    class_ref,
-    table_ref,
+    gate_ref,
     k_ref,
     v_ref,
     g_ref,
@@ -278,16 +282,18 @@
     piece3_ref,
     split_own_ref,
     split_other_ref,
+    qo_hbm,
+    ko_hbm,
+    vo_hbm,
+    held_ref,
     qo_ref,
     ko_ref,
     vo_ref,
-    held_ref,
+    sent,
 ):
-    head_count = table_ref.shape[1]
     half = head_count // 2
     quarter = head_count // 4
     eighth = head_count // 8
-    gates = gate_columns(class_ref, table_ref, offset, offset + total)
     x_place = flag_ref[0]
     z_place = flag_ref[1] + 2 * flag_ref[2]
     core = flag_ref[inner]
@@ -310,6 +316,7 @@
             held_ref[level, pl.ds((1 - core) * half + first, eighth)] = split_other_ref[
                 level - split, rows
             ]
+    moves = []
     for head in range(head_count):
         columns = pl.ds(head * head_size, head_size)
         grad_here = g_ref[:, columns]
@@ -319,9 +326,8 @@
             state = held_ref[level, head]
             term = product(grad_here, state, 1, 1)
             row = level * head_count + head
-            on = wide(flag_ref[level])
-            query_total = query_total + (gates[:, row : row + 1] * on) * term
-            state_grad = state_grad + wide(state) * (1.0 - on)
+            query_total = query_total + gate_ref[:, row : row + 1] * term
+            state_grad = state_grad + wide(state) * (1.0 - wide(flag_ref[level]))
         grad_rounded = narrow(state_grad)
         qo_ref[:, columns] = narrow(query_total)
         ko_ref[:, columns] = narrow(
@@ -330,6 +336,16 @@
         vo_ref[:, columns] = narrow(
             vl_ref[:, columns] + product(k_ref[:, columns], grad_rounded, 1, 0)
         )
+        for place, (source, target) in enumerate(
+            ((qo_ref, qo_hbm), (ko_ref, ko_hbm), (vo_ref, vo_hbm))
+        ):
+            move = pltpu.make_async_copy(
+                source.at[:, columns], target.at[:, columns], sent.at[place, head]
+            )
+            move.start()
+            moves.append(move)
+    for move in moves:
+        move.wait()
 
 
 def per_device(query_rows, key_rows, value_rows, out_grad, gate_class, gate_table):
@@ -369,7 +385,7 @@
     def cells(*lead):
         return jax.ShapeDtypeStruct(lead + cell, jnp.bfloat16)
 
-    def call(kernel, in_specs, outs, operands, flops=0, scratch=(), grant=VMEM_BYTES, carry=()):
+    def call(kernel, in_specs, outs, operands, flops=0, scratch=(), grant=VMEM_BYTES, carry=(), out_space=vmem):
         moved = sum(operand.size * operand.dtype.itemsize for operand in operands)
         outs = tuple(outs) if isinstance(outs, (tuple, list)) else (outs,)
         count, taken = len(outs), len(operands)
@@ -384,7 +400,7 @@
             kernel,
             out_shape=outs + tuple(jax.ShapeDtypeStruct(item.shape, item.dtype) for item in carry),
             in_specs=in_specs + [anywhere] * len(carry),
-            out_specs=(vmem,) * count + (anywhere,) * len(carry),
+            out_specs=(out_space,) * count + (anywhere,) * len(carry),
             input_output_aliases={taken + place: count + place for place in range(len(carry))},
             scratch_shapes=scratch,
             compiler_params=pltpu.CompilerParams(vmem_limit_bytes=grant),
@@ -442,11 +458,12 @@
         carry=(zero,),
     )
     big = jax.ShapeDtypeStruct((row_count, width), jnp.float32)
-    query_local, key_local, value_local = call(
-        functools.partial(local_kernel, block_depth, head_size),
-        [vmem] * 6 + [anywhere],
-        (big, big, big),
-        (class_lanes, table, query_rows, key_rows, value_rows, out_grad, own_share),
+    gate_shape = jax.ShapeDtypeStruct((row_count, total * head_count), jnp.float32)
+    query_local, key_local, value_local, gate_columns = call(
+        functools.partial(local_kernel, block_depth, head_size, total),
+        [smem] + [vmem] * 6 + [anywhere],
+        (big, big, big, gate_shape),
+        (flag_bits, class_lanes, table, query_rows, key_rows, value_rows, out_grad, own_share),
         flops=10 * row_count * width * row_count,
     )
 
@@ -516,13 +533,12 @@
 
     small = jax.ShapeDtypeStruct((row_count, width), jnp.bfloat16)
     return call(
-        functools.partial(final_kernel, offset, head_size, total, inner_bits),
-        [smem] + [vmem] * 18,
+        functools.partial(final_kernel, head_count, head_size, total, inner_bits),
+        [smem] + [vmem] * 17,
         (small, small, small),
         (
             flag_bits,
-            class_lanes,
-            table,
+            gate_columns,
             key_rows,
             value_rows,
             out_grad,
@@ -538,7 +554,14 @@
             split_other,
         ),
         flops=(2 * total + 4) * row_count * width * head_size,
-        scratch=[pltpu.VMEM((total, head_count) + cell, jnp.bfloat16)],
+        scratch=[
+            pltpu.VMEM((total, head_count) + cell, jnp.bfloat16),
+            block,
+            block,
+            block,
+            pltpu.SemaphoreType.DMA((3, head_count)),
+        ],
+        out_space=hbm,
     )
 
 

time: 47.2 us -> 48.3 us (1.023)
  starting transfers between devices: 23.4 us -> 25 us
  waiting for transfers between devices: 13.5 us -> 12.6 us
  Pallas kernels: 9.12 us -> 9.64 us
    ppermute x14, starting transfers between devices: 20.4 us -> 22.4 us  [swap(): return lax.ppermute(block, 'gy', [(i, i ^ mask) for i in range(inner_size)])]
    ppermute x14, waiting for transfers between devices: 11.3 us -> 10.4 us  [swap(): return lax.ppermute(block, 'gy', [(i, i ^ mask) for i in range(inner_size)])]
    pallas_call x11, Pallas kernels: 9.12 us -> 9.64 us  [call(): pl.pallas_call(kernel, out_shape=outs + tuple((jax.ShapeDtypeStruct(item....]
  transfers between devices with their start and end apart: 18 -> 18, of which waited for: 7 -> 8; matrix products, arithmetic and copies ran while one was open for 0% -> 0% of each run, Pallas kernels for 9% -> 10%
where the time goes in v7:
time: 48.3 us; the launch traced here: 48.2 us
  starting transfers between devices  25 us (52%)
  waiting for transfers between devices  12.6 us (26%)
  Pallas kernels  9.64 us (20%)
  between operations  0.82 us (2%)
    ppermute x14, starting transfers between devices, swap(): return lax.ppermute(block, 'gy', [(i, i ^ mask) for i in range(inner_size)])  22.4 us
    ppermute x14, waiting for transfers between devices, swap(): return lax.ppermute(block, 'gy', [(i, i ^ mask) for i in range(inner_size)])  10.4 us
    pallas_call x11, Pallas kernels, call(): pl.pallas_call(kernel, out_shape=outs + tuple((jax.ShapeDtypeStruct(item....  9.64 us
    ppermute x1, starting transfers between devices, swap(): lax.ppermute(block, ('gx', 'gy'), [(i, i ^ mask) for i in range(device_co...  1.49 us
    ppermute x3, waiting for transfers between devices, swap(): return lax.ppermute(block, 'gx', [(i, i ^ mask) for i in range(size)])  1.32 us
    ppermute x3, starting transfers between devices, swap(): return lax.ppermute(block, 'gx', [(i, i ^ mask) for i in range(size)])  1.09 us
  transfers between devices with their start and end apart: 18, of which 8 were waited for; matrix products, arithmetic and copies ran while one was open for 0% of the time, Pallas kernels for 10%

profile of v7, /device:TPU:0, one launch (start us, length us, event | category | flops | bytes accessed | tf_op | source)
XLA Modules:
  0.0 48.2 jit_solution(14715880489862890697)
XLA Ops:
  0.7 2.3 %shard_map.85 = (bf16[12,128,128]{2,1,0:T(8,128)(2,1)S(1)}, bf16[4,128,128]{2,1,0:T(8,128)(2,1)S(1)}) custom-call(s32[5]{0:T(128)S(1)} %shift-right-arithmetic_and_fusion.flag_ref.refs_0_, s32[1,128]{1,0:T(1,128)} %bitcast.5, f32[20,8,32]{2,1,0:T(8,128)} %bitcast.2, bf16[128,1024]{1,0:T(8,128)(2,1)} %q_ref.3, bf16[128,1024]{1,0:T(8,128)(2,1)} %k_ref.5, ...), custom_call_target="tpu_custom_call" | custom-call | flops 67108864 | bytes 1069588 | tf_op jit(solution)/shard_map/pallas_call | solution.py:399
  3.0 0.5 %collective-permute-start = (bf16[12,128,128]{2,1,0:T(8,128)(2,1)S(1)}, bf16[12,128,128]{2,1,0:T(8,128)(2,1)S(1)}, u32[]{:S(2)}, u32[]{:S(2)}) collective-permute-start(bf16[12,128,128]{2,1,0:T(8,128)(2,1)S(1)} %get-tuple-element.20), channel_id=1, source_target_pairs={{0,8},{8,0},{16,24},{24,16},{1,9},{9,1},{17,25},{25,17},{2,10},{10... | collective-permute-start | bytes 1179656 | tf_op jit(solution)/shard_map/ppermute | solution.py:374
  3.5 0.1 copy-done.5
  3.6 1.2 %shard_map.86 = (bf16[4,128,128]{2,1,0:T(8,128)(2,1)S(1)}, bf16[4,128,128]{2,1,0:T(8,128)(2,1)S(1)}, bf16[8,128,128]{2,1,0:T(8,128)(2,1)S(1)}, bf16[8,128,128]{2,1,0:T(8,128)(2,1)S(1)}) custom-call(s32[5]{0:T(128)S(1)} %shift-right-arithmetic_and_fusion.flag_ref.refs_0_, s32[1,128]{1,0:T(1,128)S(1)} %bitcast.6, f32[20,8,32]{2,1,0:T(8,128)S(1)} %bitcast.3, ...), custom_call_target="tpu_custom_call" | custom-call | flops 100663296 | bytes 1200660 | tf_op jit(solution)/shard_map/pallas_call | solution.py:399
  4.8 3.0 %collective-permute-start.4 = (bf16[4,128,128]{2,1,0:T(8,128)(2,1)S(1)}, bf16[4,128,128]{2,1,0:T(8,128)(2,1)S(1)}, u32[]{:S(2)}, u32[]{:S(2)}) collective-permute-start(bf16[4,128,128]{2,1,0:T(8,128)(2,1)S(1)} %get-tuple-element.31), channel_id=1, source_target_pairs={{0,1},{1,0},{2,3},{3,2},{4,5},{5,4},{6,7},{7,6},{8,9},{9,8},{10,11... | collective-permute-start | bytes 393224 | tf_op jit(solution)/shard_map/ppermute | solution.py:370
  7.8 0.1 collective-permute-start.2
  7.9 0.6 %shard_map.87 = (bf16[3,128,128]{2,1,0:T(8,128)(2,1)S(1)}, bf16[3,128,128]{2,1,0:T(8,128)(2,1)S(1)}, bf16[3,128,128]{2,1,0:T(8,128)(2,1)S(1)}, bf16[3,128,128]{2,1,0:T(8,128)(2,1)S(1)}, bf16[8,128,128]{2,1,0:T(8,128)(2,1)S(1)}) custom-call(s32[5]{0:T(128)S(1)} %shift-right-arithmetic_and_fusion.flag_ref.refs_0_, ...), custom_call_target="tpu_custom_call", output_to_operand_aliasing={{4}: (4, {})} | custom-call | bytes 655380 | tf_op jit(solution)/shard_map/pallas_call | solution.py:399
  8.5 4.1 %collective-permute-start.8 = (bf16[3,128,128]{2,1,0:T(8,128)(2,1)S(1)}, bf16[3,128,128]{2,1,0:T(8,128)(2,1)S(1)}, u32[]{:S(2)}, u32[]{:S(2)}) collective-permute-start(bf16[3,128,128]{2,1,0:T(8,128)(2,1)S(1)} %get-tuple-element.32), channel_id=1, source_target_pairs={{0,6},{1,7},{2,4},{3,5},{4,2},{5,3},{6,0},{7,1},{8,14},{9,15},{10,... | collective-permute-start | bytes 294920 | tf_op jit(solution)/shard_map/ppermute | solution.py:370
  12.6 1.5 %collective-permute-start.1 = (bf16[8,128,128]{2,1,0:T(8,128)(2,1)S(1)}, bf16[8,128,128]{2,1,0:T(8,128)(2,1)S(1)}, u32[]{:S(2)}, u32[]{:S(2)}) collective-permute-start(bf16[8,128,128]{2,1,0:T(8,128)(2,1)S(1)} %get-tuple-element.29), channel_id=1, source_target_pairs={{0,1},{1,0},{2,3},{3,2},{4,5},{5,4},{6,7},{7,6},{8,9},{9,8},{10,11... | collective-permute-start | bytes 786440 | tf_op jit(solution)/shard_map/ppermute | solution.py:370
  14.1 2.7 %shard_map.88 = (f32[128,1024]{1,0:T(8,128)S(1)}, f32[128,1024]{1,0:T(8,128)S(1)}, f32[128,1024]{1,0:T(8,128)S(1)}, f32[128,40]{1,0:T(8,128)S(1)}) custom-call(s32[5]{0:T(128)S(1)} %shift-right-arithmetic_and_fusion.flag_ref.refs_0_, s32[1,128]{1,0:T(1,128)S(1)} %bitcast.7, f32[20,8,32]{2,1,0:T(8,128)S(1)} %bitcast.4, bf16[128,1024]{1,0:T(8,128)(2,1)S(1)} %copy-done.3, ...), custom_call_target="tpu_custom_call" | custom-call | flops 167772160 | bytes 1167892 | tf_op jit(solution)/shard_map/pallas_call | solution.py:399
  16.8 0.8 %collective-permute-start.10 = (bf16[3,128,128]{2,1,0:T(8,128)(2,1)S(1)}, bf16[3,128,128]{2,1,0:T(8,128)(2,1)S(1)}, u32[]{:S(2)}, u32[]{:S(2)}) collective-permute-start(bf16[3,128,128]{2,1,0:T(8,128)(2,1)S(1)} %get-tuple-element.34), channel_id=1, source_target_pairs={{0,2},{1,3},{2,0},{3,1},{4,6},{5,7},{6,4},{7,5},{8,10},{9,11},{10,... | collective-permute-start | bytes 294920 | tf_op jit(solution)/shard_map/ppermute | solution.py:370
  17.7 2.0 %collective-permute-start.5 = (bf16[4,128,128]{2,1,0:T(8,128)(2,1)S(1)}, bf16[4,128,128]{2,1,0:T(8,128)(2,1)S(1)}, u32[]{:S(2)}, u32[]{:S(2)}) collective-permute-start(bf16[4,128,128]{2,1,0:T(8,128)(2,1)S(1)} %shard_map.90.own_ref.after_ref), channel_id=1, source_target_pairs={{0,2},{1,3},{2,0},{3,1},{4,6},{5,7},{6,4},{7,5},{8,10},{9,11},{10,... | collective-permute-start | bytes 393224 | tf_op jit(solution)/shard_map/ppermute | solution.py:370
  19.7 0.9 %collective-permute-done.9.refs_1_ = bf16[3,128,128]{2,1,0:T(8,128)(2,1)S(1)} collective-permute-done((bf16[3,128,128]{2,1,0:T(8,128)(2,1)S(1)}, bf16[3,128,128]{2,1,0:T(8,128)(2,1)S(1)}, u32[]{:S(2)}, u32[]{:S(2)}) %collective-permute-start.9) | collective-permute-done | bytes 98336 | tf_op jit(solution)/shard_map/ppermute | solution.py:370
  20.6 2.2 %collective-permute-done.10.refs_2_ = bf16[3,128,128]{2,1,0:T(8,128)(2,1)S(1)} collective-permute-done((bf16[3,128,128]{2,1,0:T(8,128)(2,1)S(1)}, bf16[3,128,128]{2,1,0:T(8,128)(2,1)S(1)}, u32[]{:S(2)}, u32[]{:S(2)}) %collective-permute-start.10) | collective-permute-done | bytes 98336 | tf_op jit(solution)/shard_map/ppermute | solution.py:370
  22.7 0.1 shard_map.92
  22.8 1.6 %collective-permute-start.11 = (bf16[2,128,128]{2,1,0:T(8,128)(2,1)S(1)}, bf16[2,128,128]{2,1,0:T(8,128)(2,1)S(1)}, u32[]{:S(2)}, u32[]{:S(2)}) collective-permute-start(bf16[2,128,128]{2,1,0:T(8,128)(2,1)S(1)} %get-tuple-element.35.below_ref), channel_id=1, source_target_pairs={{0,1},{1,0},{2,3},{3,2},{4,5},{5,4},{6,7},{7,6},{8,9},{9,8},{10,11... | collective-permute-start | bytes 196616 | tf_op jit(solution)/shard_map/ppermute | solution.py:370
  24.4 1.5 %collective-permute-start.13 = (bf16[1,128,128]{2,1,0:T(8,128)(2,1)S(1)}, bf16[1,128,128]{2,1,0:T(8,128)(2,1)S(1)}, u32[]{:S(2)}, u32[]{:S(2)}) collective-permute-start(bf16[1,128,128]{2,1,0:T(8,128)(2,1)S(1)} %get-tuple-element.36), channel_id=1, source_target_pairs={{0,17},{1,16},{2,19},{3,18},{4,21},{5,20},{6,23},{7,22},{8,25},{9,... | collective-permute-start | bytes 98312 | tf_op jit(solution)/shard_map/ppermute | solution.py:375
  25.8 0.5 %collective-permute-start.12 = (bf16[1,128,128]{2,1,0:T(8,128)(2,1)S(1)}, bf16[1,128,128]{2,1,0:T(8,128)(2,1)S(1)}, u32[]{:S(2)}, u32[]{:S(2)}) collective-permute-start(bf16[1,128,128]{2,1,0:T(8,128)(2,1)S(1)} %get-tuple-element.36), channel_id=1, source_target_pairs={{0,16},{8,24},{16,0},{24,8},{1,17},{9,25},{17,1},{25,9},{2,18},{10... | collective-permute-start | bytes 98312 | tf_op jit(solution)/shard_map/ppermute | solution.py:374
  26.4 1.8 %collective-permute-start.6 = (bf16[4,128,128]{2,1,0:T(8,128)(2,1)S(1)}, bf16[4,128,128]{2,1,0:T(8,128)(2,1)S(1)}, u32[]{:S(2)}, u32[]{:S(2)}) collective-permute-start(bf16[4,128,128]{2,1,0:T(8,128)(2,1)S(1)} %shard_map.91.refs_0_), channel_id=1, source_target_pairs={{0,4},{1,5},{2,6},{3,7},{4,0},{5,1},{6,2},{7,3},{8,12},{9,13},{10,... | collective-permute-start | bytes 393224 | tf_op jit(solution)/shard_map/ppermute | solution.py:370
  28.2 0.1 shard_map.89.refs_1_
  28.3 0.9 %collective-permute-done.13.far_top_ref = bf16[1,128,128]{2,1,0:T(8,128)(2,1)S(1)} collective-permute-done((bf16[1,128,128]{2,1,0:T(8,128)(2,1)S(1)}, bf16[1,128,128]{2,1,0:T(8,128)(2,1)S(1)}, u32[]{:S(2)}, u32[]{:S(2)}) %collective-permute-start.13) | collective-permute-done | bytes 32800 | tf_op jit(solution)/shard_map/ppermute | solution.py:375
  29.2 1.0 %collective-permute-start.3 = (bf16[8,128,128]{2,1,0:T(8,128)(2,1)S(1)}, bf16[8,128,128]{2,1,0:T(8,128)(2,1)S(1)}, u32[]{:S(2)}, u32[]{:S(2)}) collective-permute-start(bf16[8,128,128]{2,1,0:T(8,128)(2,1)S(1)} %shard_map.89.refs_1_), channel_id=1, source_target_pairs={{0,2},{1,3},{2,0},{3,1},{4,6},{5,7},{6,4},{7,5},{8,10},{9,11},{10,... | collective-permute-start | bytes 786440 | tf_op jit(solution)/shard_map/ppermute | solution.py:370
  30.2 2.6 %collective-permute-start.16 = (bf16[3,128,128]{2,1,0:T(8,128)(2,1)S(1)}, bf16[3,128,128]{2,1,0:T(8,128)(2,1)S(1)}, u32[]{:S(2)}, u32[]{:S(2)}) collective-permute-start(bf16[3,128,128]{2,1,0:T(8,128)(2,1)S(1)} %shard_map.93.piece0_ref), channel_id=1, source_target_pairs={{0,6},{1,7},{2,4},{3,5},{4,2},{5,3},{6,0},{7,1},{8,14},{9,15},{10,... | collective-permute-start | bytes 294920 | tf_op jit(solution)/shard_map/ppermute | solution.py:370
  32.9 1.8 %collective-permute-start.14 = (bf16[3,128,128]{2,1,0:T(8,128)(2,1)S(1)}, bf16[3,128,128]{2,1,0:T(8,128)(2,1)S(1)}, u32[]{:S(2)}, u32[]{:S(2)}) collective-permute-start(bf16[3,128,128]{2,1,0:T(8,128)(2,1)S(1)} %shard_map.93.piece0_ref), channel_id=1, source_target_pairs={{0,2},{1,3},{2,0},{3,1},{4,6},{5,7},{6,4},{7,5},{8,10},{9,11},{10,... | collective-permute-start | bytes 294920 | tf_op jit(solution)/shard_map/ppermute | solution.py:370
  34.7 0.5 %collective-permute-done.6.after_ref.two_own_ref = bf16[4,128,128]{2,1,0:T(8,128)(2,1)S(1)} collective-permute-done((bf16[4,128,128]{2,1,0:T(8,128)(2,1)S(1)}, bf16[4,128,128]{2,1,0:T(8,128)(2,1)S(1)}, u32[]{:S(2)}, u32[]{:S(2)}) %collective-permute-start.6) | collective-permute-done | bytes 131104 | tf_op jit(solution)/shard_map/ppermute | solution.py:370
  35.2 2.1 %collective-permute-start.7 = (bf16[4,128,128]{2,1,0:T(8,128)(2,1)S(1)}, bf16[4,128,128]{2,1,0:T(8,128)(2,1)S(1)}, u32[]{:S(2)}, u32[]{:S(2)}) collective-permute-start(bf16[4,128,128]{2,1,0:T(8,128)(2,1)S(1)} %collective-permute-done.6.after_ref.two_own_ref), channel_id=1, source_target_pairs={{0,1},{1,0},{2,3},{3,2},{4,5},{5,4},{6,7},{7,6},{8,9},{9,8},{10,11... | collective-permute-start | bytes 393224 | tf_op jit(solution)/shard_map/ppermute | solution.py:370
  37.3 4.4 %collective-permute-done.16.piece3_ref = bf16[3,128,128]{2,1,0:T(8,128)(2,1)S(1)} collective-permute-done((bf16[3,128,128]{2,1,0:T(8,128)(2,1)S(1)}, bf16[3,128,128]{2,1,0:T(8,128)(2,1)S(1)}, u32[]{:S(2)}, u32[]{:S(2)}) %collective-permute-start.16) | collective-permute-done | bytes 98336 | tf_op jit(solution)/shard_map/ppermute | solution.py:370
  41.6 1.5 %collective-permute-done.15.piece2_ref = bf16[3,128,128]{2,1,0:T(8,128)(2,1)S(1)} collective-permute-done((bf16[3,128,128]{2,1,0:T(8,128)(2,1)S(1)}, bf16[3,128,128]{2,1,0:T(8,128)(2,1)S(1)}, u32[]{:S(2)}, u32[]{:S(2)}) %collective-permute-start.15) | collective-permute-done | bytes 98336 | tf_op jit(solution)/shard_map/ppermute | solution.py:370
  43.1 0.9 %collective-permute-done.14.piece1_ref = bf16[3,128,128]{2,1,0:T(8,128)(2,1)S(1)} collective-permute-done((bf16[3,128,128]{2,1,0:T(8,128)(2,1)S(1)}, bf16[3,128,128]{2,1,0:T(8,128)(2,1)S(1)}, u32[]{:S(2)}, u32[]{:S(2)}) %collective-permute-start.14) | collective-permute-done | bytes 98336 | tf_op jit(solution)/shard_map/ppermute | solution.py:370
  44.1 0.1 collective-permute-start.17
  44.2 1.3 %collective-permute-done.17.split_other_ref = bf16[1,4,128,128]{3,2,1,0:T(8,128)(2,1)S(1)} collective-permute-done((bf16[1,4,128,128]{3,2,1,0:T(8,128)(2,1)S(1)}, bf16[1,4,128,128]{3,2,1,0:T(8,128)(2,1)S(1)}, u32[]{:S(2)}, u32[]{:S(2)}) %collective-permute-start.17) | collective-permute-done | bytes 131104 | tf_op jit(solution)/shard_map/ppermute | solution.py:374
  45.5 2.7 %shard_map.95 = (bf16[128,1024]{1,0:T(8,128)(2,1)}, bf16[128,1024]{1,0:T(8,128)(2,1)}, bf16[128,1024]{1,0:T(8,128)(2,1)}) custom-call(s32[5]{0:T(128)S(1)} %shift-right-arithmetic_and_fusion.flag_ref.refs_0_, f32[128,40]{1,0:T(8,128)S(1)} %get-tuple-element.25.gate_ref, bf16[128,1024]{1,0:T(8,128)(2,1)S(1)} %copy-done, bf16[128,1024]{1,0:T(8,128)(2,1)S(1)} %copy-done.1, ...), custom_call_target="tpu_custom_call" | custom-call | flops 234881024 | bytes 3821588 | tf_op jit(solution)/shard_map/pallas_call | solution.py:399
  (28 shorter events, 0.2 us)
Async XLA Ops:
  0.6 2.9 %copy-start = (bf16[128,1024]{1,0:T(8,128)(2,1)S(1)}, bf16[128,1024]{1,0:T(8,128)(2,1)}, u32[]{:S(2)}) copy-start(bf16[128,1024]{1,0:T(8,128)(2,1)} %k_ref.5) | copy-start | bytes 786436
  0.7 2.9 %copy-start.1 = (bf16[128,1024]{1,0:T(8,128)(2,1)S(1)}, bf16[128,1024]{1,0:T(8,128)(2,1)}, u32[]{:S(2)}) copy-start(bf16[128,1024]{1,0:T(8,128)(2,1)} %v_ref.5) | copy-start | bytes 786436
  0.7 2.9 %copy-start.2 = (bf16[128,1024]{1,0:T(8,128)(2,1)S(1)}, bf16[128,1024]{1,0:T(8,128)(2,1)}, u32[]{:S(2)}) copy-start(bf16[128,1024]{1,0:T(8,128)(2,1)} %g_ref.5) | copy-start | bytes 786436
  0.7 2.8 %copy-start.3 = (bf16[128,1024]{1,0:T(8,128)(2,1)S(1)}, bf16[128,1024]{1,0:T(8,128)(2,1)}, u32[]{:S(2)}) copy-start(bf16[128,1024]{1,0:T(8,128)(2,1)} %q_ref.3) | copy-start | bytes 786436
  0.7 2.8 %copy-start.4 = (f32[32,20,8]{0,2,1:T(8,128)S(1)}, f32[32,20,8]{0,2,1:T(8,128)}, u32[]{:S(2)}) copy-start(f32[32,20,8]{0,2,1:T(8,128)} %param.11) | copy-start | bytes 61444
  3.0 0.7 %copy-start.5 = (s32[128]{0:T(128)S(1)}, s32[128]{0:T(128)}, u32[]{:S(2)}) copy-start(s32[128]{0:T(128)} %param.10) | copy-start | bytes 1540
  3.0 4.9 %collective-permute-start = (bf16[12,128,128]{2,1,0:T(8,128)(2,1)S(1)}, bf16[12,128,128]{2,1,0:T(8,128)(2,1)S(1)}, u32[]{:S(2)}, u32[]{:S(2)}) collective-permute-start(bf16[12,128,128]{2,1,0:T(8,128)(2,1)S(1)} %get-tuple-element.20), channel_id=1, source_target_pairs={{0,8},{8,0},{16,24},{24,16},{1,9},{9,1},{17,25},{25,17},{2,10},{10... | collective-permute-start | bytes 1179656 | tf_op jit(solution)/shard_map/ppermute | solution.py:374
  4.8 12.0 %collective-permute-start.4 = (bf16[4,128,128]{2,1,0:T(8,128)(2,1)S(1)}, bf16[4,128,128]{2,1,0:T(8,128)(2,1)S(1)}, u32[]{:S(2)}, u32[]{:S(2)}) collective-permute-start(bf16[4,128,128]{2,1,0:T(8,128)(2,1)S(1)} %get-tuple-element.31), channel_id=1, source_target_pairs={{0,1},{1,0},{2,3},{3,2},{4,5},{5,4},{6,7},{7,6},{8,9},{9,8},{10,11... | collective-permute-start | bytes 393224 | tf_op jit(solution)/shard_map/ppermute | solution.py:370
  7.8 18.6 %collective-permute-start.2 = (bf16[8,128,128]{2,1,0:T(8,128)(2,1)S(1)}, bf16[8,128,128]{2,1,0:T(8,128)(2,1)S(1)}, u32[]{:S(2)}, u32[]{:S(2)}) collective-permute-start(bf16[8,128,128]{2,1,0:T(8,128)(2,1)S(1)} %get-tuple-element.30.own_ref), channel_id=1, source_target_pairs={{0,1},{1,0},{2,3},{3,2},{4,5},{5,4},{6,7},{7,6},{8,9},{9,8},{10,11... | collective-permute-start | bytes 786440 | tf_op jit(solution)/shard_map/ppermute | solution.py:370
  8.5 9.2 %collective-permute-start.8 = (bf16[3,128,128]{2,1,0:T(8,128)(2,1)S(1)}, bf16[3,128,128]{2,1,0:T(8,128)(2,1)S(1)}, u32[]{:S(2)}, u32[]{:S(2)}) collective-permute-start(bf16[3,128,128]{2,1,0:T(8,128)(2,1)S(1)} %get-tuple-element.32), channel_id=1, source_target_pairs={{0,6},{1,7},{2,4},{3,5},{4,2},{5,3},{6,0},{7,1},{8,14},{9,15},{10,... | collective-permute-start | bytes 294920 | tf_op jit(solution)/shard_map/ppermute | solution.py:370
  12.6 17.5 %collective-permute-start.1 = (bf16[8,128,128]{2,1,0:T(8,128)(2,1)S(1)}, bf16[8,128,128]{2,1,0:T(8,128)(2,1)S(1)}, u32[]{:S(2)}, u32[]{:S(2)}) collective-permute-start(bf16[8,128,128]{2,1,0:T(8,128)(2,1)S(1)} %get-tuple-element.29), channel_id=1, source_target_pairs={{0,1},{1,0},{2,3},{3,2},{4,5},{5,4},{6,7},{7,6},{8,9},{9,8},{10,11... | collective-permute-start | bytes 786440 | tf_op jit(solution)/shard_map/ppermute | solution.py:370
  14.1 6.5 %collective-permute-start.9 = (bf16[3,128,128]{2,1,0:T(8,128)(2,1)S(1)}, bf16[3,128,128]{2,1,0:T(8,128)(2,1)S(1)}, u32[]{:S(2)}, u32[]{:S(2)}) collective-permute-start(bf16[3,128,128]{2,1,0:T(8,128)(2,1)S(1)} %get-tuple-element.33), channel_id=1, source_target_pairs={{0,4},{1,5},{2,6},{3,7},{4,0},{5,1},{6,2},{7,3},{8,12},{9,13},{10,... | collective-permute-start | bytes 294920 | tf_op jit(solution)/shard_map/ppermute | solution.py:370
  16.8 5.9 %collective-permute-start.10 = (bf16[3,128,128]{2,1,0:T(8,128)(2,1)S(1)}, bf16[3,128,128]{2,1,0:T(8,128)(2,1)S(1)}, u32[]{:S(2)}, u32[]{:S(2)}) collective-permute-start(bf16[3,128,128]{2,1,0:T(8,128)(2,1)S(1)} %get-tuple-element.34), channel_id=1, source_target_pairs={{0,2},{1,3},{2,0},{3,1},{4,6},{5,7},{6,4},{7,5},{8,10},{9,11},{10,... | collective-permute-start | bytes 294920 | tf_op jit(solution)/shard_map/ppermute | solution.py:370
  17.7 8.1 %collective-permute-start.5 = (bf16[4,128,128]{2,1,0:T(8,128)(2,1)S(1)}, bf16[4,128,128]{2,1,0:T(8,128)(2,1)S(1)}, u32[]{:S(2)}, u32[]{:S(2)}) collective-permute-start(bf16[4,128,128]{2,1,0:T(8,128)(2,1)S(1)} %shard_map.90.own_ref.after_ref), channel_id=1, source_target_pairs={{0,2},{1,3},{2,0},{3,1},{4,6},{5,7},{6,4},{7,5},{8,10},{9,11},{10,... | collective-permute-start | bytes 393224 | tf_op jit(solution)/shard_map/ppermute | solution.py:370
  22.8 7.4 %collective-permute-start.11 = (bf16[2,128,128]{2,1,0:T(8,128)(2,1)S(1)}, bf16[2,128,128]{2,1,0:T(8,128)(2,1)S(1)}, u32[]{:S(2)}, u32[]{:S(2)}) collective-permute-start(bf16[2,128,128]{2,1,0:T(8,128)(2,1)S(1)} %get-tuple-element.35.below_ref), channel_id=1, source_target_pairs={{0,1},{1,0},{2,3},{3,2},{4,5},{5,4},{6,7},{7,6},{8,9},{9,8},{10,11... | collective-permute-start | bytes 196616 | tf_op jit(solution)/shard_map/ppermute | solution.py:370
  24.4 4.8 %collective-permute-start.13 = (bf16[1,128,128]{2,1,0:T(8,128)(2,1)S(1)}, bf16[1,128,128]{2,1,0:T(8,128)(2,1)S(1)}, u32[]{:S(2)}, u32[]{:S(2)}) collective-permute-start(bf16[1,128,128]{2,1,0:T(8,128)(2,1)S(1)} %get-tuple-element.36), channel_id=1, source_target_pairs={{0,17},{1,16},{2,19},{3,18},{4,21},{5,20},{6,23},{7,22},{8,25},{9,... | collective-permute-start | bytes 98312 | tf_op jit(solution)/shard_map/ppermute | solution.py:375
  25.8 4.3 %collective-permute-start.12 = (bf16[1,128,128]{2,1,0:T(8,128)(2,1)S(1)}, bf16[1,128,128]{2,1,0:T(8,128)(2,1)S(1)}, u32[]{:S(2)}, u32[]{:S(2)}) collective-permute-start(bf16[1,128,128]{2,1,0:T(8,128)(2,1)S(1)} %get-tuple-element.36), channel_id=1, source_target_pairs={{0,16},{8,24},{16,0},{24,8},{1,17},{9,25},{17,1},{25,9},{2,18},{10... | collective-permute-start | bytes 98312 | tf_op jit(solution)/shard_map/ppermute | solution.py:374
  26.4 8.8 %collective-permute-start.6 = (bf16[4,128,128]{2,1,0:T(8,128)(2,1)S(1)}, bf16[4,128,128]{2,1,0:T(8,128)(2,1)S(1)}, u32[]{:S(2)}, u32[]{:S(2)}) collective-permute-start(bf16[4,128,128]{2,1,0:T(8,128)(2,1)S(1)} %shard_map.91.refs_0_), channel_id=1, source_target_pairs={{0,4},{1,5},{2,6},{3,7},{4,0},{5,1},{6,2},{7,3},{8,12},{9,13},{10,... | collective-permute-start | bytes 393224 | tf_op jit(solution)/shard_map/ppermute | solution.py:370
  29.2 15.0 %collective-permute-start.3 = (bf16[8,128,128]{2,1,0:T(8,128)(2,1)S(1)}, bf16[8,128,128]{2,1,0:T(8,128)(2,1)S(1)}, u32[]{:S(2)}, u32[]{:S(2)}) collective-permute-start(bf16[8,128,128]{2,1,0:T(8,128)(2,1)S(1)} %shard_map.89.refs_1_), channel_id=1, source_target_pairs={{0,2},{1,3},{2,0},{3,1},{4,6},{5,7},{6,4},{7,5},{8,10},{9,11},{10,... | collective-permute-start | bytes 786440 | tf_op jit(solution)/shard_map/ppermute | solution.py:370
  30.2 11.4 %collective-permute-start.16 = (bf16[3,128,128]{2,1,0:T(8,128)(2,1)S(1)}, bf16[3,128,128]{2,1,0:T(8,128)(2,1)S(1)}, u32[]{:S(2)}, u32[]{:S(2)}) collective-permute-start(bf16[3,128,128]{2,1,0:T(8,128)(2,1)S(1)} %shard_map.93.piece0_ref), channel_id=1, source_target_pairs={{0,6},{1,7},{2,4},{3,5},{4,2},{5,3},{6,0},{7,1},{8,14},{9,15},{10,... | collective-permute-start | bytes 294920 | tf_op jit(solution)/shard_map/ppermute | solution.py:370
  32.8 10.3 %collective-permute-start.15 = (bf16[3,128,128]{2,1,0:T(8,128)(2,1)S(1)}, bf16[3,128,128]{2,1,0:T(8,128)(2,1)S(1)}, u32[]{:S(2)}, u32[]{:S(2)}) collective-permute-start(bf16[3,128,128]{2,1,0:T(8,128)(2,1)S(1)} %shard_map.93.piece0_ref), channel_id=1, source_target_pairs={{0,4},{1,5},{2,6},{3,7},{4,0},{5,1},{6,2},{7,3},{8,12},{9,13},{10,... | collective-permute-start | bytes 294920 | tf_op jit(solution)/shard_map/ppermute | solution.py:370
  32.9 11.2 %collective-permute-start.14 = (bf16[3,128,128]{2,1,0:T(8,128)(2,1)S(1)}, bf16[3,128,128]{2,1,0:T(8,128)(2,1)S(1)}, u32[]{:S(2)}, u32[]{:S(2)}) collective-permute-start(bf16[3,128,128]{2,1,0:T(8,128)(2,1)S(1)} %shard_map.93.piece0_ref), channel_id=1, source_target_pairs={{0,2},{1,3},{2,0},{3,1},{4,6},{5,7},{6,4},{7,5},{8,10},{9,11},{10,... | collective-permute-start | bytes 294920 | tf_op jit(solution)/shard_map/ppermute | solution.py:370
  35.2 8.9 %collective-permute-start.7 = (bf16[4,128,128]{2,1,0:T(8,128)(2,1)S(1)}, bf16[4,128,128]{2,1,0:T(8,128)(2,1)S(1)}, u32[]{:S(2)}, u32[]{:S(2)}) collective-permute-start(bf16[4,128,128]{2,1,0:T(8,128)(2,1)S(1)} %collective-permute-done.6.after_ref.two_own_ref), channel_id=1, source_target_pairs={{0,1},{1,0},{2,3},{3,2},{4,5},{5,4},{6,7},{7,6},{8,9},{9,8},{10,11... | collective-permute-start | bytes 393224 | tf_op jit(solution)/shard_map/ppermute | solution.py:370
  44.1 1.4 %collective-permute-start.17 = (bf16[1,4,128,128]{3,2,1,0:T(8,128)(2,1)S(1)}, bf16[1,4,128,128]{3,2,1,0:T(8,128)(2,1)S(1)}, u32[]{:S(2)}, u32[]{:S(2)}) collective-permute-start(bf16[1,4,128,128]{3,2,1,0:T(8,128)(2,1)S(1)} %shard_map.94.split_own_ref), channel_id=1, source_target_pairs={{0,8},{8,0},{16,24},{24,16},{1,9},{9,1},{17,25},{25,17},{2,10},{10... | collective-permute-start | bytes 393224 | tf_op jit(solution)/shard_map/ppermute | solution.py:374

commit v8 on v6

--- a/solution.py
+++ b/solution.py
@@ -205,6 +205,10 @@
         for level in range(split_levels):
             first = cut + level * eighth
             out_ref[level, offs * eighth : (offs + 1) * eighth] = piece_ref[first : first + eighth]
+
+
+def tick_kernel(after_ref, out_ref):
+    out_ref[...] = jnp.zeros_like(out_ref)
 
 
 def two_sum_kernel(own_ref, seen_ref, after_ref, out_ref):
@@ -441,12 +445,18 @@
         (flag_bits, seen, keep, two_own, *lead),
         carry=(zero,),
     )
+    two_sum = call(
+        two_sum_kernel,
+        [vmem] * 2 + [anywhere],
+        cells(half),
+        (two_own, swap(two_other, 0), own_share),
+    )
     big = jax.ShapeDtypeStruct((row_count, width), jnp.float32)
     query_local, key_local, value_local = call(
         functools.partial(local_kernel, block_depth, head_size),
         [vmem] * 6 + [anywhere],
         (big, big, big),
-        (class_lanes, table, query_rows, key_rows, value_rows, out_grad, own_share),
+        (class_lanes, table, query_rows, key_rows, value_rows, out_grad, two_sum),
         flops=10 * row_count * width * row_count,
     )
 
@@ -483,12 +493,6 @@
                 row += size
         below = narrow(jnp.concatenate([parts[level] for level in range(NEAR, top)], axis=0))
         top_sent = narrow(parts[top])
-    two_sum = call(
-        two_sum_kernel,
-        [vmem] * 2 + [anywhere],
-        cells(half),
-        (two_own, swap(two_other, 0), query_local),
-    )
     two_sum = call(
         two_sum_kernel, [vmem] * 2 + [anywhere], cells(half), (two_sum, swap(two_sum, 1), two_sum)
     )

time: 47.2 us -> 45.7 us (0.968)
  waiting for transfers between devices: 13.5 us -> 8.28 us
  starting transfers between devices: 23.4 us -> 27.2 us
    ppermute x14, waiting for transfers between devices: 11.3 us -> 6.39 us  [swap(): return lax.ppermute(block, 'gy', [(i, i ^ mask) for i in range(inner_size)])]
    ppermute x14, starting transfers between devices: 20.4 us -> 25.1 us  [swap(): return lax.ppermute(block, 'gy', [(i, i ^ mask) for i in range(inner_size)])]
    ppermute x1, starting transfers between devices: 1.93 us -> 1.03 us  [swap(): lax.ppermute(block, ('gx', 'gy'), [(i, i ^ mask) for i in range(device_co...]
  transfers between devices with their start and end apart: 18 -> 18, of which waited for: 7 -> 5; matrix products, arithmetic and copies ran while one was open for 0% -> 0% of each run, Pallas kernels for 9% -> 9%
where the time goes in v8:
time: 45.7 us; the launch traced here: 45.5 us
  starting transfers between devices  27.2 us (60%)
  Pallas kernels  9.11 us (20%)
  waiting for transfers between devices  8.28 us (18%)
  between operations  0.82 us (2%)
    ppermute x14, starting transfers between devices, swap(): return lax.ppermute(block, 'gy', [(i, i ^ mask) for i in range(inner_size)])  25.1 us
    pallas_call x11, Pallas kernels, call(): pl.pallas_call(kernel, out_shape=outs + tuple((jax.ShapeDtypeStruct(item....  9.11 us
    ppermute x14, waiting for transfers between devices, swap(): return lax.ppermute(block, 'gy', [(i, i ^ mask) for i in range(inner_size)])  6.39 us
    ppermute x3, waiting for transfers between devices, swap(): return lax.ppermute(block, 'gx', [(i, i ^ mask) for i in range(size)])  1.32 us
    ppermute x3, starting transfers between devices, swap(): return lax.ppermute(block, 'gx', [(i, i ^ mask) for i in range(size)])  1.1 us
    ppermute x1, starting transfers between devices, swap(): lax.ppermute(block, ('gx', 'gy'), [(i, i ^ mask) for i in range(device_co...  1.03 us
  transfers between devices with their start and end apart: 18, of which 5 were waited for; matrix products, arithmetic and copies ran while one was open for 0% of the time, Pallas kernels for 9%

profile of v8, /device:TPU:0, one launch (start us, length us, event | category | flops | bytes accessed | tf_op | source)
XLA Modules:
  0.0 45.5 jit_solution(15685164479585905192)
XLA Ops:
  0.7 0.0 copy-start.1
  0.7 2.3 %shard_map.85 = (bf16[12,128,128]{2,1,0:T(8,128)(2,1)S(1)}, bf16[4,128,128]{2,1,0:T(8,128)(2,1)S(1)}) custom-call(s32[5]{0:T(128)S(1)} %shift-right-arithmetic_and_fusion.flag_ref.refs_0_, s32[1,128]{1,0:T(1,128)} %bitcast.6, f32[20,8,32]{2,1,0:T(8,128)} %bitcast.2, bf16[128,1024]{1,0:T(8,128)(2,1)} %q_ref.3, bf16[128,1024]{1,0:T(8,128)(2,1)} %k_ref.5, ...), custom_call_target="tpu_custom_call" | custom-call | flops 67108864 | bytes 1069588 | tf_op jit(solution)/shard_map/pallas_call | solution.py:387
  3.0 0.5 %collective-permute-start.1 = (bf16[12,128,128]{2,1,0:T(8,128)(2,1)S(1)}, bf16[12,128,128]{2,1,0:T(8,128)(2,1)S(1)}, u32[]{:S(2)}, u32[]{:S(2)}) collective-permute-start(bf16[12,128,128]{2,1,0:T(8,128)(2,1)S(1)} %get-tuple-element.22), channel_id=1, source_target_pairs={{0,8},{8,0},{16,24},{24,16},{1,9},{9,1},{17,25},{25,17},{2,10},{10... | collective-permute-start | bytes 1179656 | tf_op jit(solution)/shard_map/ppermute | solution.py:362
  3.5 0.1 copy-done.5
  3.6 1.2 %shard_map.86 = (bf16[4,128,128]{2,1,0:T(8,128)(2,1)S(1)}, bf16[4,128,128]{2,1,0:T(8,128)(2,1)S(1)}, bf16[8,128,128]{2,1,0:T(8,128)(2,1)S(1)}, bf16[8,128,128]{2,1,0:T(8,128)(2,1)S(1)}) custom-call(s32[5]{0:T(128)S(1)} %shift-right-arithmetic_and_fusion.flag_ref.refs_0_, s32[1,128]{1,0:T(1,128)S(1)} %bitcast.7, f32[20,8,32]{2,1,0:T(8,128)S(1)} %bitcast.3, ...), custom_call_target="tpu_custom_call" | custom-call | flops 100663296 | bytes 1200660 | tf_op jit(solution)/shard_map/pallas_call | solution.py:387
  4.8 3.0 %collective-permute-start = (bf16[4,128,128]{2,1,0:T(8,128)(2,1)S(1)}, bf16[4,128,128]{2,1,0:T(8,128)(2,1)S(1)}, u32[]{:S(2)}, u32[]{:S(2)}) collective-permute-start(bf16[4,128,128]{2,1,0:T(8,128)(2,1)S(1)} %get-tuple-element.21), channel_id=1, source_target_pairs={{0,1},{1,0},{2,3},{3,2},{4,5},{5,4},{6,7},{7,6},{8,9},{9,8},{10,11... | collective-permute-start | bytes 393224 | tf_op jit(solution)/shard_map/ppermute | solution.py:358
  7.8 0.1 collective-permute-start.3
  7.9 0.6 %shard_map.87 = (bf16[3,128,128]{2,1,0:T(8,128)(2,1)S(1)}, bf16[3,128,128]{2,1,0:T(8,128)(2,1)S(1)}, bf16[3,128,128]{2,1,0:T(8,128)(2,1)S(1)}, bf16[3,128,128]{2,1,0:T(8,128)(2,1)S(1)}, bf16[8,128,128]{2,1,0:T(8,128)(2,1)S(1)}) custom-call(s32[5]{0:T(128)S(1)} %shift-right-arithmetic_and_fusion.flag_ref.refs_0_, ...), custom_call_target="tpu_custom_call", output_to_operand_aliasing={{4}: (4, {})} | custom-call | bytes 655380 | tf_op jit(solution)/shard_map/pallas_call | solution.py:387
  8.5 4.1 %collective-permute-start.8 = (bf16[3,128,128]{2,1,0:T(8,128)(2,1)S(1)}, bf16[3,128,128]{2,1,0:T(8,128)(2,1)S(1)}, u32[]{:S(2)}, u32[]{:S(2)}) collective-permute-start(bf16[3,128,128]{2,1,0:T(8,128)(2,1)S(1)} %get-tuple-element.30), channel_id=1, source_target_pairs={{0,6},{1,7},{2,4},{3,5},{4,2},{5,3},{6,0},{7,1},{8,14},{9,15},{10,... | collective-permute-start | bytes 294920 | tf_op jit(solution)/shard_map/ppermute | solution.py:358
  12.6 1.5 %collective-permute-start.2 = (bf16[8,128,128]{2,1,0:T(8,128)(2,1)S(1)}, bf16[8,128,128]{2,1,0:T(8,128)(2,1)S(1)}, u32[]{:S(2)}, u32[]{:S(2)}) collective-permute-start(bf16[8,128,128]{2,1,0:T(8,128)(2,1)S(1)} %get-tuple-element.28), channel_id=1, source_target_pairs={{0,1},{1,0},{2,3},{3,2},{4,5},{5,4},{6,7},{7,6},{8,9},{9,8},{10,11... | collective-permute-start | bytes 786440 | tf_op jit(solution)/shard_map/ppermute | solution.py:358
  14.1 0.8 %collective-permute-start.10 = (bf16[3,128,128]{2,1,0:T(8,128)(2,1)S(1)}, bf16[3,128,128]{2,1,0:T(8,128)(2,1)S(1)}, u32[]{:S(2)}, u32[]{:S(2)}) collective-permute-start(bf16[3,128,128]{2,1,0:T(8,128)(2,1)S(1)} %get-tuple-element.32), channel_id=1, source_target_pairs={{0,2},{1,3},{2,0},{3,1},{4,6},{5,7},{6,4},{7,5},{8,10},{9,11},{10,... | collective-permute-start | bytes 294920 | tf_op jit(solution)/shard_map/ppermute | solution.py:358
  14.9 0.8 %collective-permute-done.8.refs_0_ = bf16[3,128,128]{2,1,0:T(8,128)(2,1)S(1)} collective-permute-done((bf16[3,128,128]{2,1,0:T(8,128)(2,1)S(1)}, bf16[3,128,128]{2,1,0:T(8,128)(2,1)S(1)}, u32[]{:S(2)}, u32[]{:S(2)}) %collective-permute-start.8) | collective-permute-done | bytes 98336 | tf_op jit(solution)/shard_map/ppermute | solution.py:358
  15.7 3.4 %collective-permute-start.5 = (bf16[4,128,128]{2,1,0:T(8,128)(2,1)S(1)}, bf16[4,128,128]{2,1,0:T(8,128)(2,1)S(1)}, u32[]{:S(2)}, u32[]{:S(2)}) collective-permute-start(bf16[4,128,128]{2,1,0:T(8,128)(2,1)S(1)} %shard_map.88.after_ref.own_ref), channel_id=1, source_target_pairs={{0,2},{1,3},{2,0},{3,1},{4,6},{5,7},{6,4},{7,5},{8,10},{9,11},{10,... | collective-permute-start | bytes 393224 | tf_op jit(solution)/shard_map/ppermute | solution.py:358
  19.2 2.0 %shard_map.89 = (f32[128,1024]{1,0:T(8,128)S(1)}, f32[128,1024]{1,0:T(8,128)S(1)}, f32[128,1024]{1,0:T(8,128)S(1)}) custom-call(s32[1,128]{1,0:T(1,128)S(1)} %bitcast.8, f32[20,8,32]{2,1,0:T(8,128)S(1)} %bitcast.4, bf16[128,1024]{1,0:T(8,128)(2,1)S(1)} %copy-done.3, bf16[128,1024]{1,0:T(8,128)(2,1)S(1)} %copy-done, bf16[128,1024]{1,0:T(8,128)(2,1)S(1)} %copy-done.1, ...), custom_call_target="tpu_custom_call" | custom-call | flops 167772160 | bytes 1200640 | tf_op jit(solution)/shard_map/pallas_call | solution.py:387
  21.2 0.1 shard_map.92
  21.3 2.1 %collective-permute-start.11 = (bf16[2,128,128]{2,1,0:T(8,128)(2,1)S(1)}, bf16[2,128,128]{2,1,0:T(8,128)(2,1)S(1)}, u32[]{:S(2)}, u32[]{:S(2)}) collective-permute-start(bf16[2,128,128]{2,1,0:T(8,128)(2,1)S(1)} %get-tuple-element.33.below_ref), channel_id=1, source_target_pairs={{0,1},{1,0},{2,3},{3,2},{4,5},{5,4},{6,7},{7,6},{8,9},{9,8},{10,11... | collective-permute-start | bytes 196616 | tf_op jit(solution)/shard_map/ppermute | solution.py:358
  23.4 1.0 %collective-permute-start.13 = (bf16[1,128,128]{2,1,0:T(8,128)(2,1)S(1)}, bf16[1,128,128]{2,1,0:T(8,128)(2,1)S(1)}, u32[]{:S(2)}, u32[]{:S(2)}) collective-permute-start(bf16[1,128,128]{2,1,0:T(8,128)(2,1)S(1)} %get-tuple-element.34), channel_id=1, source_target_pairs={{0,17},{1,16},{2,19},{3,18},{4,21},{5,20},{6,23},{7,22},{8,25},{9,... | collective-permute-start | bytes 98312 | tf_op jit(solution)/shard_map/ppermute | solution.py:363
  24.4 0.5 %collective-permute-start.12 = (bf16[1,128,128]{2,1,0:T(8,128)(2,1)S(1)}, bf16[1,128,128]{2,1,0:T(8,128)(2,1)S(1)}, u32[]{:S(2)}, u32[]{:S(2)}) collective-permute-start(bf16[1,128,128]{2,1,0:T(8,128)(2,1)S(1)} %get-tuple-element.34), channel_id=1, source_target_pairs={{0,16},{8,24},{16,0},{24,8},{1,17},{9,25},{17,1},{25,9},{2,18},{10... | collective-permute-start | bytes 98312 | tf_op jit(solution)/shard_map/ppermute | solution.py:362
  25.0 2.6 %collective-permute-start.6 = (bf16[4,128,128]{2,1,0:T(8,128)(2,1)S(1)}, bf16[4,128,128]{2,1,0:T(8,128)(2,1)S(1)}, u32[]{:S(2)}, u32[]{:S(2)}) collective-permute-start(bf16[4,128,128]{2,1,0:T(8,128)(2,1)S(1)} %shard_map.91.refs_0_), channel_id=1, source_target_pairs={{0,4},{1,5},{2,6},{3,7},{4,0},{5,1},{6,2},{7,3},{8,12},{9,13},{10,... | collective-permute-start | bytes 393224 | tf_op jit(solution)/shard_map/ppermute | solution.py:358
  27.6 0.1 shard_map.90.refs_1_
  27.6 0.6 %collective-permute-done.13.far_top_ref = bf16[1,128,128]{2,1,0:T(8,128)(2,1)S(1)} collective-permute-done((bf16[1,128,128]{2,1,0:T(8,128)(2,1)S(1)}, bf16[1,128,128]{2,1,0:T(8,128)(2,1)S(1)}, u32[]{:S(2)}, u32[]{:S(2)}) %collective-permute-start.13) | collective-permute-done | bytes 32800 | tf_op jit(solution)/shard_map/ppermute | solution.py:363
  28.2 0.7 %collective-permute-start.4 = (bf16[8,128,128]{2,1,0:T(8,128)(2,1)S(1)}, bf16[8,128,128]{2,1,0:T(8,128)(2,1)S(1)}, u32[]{:S(2)}, u32[]{:S(2)}) collective-permute-start(bf16[8,128,128]{2,1,0:T(8,128)(2,1)S(1)} %shard_map.90.refs_1_), channel_id=1, source_target_pairs={{0,2},{1,3},{2,0},{3,1},{4,6},{5,7},{6,4},{7,5},{8,10},{9,11},{10,... | collective-permute-start | bytes 786440 | tf_op jit(solution)/shard_map/ppermute | solution.py:358
  29.0 2.6 %collective-permute-start.16 = (bf16[3,128,128]{2,1,0:T(8,128)(2,1)S(1)}, bf16[3,128,128]{2,1,0:T(8,128)(2,1)S(1)}, u32[]{:S(2)}, u32[]{:S(2)}) collective-permute-start(bf16[3,128,128]{2,1,0:T(8,128)(2,1)S(1)} %shard_map.93.piece0_ref), channel_id=1, source_target_pairs={{0,6},{1,7},{2,4},{3,5},{4,2},{5,3},{6,0},{7,1},{8,14},{9,15},{10,... | collective-permute-start | bytes 294920 | tf_op jit(solution)/shard_map/ppermute | solution.py:358
  31.6 0.3 collective-permute-start.15
  31.9 1.5 %collective-permute-start.14 = (bf16[3,128,128]{2,1,0:T(8,128)(2,1)S(1)}, bf16[3,128,128]{2,1,0:T(8,128)(2,1)S(1)}, u32[]{:S(2)}, u32[]{:S(2)}) collective-permute-start(bf16[3,128,128]{2,1,0:T(8,128)(2,1)S(1)} %shard_map.93.piece0_ref), channel_id=1, source_target_pairs={{0,2},{1,3},{2,0},{3,1},{4,6},{5,7},{6,4},{7,5},{8,10},{9,11},{10,... | collective-permute-start | bytes 294920 | tf_op jit(solution)/shard_map/ppermute | solution.py:358
  33.4 0.0 collective-permute-done.6.after_ref.two_own_ref
  33.5 2.3 %collective-permute-start.7 = (bf16[4,128,128]{2,1,0:T(8,128)(2,1)S(1)}, bf16[4,128,128]{2,1,0:T(8,128)(2,1)S(1)}, u32[]{:S(2)}, u32[]{:S(2)}) collective-permute-start(bf16[4,128,128]{2,1,0:T(8,128)(2,1)S(1)} %collective-permute-done.6.after_ref.two_own_ref), channel_id=1, source_target_pairs={{0,1},{1,0},{2,3},{3,2},{4,5},{5,4},{6,7},{7,6},{8,9},{9,8},{10,11... | collective-permute-start | bytes 393224 | tf_op jit(solution)/shard_map/ppermute | solution.py:358
  35.7 4.8 %collective-permute-done.16.piece3_ref = bf16[3,128,128]{2,1,0:T(8,128)(2,1)S(1)} collective-permute-done((bf16[3,128,128]{2,1,0:T(8,128)(2,1)S(1)}, bf16[3,128,128]{2,1,0:T(8,128)(2,1)S(1)}, u32[]{:S(2)}, u32[]{:S(2)}) %collective-permute-start.16) | collective-permute-done | bytes 98336 | tf_op jit(solution)/shard_map/ppermute | solution.py:358
  40.5 0.7 %collective-permute-done.14.piece1_ref = bf16[3,128,128]{2,1,0:T(8,128)(2,1)S(1)} collective-permute-done((bf16[3,128,128]{2,1,0:T(8,128)(2,1)S(1)}, bf16[3,128,128]{2,1,0:T(8,128)(2,1)S(1)}, u32[]{:S(2)}, u32[]{:S(2)}) %collective-permute-start.14) | collective-permute-done | bytes 98336 | tf_op jit(solution)/shard_map/ppermute | solution.py:358
  41.3 0.1 collective-permute-start.17
  41.4 1.3 %collective-permute-done.17.split_other_ref = bf16[1,4,128,128]{3,2,1,0:T(8,128)(2,1)S(1)} collective-permute-done((bf16[1,4,128,128]{3,2,1,0:T(8,128)(2,1)S(1)}, bf16[1,4,128,128]{3,2,1,0:T(8,128)(2,1)S(1)}, u32[]{:S(2)}, u32[]{:S(2)}) %collective-permute-start.17) | collective-permute-done | bytes 131104 | tf_op jit(solution)/shard_map/ppermute | solution.py:362
  42.7 2.8 %shard_map.95 = (bf16[128,1024]{1,0:T(8,128)(2,1)}, bf16[128,1024]{1,0:T(8,128)(2,1)}, bf16[128,1024]{1,0:T(8,128)(2,1)}) custom-call(s32[5]{0:T(128)S(1)} %shift-right-arithmetic_and_fusion.flag_ref.refs_0_, s32[1,128]{1,0:T(1,128)S(1)} %bitcast.9, f32[20,8,32]{2,1,0:T(8,128)S(1)} %bitcast.5, bf16[128,1024]{1,0:T(8,128)(2,1)S(1)} %copy-done, ...), custom_call_target="tpu_custom_call" | custom-call | flops 234881024 | bytes 3822100 | tf_op jit(solution)/shard_map/pallas_call | solution.py:387
  (28 shorter events, 0.2 us)
Async XLA Ops:
  0.6 2.9 %copy-start = (bf16[128,1024]{1,0:T(8,128)(2,1)S(1)}, bf16[128,1024]{1,0:T(8,128)(2,1)}, u32[]{:S(2)}) copy-start(bf16[128,1024]{1,0:T(8,128)(2,1)} %k_ref.5) | copy-start | bytes 786436
  0.7 2.9 %copy-start.1 = (bf16[128,1024]{1,0:T(8,128)(2,1)S(1)}, bf16[128,1024]{1,0:T(8,128)(2,1)}, u32[]{:S(2)}) copy-start(bf16[128,1024]{1,0:T(8,128)(2,1)} %v_ref.5) | copy-start | bytes 786436
  0.7 2.9 %copy-start.2 = (bf16[128,1024]{1,0:T(8,128)(2,1)S(1)}, bf16[128,1024]{1,0:T(8,128)(2,1)}, u32[]{:S(2)}) copy-start(bf16[128,1024]{1,0:T(8,128)(2,1)} %g_ref.5) | copy-start | bytes 786436
  0.7 2.8 %copy-start.3 = (bf16[128,1024]{1,0:T(8,128)(2,1)S(1)}, bf16[128,1024]{1,0:T(8,128)(2,1)}, u32[]{:S(2)}) copy-start(bf16[128,1024]{1,0:T(8,128)(2,1)} %q_ref.3) | copy-start | bytes 786436
  0.7 2.8 %copy-start.4 = (f32[32,20,8]{0,2,1:T(8,128)S(1)}, f32[32,20,8]{0,2,1:T(8,128)}, u32[]{:S(2)}) copy-start(f32[32,20,8]{0,2,1:T(8,128)} %param.11) | copy-start | bytes 61444
  3.0 0.7 %copy-start.5 = (s32[128]{0:T(128)S(1)}, s32[128]{0:T(128)}, u32[]{:S(2)}) copy-start(s32[128]{0:T(128)} %param.10) | copy-start | bytes 1540
  3.0 4.9 %collective-permute-start.1 = (bf16[12,128,128]{2,1,0:T(8,128)(2,1)S(1)}, bf16[12,128,128]{2,1,0:T(8,128)(2,1)S(1)}, u32[]{:S(2)}, u32[]{:S(2)}) collective-permute-start(bf16[12,128,128]{2,1,0:T(8,128)(2,1)S(1)} %get-tuple-element.22), channel_id=1, source_target_pairs={{0,8},{8,0},{16,24},{24,16},{1,9},{9,1},{17,25},{25,17},{2,10},{10... | collective-permute-start | bytes 1179656 | tf_op jit(solution)/shard_map/ppermute | solution.py:362
  4.8 9.3 %collective-permute-start = (bf16[4,128,128]{2,1,0:T(8,128)(2,1)S(1)}, bf16[4,128,128]{2,1,0:T(8,128)(2,1)S(1)}, u32[]{:S(2)}, u32[]{:S(2)}) collective-permute-start(bf16[4,128,128]{2,1,0:T(8,128)(2,1)S(1)} %get-tuple-element.21), channel_id=1, source_target_pairs={{0,1},{1,0},{2,3},{3,2},{4,5},{5,4},{6,7},{7,6},{8,9},{9,8},{10,11... | collective-permute-start | bytes 393224 | tf_op jit(solution)/shard_map/ppermute | solution.py:358
  7.8 17.1 %collective-permute-start.3 = (bf16[8,128,128]{2,1,0:T(8,128)(2,1)S(1)}, bf16[8,128,128]{2,1,0:T(8,128)(2,1)S(1)}, u32[]{:S(2)}, u32[]{:S(2)}) collective-permute-start(bf16[8,128,128]{2,1,0:T(8,128)(2,1)S(1)} %get-tuple-element.29.own_ref), channel_id=1, source_target_pairs={{0,1},{1,0},{2,3},{3,2},{4,5},{5,4},{6,7},{7,6},{8,9},{9,8},{10,11... | collective-permute-start | bytes 786440 | tf_op jit(solution)/shard_map/ppermute | solution.py:358
  8.5 7.2 %collective-permute-start.8 = (bf16[3,128,128]{2,1,0:T(8,128)(2,1)S(1)}, bf16[3,128,128]{2,1,0:T(8,128)(2,1)S(1)}, u32[]{:S(2)}, u32[]{:S(2)}) collective-permute-start(bf16[3,128,128]{2,1,0:T(8,128)(2,1)S(1)} %get-tuple-element.30), channel_id=1, source_target_pairs={{0,6},{1,7},{2,4},{3,5},{4,2},{5,3},{6,0},{7,1},{8,14},{9,15},{10,... | collective-permute-start | bytes 294920 | tf_op jit(solution)/shard_map/ppermute | solution.py:358
  12.6 16.3 %collective-permute-start.2 = (bf16[8,128,128]{2,1,0:T(8,128)(2,1)S(1)}, bf16[8,128,128]{2,1,0:T(8,128)(2,1)S(1)}, u32[]{:S(2)}, u32[]{:S(2)}) collective-permute-start(bf16[8,128,128]{2,1,0:T(8,128)(2,1)S(1)} %get-tuple-element.28), channel_id=1, source_target_pairs={{0,1},{1,0},{2,3},{3,2},{4,5},{5,4},{6,7},{7,6},{8,9},{9,8},{10,11... | collective-permute-start | bytes 786440 | tf_op jit(solution)/shard_map/ppermute | solution.py:358
  14.1 7.1 %collective-permute-start.9 = (bf16[3,128,128]{2,1,0:T(8,128)(2,1)S(1)}, bf16[3,128,128]{2,1,0:T(8,128)(2,1)S(1)}, u32[]{:S(2)}, u32[]{:S(2)}) collective-permute-start(bf16[3,128,128]{2,1,0:T(8,128)(2,1)S(1)} %get-tuple-element.31), channel_id=1, source_target_pairs={{0,4},{1,5},{2,6},{3,7},{4,0},{5,1},{6,2},{7,3},{8,12},{9,13},{10,... | collective-permute-start | bytes 294920 | tf_op jit(solution)/shard_map/ppermute | solution.py:358
  14.1 7.1 %collective-permute-start.10 = (bf16[3,128,128]{2,1,0:T(8,128)(2,1)S(1)}, bf16[3,128,128]{2,1,0:T(8,128)(2,1)S(1)}, u32[]{:S(2)}, u32[]{:S(2)}) collective-permute-start(bf16[3,128,128]{2,1,0:T(8,128)(2,1)S(1)} %get-tuple-element.32), channel_id=1, source_target_pairs={{0,2},{1,3},{2,0},{3,1},{4,6},{5,7},{6,4},{7,5},{8,10},{9,11},{10,... | collective-permute-start | bytes 294920 | tf_op jit(solution)/shard_map/ppermute | solution.py:358
  15.7 8.7 %collective-permute-start.5 = (bf16[4,128,128]{2,1,0:T(8,128)(2,1)S(1)}, bf16[4,128,128]{2,1,0:T(8,128)(2,1)S(1)}, u32[]{:S(2)}, u32[]{:S(2)}) collective-permute-start(bf16[4,128,128]{2,1,0:T(8,128)(2,1)S(1)} %shard_map.88.after_ref.own_ref), channel_id=1, source_target_pairs={{0,2},{1,3},{2,0},{3,1},{4,6},{5,7},{6,4},{7,5},{8,10},{9,11},{10,... | collective-permute-start | bytes 393224 | tf_op jit(solution)/shard_map/ppermute | solution.py:358
  21.3 7.6 %collective-permute-start.11 = (bf16[2,128,128]{2,1,0:T(8,128)(2,1)S(1)}, bf16[2,128,128]{2,1,0:T(8,128)(2,1)S(1)}, u32[]{:S(2)}, u32[]{:S(2)}) collective-permute-start(bf16[2,128,128]{2,1,0:T(8,128)(2,1)S(1)} %get-tuple-element.33.below_ref), channel_id=1, source_target_pairs={{0,1},{1,0},{2,3},{3,2},{4,5},{5,4},{6,7},{7,6},{8,9},{9,8},{10,11... | collective-permute-start | bytes 196616 | tf_op jit(solution)/shard_map/ppermute | solution.py:358
  23.4 4.8 %collective-permute-start.13 = (bf16[1,128,128]{2,1,0:T(8,128)(2,1)S(1)}, bf16[1,128,128]{2,1,0:T(8,128)(2,1)S(1)}, u32[]{:S(2)}, u32[]{:S(2)}) collective-permute-start(bf16[1,128,128]{2,1,0:T(8,128)(2,1)S(1)} %get-tuple-element.34), channel_id=1, source_target_pairs={{0,17},{1,16},{2,19},{3,18},{4,21},{5,20},{6,23},{7,22},{8,25},{9,... | collective-permute-start | bytes 98312 | tf_op jit(solution)/shard_map/ppermute | solution.py:363
  24.4 4.5 %collective-permute-start.12 = (bf16[1,128,128]{2,1,0:T(8,128)(2,1)S(1)}, bf16[1,128,128]{2,1,0:T(8,128)(2,1)S(1)}, u32[]{:S(2)}, u32[]{:S(2)}) collective-permute-start(bf16[1,128,128]{2,1,0:T(8,128)(2,1)S(1)} %get-tuple-element.34), channel_id=1, source_target_pairs={{0,16},{8,24},{16,0},{24,8},{1,17},{9,25},{17,1},{25,9},{2,18},{10... | collective-permute-start | bytes 98312 | tf_op jit(solution)/shard_map/ppermute | solution.py:362
  25.0 8.5 %collective-permute-start.6 = (bf16[4,128,128]{2,1,0:T(8,128)(2,1)S(1)}, bf16[4,128,128]{2,1,0:T(8,128)(2,1)S(1)}, u32[]{:S(2)}, u32[]{:S(2)}) collective-permute-start(bf16[4,128,128]{2,1,0:T(8,128)(2,1)S(1)} %shard_map.91.refs_0_), channel_id=1, source_target_pairs={{0,4},{1,5},{2,6},{3,7},{4,0},{5,1},{6,2},{7,3},{8,12},{9,13},{10,... | collective-permute-start | bytes 393224 | tf_op jit(solution)/shard_map/ppermute | solution.py:358
  28.2 13.2 %collective-permute-start.4 = (bf16[8,128,128]{2,1,0:T(8,128)(2,1)S(1)}, bf16[8,128,128]{2,1,0:T(8,128)(2,1)S(1)}, u32[]{:S(2)}, u32[]{:S(2)}) collective-permute-start(bf16[8,128,128]{2,1,0:T(8,128)(2,1)S(1)} %shard_map.90.refs_1_), channel_id=1, source_target_pairs={{0,2},{1,3},{2,0},{3,1},{4,6},{5,7},{6,4},{7,5},{8,10},{9,11},{10,... | collective-permute-start | bytes 786440 | tf_op jit(solution)/shard_map/ppermute | solution.py:358
  29.0 11.6 %collective-permute-start.16 = (bf16[3,128,128]{2,1,0:T(8,128)(2,1)S(1)}, bf16[3,128,128]{2,1,0:T(8,128)(2,1)S(1)}, u32[]{:S(2)}, u32[]{:S(2)}) collective-permute-start(bf16[3,128,128]{2,1,0:T(8,128)(2,1)S(1)} %shard_map.93.piece0_ref), channel_id=1, source_target_pairs={{0,6},{1,7},{2,4},{3,5},{4,2},{5,3},{6,0},{7,1},{8,14},{9,15},{10,... | collective-permute-start | bytes 294920 | tf_op jit(solution)/shard_map/ppermute | solution.py:358
  31.6 8.9 %collective-permute-start.15 = (bf16[3,128,128]{2,1,0:T(8,128)(2,1)S(1)}, bf16[3,128,128]{2,1,0:T(8,128)(2,1)S(1)}, u32[]{:S(2)}, u32[]{:S(2)}) collective-permute-start(bf16[3,128,128]{2,1,0:T(8,128)(2,1)S(1)} %shard_map.93.piece0_ref), channel_id=1, source_target_pairs={{0,4},{1,5},{2,6},{3,7},{4,0},{5,1},{6,2},{7,3},{8,12},{9,13},{10,... | collective-permute-start | bytes 294920 | tf_op jit(solution)/shard_map/ppermute | solution.py:358
  31.9 9.4 %collective-permute-start.14 = (bf16[3,128,128]{2,1,0:T(8,128)(2,1)S(1)}, bf16[3,128,128]{2,1,0:T(8,128)(2,1)S(1)}, u32[]{:S(2)}, u32[]{:S(2)}) collective-permute-start(bf16[3,128,128]{2,1,0:T(8,128)(2,1)S(1)} %shard_map.93.piece0_ref), channel_id=1, source_target_pairs={{0,2},{1,3},{2,0},{3,1},{4,6},{5,7},{6,4},{7,5},{8,10},{9,11},{10,... | collective-permute-start | bytes 294920 | tf_op jit(solution)/shard_map/ppermute | solution.py:358
  33.5 7.9 %collective-permute-start.7 = (bf16[4,128,128]{2,1,0:T(8,128)(2,1)S(1)}, bf16[4,128,128]{2,1,0:T(8,128)(2,1)S(1)}, u32[]{:S(2)}, u32[]{:S(2)}) collective-permute-start(bf16[4,128,128]{2,1,0:T(8,128)(2,1)S(1)} %collective-permute-done.6.after_ref.two_own_ref), channel_id=1, source_target_pairs={{0,1},{1,0},{2,3},{3,2},{4,5},{5,4},{6,7},{7,6},{8,9},{9,8},{10,11... | collective-permute-start | bytes 393224 | tf_op jit(solution)/shard_map/ppermute | solution.py:358
  41.3 1.4 %collective-permute-start.17 = (bf16[1,4,128,128]{3,2,1,0:T(8,128)(2,1)S(1)}, bf16[1,4,128,128]{3,2,1,0:T(8,128)(2,1)S(1)}, u32[]{:S(2)}, u32[]{:S(2)}) collective-permute-start(bf16[1,4,128,128]{3,2,1,0:T(8,128)(2,1)S(1)} %shard_map.94.split_own_ref), channel_id=1, source_target_pairs={{0,8},{8,0},{16,24},{24,16},{1,9},{9,1},{17,25},{25,17},{2,10},{10... | collective-permute-start | bytes 393224 | tf_op jit(solution)/shard_map/ppermute | solution.py:362

commit v9 on v4

--- a/solution.py
+++ b/solution.py
@@ -195,13 +195,14 @@
     top_ref[...] = narrow(total[rows:])
 
 
-def pair_sum_kernel(below_ref, far_ref, near_top_ref, far_top_ref, out_ref):
+def pair_sum_kernel(below_ref, far_ref, near_top_ref, far_top_ref, *refs):
+    out_ref = refs[-1]
     rows = below_ref.shape[0]
     out_ref[:rows] = narrow(wide(below_ref[...]) + wide(far_ref[...]))
     out_ref[rows:] = narrow(wide(near_top_ref[...]) + wide(far_top_ref[...]))
 
 
-def gather_kernel(cut, piece0_ref, piece1_ref, piece2_ref, piece3_ref, out_ref):
+def gather_kernel(cut, piece0_ref, piece1_ref, piece2_ref, piece3_ref, after_ref, out_ref):
     for offs, piece_ref in enumerate((piece0_ref, piece1_ref, piece2_ref, piece3_ref)):
         split_levels = out_ref.shape[0]
         eighth = out_ref.shape[1] // 4
@@ -210,10 +211,13 @@
             out_ref[level, offs * eighth : (offs + 1) * eighth] = piece_ref[first : first + eighth]
 
 
-def lower_sum_kernel(own_ref, sent_ref, seen_ref, after_ref, two_ref, one_ref):
-    half = own_ref.shape[0]
-    two_ref[...] = narrow(wide(own_ref[...]) + wide(seen_ref[:half]))
-    one_ref[...] = narrow(wide(sent_ref[half:]) + wide(seen_ref[half:]))
+def two_sum_kernel(own_ref, seen_ref, after_ref, two_ref):
+    two_ref[...] = narrow(wide(own_ref[...]) + wide(seen_ref[: own_ref.shape[0]]))
+
+
+def one_sum_kernel(sent_ref, seen_ref, after_ref, one_ref):
+    first = sent_ref.shape[0] - one_ref.shape[0]
+    one_ref[...] = narrow(wide(sent_ref[first:]) + wide(seen_ref[first:]))
 
 
 def local_kernel(
@@ -226,11 +230,9 @@
     v_ref,
     g_ref,
     after_ref,
-    held_ref,
     qo_ref,
     ko_ref,
     vo_ref,
-    held_out_ref,
 ):
     head_count = table_ref.shape[1]
     tokens = q_ref.shape[0]
@@ -437,14 +439,16 @@
         (cells(share_rows),) * 4,
         (flag_bits, seen, keep, two_own, *lead),
     )
+    lower_seen = swap(lower_sent, 0)
+    two_sum = call(
+        two_sum_kernel, [vmem] * 2 + [anywhere], cells(half), (two_own, lower_seen, own_share)
+    )
     big = jax.ShapeDtypeStruct((row_count, width), jnp.float32)
-    query_local, key_local, value_local, zero = call(
+    query_local, key_local, value_local = call(
         functools.partial(local_kernel, block_depth, head_size),
-        [vmem] * 6 + [anywhere] * 2,
-        (big, big, big, cells(head_count)),
-        (class_lanes, table, query_rows, key_rows, value_rows, out_grad, own_share, zero),
-        out_specs=(vmem, vmem, vmem, anywhere),
-        aliases={7: 3},
+        [vmem] * 6 + [anywhere],
+        (big, big, big),
+        (class_lanes, table, query_rows, key_rows, value_rows, out_grad, own_share),
         flops=10 * row_count * width * row_count,
     )
 
@@ -481,29 +485,33 @@
                 row += size
         below = narrow(jnp.concatenate([parts[level] for level in range(NEAR, top)], axis=0))
         top_sent = narrow(parts[top])
-    shares = call(
-        pair_sum_kernel,
-        [vmem] * 4,
-        cells(share_rows),
-        (below, swap(below, 0), swap(top_sent, top), swap(top_sent, 0, top)),
-    )
-    pieces = [shares] + [swap(shares, *z_bits(offs)) for offs in (1, 2, 3)]
-    split_own = call(
-        functools.partial(gather_kernel, cut), [vmem] * 4, cells(split_levels, half), pieces
-    )
-    split_other = swap(split_own, inner_bits)
-
-    two_sum, one_sum = call(
-        lower_sum_kernel,
-        [vmem] * 3 + [anywhere],
-        (cells(half), cells(head_count)),
-        (two_own, lower_sent, swap(lower_sent, 0), query_local),
-    )
-    two_sum = narrow(wide(two_sum) + wide(swap(two_sum, 1)))
+    one_sum = call(
+        one_sum_kernel,
+        [vmem] * 2 + [anywhere],
+        cells(head_count),
+        (lower_sent, lower_seen, below),
+    )
+    two_sum = call(
+        two_sum_kernel, [vmem] * 2 + [anywhere], cells(half), (two_sum, swap(two_sum, 1), two_sum)
+    )
     two_half = swap(two_sum, 2)
     two_rest = swap(two_half, 0)
     one_done = swap(one_sum, 1)
     zero_done = swap(zero, 0)
+    shares = call(
+        pair_sum_kernel,
+        [vmem] * 4 + [anywhere] * 2,
+        cells(share_rows),
+        (below, swap(below, 0), swap(top_sent, top), swap(top_sent, 0, top), two_sum, zero_done),
+    )
+    pieces = [shares] + [swap(shares, *z_bits(offs)) for offs in (1, 2, 3)]
+    split_own = call(
+        functools.partial(gather_kernel, cut),
+        [vmem] * 4 + [anywhere],
+        cells(split_levels, half),
+        (*pieces, two_half),
+    )
+    split_other = swap(split_own, inner_bits)
 
     small = jax.ShapeDtypeStruct((row_count, width), jnp.bfloat16)
     return call(

time: 53.2 us -> 46.8 us (0.88)
  waiting for transfers between devices: 21.7 us -> 13.1 us
  starting transfers between devices: 21.3 us -> 23.5 us
    ppermute x13, waiting for transfers between devices: 19.1 us -> 11.7 us  [swap(): return lax.ppermute(block, 'gy', [(i, i ^ mask) for i in range(inner_size)])]
    ppermute x13, starting transfers between devices: 17.7 us -> 20.9 us  [swap(): return lax.ppermute(block, 'gy', [(i, i ^ mask) for i in range(inner_size)])]
    ppermute x1, waiting for transfers between devices: 2.05 us -> 0.01 us  [swap(): lax.ppermute(block, ('gx', 'gy'), [(i, i ^ mask) for i in range(device_co...]
    ppermute x1, starting transfers between devices: 2.55 us -> 1.49 us  [swap(): lax.ppermute(block, ('gx', 'gy'), [(i, i ^ mask) for i in range(device_co...]
    ppermute x3, waiting for transfers between devices: 0.5 us -> 1.42 us  [swap(): return lax.ppermute(block, 'gx', [(i, i ^ mask) for i in range(size)])]
    pallas_call x9 -> x11, Pallas kernels: 9.08 us -> 9.13 us  [call(): pl.pallas_call(kernel, out_shape=outs, in_specs=in_specs, out_specs=out_s...]
  transfers between devices with their start and end apart: 17 -> 17, of which waited for: 9 -> 7; matrix products, arithmetic and copies ran while one was open for 0% -> 0% of each run, Pallas kernels for 8% -> 9%
where the time goes in v9:
time: 46.8 us; the launch traced here: 46.6 us
  starting transfers between devices  23.5 us (50%)
  waiting for transfers between devices  13.1 us (28%)
  Pallas kernels  9.13 us (20%)
  between operations  0.82 us (2%)
    ppermute x13, starting transfers between devices, swap(): return lax.ppermute(block, 'gy', [(i, i ^ mask) for i in range(inner_size)])  20.9 us
    ppermute x13, waiting for transfers between devices, swap(): return lax.ppermute(block, 'gy', [(i, i ^ mask) for i in range(inner_size)])  11.7 us
    pallas_call x11, Pallas kernels, call(): pl.pallas_call(kernel, out_shape=outs, in_specs=in_specs, out_specs=out_s...  9.13 us
    ppermute x1, starting transfers between devices, swap(): lax.ppermute(block, ('gx', 'gy'), [(i, i ^ mask) for i in range(device_co...  1.49 us
    ppermute x3, waiting for transfers between devices, swap(): return lax.ppermute(block, 'gx', [(i, i ^ mask) for i in range(size)])  1.42 us
    ppermute x3, starting transfers between devices, swap(): return lax.ppermute(block, 'gx', [(i, i ^ mask) for i in range(size)])  1.1 us
  transfers between devices with their start and end apart: 17, of which 7 were waited for; matrix products, arithmetic and copies ran while one was open for 0% of the time, Pallas kernels for 9%

profile of v9, /device:TPU:0, one launch (start us, length us, event | category | flops | bytes accessed | tf_op | source)
XLA Modules:
  0.0 46.6 jit_solution(671877720154914139)
XLA Ops:
  0.6 0.0 copy-start
  0.7 2.3 %shard_map.85 = (bf16[12,128,128]{2,1,0:T(8,128)(2,1)S(1)}, bf16[4,128,128]{2,1,0:T(8,128)(2,1)S(1)}) custom-call(s32[5]{0:T(128)S(1)} %shift-right-arithmetic_and_fusion.flag_ref, s32[1,128]{1,0:T(1,128)} %bitcast.6, f32[20,8,32]{2,1,0:T(8,128)} %bitcast.2, bf16[128,1024]{1,0:T(8,128)(2,1)} %q_ref.3, bf16[128,1024]{1,0:T(8,128)(2,1)} %k_ref.5, ...), custom_call_target="tpu_custom_call" | custom-call | flops 67108864 | bytes 1069588 | tf_op jit(solution)/shard_map/pallas_call | solution.py:383
  3.0 0.5 %collective-permute-start = (bf16[12,128,128]{2,1,0:T(8,128)(2,1)S(1)}, bf16[12,128,128]{2,1,0:T(8,128)(2,1)S(1)}, u32[]{:S(2)}, u32[]{:S(2)}) collective-permute-start(bf16[12,128,128]{2,1,0:T(8,128)(2,1)S(1)} %get-tuple-element.17), channel_id=1, source_target_pairs={{0,8},{8,0},{16,24},{24,16},{1,9},{9,1},{17,25},{25,17},{2,10},{10... | collective-permute-start | bytes 1179656 | tf_op jit(solution)/shard_map/ppermute | solution.py:367
  3.5 0.1 copy-done.5
  3.6 1.2 %shard_map.86 = (bf16[4,128,128]{2,1,0:T(8,128)(2,1)S(1)}, bf16[12,128,128]{2,1,0:T(8,128)(2,1)S(1)}, bf16[8,128,128]{2,1,0:T(8,128)(2,1)S(1)}) custom-call(s32[5]{0:T(128)S(1)} %shift-right-arithmetic_and_fusion.flag_ref, s32[1,128]{1,0:T(1,128)S(1)} %bitcast.7, f32[20,8,32]{2,1,0:T(8,128)S(1)} %bitcast.3, bf16[128,1024]{1,0:T(8,128)(2,1)S(1)} %copy-done.3, ...), custom_call_target="tpu_custom_call" | custom-call | flops 100663296 | bytes 1200660 | tf_op jit(solution)/shard_map/pallas_call | solution.py:383
  4.8 3.0 %collective-permute-start.2 = (bf16[12,128,128]{2,1,0:T(8,128)(2,1)S(1)}, bf16[12,128,128]{2,1,0:T(8,128)(2,1)S(1)}, u32[]{:S(2)}, u32[]{:S(2)}) collective-permute-start(bf16[12,128,128]{2,1,0:T(8,128)(2,1)S(1)} %get-tuple-element.25.sent_ref), channel_id=1, source_target_pairs={{0,1},{1,0},{2,3},{3,2},{4,5},{5,4},{6,7},{7,6},{8,9},{9,8},{10,11... | collective-permute-start | bytes 1179656 | tf_op jit(solution)/shard_map/ppermute | solution.py:363
  7.8 0.1 collective-permute-start.1
  7.9 0.6 %shard_map.87 = (bf16[3,128,128]{2,1,0:T(8,128)(2,1)S(1)}, bf16[3,128,128]{2,1,0:T(8,128)(2,1)S(1)}, bf16[3,128,128]{2,1,0:T(8,128)(2,1)S(1)}, bf16[3,128,128]{2,1,0:T(8,128)(2,1)S(1)}) custom-call(s32[5]{0:T(128)S(1)} %shift-right-arithmetic_and_fusion.flag_ref, bf16[12,128,128]{2,1,0:T(8,128)(2,1)S(1)} %collective-permute-done.seen_ref, ...), custom_call_target="tpu_custom_call" | custom-call | bytes 655380 | tf_op jit(solution)/shard_map/pallas_call | solution.py:383
  8.5 4.1 %collective-permute-start.3 = (bf16[3,128,128]{2,1,0:T(8,128)(2,1)S(1)}, bf16[3,128,128]{2,1,0:T(8,128)(2,1)S(1)}, u32[]{:S(2)}, u32[]{:S(2)}) collective-permute-start(bf16[3,128,128]{2,1,0:T(8,128)(2,1)S(1)} %get-tuple-element.26), channel_id=1, source_target_pairs={{0,6},{1,7},{2,4},{3,5},{4,2},{5,3},{6,0},{7,1},{8,14},{9,15},{10,... | collective-permute-start | bytes 294920 | tf_op jit(solution)/shard_map/ppermute | solution.py:363
  12.6 0.6 %collective-permute-start.5 = (bf16[3,128,128]{2,1,0:T(8,128)(2,1)S(1)}, bf16[3,128,128]{2,1,0:T(8,128)(2,1)S(1)}, u32[]{:S(2)}, u32[]{:S(2)}) collective-permute-start(bf16[3,128,128]{2,1,0:T(8,128)(2,1)S(1)} %get-tuple-element.28), channel_id=1, source_target_pairs={{0,2},{1,3},{2,0},{3,1},{4,6},{5,7},{6,4},{7,5},{8,10},{9,11},{10,... | collective-permute-start | bytes 294920 | tf_op jit(solution)/shard_map/ppermute | solution.py:363
  13.3 4.5 %collective-permute-done.2.seen_ref = bf16[12,128,128]{2,1,0:T(8,128)(2,1)S(1)} collective-permute-done((bf16[12,128,128]{2,1,0:T(8,128)(2,1)S(1)}, bf16[12,128,128]{2,1,0:T(8,128)(2,1)S(1)}, u32[]{:S(2)}, u32[]{:S(2)}) %collective-permute-start.2) | collective-permute-done | bytes 393248 | tf_op jit(solution)/shard_map/ppermute | solution.py:363
  17.8 2.2 %collective-permute-start.7 = (bf16[4,128,128]{2,1,0:T(8,128)(2,1)S(1)}, bf16[4,128,128]{2,1,0:T(8,128)(2,1)S(1)}, u32[]{:S(2)}, u32[]{:S(2)}) collective-permute-start(bf16[4,128,128]{2,1,0:T(8,128)(2,1)S(1)} %shard_map.91.own_ref.after_ref), channel_id=1, source_target_pairs={{0,2},{1,3},{2,0},{3,1},{4,6},{5,7},{6,4},{7,5},{8,10},{9,11},{10,... | collective-permute-start | bytes 393224 | tf_op jit(solution)/shard_map/ppermute | solution.py:363
  20.0 2.0 %shard_map.88 = (f32[128,1024]{1,0:T(8,128)S(1)}, f32[128,1024]{1,0:T(8,128)S(1)}, f32[128,1024]{1,0:T(8,128)S(1)}) custom-call(s32[1,128]{1,0:T(1,128)S(1)} %bitcast.8, f32[20,8,32]{2,1,0:T(8,128)S(1)} %bitcast.4, bf16[128,1024]{1,0:T(8,128)(2,1)S(1)} %copy-done.3, bf16[128,1024]{1,0:T(8,128)(2,1)S(1)} %copy-done, bf16[128,1024]{1,0:T(8,128)(2,1)S(1)} %copy-done.1, ...), custom_call_target="tpu_custom_call" | custom-call | flops 167772160 | bytes 1167872 | tf_op jit(solution)/shard_map/pallas_call | solution.py:383
  22.1 0.1 shard_map.89
  22.1 1.6 %collective-permute-start.10 = (bf16[2,128,128]{2,1,0:T(8,128)(2,1)S(1)}, bf16[2,128,128]{2,1,0:T(8,128)(2,1)S(1)}, u32[]{:S(2)}, u32[]{:S(2)}) collective-permute-start(bf16[2,128,128]{2,1,0:T(8,128)(2,1)S(1)} %get-tuple-element.29.after_ref.below_ref), channel_id=1, source_target_pairs={{0,1},{1,0},{2,3},{3,2},{4,5},{5,4},{6,7},{7,6},{8,9},{9,8},{10,11... | collective-permute-start | bytes 196616 | tf_op jit(solution)/shard_map/ppermute | solution.py:363
  23.7 1.5 %collective-permute-start.12 = (bf16[1,128,128]{2,1,0:T(8,128)(2,1)S(1)}, bf16[1,128,128]{2,1,0:T(8,128)(2,1)S(1)}, u32[]{:S(2)}, u32[]{:S(2)}) collective-permute-start(bf16[1,128,128]{2,1,0:T(8,128)(2,1)S(1)} %get-tuple-element.30), channel_id=1, source_target_pairs={{0,17},{1,16},{2,19},{3,18},{4,21},{5,20},{6,23},{7,22},{8,25},{9,... | collective-permute-start | bytes 98312 | tf_op jit(solution)/shard_map/ppermute | solution.py:368
  25.2 0.5 %collective-permute-start.11 = (bf16[1,128,128]{2,1,0:T(8,128)(2,1)S(1)}, bf16[1,128,128]{2,1,0:T(8,128)(2,1)S(1)}, u32[]{:S(2)}, u32[]{:S(2)}) collective-permute-start(bf16[1,128,128]{2,1,0:T(8,128)(2,1)S(1)} %get-tuple-element.30), channel_id=1, source_target_pairs={{0,16},{8,24},{16,0},{24,8},{1,17},{9,25},{17,1},{25,9},{2,18},{10... | collective-permute-start | bytes 98312 | tf_op jit(solution)/shard_map/ppermute | solution.py:367
  25.7 2.7 %collective-permute-start.8 = (bf16[4,128,128]{2,1,0:T(8,128)(2,1)S(1)}, bf16[4,128,128]{2,1,0:T(8,128)(2,1)S(1)}, u32[]{:S(2)}, u32[]{:S(2)}) collective-permute-start(bf16[4,128,128]{2,1,0:T(8,128)(2,1)S(1)} %shard_map.92.refs_0_), channel_id=1, source_target_pairs={{0,4},{1,5},{2,6},{3,7},{4,0},{5,1},{6,2},{7,3},{8,12},{9,13},{10,... | collective-permute-start | bytes 393224 | tf_op jit(solution)/shard_map/ppermute | solution.py:363
  28.4 0.1 shard_map.90
  28.5 0.5 %collective-permute-start.6 = (bf16[8,128,128]{2,1,0:T(8,128)(2,1)S(1)}, bf16[8,128,128]{2,1,0:T(8,128)(2,1)S(1)}, u32[]{:S(2)}, u32[]{:S(2)}) collective-permute-start(bf16[8,128,128]{2,1,0:T(8,128)(2,1)S(1)} %shard_map.90), channel_id=1, source_target_pairs={{0,2},{1,3},{2,0},{3,1},{4,6},{5,7},{6,4},{7,5},{8,10},{9,11},{10,... | collective-permute-start | bytes 786440 | tf_op jit(solution)/shard_map/ppermute | solution.py:363
  29.0 0.1 collective-permute-done.11.near_top_ref
  29.1 2.5 %collective-permute-start.15 = (bf16[3,128,128]{2,1,0:T(8,128)(2,1)S(1)}, bf16[3,128,128]{2,1,0:T(8,128)(2,1)S(1)}, u32[]{:S(2)}, u32[]{:S(2)}) collective-permute-start(bf16[3,128,128]{2,1,0:T(8,128)(2,1)S(1)} %shard_map.93.piece0_ref), channel_id=1, source_target_pairs={{0,6},{1,7},{2,4},{3,5},{4,2},{5,3},{6,0},{7,1},{8,14},{9,15},{10,... | collective-permute-start | bytes 294920 | tf_op jit(solution)/shard_map/ppermute | solution.py:363
  31.7 0.5 collective-permute-start.14
  32.1 1.5 %collective-permute-start.13 = (bf16[3,128,128]{2,1,0:T(8,128)(2,1)S(1)}, bf16[3,128,128]{2,1,0:T(8,128)(2,1)S(1)}, u32[]{:S(2)}, u32[]{:S(2)}) collective-permute-start(bf16[3,128,128]{2,1,0:T(8,128)(2,1)S(1)} %shard_map.93.piece0_ref), channel_id=1, source_target_pairs={{0,2},{1,3},{2,0},{3,1},{4,6},{5,7},{6,4},{7,5},{8,10},{9,11},{10,... | collective-permute-start | bytes 294920 | tf_op jit(solution)/shard_map/ppermute | solution.py:363
  33.6 2.5 %collective-permute-done.8.after_ref.two_own_ref = bf16[4,128,128]{2,1,0:T(8,128)(2,1)S(1)} collective-permute-done((bf16[4,128,128]{2,1,0:T(8,128)(2,1)S(1)}, bf16[4,128,128]{2,1,0:T(8,128)(2,1)S(1)}, u32[]{:S(2)}, u32[]{:S(2)}) %collective-permute-start.8) | collective-permute-done | bytes 131104 | tf_op jit(solution)/shard_map/ppermute | solution.py:363
  36.1 1.6 %collective-permute-start.9 = (bf16[4,128,128]{2,1,0:T(8,128)(2,1)S(1)}, bf16[4,128,128]{2,1,0:T(8,128)(2,1)S(1)}, u32[]{:S(2)}, u32[]{:S(2)}) collective-permute-start(bf16[4,128,128]{2,1,0:T(8,128)(2,1)S(1)} %collective-permute-done.8.after_ref.two_own_ref), channel_id=1, source_target_pairs={{0,1},{1,0},{2,3},{3,2},{4,5},{5,4},{6,7},{7,6},{8,9},{9,8},{10,11... | collective-permute-start | bytes 393224 | tf_op jit(solution)/shard_map/ppermute | solution.py:363
  37.7 1.4 %collective-permute-done.15.piece3_ref = bf16[3,128,128]{2,1,0:T(8,128)(2,1)S(1)} collective-permute-done((bf16[3,128,128]{2,1,0:T(8,128)(2,1)S(1)}, bf16[3,128,128]{2,1,0:T(8,128)(2,1)S(1)}, u32[]{:S(2)}, u32[]{:S(2)}) %collective-permute-start.15) | collective-permute-done | bytes 98336 | tf_op jit(solution)/shard_map/ppermute | solution.py:363
  39.1 1.4 %collective-permute-done.14.piece2_ref = bf16[3,128,128]{2,1,0:T(8,128)(2,1)S(1)} collective-permute-done((bf16[3,128,128]{2,1,0:T(8,128)(2,1)S(1)}, bf16[3,128,128]{2,1,0:T(8,128)(2,1)S(1)}, u32[]{:S(2)}, u32[]{:S(2)}) %collective-permute-start.14) | collective-permute-done | bytes 98336 | tf_op jit(solution)/shard_map/ppermute | solution.py:363
  40.5 1.9 %collective-permute-done.13.piece1_ref = bf16[3,128,128]{2,1,0:T(8,128)(2,1)S(1)} collective-permute-done((bf16[3,128,128]{2,1,0:T(8,128)(2,1)S(1)}, bf16[3,128,128]{2,1,0:T(8,128)(2,1)S(1)}, u32[]{:S(2)}, u32[]{:S(2)}) %collective-permute-start.13) | collective-permute-done | bytes 98336 | tf_op jit(solution)/shard_map/ppermute | solution.py:363
  42.4 0.1 collective-permute-start.16
  42.5 1.3 %collective-permute-done.16.split_other_ref = bf16[1,4,128,128]{3,2,1,0:T(8,128)(2,1)S(1)} collective-permute-done((bf16[1,4,128,128]{3,2,1,0:T(8,128)(2,1)S(1)}, bf16[1,4,128,128]{3,2,1,0:T(8,128)(2,1)S(1)}, u32[]{:S(2)}, u32[]{:S(2)}) %collective-permute-start.16) | collective-permute-done | bytes 131104 | tf_op jit(solution)/shard_map/ppermute | solution.py:367
  43.8 2.8 %shard_map.95 = (bf16[128,1024]{1,0:T(8,128)(2,1)}, bf16[128,1024]{1,0:T(8,128)(2,1)}, bf16[128,1024]{1,0:T(8,128)(2,1)}) custom-call(s32[5]{0:T(128)S(1)} %shift-right-arithmetic_and_fusion.flag_ref, s32[1,128]{1,0:T(1,128)S(1)} %bitcast.9, f32[20,8,32]{2,1,0:T(8,128)S(1)} %bitcast.5, bf16[128,1024]{1,0:T(8,128)(2,1)S(1)} %copy-done, ...), custom_call_target="tpu_custom_call" | custom-call | flops 234881024 | bytes 3822100 | tf_op jit(solution)/shard_map/pallas_call | solution.py:383
  (26 shorter events, 0.2 us)
Async XLA Ops:
  0.6 2.9 %copy-start = (bf16[128,1024]{1,0:T(8,128)(2,1)S(1)}, bf16[128,1024]{1,0:T(8,128)(2,1)}, u32[]{:S(2)}) copy-start(bf16[128,1024]{1,0:T(8,128)(2,1)} %k_ref.5) | copy-start | bytes 786436
  0.7 2.9 %copy-start.1 = (bf16[128,1024]{1,0:T(8,128)(2,1)S(1)}, bf16[128,1024]{1,0:T(8,128)(2,1)}, u32[]{:S(2)}) copy-start(bf16[128,1024]{1,0:T(8,128)(2,1)} %v_ref.5) | copy-start | bytes 786436
  0.7 2.9 %copy-start.2 = (bf16[128,1024]{1,0:T(8,128)(2,1)S(1)}, bf16[128,1024]{1,0:T(8,128)(2,1)}, u32[]{:S(2)}) copy-start(bf16[128,1024]{1,0:T(8,128)(2,1)} %g_ref.5) | copy-start | bytes 786436
  0.7 2.8 %copy-start.3 = (bf16[128,1024]{1,0:T(8,128)(2,1)S(1)}, bf16[128,1024]{1,0:T(8,128)(2,1)}, u32[]{:S(2)}) copy-start(bf16[128,1024]{1,0:T(8,128)(2,1)} %q_ref.3) | copy-start | bytes 786436
  0.7 2.8 %copy-start.4 = (f32[32,20,8]{0,2,1:T(8,128)S(1)}, f32[32,20,8]{0,2,1:T(8,128)}, u32[]{:S(2)}) copy-start(f32[32,20,8]{0,2,1:T(8,128)} %param.11) | copy-start | bytes 61444
  3.0 0.7 %copy-start.5 = (s32[128]{0:T(128)S(1)}, s32[128]{0:T(128)}, u32[]{:S(2)}) copy-start(s32[128]{0:T(128)} %param.10) | copy-start | bytes 1540
  3.0 4.9 %collective-permute-start = (bf16[12,128,128]{2,1,0:T(8,128)(2,1)S(1)}, bf16[12,128,128]{2,1,0:T(8,128)(2,1)S(1)}, u32[]{:S(2)}, u32[]{:S(2)}) collective-permute-start(bf16[12,128,128]{2,1,0:T(8,128)(2,1)S(1)} %get-tuple-element.17), channel_id=1, source_target_pairs={{0,8},{8,0},{16,24},{24,16},{1,9},{9,1},{17,25},{25,17},{2,10},{10... | collective-permute-start | bytes 1179656 | tf_op jit(solution)/shard_map/ppermute | solution.py:367
  4.8 12.9 %collective-permute-start.2 = (bf16[12,128,128]{2,1,0:T(8,128)(2,1)S(1)}, bf16[12,128,128]{2,1,0:T(8,128)(2,1)S(1)}, u32[]{:S(2)}, u32[]{:S(2)}) collective-permute-start(bf16[12,128,128]{2,1,0:T(8,128)(2,1)S(1)} %get-tuple-element.25.sent_ref), channel_id=1, source_target_pairs={{0,1},{1,0},{2,3},{3,2},{4,5},{5,4},{6,7},{7,6},{8,9},{9,8},{10,11... | collective-permute-start | bytes 1179656 | tf_op jit(solution)/shard_map/ppermute | solution.py:363
  7.8 20.6 %collective-permute-start.1 = (bf16[8,128,128]{2,1,0:T(8,128)(2,1)S(1)}, bf16[8,128,128]{2,1,0:T(8,128)(2,1)S(1)}, u32[]{:S(2)}, u32[]{:S(2)}) collective-permute-start(bf16[8,128,128]{2,1,0:T(8,128)(2,1)S(1)} %get-tuple-element.24), channel_id=1, source_target_pairs={{0,1},{1,0},{2,3},{3,2},{4,5},{5,4},{6,7},{7,6},{8,9},{9,8},{10,11... | collective-permute-start | bytes 786440 | tf_op jit(solution)/shard_map/ppermute | solution.py:363
  8.5 13.5 %collective-permute-start.3 = (bf16[3,128,128]{2,1,0:T(8,128)(2,1)S(1)}, bf16[3,128,128]{2,1,0:T(8,128)(2,1)S(1)}, u32[]{:S(2)}, u32[]{:S(2)}) collective-permute-start(bf16[3,128,128]{2,1,0:T(8,128)(2,1)S(1)} %get-tuple-element.26), channel_id=1, source_target_pairs={{0,6},{1,7},{2,4},{3,5},{4,2},{5,3},{6,0},{7,1},{8,14},{9,15},{10,... | collective-permute-start | bytes 294920 | tf_op jit(solution)/shard_map/ppermute | solution.py:363
  12.6 9.4 %collective-permute-start.4 = (bf16[3,128,128]{2,1,0:T(8,128)(2,1)S(1)}, bf16[3,128,128]{2,1,0:T(8,128)(2,1)S(1)}, u32[]{:S(2)}, u32[]{:S(2)}) collective-permute-start(bf16[3,128,128]{2,1,0:T(8,128)(2,1)S(1)} %get-tuple-element.27), channel_id=1, source_target_pairs={{0,4},{1,5},{2,6},{3,7},{4,0},{5,1},{6,2},{7,3},{8,12},{9,13},{10,... | collective-permute-start | bytes 294920 | tf_op jit(solution)/shard_map/ppermute | solution.py:363
  12.6 9.4 %collective-permute-start.5 = (bf16[3,128,128]{2,1,0:T(8,128)(2,1)S(1)}, bf16[3,128,128]{2,1,0:T(8,128)(2,1)S(1)}, u32[]{:S(2)}, u32[]{:S(2)}) collective-permute-start(bf16[3,128,128]{2,1,0:T(8,128)(2,1)S(1)} %get-tuple-element.28), channel_id=1, source_target_pairs={{0,2},{1,3},{2,0},{3,1},{4,6},{5,7},{6,4},{7,5},{8,10},{9,11},{10,... | collective-permute-start | bytes 294920 | tf_op jit(solution)/shard_map/ppermute | solution.py:363
  17.8 7.9 %collective-permute-start.7 = (bf16[4,128,128]{2,1,0:T(8,128)(2,1)S(1)}, bf16[4,128,128]{2,1,0:T(8,128)(2,1)S(1)}, u32[]{:S(2)}, u32[]{:S(2)}) collective-permute-start(bf16[4,128,128]{2,1,0:T(8,128)(2,1)S(1)} %shard_map.91.own_ref.after_ref), channel_id=1, source_target_pairs={{0,2},{1,3},{2,0},{3,1},{4,6},{5,7},{6,4},{7,5},{8,10},{9,11},{10,... | collective-permute-start | bytes 393224 | tf_op jit(solution)/shard_map/ppermute | solution.py:363
  22.1 7.0 %collective-permute-start.10 = (bf16[2,128,128]{2,1,0:T(8,128)(2,1)S(1)}, bf16[2,128,128]{2,1,0:T(8,128)(2,1)S(1)}, u32[]{:S(2)}, u32[]{:S(2)}) collective-permute-start(bf16[2,128,128]{2,1,0:T(8,128)(2,1)S(1)} %get-tuple-element.29.after_ref.below_ref), channel_id=1, source_target_pairs={{0,1},{1,0},{2,3},{3,2},{4,5},{5,4},{6,7},{7,6},{8,9},{9,8},{10,11... | collective-permute-start | bytes 196616 | tf_op jit(solution)/shard_map/ppermute | solution.py:363
  23.7 5.3 %collective-permute-start.12 = (bf16[1,128,128]{2,1,0:T(8,128)(2,1)S(1)}, bf16[1,128,128]{2,1,0:T(8,128)(2,1)S(1)}, u32[]{:S(2)}, u32[]{:S(2)}) collective-permute-start(bf16[1,128,128]{2,1,0:T(8,128)(2,1)S(1)} %get-tuple-element.30), channel_id=1, source_target_pairs={{0,17},{1,16},{2,19},{3,18},{4,21},{5,20},{6,23},{7,22},{8,25},{9,... | collective-permute-start | bytes 98312 | tf_op jit(solution)/shard_map/ppermute | solution.py:368
  25.2 3.9 %collective-permute-start.11 = (bf16[1,128,128]{2,1,0:T(8,128)(2,1)S(1)}, bf16[1,128,128]{2,1,0:T(8,128)(2,1)S(1)}, u32[]{:S(2)}, u32[]{:S(2)}) collective-permute-start(bf16[1,128,128]{2,1,0:T(8,128)(2,1)S(1)} %get-tuple-element.30), channel_id=1, source_target_pairs={{0,16},{8,24},{16,0},{24,8},{1,17},{9,25},{17,1},{25,9},{2,18},{10... | collective-permute-start | bytes 98312 | tf_op jit(solution)/shard_map/ppermute | solution.py:367
  25.7 10.4 %collective-permute-start.8 = (bf16[4,128,128]{2,1,0:T(8,128)(2,1)S(1)}, bf16[4,128,128]{2,1,0:T(8,128)(2,1)S(1)}, u32[]{:S(2)}, u32[]{:S(2)}) collective-permute-start(bf16[4,128,128]{2,1,0:T(8,128)(2,1)S(1)} %shard_map.92.refs_0_), channel_id=1, source_target_pairs={{0,4},{1,5},{2,6},{3,7},{4,0},{5,1},{6,2},{7,3},{8,12},{9,13},{10,... | collective-permute-start | bytes 393224 | tf_op jit(solution)/shard_map/ppermute | solution.py:363
  28.5 14.0 %collective-permute-start.6 = (bf16[8,128,128]{2,1,0:T(8,128)(2,1)S(1)}, bf16[8,128,128]{2,1,0:T(8,128)(2,1)S(1)}, u32[]{:S(2)}, u32[]{:S(2)}) collective-permute-start(bf16[8,128,128]{2,1,0:T(8,128)(2,1)S(1)} %shard_map.90), channel_id=1, source_target_pairs={{0,2},{1,3},{2,0},{3,1},{4,6},{5,7},{6,4},{7,5},{8,10},{9,11},{10,... | collective-permute-start | bytes 786440 | tf_op jit(solution)/shard_map/ppermute | solution.py:363
  29.1 10.0 %collective-permute-start.15 = (bf16[3,128,128]{2,1,0:T(8,128)(2,1)S(1)}, bf16[3,128,128]{2,1,0:T(8,128)(2,1)S(1)}, u32[]{:S(2)}, u32[]{:S(2)}) collective-permute-start(bf16[3,128,128]{2,1,0:T(8,128)(2,1)S(1)} %shard_map.93.piece0_ref), channel_id=1, source_target_pairs={{0,6},{1,7},{2,4},{3,5},{4,2},{5,3},{6,0},{7,1},{8,14},{9,15},{10,... | collective-permute-start | bytes 294920 | tf_op jit(solution)/shard_map/ppermute | solution.py:363
  31.7 8.8 %collective-permute-start.14 = (bf16[3,128,128]{2,1,0:T(8,128)(2,1)S(1)}, bf16[3,128,128]{2,1,0:T(8,128)(2,1)S(1)}, u32[]{:S(2)}, u32[]{:S(2)}) collective-permute-start(bf16[3,128,128]{2,1,0:T(8,128)(2,1)S(1)} %shard_map.93.piece0_ref), channel_id=1, source_target_pairs={{0,4},{1,5},{2,6},{3,7},{4,0},{5,1},{6,2},{7,3},{8,12},{9,13},{10,... | collective-permute-start | bytes 294920 | tf_op jit(solution)/shard_map/ppermute | solution.py:363
  32.1 10.3 %collective-permute-start.13 = (bf16[3,128,128]{2,1,0:T(8,128)(2,1)S(1)}, bf16[3,128,128]{2,1,0:T(8,128)(2,1)S(1)}, u32[]{:S(2)}, u32[]{:S(2)}) collective-permute-start(bf16[3,128,128]{2,1,0:T(8,128)(2,1)S(1)} %shard_map.93.piece0_ref), channel_id=1, source_target_pairs={{0,2},{1,3},{2,0},{3,1},{4,6},{5,7},{6,4},{7,5},{8,10},{9,11},{10,... | collective-permute-start | bytes 294920 | tf_op jit(solution)/shard_map/ppermute | solution.py:363
  36.1 6.4 %collective-permute-start.9 = (bf16[4,128,128]{2,1,0:T(8,128)(2,1)S(1)}, bf16[4,128,128]{2,1,0:T(8,128)(2,1)S(1)}, u32[]{:S(2)}, u32[]{:S(2)}) collective-permute-start(bf16[4,128,128]{2,1,0:T(8,128)(2,1)S(1)} %collective-permute-done.8.after_ref.two_own_ref), channel_id=1, source_target_pairs={{0,1},{1,0},{2,3},{3,2},{4,5},{5,4},{6,7},{7,6},{8,9},{9,8},{10,11... | collective-permute-start | bytes 393224 | tf_op jit(solution)/shard_map/ppermute | solution.py:363
  42.4 1.4 %collective-permute-start.16 = (bf16[1,4,128,128]{3,2,1,0:T(8,128)(2,1)S(1)}, bf16[1,4,128,128]{3,2,1,0:T(8,128)(2,1)S(1)}, u32[]{:S(2)}, u32[]{:S(2)}) collective-permute-start(bf16[1,4,128,128]{3,2,1,0:T(8,128)(2,1)S(1)} %shard_map.94.split_own_ref), channel_id=1, source_target_pairs={{0,8},{8,0},{16,24},{24,16},{1,9},{9,1},{17,25},{25,17},{2,10},{10... | collective-permute-start | bytes 393224 | tf_op jit(solution)/shard_map/ppermute | solution.py:367

commit v10 on v9

--- a/solution.py
+++ b/solution.py
@@ -202,7 +202,7 @@
     out_ref[rows:] = narrow(wide(near_top_ref[...]) + wide(far_top_ref[...]))
 
 
-def gather_kernel(cut, piece0_ref, piece1_ref, piece2_ref, piece3_ref, after_ref, out_ref):
+def gather_kernel(cut, piece0_ref, piece1_ref, piece2_ref, piece3_ref, after_ref, local_ref, out_ref):
     for offs, piece_ref in enumerate((piece0_ref, piece1_ref, piece2_ref, piece3_ref)):
         split_levels = out_ref.shape[0]
         eighth = out_ref.shape[1] // 4
@@ -444,13 +444,6 @@
         two_sum_kernel, [vmem] * 2 + [anywhere], cells(half), (two_own, lower_seen, own_share)
     )
     big = jax.ShapeDtypeStruct((row_count, width), jnp.float32)
-    query_local, key_local, value_local = call(
-        functools.partial(local_kernel, block_depth, head_size),
-        [vmem] * 6 + [anywhere],
-        (big, big, big),
-        (class_lanes, table, query_rows, key_rows, value_rows, out_grad, own_share),
-        flops=10 * row_count * width * row_count,
-    )
 
     def z_bits(offs):
         return [bit + 1 for bit in range(2) if offs >> bit & 1]
@@ -461,7 +454,7 @@
         functools.partial(four_sum_kernel, eighth),
         [vmem, anywhere] + [vmem] * 3,
         (cells(share_rows - eighth), cells(eighth)),
-        (own_share, query_local, *came),
+        (own_share, own_share, *came),
     )
     middle = [bit for bit in range(NEAR, top) if bit != inner_bits]
     if middle:
@@ -504,12 +497,19 @@
         cells(share_rows),
         (below, swap(below, 0), swap(top_sent, top), swap(top_sent, 0, top), two_sum, zero_done),
     )
+    query_local, key_local, value_local = call(
+        functools.partial(local_kernel, block_depth, head_size),
+        [vmem] * 6 + [anywhere],
+        (big, big, big),
+        (class_lanes, table, query_rows, key_rows, value_rows, out_grad, shares),
+        flops=10 * row_count * width * row_count,
+    )
     pieces = [shares] + [swap(shares, *z_bits(offs)) for offs in (1, 2, 3)]
     split_own = call(
         functools.partial(gather_kernel, cut),
-        [vmem] * 4 + [anywhere],
+        [vmem] * 4 + [anywhere] * 2,
         cells(split_levels, half),
-        (*pieces, two_half),
+        (*pieces, two_half, query_local),
     )
     split_other = swap(split_own, inner_bits)
 

time: 46.8 us -> 45 us (0.962)
  waiting for transfers between devices: 13.1 us -> 11.4 us
    ppermute x13, waiting for transfers between devices: 11.7 us -> 10.1 us  [swap(): return lax.ppermute(block, 'gy', [(i, i ^ mask) for i in range(inner_size)])]
where the time goes in v10:
time: 45 us; the launch traced here: 44.9 us
  starting transfers between devices  23.4 us (52%)
  waiting for transfers between devices  11.4 us (25%)
  Pallas kernels  9.11 us (20%)
  between operations  0.8 us (2%)
    ppermute x13, starting transfers between devices, swap(): return lax.ppermute(block, 'gy', [(i, i ^ mask) for i in range(inner_size)])  20.8 us
    ppermute x13, waiting for transfers between devices, swap(): return lax.ppermute(block, 'gy', [(i, i ^ mask) for i in range(inner_size)])  10.1 us
    pallas_call x11, Pallas kernels, call(): pl.pallas_call(kernel, out_shape=outs, in_specs=in_specs, out_specs=out_s...  9.11 us
    ppermute x1, starting transfers between devices, swap(): lax.ppermute(block, ('gx', 'gy'), [(i, i ^ mask) for i in range(device_co...  1.49 us
    ppermute x3, waiting for transfers between devices, swap(): return lax.ppermute(block, 'gx', [(i, i ^ mask) for i in range(size)])  1.32 us
    ppermute x3, starting transfers between devices, swap(): return lax.ppermute(block, 'gx', [(i, i ^ mask) for i in range(size)])  1.14 us
  transfers between devices with their start and end apart: 17, of which 7 were waited for; matrix products, arithmetic and copies ran while one was open for 0% of the time, Pallas kernels for 9%

profile of v10, /device:TPU:0, one launch (start us, length us, event | category | flops | bytes accessed | tf_op | source)
XLA Modules:
  0.0 44.9 jit_solution(7262664494438718345)
XLA Ops:
  0.6 0.0 copy-start
  0.7 0.0 copy-start.2
  0.7 2.3 %shard_map.85 = (bf16[12,128,128]{2,1,0:T(8,128)(2,1)S(1)}, bf16[4,128,128]{2,1,0:T(8,128)(2,1)S(1)}) custom-call(s32[5]{0:T(128)S(1)} %shift-right-arithmetic_and_fusion.flag_ref, s32[1,128]{1,0:T(1,128)} %bitcast.6, f32[20,8,32]{2,1,0:T(8,128)} %bitcast.2, bf16[128,1024]{1,0:T(8,128)(2,1)} %q_ref.3, bf16[128,1024]{1,0:T(8,128)(2,1)} %k_ref.5, ...), custom_call_target="tpu_custom_call" | custom-call | flops 67108864 | bytes 1069588 | tf_op jit(solution)/shard_map/pallas_call | solution.py:383
  3.0 0.5 %collective-permute-start = (bf16[12,128,128]{2,1,0:T(8,128)(2,1)S(1)}, bf16[12,128,128]{2,1,0:T(8,128)(2,1)S(1)}, u32[]{:S(2)}, u32[]{:S(2)}) collective-permute-start(bf16[12,128,128]{2,1,0:T(8,128)(2,1)S(1)} %get-tuple-element.17), channel_id=1, source_target_pairs={{0,8},{8,0},{16,24},{24,16},{1,9},{9,1},{17,25},{25,17},{2,10},{10... | collective-permute-start | bytes 1179656 | tf_op jit(solution)/shard_map/ppermute | solution.py:367
  3.5 0.1 copy-done.5
  3.6 1.2 %shard_map.86 = (bf16[4,128,128]{2,1,0:T(8,128)(2,1)S(1)}, bf16[12,128,128]{2,1,0:T(8,128)(2,1)S(1)}, bf16[8,128,128]{2,1,0:T(8,128)(2,1)S(1)}) custom-call(s32[5]{0:T(128)S(1)} %shift-right-arithmetic_and_fusion.flag_ref, s32[1,128]{1,0:T(1,128)S(1)} %bitcast.7, f32[20,8,32]{2,1,0:T(8,128)S(1)} %bitcast.3, bf16[128,1024]{1,0:T(8,128)(2,1)S(1)} %copy-done.3, ...), custom_call_target="tpu_custom_call" | custom-call | flops 100663296 | bytes 1200660 | tf_op jit(solution)/shard_map/pallas_call | solution.py:383
  4.8 3.0 %collective-permute-start.7 = (bf16[12,128,128]{2,1,0:T(8,128)(2,1)S(1)}, bf16[12,128,128]{2,1,0:T(8,128)(2,1)S(1)}, u32[]{:S(2)}, u32[]{:S(2)}) collective-permute-start(bf16[12,128,128]{2,1,0:T(8,128)(2,1)S(1)} %get-tuple-element.26.sent_ref), channel_id=1, source_target_pairs={{0,1},{1,0},{2,3},{3,2},{4,5},{5,4},{6,7},{7,6},{8,9},{9,8},{10,11... | collective-permute-start | bytes 1179656 | tf_op jit(solution)/shard_map/ppermute | solution.py:363
  7.8 0.1 collective-permute-start.9
  7.9 0.6 %shard_map.87 = (bf16[3,128,128]{2,1,0:T(8,128)(2,1)S(1)}, bf16[3,128,128]{2,1,0:T(8,128)(2,1)S(1)}, bf16[3,128,128]{2,1,0:T(8,128)(2,1)S(1)}, bf16[3,128,128]{2,1,0:T(8,128)(2,1)S(1)}) custom-call(s32[5]{0:T(128)S(1)} %shift-right-arithmetic_and_fusion.flag_ref, bf16[12,128,128]{2,1,0:T(8,128)(2,1)S(1)} %collective-permute-done.seen_ref, ...), custom_call_target="tpu_custom_call" | custom-call | bytes 655380 | tf_op jit(solution)/shard_map/pallas_call | solution.py:383
  8.5 4.1 %collective-permute-start.1 = (bf16[3,128,128]{2,1,0:T(8,128)(2,1)S(1)}, bf16[3,128,128]{2,1,0:T(8,128)(2,1)S(1)}, u32[]{:S(2)}, u32[]{:S(2)}) collective-permute-start(bf16[3,128,128]{2,1,0:T(8,128)(2,1)S(1)} %get-tuple-element.21), channel_id=1, source_target_pairs={{0,6},{1,7},{2,4},{3,5},{4,2},{5,3},{6,0},{7,1},{8,14},{9,15},{10,... | collective-permute-start | bytes 294920 | tf_op jit(solution)/shard_map/ppermute | solution.py:363
  12.6 0.6 %collective-permute-start.3 = (bf16[3,128,128]{2,1,0:T(8,128)(2,1)S(1)}, bf16[3,128,128]{2,1,0:T(8,128)(2,1)S(1)}, u32[]{:S(2)}, u32[]{:S(2)}) collective-permute-start(bf16[3,128,128]{2,1,0:T(8,128)(2,1)S(1)} %get-tuple-element.23), channel_id=1, source_target_pairs={{0,2},{1,3},{2,0},{3,1},{4,6},{5,7},{6,4},{7,5},{8,10},{9,11},{10,... | collective-permute-start | bytes 294920 | tf_op jit(solution)/shard_map/ppermute | solution.py:363
  13.3 4.5 %collective-permute-done.7.seen_ref = bf16[12,128,128]{2,1,0:T(8,128)(2,1)S(1)} collective-permute-done((bf16[12,128,128]{2,1,0:T(8,128)(2,1)S(1)}, bf16[12,128,128]{2,1,0:T(8,128)(2,1)S(1)}, u32[]{:S(2)}, u32[]{:S(2)}) %collective-permute-start.7) | collective-permute-done | bytes 393248 | tf_op jit(solution)/shard_map/ppermute | solution.py:363
  17.8 2.2 %collective-permute-start.8 = (bf16[4,128,128]{2,1,0:T(8,128)(2,1)S(1)}, bf16[4,128,128]{2,1,0:T(8,128)(2,1)S(1)}, u32[]{:S(2)}, u32[]{:S(2)}) collective-permute-start(bf16[4,128,128]{2,1,0:T(8,128)(2,1)S(1)} %shard_map.89.own_ref.after_ref), channel_id=1, source_target_pairs={{0,2},{1,3},{2,0},{3,1},{4,6},{5,7},{6,4},{7,5},{8,10},{9,11},{10,... | collective-permute-start | bytes 393224 | tf_op jit(solution)/shard_map/ppermute | solution.py:363
  20.0 0.6 %collective-permute-done.2.refs_1_ = bf16[3,128,128]{2,1,0:T(8,128)(2,1)S(1)} collective-permute-done((bf16[3,128,128]{2,1,0:T(8,128)(2,1)S(1)}, bf16[3,128,128]{2,1,0:T(8,128)(2,1)S(1)}, u32[]{:S(2)}, u32[]{:S(2)}) %collective-permute-start.2) | collective-permute-done | bytes 98336 | tf_op jit(solution)/shard_map/ppermute | solution.py:363
  20.6 0.1 shard_map.88
  20.6 1.5 %collective-permute-start.4 = (bf16[2,128,128]{2,1,0:T(8,128)(2,1)S(1)}, bf16[2,128,128]{2,1,0:T(8,128)(2,1)S(1)}, u32[]{:S(2)}, u32[]{:S(2)}) collective-permute-start(bf16[2,128,128]{2,1,0:T(8,128)(2,1)S(1)} %get-tuple-element.24.below_ref.after_ref), channel_id=1, source_target_pairs={{0,1},{1,0},{2,3},{3,2},{4,5},{5,4},{6,7},{7,6},{8,9},{9,8},{10,11... | collective-permute-start | bytes 196616 | tf_op jit(solution)/shard_map/ppermute | solution.py:363
  22.1 1.5 %collective-permute-start.6 = (bf16[1,128,128]{2,1,0:T(8,128)(2,1)S(1)}, bf16[1,128,128]{2,1,0:T(8,128)(2,1)S(1)}, u32[]{:S(2)}, u32[]{:S(2)}) collective-permute-start(bf16[1,128,128]{2,1,0:T(8,128)(2,1)S(1)} %get-tuple-element.25), channel_id=1, source_target_pairs={{0,17},{1,16},{2,19},{3,18},{4,21},{5,20},{6,23},{7,22},{8,25},{9,... | collective-permute-start | bytes 98312 | tf_op jit(solution)/shard_map/ppermute | solution.py:368
  23.6 0.5 %collective-permute-start.5 = (bf16[1,128,128]{2,1,0:T(8,128)(2,1)S(1)}, bf16[1,128,128]{2,1,0:T(8,128)(2,1)S(1)}, u32[]{:S(2)}, u32[]{:S(2)}) collective-permute-start(bf16[1,128,128]{2,1,0:T(8,128)(2,1)S(1)} %get-tuple-element.25), channel_id=1, source_target_pairs={{0,16},{8,24},{16,0},{24,8},{1,17},{9,25},{17,1},{25,9},{2,18},{10... | collective-permute-start | bytes 98312 | tf_op jit(solution)/shard_map/ppermute | solution.py:367
  24.2 2.1 %collective-permute-start.11 = (bf16[4,128,128]{2,1,0:T(8,128)(2,1)S(1)}, bf16[4,128,128]{2,1,0:T(8,128)(2,1)S(1)}, u32[]{:S(2)}, u32[]{:S(2)}) collective-permute-start(bf16[4,128,128]{2,1,0:T(8,128)(2,1)S(1)} %shard_map.90.refs_0_), channel_id=1, source_target_pairs={{0,4},{1,5},{2,6},{3,7},{4,0},{5,1},{6,2},{7,3},{8,12},{9,13},{10,... | collective-permute-start | bytes 393224 | tf_op jit(solution)/shard_map/ppermute | solution.py:363
  26.3 0.1 shard_map.93
  26.4 1.4 %collective-permute-start.10 = (bf16[8,128,128]{2,1,0:T(8,128)(2,1)S(1)}, bf16[8,128,128]{2,1,0:T(8,128)(2,1)S(1)}, u32[]{:S(2)}, u32[]{:S(2)}) collective-permute-start(bf16[8,128,128]{2,1,0:T(8,128)(2,1)S(1)} %shard_map.93), channel_id=1, source_target_pairs={{0,2},{1,3},{2,0},{3,1},{4,6},{5,7},{6,4},{7,5},{8,10},{9,11},{10,... | collective-permute-start | bytes 786440 | tf_op jit(solution)/shard_map/ppermute | solution.py:363
  27.9 2.3 %collective-permute-start.15 = (bf16[3,128,128]{2,1,0:T(8,128)(2,1)S(1)}, bf16[3,128,128]{2,1,0:T(8,128)(2,1)S(1)}, u32[]{:S(2)}, u32[]{:S(2)}) collective-permute-start(bf16[3,128,128]{2,1,0:T(8,128)(2,1)S(1)} %shard_map.91.after_ref.piece0_ref), channel_id=1, source_target_pairs={{0,6},{1,7},{2,4},{3,5},{4,2},{5,3},{6,0},{7,1},{8,14},{9,15},{10,... | collective-permute-start | bytes 294920 | tf_op jit(solution)/shard_map/ppermute | solution.py:363
  30.1 2.2 %collective-permute-start.13 = (bf16[3,128,128]{2,1,0:T(8,128)(2,1)S(1)}, bf16[3,128,128]{2,1,0:T(8,128)(2,1)S(1)}, u32[]{:S(2)}, u32[]{:S(2)}) collective-permute-start(bf16[3,128,128]{2,1,0:T(8,128)(2,1)S(1)} %shard_map.91.after_ref.piece0_ref), channel_id=1, source_target_pairs={{0,2},{1,3},{2,0},{3,1},{4,6},{5,7},{6,4},{7,5},{8,10},{9,11},{10,... | collective-permute-start | bytes 294920 | tf_op jit(solution)/shard_map/ppermute | solution.py:363
  32.3 2.0 %shard_map.92 = (f32[128,1024]{1,0:T(8,128)S(1)}, f32[128,1024]{1,0:T(8,128)S(1)}, f32[128,1024]{1,0:T(8,128)S(1)}) custom-call(s32[1,128]{1,0:T(1,128)S(1)} %bitcast.8, f32[20,8,32]{2,1,0:T(8,128)S(1)} %bitcast.4, bf16[128,1024]{1,0:T(8,128)(2,1)S(1)} %copy-done.3, bf16[128,1024]{1,0:T(8,128)(2,1)S(1)} %copy-done, bf16[128,1024]{1,0:T(8,128)(2,1)S(1)} %copy-done.1, ...), custom_call_target="tpu_custom_call" | custom-call | flops 167772160 | bytes 1167872 | tf_op jit(solution)/shard_map/pallas_call | solution.py:383
  34.3 0.4 collective-permute-done.11.after_ref.two_own_ref
  34.7 1.3 %collective-permute-start.12 = (bf16[4,128,128]{2,1,0:T(8,128)(2,1)S(1)}, bf16[4,128,128]{2,1,0:T(8,128)(2,1)S(1)}, u32[]{:S(2)}, u32[]{:S(2)}) collective-permute-start(bf16[4,128,128]{2,1,0:T(8,128)(2,1)S(1)} %collective-permute-done.11.after_ref.two_own_ref), channel_id=1, source_target_pairs={{0,1},{1,0},{2,3},{3,2},{4,5},{5,4},{6,7},{7,6},{8,9},{9,8},{10,11... | collective-permute-start | bytes 393224 | tf_op jit(solution)/shard_map/ppermute | solution.py:363
  36.0 2.7 %collective-permute-done.15.piece3_ref = bf16[3,128,128]{2,1,0:T(8,128)(2,1)S(1)} collective-permute-done((bf16[3,128,128]{2,1,0:T(8,128)(2,1)S(1)}, bf16[3,128,128]{2,1,0:T(8,128)(2,1)S(1)}, u32[]{:S(2)}, u32[]{:S(2)}) %collective-permute-start.15) | collective-permute-done | bytes 98336 | tf_op jit(solution)/shard_map/ppermute | solution.py:363
  38.7 1.2 %collective-permute-done.14.piece2_ref = bf16[3,128,128]{2,1,0:T(8,128)(2,1)S(1)} collective-permute-done((bf16[3,128,128]{2,1,0:T(8,128)(2,1)S(1)}, bf16[3,128,128]{2,1,0:T(8,128)(2,1)S(1)}, u32[]{:S(2)}, u32[]{:S(2)}) %collective-permute-start.14) | collective-permute-done | bytes 98336 | tf_op jit(solution)/shard_map/ppermute | solution.py:363
  39.9 0.7 %collective-permute-done.13.piece1_ref = bf16[3,128,128]{2,1,0:T(8,128)(2,1)S(1)} collective-permute-done((bf16[3,128,128]{2,1,0:T(8,128)(2,1)S(1)}, bf16[3,128,128]{2,1,0:T(8,128)(2,1)S(1)}, u32[]{:S(2)}, u32[]{:S(2)}) %collective-permute-start.13) | collective-permute-done | bytes 98336 | tf_op jit(solution)/shard_map/ppermute | solution.py:363
  40.6 0.1 collective-permute-start.16
  40.7 1.3 %collective-permute-done.16.split_other_ref = bf16[1,4,128,128]{3,2,1,0:T(8,128)(2,1)S(1)} collective-permute-done((bf16[1,4,128,128]{3,2,1,0:T(8,128)(2,1)S(1)}, bf16[1,4,128,128]{3,2,1,0:T(8,128)(2,1)S(1)}, u32[]{:S(2)}, u32[]{:S(2)}) %collective-permute-start.16) | collective-permute-done | bytes 131104 | tf_op jit(solution)/shard_map/ppermute | solution.py:367
  42.1 2.8 %shard_map.95 = (bf16[128,1024]{1,0:T(8,128)(2,1)}, bf16[128,1024]{1,0:T(8,128)(2,1)}, bf16[128,1024]{1,0:T(8,128)(2,1)}) custom-call(s32[5]{0:T(128)S(1)} %shift-right-arithmetic_and_fusion.flag_ref, s32[1,128]{1,0:T(1,128)S(1)} %bitcast.9, f32[20,8,32]{2,1,0:T(8,128)S(1)} %bitcast.5, bf16[128,1024]{1,0:T(8,128)(2,1)S(1)} %copy-done, ...), custom_call_target="tpu_custom_call" | custom-call | flops 234881024 | bytes 3822100 | tf_op jit(solution)/shard_map/pallas_call | solution.py:383
  (26 shorter events, 0.2 us)
Async XLA Ops:
  0.6 2.9 %copy-start = (bf16[128,1024]{1,0:T(8,128)(2,1)S(1)}, bf16[128,1024]{1,0:T(8,128)(2,1)}, u32[]{:S(2)}) copy-start(bf16[128,1024]{1,0:T(8,128)(2,1)} %k_ref.5) | copy-start | bytes 786436
  0.7 2.9 %copy-start.1 = (bf16[128,1024]{1,0:T(8,128)(2,1)S(1)}, bf16[128,1024]{1,0:T(8,128)(2,1)}, u32[]{:S(2)}) copy-start(bf16[128,1024]{1,0:T(8,128)(2,1)} %v_ref.5) | copy-start | bytes 786436
  0.7 2.9 %copy-start.2 = (bf16[128,1024]{1,0:T(8,128)(2,1)S(1)}, bf16[128,1024]{1,0:T(8,128)(2,1)}, u32[]{:S(2)}) copy-start(bf16[128,1024]{1,0:T(8,128)(2,1)} %g_ref.5) | copy-start | bytes 786436
  0.7 2.8 %copy-start.3 = (bf16[128,1024]{1,0:T(8,128)(2,1)S(1)}, bf16[128,1024]{1,0:T(8,128)(2,1)}, u32[]{:S(2)}) copy-start(bf16[128,1024]{1,0:T(8,128)(2,1)} %q_ref.3) | copy-start | bytes 786436
  0.7 2.8 %copy-start.4 = (f32[32,20,8]{0,2,1:T(8,128)S(1)}, f32[32,20,8]{0,2,1:T(8,128)}, u32[]{:S(2)}) copy-start(f32[32,20,8]{0,2,1:T(8,128)} %param.11) | copy-start | bytes 61444
  3.0 0.7 %copy-start.5 = (s32[128]{0:T(128)S(1)}, s32[128]{0:T(128)}, u32[]{:S(2)}) copy-start(s32[128]{0:T(128)} %param.10) | copy-start | bytes 1540
  3.0 4.9 %collective-permute-start = (bf16[12,128,128]{2,1,0:T(8,128)(2,1)S(1)}, bf16[12,128,128]{2,1,0:T(8,128)(2,1)S(1)}, u32[]{:S(2)}, u32[]{:S(2)}) collective-permute-start(bf16[12,128,128]{2,1,0:T(8,128)(2,1)S(1)} %get-tuple-element.17), channel_id=1, source_target_pairs={{0,8},{8,0},{16,24},{24,16},{1,9},{9,1},{17,25},{25,17},{2,10},{10... | collective-permute-start | bytes 1179656 | tf_op jit(solution)/shard_map/ppermute | solution.py:367
  4.8 12.9 %collective-permute-start.7 = (bf16[12,128,128]{2,1,0:T(8,128)(2,1)S(1)}, bf16[12,128,128]{2,1,0:T(8,128)(2,1)S(1)}, u32[]{:S(2)}, u32[]{:S(2)}) collective-permute-start(bf16[12,128,128]{2,1,0:T(8,128)(2,1)S(1)} %get-tuple-element.26.sent_ref), channel_id=1, source_target_pairs={{0,1},{1,0},{2,3},{3,2},{4,5},{5,4},{6,7},{7,6},{8,9},{9,8},{10,11... | collective-permute-start | bytes 1179656 | tf_op jit(solution)/shard_map/ppermute | solution.py:363
  7.8 18.6 %collective-permute-start.9 = (bf16[8,128,128]{2,1,0:T(8,128)(2,1)S(1)}, bf16[8,128,128]{2,1,0:T(8,128)(2,1)S(1)}, u32[]{:S(2)}, u32[]{:S(2)}) collective-permute-start(bf16[8,128,128]{2,1,0:T(8,128)(2,1)S(1)} %get-tuple-element.27), channel_id=1, source_target_pairs={{0,1},{1,0},{2,3},{3,2},{4,5},{5,4},{6,7},{7,6},{8,9},{9,8},{10,11... | collective-permute-start | bytes 786440 | tf_op jit(solution)/shard_map/ppermute | solution.py:363
  8.5 11.5 %collective-permute-start.1 = (bf16[3,128,128]{2,1,0:T(8,128)(2,1)S(1)}, bf16[3,128,128]{2,1,0:T(8,128)(2,1)S(1)}, u32[]{:S(2)}, u32[]{:S(2)}) collective-permute-start(bf16[3,128,128]{2,1,0:T(8,128)(2,1)S(1)} %get-tuple-element.21), channel_id=1, source_target_pairs={{0,6},{1,7},{2,4},{3,5},{4,2},{5,3},{6,0},{7,1},{8,14},{9,15},{10,... | collective-permute-start | bytes 294920 | tf_op jit(solution)/shard_map/ppermute | solution.py:363
  12.6 7.9 %collective-permute-start.2 = (bf16[3,128,128]{2,1,0:T(8,128)(2,1)S(1)}, bf16[3,128,128]{2,1,0:T(8,128)(2,1)S(1)}, u32[]{:S(2)}, u32[]{:S(2)}) collective-permute-start(bf16[3,128,128]{2,1,0:T(8,128)(2,1)S(1)} %get-tuple-element.22), channel_id=1, source_target_pairs={{0,4},{1,5},{2,6},{3,7},{4,0},{5,1},{6,2},{7,3},{8,12},{9,13},{10,... | collective-permute-start | bytes 294920 | tf_op jit(solution)/shard_map/ppermute | solution.py:363
  12.6 7.9 %collective-permute-start.3 = (bf16[3,128,128]{2,1,0:T(8,128)(2,1)S(1)}, bf16[3,128,128]{2,1,0:T(8,128)(2,1)S(1)}, u32[]{:S(2)}, u32[]{:S(2)}) collective-permute-start(bf16[3,128,128]{2,1,0:T(8,128)(2,1)S(1)} %get-tuple-element.23), channel_id=1, source_target_pairs={{0,2},{1,3},{2,0},{3,1},{4,6},{5,7},{6,4},{7,5},{8,10},{9,11},{10,... | collective-permute-start | bytes 294920 | tf_op jit(solution)/shard_map/ppermute | solution.py:363
  17.8 6.4 %collective-permute-start.8 = (bf16[4,128,128]{2,1,0:T(8,128)(2,1)S(1)}, bf16[4,128,128]{2,1,0:T(8,128)(2,1)S(1)}, u32[]{:S(2)}, u32[]{:S(2)}) collective-permute-start(bf16[4,128,128]{2,1,0:T(8,128)(2,1)S(1)} %shard_map.89.own_ref.after_ref), channel_id=1, source_target_pairs={{0,2},{1,3},{2,0},{3,1},{4,6},{5,7},{6,4},{7,5},{8,10},{9,11},{10,... | collective-permute-start | bytes 393224 | tf_op jit(solution)/shard_map/ppermute | solution.py:363
  20.6 7.2 %collective-permute-start.4 = (bf16[2,128,128]{2,1,0:T(8,128)(2,1)S(1)}, bf16[2,128,128]{2,1,0:T(8,128)(2,1)S(1)}, u32[]{:S(2)}, u32[]{:S(2)}) collective-permute-start(bf16[2,128,128]{2,1,0:T(8,128)(2,1)S(1)} %get-tuple-element.24.below_ref.after_ref), channel_id=1, source_target_pairs={{0,1},{1,0},{2,3},{3,2},{4,5},{5,4},{6,7},{7,6},{8,9},{9,8},{10,11... | collective-permute-start | bytes 196616 | tf_op jit(solution)/shard_map/ppermute | solution.py:363
  22.1 5.7 %collective-permute-start.6 = (bf16[1,128,128]{2,1,0:T(8,128)(2,1)S(1)}, bf16[1,128,128]{2,1,0:T(8,128)(2,1)S(1)}, u32[]{:S(2)}, u32[]{:S(2)}) collective-permute-start(bf16[1,128,128]{2,1,0:T(8,128)(2,1)S(1)} %get-tuple-element.25), channel_id=1, source_target_pairs={{0,17},{1,16},{2,19},{3,18},{4,21},{5,20},{6,23},{7,22},{8,25},{9,... | collective-permute-start | bytes 98312 | tf_op jit(solution)/shard_map/ppermute | solution.py:368
  23.6 4.2 %collective-permute-start.5 = (bf16[1,128,128]{2,1,0:T(8,128)(2,1)S(1)}, bf16[1,128,128]{2,1,0:T(8,128)(2,1)S(1)}, u32[]{:S(2)}, u32[]{:S(2)}) collective-permute-start(bf16[1,128,128]{2,1,0:T(8,128)(2,1)S(1)} %get-tuple-element.25), channel_id=1, source_target_pairs={{0,16},{8,24},{16,0},{24,8},{1,17},{9,25},{17,1},{25,9},{2,18},{10... | collective-permute-start | bytes 98312 | tf_op jit(solution)/shard_map/ppermute | solution.py:367
  24.2 10.5 %collective-permute-start.11 = (bf16[4,128,128]{2,1,0:T(8,128)(2,1)S(1)}, bf16[4,128,128]{2,1,0:T(8,128)(2,1)S(1)}, u32[]{:S(2)}, u32[]{:S(2)}) collective-permute-start(bf16[4,128,128]{2,1,0:T(8,128)(2,1)S(1)} %shard_map.90.refs_0_), channel_id=1, source_target_pairs={{0,4},{1,5},{2,6},{3,7},{4,0},{5,1},{6,2},{7,3},{8,12},{9,13},{10,... | collective-permute-start | bytes 393224 | tf_op jit(solution)/shard_map/ppermute | solution.py:363
  26.4 14.3 %collective-permute-start.10 = (bf16[8,128,128]{2,1,0:T(8,128)(2,1)S(1)}, bf16[8,128,128]{2,1,0:T(8,128)(2,1)S(1)}, u32[]{:S(2)}, u32[]{:S(2)}) collective-permute-start(bf16[8,128,128]{2,1,0:T(8,128)(2,1)S(1)} %shard_map.93), channel_id=1, source_target_pairs={{0,2},{1,3},{2,0},{3,1},{4,6},{5,7},{6,4},{7,5},{8,10},{9,11},{10,... | collective-permute-start | bytes 786440 | tf_op jit(solution)/shard_map/ppermute | solution.py:363
  27.9 10.9 %collective-permute-start.15 = (bf16[3,128,128]{2,1,0:T(8,128)(2,1)S(1)}, bf16[3,128,128]{2,1,0:T(8,128)(2,1)S(1)}, u32[]{:S(2)}, u32[]{:S(2)}) collective-permute-start(bf16[3,128,128]{2,1,0:T(8,128)(2,1)S(1)} %shard_map.91.after_ref.piece0_ref), channel_id=1, source_target_pairs={{0,6},{1,7},{2,4},{3,5},{4,2},{5,3},{6,0},{7,1},{8,14},{9,15},{10,... | collective-permute-start | bytes 294920 | tf_op jit(solution)/shard_map/ppermute | solution.py:363
  30.1 9.8 %collective-permute-start.14 = (bf16[3,128,128]{2,1,0:T(8,128)(2,1)S(1)}, bf16[3,128,128]{2,1,0:T(8,128)(2,1)S(1)}, u32[]{:S(2)}, u32[]{:S(2)}) collective-permute-start(bf16[3,128,128]{2,1,0:T(8,128)(2,1)S(1)} %shard_map.91.after_ref.piece0_ref), channel_id=1, source_target_pairs={{0,4},{1,5},{2,6},{3,7},{4,0},{5,1},{6,2},{7,3},{8,12},{9,13},{10,... | collective-permute-start | bytes 294920 | tf_op jit(solution)/shard_map/ppermute | solution.py:363
  30.1 10.5 %collective-permute-start.13 = (bf16[3,128,128]{2,1,0:T(8,128)(2,1)S(1)}, bf16[3,128,128]{2,1,0:T(8,128)(2,1)S(1)}, u32[]{:S(2)}, u32[]{:S(2)}) collective-permute-start(bf16[3,128,128]{2,1,0:T(8,128)(2,1)S(1)} %shard_map.91.after_ref.piece0_ref), channel_id=1, source_target_pairs={{0,2},{1,3},{2,0},{3,1},{4,6},{5,7},{6,4},{7,5},{8,10},{9,11},{10,... | collective-permute-start | bytes 294920 | tf_op jit(solution)/shard_map/ppermute | solution.py:363
  34.7 6.0 %collective-permute-start.12 = (bf16[4,128,128]{2,1,0:T(8,128)(2,1)S(1)}, bf16[4,128,128]{2,1,0:T(8,128)(2,1)S(1)}, u32[]{:S(2)}, u32[]{:S(2)}) collective-permute-start(bf16[4,128,128]{2,1,0:T(8,128)(2,1)S(1)} %collective-permute-done.11.after_ref.two_own_ref), channel_id=1, source_target_pairs={{0,1},{1,0},{2,3},{3,2},{4,5},{5,4},{6,7},{7,6},{8,9},{9,8},{10,11... | collective-permute-start | bytes 393224 | tf_op jit(solution)/shard_map/ppermute | solution.py:363
  40.6 1.4 %collective-permute-start.16 = (bf16[1,4,128,128]{3,2,1,0:T(8,128)(2,1)S(1)}, bf16[1,4,128,128]{3,2,1,0:T(8,128)(2,1)S(1)}, u32[]{:S(2)}, u32[]{:S(2)}) collective-permute-start(bf16[1,4,128,128]{3,2,1,0:T(8,128)(2,1)S(1)} %shard_map.94.split_own_ref), channel_id=1, source_target_pairs={{0,8},{8,0},{16,24},{24,16},{1,9},{9,1},{17,25},{25,17},{2,10},{10... | collective-permute-start | bytes 393224 | tf_op jit(solution)/shard_map/ppermute | solution.py:367

commit v11 on v10

--- a/solution.py
+++ b/solution.py
@@ -211,8 +211,23 @@
             out_ref[level, offs * eighth : (offs + 1) * eighth] = piece_ref[first : first + eighth]
 
 
-def two_sum_kernel(own_ref, seen_ref, after_ref, two_ref):
-    two_ref[...] = narrow(wide(own_ref[...]) + wide(seen_ref[: own_ref.shape[0]]))
+def two_sum_kernel(flag_ref, own_ref, seen_ref, after_ref, near_ref, far_ref):
+    rows = near_ref.shape[0]
+    place = flag_ref[1]
+    for out_ref, part in ((near_ref, place), (far_ref, 1 - place)):
+        cells = pl.ds(part * rows, rows)
+        out_ref[...] = narrow(wide(own_ref[cells]) + wide(seen_ref[cells]))
+
+
+def cross_kernel(near_ref, far_ref, out_ref):
+    out_ref[...] = narrow(wide(near_ref[...]) + wide(far_ref[...]))
+
+
+def join_kernel(flag_ref, own_ref, other_ref, out_ref):
+    rows = own_ref.shape[0]
+    place = flag_ref[1]
+    out_ref[pl.ds(place * rows, rows)] = own_ref[...]
+    out_ref[pl.ds((1 - place) * rows, rows)] = other_ref[...]
 
 
 def one_sum_kernel(sent_ref, seen_ref, after_ref, one_ref):
@@ -440,8 +455,14 @@
         (flag_bits, seen, keep, two_own, *lead),
     )
     lower_seen = swap(lower_sent, 0)
-    two_sum = call(
-        two_sum_kernel, [vmem] * 2 + [anywhere], cells(half), (two_own, lower_seen, own_share)
+    two_near, two_far = call(
+        two_sum_kernel,
+        [smem] + [vmem] * 2 + [anywhere],
+        (cells(quarter), cells(quarter)),
+        (flag_bits, two_own, lower_seen, own_share),
+    )
+    two_cross = call(
+        cross_kernel, [vmem] * 2, cells(quarter), (swap(two_near, 2), swap(two_far, 1, 2))
     )
     big = jax.ShapeDtypeStruct((row_count, width), jnp.float32)
 
@@ -484,10 +505,12 @@
         cells(head_count),
         (lower_sent, lower_seen, below),
     )
-    two_sum = call(
-        two_sum_kernel, [vmem] * 2 + [anywhere], cells(half), (two_sum, swap(two_sum, 1), two_sum)
-    )
-    two_half = swap(two_sum, 2)
+    two_half = call(
+        join_kernel,
+        [smem] + [vmem] * 2,
+        cells(half),
+        (flag_bits, two_cross, swap(two_cross, 1)),
+    )
     two_rest = swap(two_half, 0)
     one_done = swap(one_sum, 1)
     zero_done = swap(zero, 0)
@@ -495,7 +518,7 @@
         pair_sum_kernel,
         [vmem] * 4 + [anywhere] * 2,
         cells(share_rows),
-        (below, swap(below, 0), swap(top_sent, top), swap(top_sent, 0, top), two_sum, zero_done),
+        (below, swap(below, 0), swap(top_sent, top), swap(top_sent, 0, top), two_cross, zero_done),
     )
     query_local, key_local, value_local = call(
         functools.partial(local_kernel, block_depth, head_size),

time: 45 us -> 50.2 us (1.12)
  waiting for transfers between devices: 11.4 us -> 15.4 us
  Pallas kernels: 9.11 us -> 10.2 us
    ppermute x13 -> x14, waiting for transfers between devices: 10.1 us -> 13.1 us  [swap(): return lax.ppermute(block, 'gy', [(i, i ^ mask) for i in range(inner_size)])]
    ppermute x1, waiting for transfers between devices: 0.01 us -> 1.63 us  [swap(): lax.ppermute(block, ('gx', 'gy'), [(i, i ^ mask) for i in range(device_co...]
    pallas_call x11 -> x12, Pallas kernels: 9.11 us -> 10.2 us  [call(): pl.pallas_call(kernel, out_shape=outs, in_specs=in_specs, out_specs=out_s...]
    ppermute x3, starting transfers between devices: 1.14 us -> 1.89 us  [swap(): return lax.ppermute(block, 'gx', [(i, i ^ mask) for i in range(size)])]
    ppermute x13 -> x14, starting transfers between devices: 20.8 us -> 20.1 us  [swap(): return lax.ppermute(block, 'gy', [(i, i ^ mask) for i in range(inner_size)])]
    ppermute x3, waiting for transfers between devices: 1.32 us -> 0.62 us  [swap(): return lax.ppermute(block, 'gx', [(i, i ^ mask) for i in range(size)])]
  transfers between devices with their start and end apart: 17 -> 18, of which waited for: 7 -> 6; matrix products, arithmetic and copies ran while one was open for 0% -> 0% of each run, Pallas kernels for 9% -> 10%
where the time goes in v11:
time: 50.2 us; the launch traced here: 50 us
  starting transfers between devices  23.5 us (47%)
  waiting for transfers between devices  15.4 us (31%)
  Pallas kernels  10.2 us (20%)
  between operations  0.82 us (2%)
    ppermute x14, starting transfers between devices, swap(): return lax.ppermute(block, 'gy', [(i, i ^ mask) for i in range(inner_size)])  20.1 us
    ppermute x14, waiting for transfers between devices, swap(): return lax.ppermute(block, 'gy', [(i, i ^ mask) for i in range(inner_size)])  13.1 us
    pallas_call x12, Pallas kernels, call(): pl.pallas_call(kernel, out_shape=outs, in_specs=in_specs, out_specs=out_s...  10.2 us
    ppermute x3, starting transfers between devices, swap(): return lax.ppermute(block, 'gx', [(i, i ^ mask) for i in range(size)])  1.89 us
    ppermute x1, waiting for transfers between devices, swap(): lax.ppermute(block, ('gx', 'gy'), [(i, i ^ mask) for i in range(device_co...  1.63 us
    ppermute x1, starting transfers between devices, swap(): lax.ppermute(block, ('gx', 'gy'), [(i, i ^ mask) for i in range(device_co...  1.49 us
  transfers between devices with their start and end apart: 18, of which 6 were waited for; matrix products, arithmetic and copies ran while one was open for 0% of the time, Pallas kernels for 10%

profile of v11, /device:TPU:0, one launch (start us, length us, event | category | flops | bytes accessed | tf_op | source)
XLA Modules:
  0.0 50.0 jit_solution(16507770495833584525)
XLA Ops:
  0.7 2.3 %shard_map.85 = (bf16[12,128,128]{2,1,0:T(8,128)(2,1)S(1)}, bf16[4,128,128]{2,1,0:T(8,128)(2,1)S(1)}) custom-call(s32[5]{0:T(128)S(1)} %shift-right-arithmetic_and_fusion.flag_ref, s32[1,128]{1,0:T(1,128)} %bitcast.6, f32[20,8,32]{2,1,0:T(8,128)} %bitcast.2, bf16[128,1024]{1,0:T(8,128)(2,1)} %q_ref.3, bf16[128,1024]{1,0:T(8,128)(2,1)} %k_ref.5, ...), custom_call_target="tpu_custom_call" | custom-call | flops 67108864 | bytes 1069588 | tf_op jit(solution)/shard_map/pallas_call | solution.py:398
  3.0 0.5 %collective-permute-start = (bf16[12,128,128]{2,1,0:T(8,128)(2,1)S(1)}, bf16[12,128,128]{2,1,0:T(8,128)(2,1)S(1)}, u32[]{:S(2)}, u32[]{:S(2)}) collective-permute-start(bf16[12,128,128]{2,1,0:T(8,128)(2,1)S(1)} %get-tuple-element.19), channel_id=1, source_target_pairs={{0,8},{8,0},{16,24},{24,16},{1,9},{9,1},{17,25},{25,17},{2,10},{10... | collective-permute-start | bytes 1179656 | tf_op jit(solution)/shard_map/ppermute | solution.py:382
  3.5 0.1 copy-done.5
  3.6 1.2 %shard_map.86 = (bf16[4,128,128]{2,1,0:T(8,128)(2,1)S(1)}, bf16[12,128,128]{2,1,0:T(8,128)(2,1)S(1)}, bf16[8,128,128]{2,1,0:T(8,128)(2,1)S(1)}) custom-call(s32[5]{0:T(128)S(1)} %shift-right-arithmetic_and_fusion.flag_ref, s32[1,128]{1,0:T(1,128)S(1)} %bitcast.7, f32[20,8,32]{2,1,0:T(8,128)S(1)} %bitcast.3, bf16[128,1024]{1,0:T(8,128)(2,1)S(1)} %copy-done.3, ...), custom_call_target="tpu_custom_call" | custom-call | flops 100663296 | bytes 1200660 | tf_op jit(solution)/shard_map/pallas_call | solution.py:398
  4.8 3.0 %collective-permute-start.7 = (bf16[12,128,128]{2,1,0:T(8,128)(2,1)S(1)}, bf16[12,128,128]{2,1,0:T(8,128)(2,1)S(1)}, u32[]{:S(2)}, u32[]{:S(2)}) collective-permute-start(bf16[12,128,128]{2,1,0:T(8,128)(2,1)S(1)} %get-tuple-element.28.sent_ref), channel_id=1, source_target_pairs={{0,1},{1,0},{2,3},{3,2},{4,5},{5,4},{6,7},{7,6},{8,9},{9,8},{10,11... | collective-permute-start | bytes 1179656 | tf_op jit(solution)/shard_map/ppermute | solution.py:378
  7.8 0.1 collective-permute-start.10
  7.9 0.6 %shard_map.87 = (bf16[3,128,128]{2,1,0:T(8,128)(2,1)S(1)}, bf16[3,128,128]{2,1,0:T(8,128)(2,1)S(1)}, bf16[3,128,128]{2,1,0:T(8,128)(2,1)S(1)}, bf16[3,128,128]{2,1,0:T(8,128)(2,1)S(1)}) custom-call(s32[5]{0:T(128)S(1)} %shift-right-arithmetic_and_fusion.flag_ref, bf16[12,128,128]{2,1,0:T(8,128)(2,1)S(1)} %collective-permute-done.seen_ref, ...), custom_call_target="tpu_custom_call" | custom-call | bytes 655380 | tf_op jit(solution)/shard_map/pallas_call | solution.py:398
  8.5 4.1 %collective-permute-start.1 = (bf16[3,128,128]{2,1,0:T(8,128)(2,1)S(1)}, bf16[3,128,128]{2,1,0:T(8,128)(2,1)S(1)}, u32[]{:S(2)}, u32[]{:S(2)}) collective-permute-start(bf16[3,128,128]{2,1,0:T(8,128)(2,1)S(1)} %get-tuple-element.23), channel_id=1, source_target_pairs={{0,6},{1,7},{2,4},{3,5},{4,2},{5,3},{6,0},{7,1},{8,14},{9,15},{10,... | collective-permute-start | bytes 294920 | tf_op jit(solution)/shard_map/ppermute | solution.py:378
  12.6 0.6 %collective-permute-start.3 = (bf16[3,128,128]{2,1,0:T(8,128)(2,1)S(1)}, bf16[3,128,128]{2,1,0:T(8,128)(2,1)S(1)}, u32[]{:S(2)}, u32[]{:S(2)}) collective-permute-start(bf16[3,128,128]{2,1,0:T(8,128)(2,1)S(1)} %get-tuple-element.25), channel_id=1, source_target_pairs={{0,2},{1,3},{2,0},{3,1},{4,6},{5,7},{6,4},{7,5},{8,10},{9,11},{10,... | collective-permute-start | bytes 294920 | tf_op jit(solution)/shard_map/ppermute | solution.py:378
  13.3 4.5 %collective-permute-done.7.seen_ref = bf16[12,128,128]{2,1,0:T(8,128)(2,1)S(1)} collective-permute-done((bf16[12,128,128]{2,1,0:T(8,128)(2,1)S(1)}, bf16[12,128,128]{2,1,0:T(8,128)(2,1)S(1)}, u32[]{:S(2)}, u32[]{:S(2)}) %collective-permute-start.7) | collective-permute-done | bytes 393248 | tf_op jit(solution)/shard_map/ppermute | solution.py:378
  17.8 0.6 %shard_map.89 = (bf16[2,128,128]{2,1,0:T(8,128)(2,1)S(1)}, bf16[2,128,128]{2,1,0:T(8,128)(2,1)S(1)}) custom-call(s32[5]{0:T(128)S(1)} %shift-right-arithmetic_and_fusion.flag_ref, bf16[4,128,128]{2,1,0:T(8,128)(2,1)S(1)} %get-tuple-element.21.after_ref.own_ref, bf16[12,128,128]{2,1,0:T(8,128)(2,1)S(1)} %collective-permute-done.7.seen_ref, ...), custom_call_target="tpu_custom_call" | custom-call | bytes 622612 | tf_op jit(solution)/shard_map/pallas_call | solution.py:398
  18.3 3.2 %collective-permute-start.8 = (bf16[2,128,128]{2,1,0:T(8,128)(2,1)S(1)}, bf16[2,128,128]{2,1,0:T(8,128)(2,1)S(1)}, u32[]{:S(2)}, u32[]{:S(2)}) collective-permute-start(bf16[2,128,128]{2,1,0:T(8,128)(2,1)S(1)} %get-tuple-element.29), channel_id=1, source_target_pairs={{0,4},{1,5},{2,6},{3,7},{4,0},{5,1},{6,2},{7,3},{8,12},{9,13},{10,... | collective-permute-start | bytes 196616 | tf_op jit(solution)/shard_map/ppermute | solution.py:378
  21.6 1.4 %collective-permute-start.9 = (bf16[2,128,128]{2,1,0:T(8,128)(2,1)S(1)}, bf16[2,128,128]{2,1,0:T(8,128)(2,1)S(1)}, u32[]{:S(2)}, u32[]{:S(2)}) collective-permute-start(bf16[2,128,128]{2,1,0:T(8,128)(2,1)S(1)} %get-tuple-element.30), channel_id=1, source_target_pairs={{0,6},{1,7},{2,4},{3,5},{4,2},{5,3},{6,0},{7,1},{8,14},{9,15},{10,... | collective-permute-start | bytes 196616 | tf_op jit(solution)/shard_map/ppermute | solution.py:378
  22.9 0.1 shard_map.88
  23.0 1.6 %collective-permute-start.4 = (bf16[2,128,128]{2,1,0:T(8,128)(2,1)S(1)}, bf16[2,128,128]{2,1,0:T(8,128)(2,1)S(1)}, u32[]{:S(2)}, u32[]{:S(2)}) collective-permute-start(bf16[2,128,128]{2,1,0:T(8,128)(2,1)S(1)} %get-tuple-element.26.below_ref.after_ref), channel_id=1, source_target_pairs={{0,1},{1,0},{2,3},{3,2},{4,5},{5,4},{6,7},{7,6},{8,9},{9,8},{10,11... | collective-permute-start | bytes 196616 | tf_op jit(solution)/shard_map/ppermute | solution.py:378
  24.5 1.5 %collective-permute-start.6 = (bf16[1,128,128]{2,1,0:T(8,128)(2,1)S(1)}, bf16[1,128,128]{2,1,0:T(8,128)(2,1)S(1)}, u32[]{:S(2)}, u32[]{:S(2)}) collective-permute-start(bf16[1,128,128]{2,1,0:T(8,128)(2,1)S(1)} %get-tuple-element.27), channel_id=1, source_target_pairs={{0,17},{1,16},{2,19},{3,18},{4,21},{5,20},{6,23},{7,22},{8,25},{9,... | collective-permute-start | bytes 98312 | tf_op jit(solution)/shard_map/ppermute | solution.py:383
  26.0 1.3 %collective-permute-start.5 = (bf16[1,128,128]{2,1,0:T(8,128)(2,1)S(1)}, bf16[1,128,128]{2,1,0:T(8,128)(2,1)S(1)}, u32[]{:S(2)}, u32[]{:S(2)}) collective-permute-start(bf16[1,128,128]{2,1,0:T(8,128)(2,1)S(1)} %get-tuple-element.27), channel_id=1, source_target_pairs={{0,16},{8,24},{16,0},{24,8},{1,17},{9,25},{17,1},{25,9},{2,18},{10... | collective-permute-start | bytes 98312 | tf_op jit(solution)/shard_map/ppermute | solution.py:382
  27.3 0.1 shard_map.93
  27.4 0.3 collective-permute-done.9.far_ref
  27.7 1.6 %collective-permute-done.6.far_top_ref = bf16[1,128,128]{2,1,0:T(8,128)(2,1)S(1)} collective-permute-done((bf16[1,128,128]{2,1,0:T(8,128)(2,1)S(1)}, bf16[1,128,128]{2,1,0:T(8,128)(2,1)S(1)}, u32[]{:S(2)}, u32[]{:S(2)}) %collective-permute-start.6) | collective-permute-done | bytes 32800 | tf_op jit(solution)/shard_map/ppermute | solution.py:383
  29.4 0.6 %collective-permute-done.5.near_top_ref = bf16[1,128,128]{2,1,0:T(8,128)(2,1)S(1)} collective-permute-done((bf16[1,128,128]{2,1,0:T(8,128)(2,1)S(1)}, bf16[1,128,128]{2,1,0:T(8,128)(2,1)S(1)}, u32[]{:S(2)}, u32[]{:S(2)}) %collective-permute-start.5) | collective-permute-done | bytes 32800 | tf_op jit(solution)/shard_map/ppermute | solution.py:382
  30.0 2.5 %collective-permute-start.16 = (bf16[3,128,128]{2,1,0:T(8,128)(2,1)S(1)}, bf16[3,128,128]{2,1,0:T(8,128)(2,1)S(1)}, u32[]{:S(2)}, u32[]{:S(2)}) collective-permute-start(bf16[3,128,128]{2,1,0:T(8,128)(2,1)S(1)} %shard_map.91.after_ref.piece0_ref), channel_id=1, source_target_pairs={{0,6},{1,7},{2,4},{3,5},{4,2},{5,3},{6,0},{7,1},{8,14},{9,15},{10,... | collective-permute-start | bytes 294920 | tf_op jit(solution)/shard_map/ppermute | solution.py:378
  32.5 1.9 %collective-permute-start.14 = (bf16[3,128,128]{2,1,0:T(8,128)(2,1)S(1)}, bf16[3,128,128]{2,1,0:T(8,128)(2,1)S(1)}, u32[]{:S(2)}, u32[]{:S(2)}) collective-permute-start(bf16[3,128,128]{2,1,0:T(8,128)(2,1)S(1)} %shard_map.91.after_ref.piece0_ref), channel_id=1, source_target_pairs={{0,2},{1,3},{2,0},{3,1},{4,6},{5,7},{6,4},{7,5},{8,10},{9,11},{10,... | collective-permute-start | bytes 294920 | tf_op jit(solution)/shard_map/ppermute | solution.py:378
  34.4 0.1 collective-permute-start.12
  34.6 7.0 %collective-permute-done.12.other_ref = bf16[2,128,128]{2,1,0:T(8,128)(2,1)S(1)} collective-permute-done((bf16[2,128,128]{2,1,0:T(8,128)(2,1)S(1)}, bf16[2,128,128]{2,1,0:T(8,128)(2,1)S(1)}, u32[]{:S(2)}, u32[]{:S(2)}) %collective-permute-start.12) | collective-permute-done | bytes 65568 | tf_op jit(solution)/shard_map/ppermute | solution.py:378
  41.6 0.6 %shard_map.94.after_ref.two_own_ref = bf16[4,128,128]{2,1,0:T(8,128)(2,1)S(1)} custom-call(s32[5]{0:T(128)S(1)} %shift-right-arithmetic_and_fusion.flag_ref, bf16[2,128,128]{2,1,0:T(8,128)(2,1)S(1)} %shard_map.90.refs_0_.own_ref, bf16[2,128,128]{2,1,0:T(8,128)(2,1)S(1)} %collective-permute-done.12.other_ref), custom_call_target="tpu_custom_call" | custom-call | bytes 131092 | tf_op jit(solution)/shard_map/pallas_call | solution.py:398
  42.1 1.6 %collective-permute-start.13 = (bf16[4,128,128]{2,1,0:T(8,128)(2,1)S(1)}, bf16[4,128,128]{2,1,0:T(8,128)(2,1)S(1)}, u32[]{:S(2)}, u32[]{:S(2)}) collective-permute-start(bf16[4,128,128]{2,1,0:T(8,128)(2,1)S(1)} %shard_map.94.after_ref.two_own_ref), channel_id=1, source_target_pairs={{0,1},{1,0},{2,3},{3,2},{4,5},{5,4},{6,7},{7,6},{8,9},{9,8},{10,11... | collective-permute-start | bytes 393224 | tf_op jit(solution)/shard_map/ppermute | solution.py:378
  43.7 2.0 %shard_map.92 = (f32[128,1024]{1,0:T(8,128)S(1)}, f32[128,1024]{1,0:T(8,128)S(1)}, f32[128,1024]{1,0:T(8,128)S(1)}) custom-call(s32[1,128]{1,0:T(1,128)S(1)} %bitcast.8, f32[20,8,32]{2,1,0:T(8,128)S(1)} %bitcast.4, bf16[128,1024]{1,0:T(8,128)(2,1)S(1)} %copy-done.3, bf16[128,1024]{1,0:T(8,128)(2,1)S(1)} %copy-done, bf16[128,1024]{1,0:T(8,128)(2,1)S(1)} %copy-done.1, ...), custom_call_target="tpu_custom_call" | custom-call | flops 167772160 | bytes 1167872 | tf_op jit(solution)/shard_map/pallas_call | solution.py:398
  45.8 0.1 collective-permute-start.17
  45.9 1.3 %collective-permute-done.13.two_other_ref = bf16[4,128,128]{2,1,0:T(8,128)(2,1)S(1)} collective-permute-done((bf16[4,128,128]{2,1,0:T(8,128)(2,1)S(1)}, bf16[4,128,128]{2,1,0:T(8,128)(2,1)S(1)}, u32[]{:S(2)}, u32[]{:S(2)}) %collective-permute-start.13) | collective-permute-done | bytes 131104 | tf_op jit(solution)/shard_map/ppermute | solution.py:378
  47.2 0.0 collective-permute-done.17.split_other_ref
  47.2 2.8 %shard_map.96 = (bf16[128,1024]{1,0:T(8,128)(2,1)}, bf16[128,1024]{1,0:T(8,128)(2,1)}, bf16[128,1024]{1,0:T(8,128)(2,1)}) custom-call(s32[5]{0:T(128)S(1)} %shift-right-arithmetic_and_fusion.flag_ref, s32[1,128]{1,0:T(1,128)S(1)} %bitcast.9, f32[20,8,32]{2,1,0:T(8,128)S(1)} %bitcast.5, bf16[128,1024]{1,0:T(8,128)(2,1)S(1)} %copy-done, ...), custom_call_target="tpu_custom_call" | custom-call | flops 234881024 | bytes 3822100 | tf_op jit(solution)/shard_map/pallas_call | solution.py:398
  (29 shorter events, 0.1 us)
Async XLA Ops:
  0.6 2.9 %copy-start = (bf16[128,1024]{1,0:T(8,128)(2,1)S(1)}, bf16[128,1024]{1,0:T(8,128)(2,1)}, u32[]{:S(2)}) copy-start(bf16[128,1024]{1,0:T(8,128)(2,1)} %k_ref.5) | copy-start | bytes 786436
  0.7 2.9 %copy-start.1 = (bf16[128,1024]{1,0:T(8,128)(2,1)S(1)}, bf16[128,1024]{1,0:T(8,128)(2,1)}, u32[]{:S(2)}) copy-start(bf16[128,1024]{1,0:T(8,128)(2,1)} %v_ref.5) | copy-start | bytes 786436
  0.7 2.9 %copy-start.2 = (bf16[128,1024]{1,0:T(8,128)(2,1)S(1)}, bf16[128,1024]{1,0:T(8,128)(2,1)}, u32[]{:S(2)}) copy-start(bf16[128,1024]{1,0:T(8,128)(2,1)} %g_ref.5) | copy-start | bytes 786436
  0.7 2.8 %copy-start.3 = (bf16[128,1024]{1,0:T(8,128)(2,1)S(1)}, bf16[128,1024]{1,0:T(8,128)(2,1)}, u32[]{:S(2)}) copy-start(bf16[128,1024]{1,0:T(8,128)(2,1)} %q_ref.3) | copy-start | bytes 786436
  0.7 2.8 %copy-start.4 = (f32[32,20,8]{0,2,1:T(8,128)S(1)}, f32[32,20,8]{0,2,1:T(8,128)}, u32[]{:S(2)}) copy-start(f32[32,20,8]{0,2,1:T(8,128)} %param.11) | copy-start | bytes 61444
  3.0 0.7 %copy-start.5 = (s32[128]{0:T(128)S(1)}, s32[128]{0:T(128)}, u32[]{:S(2)}) copy-start(s32[128]{0:T(128)} %param.10) | copy-start | bytes 1540
  3.0 4.9 %collective-permute-start = (bf16[12,128,128]{2,1,0:T(8,128)(2,1)S(1)}, bf16[12,128,128]{2,1,0:T(8,128)(2,1)S(1)}, u32[]{:S(2)}, u32[]{:S(2)}) collective-permute-start(bf16[12,128,128]{2,1,0:T(8,128)(2,1)S(1)} %get-tuple-element.19), channel_id=1, source_target_pairs={{0,8},{8,0},{16,24},{24,16},{1,9},{9,1},{17,25},{25,17},{2,10},{10... | collective-permute-start | bytes 1179656 | tf_op jit(solution)/shard_map/ppermute | solution.py:382
  4.8 12.9 %collective-permute-start.7 = (bf16[12,128,128]{2,1,0:T(8,128)(2,1)S(1)}, bf16[12,128,128]{2,1,0:T(8,128)(2,1)S(1)}, u32[]{:S(2)}, u32[]{:S(2)}) collective-permute-start(bf16[12,128,128]{2,1,0:T(8,128)(2,1)S(1)} %get-tuple-element.28.sent_ref), channel_id=1, source_target_pairs={{0,1},{1,0},{2,3},{3,2},{4,5},{5,4},{6,7},{7,6},{8,9},{9,8},{10,11... | collective-permute-start | bytes 1179656 | tf_op jit(solution)/shard_map/ppermute | solution.py:378
  7.8 19.9 %collective-permute-start.10 = (bf16[8,128,128]{2,1,0:T(8,128)(2,1)S(1)}, bf16[8,128,128]{2,1,0:T(8,128)(2,1)S(1)}, u32[]{:S(2)}, u32[]{:S(2)}) collective-permute-start(bf16[8,128,128]{2,1,0:T(8,128)(2,1)S(1)} %get-tuple-element.31), channel_id=1, source_target_pairs={{0,1},{1,0},{2,3},{3,2},{4,5},{5,4},{6,7},{7,6},{8,9},{9,8},{10,11... | collective-permute-start | bytes 786440 | tf_op jit(solution)/shard_map/ppermute | solution.py:378
  8.5 13.1 %collective-permute-start.1 = (bf16[3,128,128]{2,1,0:T(8,128)(2,1)S(1)}, bf16[3,128,128]{2,1,0:T(8,128)(2,1)S(1)}, u32[]{:S(2)}, u32[]{:S(2)}) collective-permute-start(bf16[3,128,128]{2,1,0:T(8,128)(2,1)S(1)} %get-tuple-element.23), channel_id=1, source_target_pairs={{0,6},{1,7},{2,4},{3,5},{4,2},{5,3},{6,0},{7,1},{8,14},{9,15},{10,... | collective-permute-start | bytes 294920 | tf_op jit(solution)/shard_map/ppermute | solution.py:378
  12.6 10.3 %collective-permute-start.2 = (bf16[3,128,128]{2,1,0:T(8,128)(2,1)S(1)}, bf16[3,128,128]{2,1,0:T(8,128)(2,1)S(1)}, u32[]{:S(2)}, u32[]{:S(2)}) collective-permute-start(bf16[3,128,128]{2,1,0:T(8,128)(2,1)S(1)} %get-tuple-element.24), channel_id=1, source_target_pairs={{0,4},{1,5},{2,6},{3,7},{4,0},{5,1},{6,2},{7,3},{8,12},{9,13},{10,... | collective-permute-start | bytes 294920 | tf_op jit(solution)/shard_map/ppermute | solution.py:378
  12.6 10.3 %collective-permute-start.3 = (bf16[3,128,128]{2,1,0:T(8,128)(2,1)S(1)}, bf16[3,128,128]{2,1,0:T(8,128)(2,1)S(1)}, u32[]{:S(2)}, u32[]{:S(2)}) collective-permute-start(bf16[3,128,128]{2,1,0:T(8,128)(2,1)S(1)} %get-tuple-element.25), channel_id=1, source_target_pairs={{0,2},{1,3},{2,0},{3,1},{4,6},{5,7},{6,4},{7,5},{8,10},{9,11},{10,... | collective-permute-start | bytes 294920 | tf_op jit(solution)/shard_map/ppermute | solution.py:378
  18.3 7.7 %collective-permute-start.8 = (bf16[2,128,128]{2,1,0:T(8,128)(2,1)S(1)}, bf16[2,128,128]{2,1,0:T(8,128)(2,1)S(1)}, u32[]{:S(2)}, u32[]{:S(2)}) collective-permute-start(bf16[2,128,128]{2,1,0:T(8,128)(2,1)S(1)} %get-tuple-element.29), channel_id=1, source_target_pairs={{0,4},{1,5},{2,6},{3,7},{4,0},{5,1},{6,2},{7,3},{8,12},{9,13},{10,... | collective-permute-start | bytes 196616 | tf_op jit(solution)/shard_map/ppermute | solution.py:378
  21.6 6.1 %collective-permute-start.9 = (bf16[2,128,128]{2,1,0:T(8,128)(2,1)S(1)}, bf16[2,128,128]{2,1,0:T(8,128)(2,1)S(1)}, u32[]{:S(2)}, u32[]{:S(2)}) collective-permute-start(bf16[2,128,128]{2,1,0:T(8,128)(2,1)S(1)} %get-tuple-element.30), channel_id=1, source_target_pairs={{0,6},{1,7},{2,4},{3,5},{4,2},{5,3},{6,0},{7,1},{8,14},{9,15},{10,... | collective-permute-start | bytes 196616 | tf_op jit(solution)/shard_map/ppermute | solution.py:378
  23.0 7.0 %collective-permute-start.4 = (bf16[2,128,128]{2,1,0:T(8,128)(2,1)S(1)}, bf16[2,128,128]{2,1,0:T(8,128)(2,1)S(1)}, u32[]{:S(2)}, u32[]{:S(2)}) collective-permute-start(bf16[2,128,128]{2,1,0:T(8,128)(2,1)S(1)} %get-tuple-element.26.below_ref.after_ref), channel_id=1, source_target_pairs={{0,1},{1,0},{2,3},{3,2},{4,5},{5,4},{6,7},{7,6},{8,9},{9,8},{10,11... | collective-permute-start | bytes 196616 | tf_op jit(solution)/shard_map/ppermute | solution.py:378
  24.5 4.8 %collective-permute-start.6 = (bf16[1,128,128]{2,1,0:T(8,128)(2,1)S(1)}, bf16[1,128,128]{2,1,0:T(8,128)(2,1)S(1)}, u32[]{:S(2)}, u32[]{:S(2)}) collective-permute-start(bf16[1,128,128]{2,1,0:T(8,128)(2,1)S(1)} %get-tuple-element.27), channel_id=1, source_target_pairs={{0,17},{1,16},{2,19},{3,18},{4,21},{5,20},{6,23},{7,22},{8,25},{9,... | collective-permute-start | bytes 98312 | tf_op jit(solution)/shard_map/ppermute | solution.py:383
  26.0 3.9 %collective-permute-start.5 = (bf16[1,128,128]{2,1,0:T(8,128)(2,1)S(1)}, bf16[1,128,128]{2,1,0:T(8,128)(2,1)S(1)}, u32[]{:S(2)}, u32[]{:S(2)}) collective-permute-start(bf16[1,128,128]{2,1,0:T(8,128)(2,1)S(1)} %get-tuple-element.27), channel_id=1, source_target_pairs={{0,16},{8,24},{16,0},{24,8},{1,17},{9,25},{17,1},{25,9},{2,18},{10... | collective-permute-start | bytes 98312 | tf_op jit(solution)/shard_map/ppermute | solution.py:382
  27.7 19.5 %collective-permute-start.11 = (bf16[8,128,128]{2,1,0:T(8,128)(2,1)S(1)}, bf16[8,128,128]{2,1,0:T(8,128)(2,1)S(1)}, u32[]{:S(2)}, u32[]{:S(2)}) collective-permute-start(bf16[8,128,128]{2,1,0:T(8,128)(2,1)S(1)} %shard_map.93), channel_id=1, source_target_pairs={{0,2},{1,3},{2,0},{3,1},{4,6},{5,7},{6,4},{7,5},{8,10},{9,11},{10,... | collective-permute-start | bytes 786440 | tf_op jit(solution)/shard_map/ppermute | solution.py:378
  30.0 15.7 %collective-permute-start.16 = (bf16[3,128,128]{2,1,0:T(8,128)(2,1)S(1)}, bf16[3,128,128]{2,1,0:T(8,128)(2,1)S(1)}, u32[]{:S(2)}, u32[]{:S(2)}) collective-permute-start(bf16[3,128,128]{2,1,0:T(8,128)(2,1)S(1)} %shard_map.91.after_ref.piece0_ref), channel_id=1, source_target_pairs={{0,6},{1,7},{2,4},{3,5},{4,2},{5,3},{6,0},{7,1},{8,14},{9,15},{10,... | collective-permute-start | bytes 294920 | tf_op jit(solution)/shard_map/ppermute | solution.py:378
  32.5 13.2 %collective-permute-start.15 = (bf16[3,128,128]{2,1,0:T(8,128)(2,1)S(1)}, bf16[3,128,128]{2,1,0:T(8,128)(2,1)S(1)}, u32[]{:S(2)}, u32[]{:S(2)}) collective-permute-start(bf16[3,128,128]{2,1,0:T(8,128)(2,1)S(1)} %shard_map.91.after_ref.piece0_ref), channel_id=1, source_target_pairs={{0,4},{1,5},{2,6},{3,7},{4,0},{5,1},{6,2},{7,3},{8,12},{9,13},{10,... | collective-permute-start | bytes 294920 | tf_op jit(solution)/shard_map/ppermute | solution.py:378
  32.5 13.2 %collective-permute-start.14 = (bf16[3,128,128]{2,1,0:T(8,128)(2,1)S(1)}, bf16[3,128,128]{2,1,0:T(8,128)(2,1)S(1)}, u32[]{:S(2)}, u32[]{:S(2)}) collective-permute-start(bf16[3,128,128]{2,1,0:T(8,128)(2,1)S(1)} %shard_map.91.after_ref.piece0_ref), channel_id=1, source_target_pairs={{0,2},{1,3},{2,0},{3,1},{4,6},{5,7},{6,4},{7,5},{8,10},{9,11},{10,... | collective-permute-start | bytes 294920 | tf_op jit(solution)/shard_map/ppermute | solution.py:378
  34.4 7.1 %collective-permute-start.12 = (bf16[2,128,128]{2,1,0:T(8,128)(2,1)S(1)}, bf16[2,128,128]{2,1,0:T(8,128)(2,1)S(1)}, u32[]{:S(2)}, u32[]{:S(2)}) collective-permute-start(bf16[2,128,128]{2,1,0:T(8,128)(2,1)S(1)} %shard_map.90.refs_0_.own_ref), channel_id=1, source_target_pairs={{0,2},{1,3},{2,0},{3,1},{4,6},{5,7},{6,4},{7,5},{8,10},{9,11},{10,... | collective-permute-start | bytes 196616 | tf_op jit(solution)/shard_map/ppermute | solution.py:378
  42.1 5.0 %collective-permute-start.13 = (bf16[4,128,128]{2,1,0:T(8,128)(2,1)S(1)}, bf16[4,128,128]{2,1,0:T(8,128)(2,1)S(1)}, u32[]{:S(2)}, u32[]{:S(2)}) collective-permute-start(bf16[4,128,128]{2,1,0:T(8,128)(2,1)S(1)} %shard_map.94.after_ref.two_own_ref), channel_id=1, source_target_pairs={{0,1},{1,0},{2,3},{3,2},{4,5},{5,4},{6,7},{7,6},{8,9},{9,8},{10,11... | collective-permute-start | bytes 393224 | tf_op jit(solution)/shard_map/ppermute | solution.py:378
  45.8 1.4 %collective-permute-start.17 = (bf16[1,4,128,128]{3,2,1,0:T(8,128)(2,1)S(1)}, bf16[1,4,128,128]{3,2,1,0:T(8,128)(2,1)S(1)}, u32[]{:S(2)}, u32[]{:S(2)}) collective-permute-start(bf16[1,4,128,128]{3,2,1,0:T(8,128)(2,1)S(1)} %shard_map.95.split_own_ref), channel_id=1, source_target_pairs={{0,8},{8,0},{16,24},{24,16},{1,9},{9,1},{17,25},{25,17},{2,10},{10... | collective-permute-start | bytes 393224 | tf_op jit(solution)/shard_map/ppermute | solution.py:382

commit v12 on v10

--- a/solution.py
+++ b/solution.py
@@ -159,7 +159,7 @@
     after_ref,
     two_own_ref,
     sent_ref,
-    zero_ref,
+    rest_ref,
     two_ref,
 ):
     head_count = table_ref.shape[1]
@@ -172,9 +172,12 @@
 
         def store(place, value):
             if place == 0:
-                zero_ref[head] = value
+                rest_ref[half + head] = value
             elif place == 1:
-                sent_ref[half + head] = value
+                if head < half:
+                    sent_ref[half + head] = value
+                else:
+                    rest_ref[head - half] = value
             else:
                 two_ref[head] = value
 
@@ -215,9 +218,10 @@
     two_ref[...] = narrow(wide(own_ref[...]) + wide(seen_ref[: own_ref.shape[0]]))
 
 
-def one_sum_kernel(sent_ref, seen_ref, after_ref, one_ref):
-    first = sent_ref.shape[0] - one_ref.shape[0]
-    one_ref[...] = narrow(wide(sent_ref[first:]) + wide(seen_ref[first:]))
+def one_sum_kernel(sent_ref, seen_ref, rest_ref, rest_seen_ref, after_ref, one_ref):
+    half = one_ref.shape[0] // 2
+    one_ref[:half] = narrow(wide(sent_ref[half:]) + wide(seen_ref[half:]))
+    one_ref[half:] = narrow(wide(rest_ref[:half]) + wide(rest_seen_ref[:half]))
 
 
 def local_kernel(
@@ -300,7 +304,7 @@
     x_place = flag_ref[0]
     z_place = flag_ref[1] + 2 * flag_ref[2]
     core = flag_ref[inner]
-    held_ref[0] = zero_ref[...]
+    held_ref[0] = zero_ref[zero_ref.shape[0] - head_count :]
     held_ref[1] = one_ref[...]
     held_ref[2, pl.ds(x_place * half, half)] = two_own_ref[...]
     held_ref[2, pl.ds((1 - x_place) * half, half)] = two_other_ref[...]
@@ -425,10 +429,10 @@
         grant=FIRST_BYTES,
     )
     seen = swap(sent, inner_bits)
-    two_own, lower_sent, zero = call(
+    two_own, lower_sent, rest = call(
         functools.partial(lower_kernel, offset, head_size),
         [smem] + [vmem] * 6 + [anywhere],
-        (cells(half), cells(half + head_count), cells(head_count)),
+        (cells(half), cells(2 * half), cells(half + head_count)),
         (flag_bits, class_lanes, table, query_rows, key_rows, value_rows, out_grad, keep),
         flops=2 * NEAR * row_count * width * head_size,
         scratch=[pltpu.VMEM((head_count,) + cell, jnp.bfloat16)],
@@ -440,6 +444,7 @@
         (flag_bits, seen, keep, two_own, *lead),
     )
     lower_seen = swap(lower_sent, 0)
+    rest_seen = swap(rest, 0)
     two_sum = call(
         two_sum_kernel, [vmem] * 2 + [anywhere], cells(half), (two_own, lower_seen, own_share)
     )
@@ -480,9 +485,9 @@
         top_sent = narrow(parts[top])
     one_sum = call(
         one_sum_kernel,
-        [vmem] * 2 + [anywhere],
+        [vmem] * 4 + [anywhere],
         cells(head_count),
-        (lower_sent, lower_seen, below),
+        (lower_sent, lower_seen, rest, rest_seen, below),
     )
     two_sum = call(
         two_sum_kernel, [vmem] * 2 + [anywhere], cells(half), (two_sum, swap(two_sum, 1), two_sum)
@@ -490,12 +495,11 @@
     two_half = swap(two_sum, 2)
     two_rest = swap(two_half, 0)
     one_done = swap(one_sum, 1)
-    zero_done = swap(zero, 0)
     shares = call(
         pair_sum_kernel,
         [vmem] * 4 + [anywhere] * 2,
         cells(share_rows),
-        (below, swap(below, 0), swap(top_sent, top), swap(top_sent, 0, top), two_sum, zero_done),
+        (below, swap(below, 0), swap(top_sent, top), swap(top_sent, 0, top), two_sum, rest_seen),
     )
     query_local, key_local, value_local = call(
         functools.partial(local_kernel, block_depth, head_size),
@@ -528,7 +532,7 @@
             query_local,
             key_local,
             value_local,
-            zero_done,
+            rest_seen,
             one_done,
             two_half,
             two_rest,

time: 45 us -> 44.7 us (level)
  no operation moved by 1% of the time
where the time goes in v12:
time: 44.7 us; the launch traced here: 44.5 us
  starting transfers between devices  23.3 us (52%)
  waiting for transfers between devices  11.2 us (25%)
  Pallas kernels  9.11 us (20%)
  between operations  0.79 us (2%)
    ppermute x13, starting transfers between devices, swap(): return lax.ppermute(block, 'gy', [(i, i ^ mask) for i in range(inner_size)])  20.8 us
    ppermute x13, waiting for transfers between devices, swap(): return lax.ppermute(block, 'gy', [(i, i ^ mask) for i in range(inner_size)])  9.68 us
    pallas_call x11, Pallas kernels, call(): pl.pallas_call(kernel, out_shape=outs, in_specs=in_specs, out_specs=out_s...  9.11 us
    ppermute x1, starting transfers between devices, swap(): lax.ppermute(block, ('gx', 'gy'), [(i, i ^ mask) for i in range(device_co...  1.49 us
    ppermute x3, waiting for transfers between devices, swap(): return lax.ppermute(block, 'gx', [(i, i ^ mask) for i in range(size)])  1.47 us
    ppermute x3, starting transfers between devices, swap(): return lax.ppermute(block, 'gx', [(i, i ^ mask) for i in range(size)])  1.03 us
  transfers between devices with their start and end apart: 17, of which 7 were waited for; matrix products, arithmetic and copies ran while one was open for 0% of the time, Pallas kernels for 9%

profile of v12, /device:TPU:0, one launch (start us, length us, event | category | flops | bytes accessed | tf_op | source)
XLA Modules:
  0.0 44.5 jit_solution(17460930985505527213)
XLA Ops:
  0.7 0.0 copy-start.1
  0.7 2.3 %shard_map.85 = (bf16[12,128,128]{2,1,0:T(8,128)(2,1)S(1)}, bf16[4,128,128]{2,1,0:T(8,128)(2,1)S(1)}) custom-call(s32[5]{0:T(128)S(1)} %shift-right-arithmetic_and_fusion.flag_ref, s32[1,128]{1,0:T(1,128)} %bitcast.6, f32[20,8,32]{2,1,0:T(8,128)} %bitcast.2, bf16[128,1024]{1,0:T(8,128)(2,1)} %q_ref.3, bf16[128,1024]{1,0:T(8,128)(2,1)} %k_ref.5, ...), custom_call_target="tpu_custom_call" | custom-call | flops 67108864 | bytes 1069588 | tf_op jit(solution)/shard_map/pallas_call | solution.py:387
  3.0 0.5 %collective-permute-start = (bf16[12,128,128]{2,1,0:T(8,128)(2,1)S(1)}, bf16[12,128,128]{2,1,0:T(8,128)(2,1)S(1)}, u32[]{:S(2)}, u32[]{:S(2)}) collective-permute-start(bf16[12,128,128]{2,1,0:T(8,128)(2,1)S(1)} %get-tuple-element.17), channel_id=1, source_target_pairs={{0,8},{8,0},{16,24},{24,16},{1,9},{9,1},{17,25},{25,17},{2,10},{10... | collective-permute-start | bytes 1179656 | tf_op jit(solution)/shard_map/ppermute | solution.py:371
  3.5 0.1 copy-done.5
  3.6 1.2 %shard_map.86 = (bf16[4,128,128]{2,1,0:T(8,128)(2,1)S(1)}, bf16[8,128,128]{2,1,0:T(8,128)(2,1)S(1)}, bf16[12,128,128]{2,1,0:T(8,128)(2,1)S(1)}) custom-call(s32[5]{0:T(128)S(1)} %shift-right-arithmetic_and_fusion.flag_ref, s32[1,128]{1,0:T(1,128)S(1)} %bitcast.7, f32[20,8,32]{2,1,0:T(8,128)S(1)} %bitcast.3, bf16[128,1024]{1,0:T(8,128)(2,1)S(1)} %copy-done.3, ...), custom_call_target="tpu_custom_call" | custom-call | flops 100663296 | bytes 1200660 | tf_op jit(solution)/shard_map/pallas_call | solution.py:387
  4.8 3.0 %collective-permute-start.7 = (bf16[8,128,128]{2,1,0:T(8,128)(2,1)S(1)}, bf16[8,128,128]{2,1,0:T(8,128)(2,1)S(1)}, u32[]{:S(2)}, u32[]{:S(2)}) collective-permute-start(bf16[8,128,128]{2,1,0:T(8,128)(2,1)S(1)} %get-tuple-element.26.sent_ref), channel_id=1, source_target_pairs={{0,1},{1,0},{2,3},{3,2},{4,5},{5,4},{6,7},{7,6},{8,9},{9,8},{10,11... | collective-permute-start | bytes 786440 | tf_op jit(solution)/shard_map/ppermute | solution.py:367
  7.8 0.1 collective-permute-start.9
  7.9 0.6 %shard_map.87 = (bf16[3,128,128]{2,1,0:T(8,128)(2,1)S(1)}, bf16[3,128,128]{2,1,0:T(8,128)(2,1)S(1)}, bf16[3,128,128]{2,1,0:T(8,128)(2,1)S(1)}, bf16[3,128,128]{2,1,0:T(8,128)(2,1)S(1)}) custom-call(s32[5]{0:T(128)S(1)} %shift-right-arithmetic_and_fusion.flag_ref, bf16[12,128,128]{2,1,0:T(8,128)(2,1)S(1)} %collective-permute-done.seen_ref, ...), custom_call_target="tpu_custom_call" | custom-call | bytes 655380 | tf_op jit(solution)/shard_map/pallas_call | solution.py:387
  8.5 4.1 %collective-permute-start.1 = (bf16[3,128,128]{2,1,0:T(8,128)(2,1)S(1)}, bf16[3,128,128]{2,1,0:T(8,128)(2,1)S(1)}, u32[]{:S(2)}, u32[]{:S(2)}) collective-permute-start(bf16[3,128,128]{2,1,0:T(8,128)(2,1)S(1)} %get-tuple-element.21), channel_id=1, source_target_pairs={{0,6},{1,7},{2,4},{3,5},{4,2},{5,3},{6,0},{7,1},{8,14},{9,15},{10,... | collective-permute-start | bytes 294920 | tf_op jit(solution)/shard_map/ppermute | solution.py:367
  12.6 0.6 %collective-permute-start.3 = (bf16[3,128,128]{2,1,0:T(8,128)(2,1)S(1)}, bf16[3,128,128]{2,1,0:T(8,128)(2,1)S(1)}, u32[]{:S(2)}, u32[]{:S(2)}) collective-permute-start(bf16[3,128,128]{2,1,0:T(8,128)(2,1)S(1)} %get-tuple-element.23), channel_id=1, source_target_pairs={{0,2},{1,3},{2,0},{3,1},{4,6},{5,7},{6,4},{7,5},{8,10},{9,11},{10,... | collective-permute-start | bytes 294920 | tf_op jit(solution)/shard_map/ppermute | solution.py:367
  13.3 1.7 %collective-permute-done.7.seen_ref = bf16[8,128,128]{2,1,0:T(8,128)(2,1)S(1)} collective-permute-done((bf16[8,128,128]{2,1,0:T(8,128)(2,1)S(1)}, bf16[8,128,128]{2,1,0:T(8,128)(2,1)S(1)}, u32[]{:S(2)}, u32[]{:S(2)}) %collective-permute-start.7) | collective-permute-done | bytes 262176 | tf_op jit(solution)/shard_map/ppermute | solution.py:367
  15.0 2.2 %collective-permute-start.8 = (bf16[4,128,128]{2,1,0:T(8,128)(2,1)S(1)}, bf16[4,128,128]{2,1,0:T(8,128)(2,1)S(1)}, u32[]{:S(2)}, u32[]{:S(2)}) collective-permute-start(bf16[4,128,128]{2,1,0:T(8,128)(2,1)S(1)} %shard_map.89.own_ref.after_ref), channel_id=1, source_target_pairs={{0,2},{1,3},{2,0},{3,1},{4,6},{5,7},{6,4},{7,5},{8,10},{9,11},{10,... | collective-permute-start | bytes 393224 | tf_op jit(solution)/shard_map/ppermute | solution.py:367
  17.2 3.4 %collective-permute-done.2.refs_1_ = bf16[3,128,128]{2,1,0:T(8,128)(2,1)S(1)} collective-permute-done((bf16[3,128,128]{2,1,0:T(8,128)(2,1)S(1)}, bf16[3,128,128]{2,1,0:T(8,128)(2,1)S(1)}, u32[]{:S(2)}, u32[]{:S(2)}) %collective-permute-start.2) | collective-permute-done | bytes 98336 | tf_op jit(solution)/shard_map/ppermute | solution.py:367
  20.6 0.1 shard_map.88
  20.6 1.6 %collective-permute-start.4 = (bf16[2,128,128]{2,1,0:T(8,128)(2,1)S(1)}, bf16[2,128,128]{2,1,0:T(8,128)(2,1)S(1)}, u32[]{:S(2)}, u32[]{:S(2)}) collective-permute-start(bf16[2,128,128]{2,1,0:T(8,128)(2,1)S(1)} %get-tuple-element.24.below_ref.after_ref), channel_id=1, source_target_pairs={{0,1},{1,0},{2,3},{3,2},{4,5},{5,4},{6,7},{7,6},{8,9},{9,8},{10,11... | collective-permute-start | bytes 196616 | tf_op jit(solution)/shard_map/ppermute | solution.py:367
  22.3 1.5 %collective-permute-start.6 = (bf16[1,128,128]{2,1,0:T(8,128)(2,1)S(1)}, bf16[1,128,128]{2,1,0:T(8,128)(2,1)S(1)}, u32[]{:S(2)}, u32[]{:S(2)}) collective-permute-start(bf16[1,128,128]{2,1,0:T(8,128)(2,1)S(1)} %get-tuple-element.25), channel_id=1, source_target_pairs={{0,17},{1,16},{2,19},{3,18},{4,21},{5,20},{6,23},{7,22},{8,25},{9,... | collective-permute-start | bytes 98312 | tf_op jit(solution)/shard_map/ppermute | solution.py:372
  23.8 0.4 collective-permute-start.5
  24.2 0.9 %collective-permute-start.11 = (bf16[4,128,128]{2,1,0:T(8,128)(2,1)S(1)}, bf16[4,128,128]{2,1,0:T(8,128)(2,1)S(1)}, u32[]{:S(2)}, u32[]{:S(2)}) collective-permute-start(bf16[4,128,128]{2,1,0:T(8,128)(2,1)S(1)} %shard_map.90.refs_0_), channel_id=1, source_target_pairs={{0,4},{1,5},{2,6},{3,7},{4,0},{5,1},{6,2},{7,3},{8,12},{9,13},{10,... | collective-permute-start | bytes 393224 | tf_op jit(solution)/shard_map/ppermute | solution.py:367
  25.1 0.1 shard_map.93
  25.2 2.3 %collective-permute-start.10 = (bf16[8,128,128]{2,1,0:T(8,128)(2,1)S(1)}, bf16[8,128,128]{2,1,0:T(8,128)(2,1)S(1)}, u32[]{:S(2)}, u32[]{:S(2)}) collective-permute-start(bf16[8,128,128]{2,1,0:T(8,128)(2,1)S(1)} %shard_map.93), channel_id=1, source_target_pairs={{0,2},{1,3},{2,0},{3,1},{4,6},{5,7},{6,4},{7,5},{8,10},{9,11},{10,... | collective-permute-start | bytes 786440 | tf_op jit(solution)/shard_map/ppermute | solution.py:367
  27.5 0.2 collective-permute-done.5.near_top_ref
  27.7 2.5 %collective-permute-start.15 = (bf16[3,128,128]{2,1,0:T(8,128)(2,1)S(1)}, bf16[3,128,128]{2,1,0:T(8,128)(2,1)S(1)}, u32[]{:S(2)}, u32[]{:S(2)}) collective-permute-start(bf16[3,128,128]{2,1,0:T(8,128)(2,1)S(1)} %shard_map.91.after_ref.piece0_ref), channel_id=1, source_target_pairs={{0,6},{1,7},{2,4},{3,5},{4,2},{5,3},{6,0},{7,1},{8,14},{9,15},{10,... | collective-permute-start | bytes 294920 | tf_op jit(solution)/shard_map/ppermute | solution.py:367
  30.2 0.8 %collective-permute-start.14 = (bf16[3,128,128]{2,1,0:T(8,128)(2,1)S(1)}, bf16[3,128,128]{2,1,0:T(8,128)(2,1)S(1)}, u32[]{:S(2)}, u32[]{:S(2)}) collective-permute-start(bf16[3,128,128]{2,1,0:T(8,128)(2,1)S(1)} %shard_map.91.after_ref.piece0_ref), channel_id=1, source_target_pairs={{0,4},{1,5},{2,6},{3,7},{4,0},{5,1},{6,2},{7,3},{8,12},{9,13},{10,... | collective-permute-start | bytes 294920 | tf_op jit(solution)/shard_map/ppermute | solution.py:367
  31.0 1.2 %collective-permute-start.13 = (bf16[3,128,128]{2,1,0:T(8,128)(2,1)S(1)}, bf16[3,128,128]{2,1,0:T(8,128)(2,1)S(1)}, u32[]{:S(2)}, u32[]{:S(2)}) collective-permute-start(bf16[3,128,128]{2,1,0:T(8,128)(2,1)S(1)} %shard_map.91.after_ref.piece0_ref), channel_id=1, source_target_pairs={{0,2},{1,3},{2,0},{3,1},{4,6},{5,7},{6,4},{7,5},{8,10},{9,11},{10,... | collective-permute-start | bytes 294920 | tf_op jit(solution)/shard_map/ppermute | solution.py:367
  32.2 2.0 %shard_map.92 = (f32[128,1024]{1,0:T(8,128)S(1)}, f32[128,1024]{1,0:T(8,128)S(1)}, f32[128,1024]{1,0:T(8,128)S(1)}) custom-call(s32[1,128]{1,0:T(1,128)S(1)} %bitcast.8, f32[20,8,32]{2,1,0:T(8,128)S(1)} %bitcast.4, bf16[128,1024]{1,0:T(8,128)(2,1)S(1)} %copy-done.3, bf16[128,1024]{1,0:T(8,128)(2,1)S(1)} %copy-done, bf16[128,1024]{1,0:T(8,128)(2,1)S(1)} %copy-done.1, ...), custom_call_target="tpu_custom_call" | custom-call | flops 167772160 | bytes 1167872 | tf_op jit(solution)/shard_map/pallas_call | solution.py:387
  34.2 1.0 %collective-permute-done.11.after_ref.two_own_ref = bf16[4,128,128]{2,1,0:T(8,128)(2,1)S(1)} collective-permute-done((bf16[4,128,128]{2,1,0:T(8,128)(2,1)S(1)}, bf16[4,128,128]{2,1,0:T(8,128)(2,1)S(1)}, u32[]{:S(2)}, u32[]{:S(2)}) %collective-permute-start.11) | collective-permute-done | bytes 131104 | tf_op jit(solution)/shard_map/ppermute | solution.py:367
  35.2 1.5 %collective-permute-start.12 = (bf16[4,128,128]{2,1,0:T(8,128)(2,1)S(1)}, bf16[4,128,128]{2,1,0:T(8,128)(2,1)S(1)}, u32[]{:S(2)}, u32[]{:S(2)}) collective-permute-start(bf16[4,128,128]{2,1,0:T(8,128)(2,1)S(1)} %collective-permute-done.11.after_ref.two_own_ref), channel_id=1, source_target_pairs={{0,1},{1,0},{2,3},{3,2},{4,5},{5,4},{6,7},{7,6},{8,9},{9,8},{10,11... | collective-permute-start | bytes 393224 | tf_op jit(solution)/shard_map/ppermute | solution.py:367
  36.7 2.1 %collective-permute-done.15.piece3_ref = bf16[3,128,128]{2,1,0:T(8,128)(2,1)S(1)} collective-permute-done((bf16[3,128,128]{2,1,0:T(8,128)(2,1)S(1)}, bf16[3,128,128]{2,1,0:T(8,128)(2,1)S(1)}, u32[]{:S(2)}, u32[]{:S(2)}) %collective-permute-start.15) | collective-permute-done | bytes 98336 | tf_op jit(solution)/shard_map/ppermute | solution.py:367
  38.8 1.5 %collective-permute-done.13.piece1_ref = bf16[3,128,128]{2,1,0:T(8,128)(2,1)S(1)} collective-permute-done((bf16[3,128,128]{2,1,0:T(8,128)(2,1)S(1)}, bf16[3,128,128]{2,1,0:T(8,128)(2,1)S(1)}, u32[]{:S(2)}, u32[]{:S(2)}) %collective-permute-start.13) | collective-permute-done | bytes 98336 | tf_op jit(solution)/shard_map/ppermute | solution.py:367
  40.3 0.1 collective-permute-start.16
  40.4 1.3 %collective-permute-done.16.split_other_ref = bf16[1,4,128,128]{3,2,1,0:T(8,128)(2,1)S(1)} collective-permute-done((bf16[1,4,128,128]{3,2,1,0:T(8,128)(2,1)S(1)}, bf16[1,4,128,128]{3,2,1,0:T(8,128)(2,1)S(1)}, u32[]{:S(2)}, u32[]{:S(2)}) %collective-permute-start.16) | collective-permute-done | bytes 131104 | tf_op jit(solution)/shard_map/ppermute | solution.py:371
  41.7 2.8 %shard_map.95 = (bf16[128,1024]{1,0:T(8,128)(2,1)}, bf16[128,1024]{1,0:T(8,128)(2,1)}, bf16[128,1024]{1,0:T(8,128)(2,1)}) custom-call(s32[5]{0:T(128)S(1)} %shift-right-arithmetic_and_fusion.flag_ref, s32[1,128]{1,0:T(1,128)S(1)} %bitcast.9, f32[20,8,32]{2,1,0:T(8,128)S(1)} %bitcast.5, bf16[128,1024]{1,0:T(8,128)(2,1)S(1)} %copy-done, ...), custom_call_target="tpu_custom_call" | custom-call | flops 234881024 | bytes 3953172 | tf_op jit(solution)/shard_map/pallas_call | solution.py:387
  (26 shorter events, 0.2 us)
Async XLA Ops:
  0.6 2.9 %copy-start = (bf16[128,1024]{1,0:T(8,128)(2,1)S(1)}, bf16[128,1024]{1,0:T(8,128)(2,1)}, u32[]{:S(2)}) copy-start(bf16[128,1024]{1,0:T(8,128)(2,1)} %k_ref.5) | copy-start | bytes 786436
  0.7 2.9 %copy-start.1 = (bf16[128,1024]{1,0:T(8,128)(2,1)S(1)}, bf16[128,1024]{1,0:T(8,128)(2,1)}, u32[]{:S(2)}) copy-start(bf16[128,1024]{1,0:T(8,128)(2,1)} %v_ref.5) | copy-start | bytes 786436
  0.7 2.9 %copy-start.2 = (bf16[128,1024]{1,0:T(8,128)(2,1)S(1)}, bf16[128,1024]{1,0:T(8,128)(2,1)}, u32[]{:S(2)}) copy-start(bf16[128,1024]{1,0:T(8,128)(2,1)} %g_ref.5) | copy-start | bytes 786436
  0.7 2.8 %copy-start.3 = (bf16[128,1024]{1,0:T(8,128)(2,1)S(1)}, bf16[128,1024]{1,0:T(8,128)(2,1)}, u32[]{:S(2)}) copy-start(bf16[128,1024]{1,0:T(8,128)(2,1)} %q_ref.3) | copy-start | bytes 786436
  0.7 2.8 %copy-start.4 = (f32[32,20,8]{0,2,1:T(8,128)S(1)}, f32[32,20,8]{0,2,1:T(8,128)}, u32[]{:S(2)}) copy-start(f32[32,20,8]{0,2,1:T(8,128)} %param.11) | copy-start | bytes 61444
  3.0 0.7 %copy-start.5 = (s32[128]{0:T(128)S(1)}, s32[128]{0:T(128)}, u32[]{:S(2)}) copy-start(s32[128]{0:T(128)} %param.10) | copy-start | bytes 1540
  3.0 4.9 %collective-permute-start = (bf16[12,128,128]{2,1,0:T(8,128)(2,1)S(1)}, bf16[12,128,128]{2,1,0:T(8,128)(2,1)S(1)}, u32[]{:S(2)}, u32[]{:S(2)}) collective-permute-start(bf16[12,128,128]{2,1,0:T(8,128)(2,1)S(1)} %get-tuple-element.17), channel_id=1, source_target_pairs={{0,8},{8,0},{16,24},{24,16},{1,9},{9,1},{17,25},{25,17},{2,10},{10... | collective-permute-start | bytes 1179656 | tf_op jit(solution)/shard_map/ppermute | solution.py:371
  4.8 10.1 %collective-permute-start.7 = (bf16[8,128,128]{2,1,0:T(8,128)(2,1)S(1)}, bf16[8,128,128]{2,1,0:T(8,128)(2,1)S(1)}, u32[]{:S(2)}, u32[]{:S(2)}) collective-permute-start(bf16[8,128,128]{2,1,0:T(8,128)(2,1)S(1)} %get-tuple-element.26.sent_ref), channel_id=1, source_target_pairs={{0,1},{1,0},{2,3},{3,2},{4,5},{5,4},{6,7},{7,6},{8,9},{9,8},{10,11... | collective-permute-start | bytes 786440 | tf_op jit(solution)/shard_map/ppermute | solution.py:367
  7.8 17.3 %collective-permute-start.9 = (bf16[12,128,128]{2,1,0:T(8,128)(2,1)S(1)}, bf16[12,128,128]{2,1,0:T(8,128)(2,1)S(1)}, u32[]{:S(2)}, u32[]{:S(2)}) collective-permute-start(bf16[12,128,128]{2,1,0:T(8,128)(2,1)S(1)} %get-tuple-element.27.rest_ref), channel_id=1, source_target_pairs={{0,1},{1,0},{2,3},{3,2},{4,5},{5,4},{6,7},{7,6},{8,9},{9,8},{10,11... | collective-permute-start | bytes 1179656 | tf_op jit(solution)/shard_map/ppermute | solution.py:367
  8.5 8.7 %collective-permute-start.1 = (bf16[3,128,128]{2,1,0:T(8,128)(2,1)S(1)}, bf16[3,128,128]{2,1,0:T(8,128)(2,1)S(1)}, u32[]{:S(2)}, u32[]{:S(2)}) collective-permute-start(bf16[3,128,128]{2,1,0:T(8,128)(2,1)S(1)} %get-tuple-element.21), channel_id=1, source_target_pairs={{0,6},{1,7},{2,4},{3,5},{4,2},{5,3},{6,0},{7,1},{8,14},{9,15},{10,... | collective-permute-start | bytes 294920 | tf_op jit(solution)/shard_map/ppermute | solution.py:367
  12.6 7.9 %collective-permute-start.2 = (bf16[3,128,128]{2,1,0:T(8,128)(2,1)S(1)}, bf16[3,128,128]{2,1,0:T(8,128)(2,1)S(1)}, u32[]{:S(2)}, u32[]{:S(2)}) collective-permute-start(bf16[3,128,128]{2,1,0:T(8,128)(2,1)S(1)} %get-tuple-element.22), channel_id=1, source_target_pairs={{0,4},{1,5},{2,6},{3,7},{4,0},{5,1},{6,2},{7,3},{8,12},{9,13},{10,... | collective-permute-start | bytes 294920 | tf_op jit(solution)/shard_map/ppermute | solution.py:367
  12.6 7.9 %collective-permute-start.3 = (bf16[3,128,128]{2,1,0:T(8,128)(2,1)S(1)}, bf16[3,128,128]{2,1,0:T(8,128)(2,1)S(1)}, u32[]{:S(2)}, u32[]{:S(2)}) collective-permute-start(bf16[3,128,128]{2,1,0:T(8,128)(2,1)S(1)} %get-tuple-element.23), channel_id=1, source_target_pairs={{0,2},{1,3},{2,0},{3,1},{4,6},{5,7},{6,4},{7,5},{8,10},{9,11},{10,... | collective-permute-start | bytes 294920 | tf_op jit(solution)/shard_map/ppermute | solution.py:367
  15.0 9.2 %collective-permute-start.8 = (bf16[4,128,128]{2,1,0:T(8,128)(2,1)S(1)}, bf16[4,128,128]{2,1,0:T(8,128)(2,1)S(1)}, u32[]{:S(2)}, u32[]{:S(2)}) collective-permute-start(bf16[4,128,128]{2,1,0:T(8,128)(2,1)S(1)} %shard_map.89.own_ref.after_ref), channel_id=1, source_target_pairs={{0,2},{1,3},{2,0},{3,1},{4,6},{5,7},{6,4},{7,5},{8,10},{9,11},{10,... | collective-permute-start | bytes 393224 | tf_op jit(solution)/shard_map/ppermute | solution.py:367
  20.6 7.0 %collective-permute-start.4 = (bf16[2,128,128]{2,1,0:T(8,128)(2,1)S(1)}, bf16[2,128,128]{2,1,0:T(8,128)(2,1)S(1)}, u32[]{:S(2)}, u32[]{:S(2)}) collective-permute-start(bf16[2,128,128]{2,1,0:T(8,128)(2,1)S(1)} %get-tuple-element.24.below_ref.after_ref), channel_id=1, source_target_pairs={{0,1},{1,0},{2,3},{3,2},{4,5},{5,4},{6,7},{7,6},{8,9},{9,8},{10,11... | collective-permute-start | bytes 196616 | tf_op jit(solution)/shard_map/ppermute | solution.py:367
  22.3 5.2 %collective-permute-start.6 = (bf16[1,128,128]{2,1,0:T(8,128)(2,1)S(1)}, bf16[1,128,128]{2,1,0:T(8,128)(2,1)S(1)}, u32[]{:S(2)}, u32[]{:S(2)}) collective-permute-start(bf16[1,128,128]{2,1,0:T(8,128)(2,1)S(1)} %get-tuple-element.25), channel_id=1, source_target_pairs={{0,17},{1,16},{2,19},{3,18},{4,21},{5,20},{6,23},{7,22},{8,25},{9,... | collective-permute-start | bytes 98312 | tf_op jit(solution)/shard_map/ppermute | solution.py:372
  23.8 3.9 %collective-permute-start.5 = (bf16[1,128,128]{2,1,0:T(8,128)(2,1)S(1)}, bf16[1,128,128]{2,1,0:T(8,128)(2,1)S(1)}, u32[]{:S(2)}, u32[]{:S(2)}) collective-permute-start(bf16[1,128,128]{2,1,0:T(8,128)(2,1)S(1)} %get-tuple-element.25), channel_id=1, source_target_pairs={{0,16},{8,24},{16,0},{24,8},{1,17},{9,25},{17,1},{25,9},{2,18},{10... | collective-permute-start | bytes 98312 | tf_op jit(solution)/shard_map/ppermute | solution.py:371
  24.2 10.9 %collective-permute-start.11 = (bf16[4,128,128]{2,1,0:T(8,128)(2,1)S(1)}, bf16[4,128,128]{2,1,0:T(8,128)(2,1)S(1)}, u32[]{:S(2)}, u32[]{:S(2)}) collective-permute-start(bf16[4,128,128]{2,1,0:T(8,128)(2,1)S(1)} %shard_map.90.refs_0_), channel_id=1, source_target_pairs={{0,4},{1,5},{2,6},{3,7},{4,0},{5,1},{6,2},{7,3},{8,12},{9,13},{10,... | collective-permute-start | bytes 393224 | tf_op jit(solution)/shard_map/ppermute | solution.py:367
  25.2 15.2 %collective-permute-start.10 = (bf16[8,128,128]{2,1,0:T(8,128)(2,1)S(1)}, bf16[8,128,128]{2,1,0:T(8,128)(2,1)S(1)}, u32[]{:S(2)}, u32[]{:S(2)}) collective-permute-start(bf16[8,128,128]{2,1,0:T(8,128)(2,1)S(1)} %shard_map.93), channel_id=1, source_target_pairs={{0,2},{1,3},{2,0},{3,1},{4,6},{5,7},{6,4},{7,5},{8,10},{9,11},{10,... | collective-permute-start | bytes 786440 | tf_op jit(solution)/shard_map/ppermute | solution.py:367
  27.7 11.1 %collective-permute-start.15 = (bf16[3,128,128]{2,1,0:T(8,128)(2,1)S(1)}, bf16[3,128,128]{2,1,0:T(8,128)(2,1)S(1)}, u32[]{:S(2)}, u32[]{:S(2)}) collective-permute-start(bf16[3,128,128]{2,1,0:T(8,128)(2,1)S(1)} %shard_map.91.after_ref.piece0_ref), channel_id=1, source_target_pairs={{0,6},{1,7},{2,4},{3,5},{4,2},{5,3},{6,0},{7,1},{8,14},{9,15},{10,... | collective-permute-start | bytes 294920 | tf_op jit(solution)/shard_map/ppermute | solution.py:367
  30.2 8.6 %collective-permute-start.14 = (bf16[3,128,128]{2,1,0:T(8,128)(2,1)S(1)}, bf16[3,128,128]{2,1,0:T(8,128)(2,1)S(1)}, u32[]{:S(2)}, u32[]{:S(2)}) collective-permute-start(bf16[3,128,128]{2,1,0:T(8,128)(2,1)S(1)} %shard_map.91.after_ref.piece0_ref), channel_id=1, source_target_pairs={{0,4},{1,5},{2,6},{3,7},{4,0},{5,1},{6,2},{7,3},{8,12},{9,13},{10,... | collective-permute-start | bytes 294920 | tf_op jit(solution)/shard_map/ppermute | solution.py:367
  31.0 9.3 %collective-permute-start.13 = (bf16[3,128,128]{2,1,0:T(8,128)(2,1)S(1)}, bf16[3,128,128]{2,1,0:T(8,128)(2,1)S(1)}, u32[]{:S(2)}, u32[]{:S(2)}) collective-permute-start(bf16[3,128,128]{2,1,0:T(8,128)(2,1)S(1)} %shard_map.91.after_ref.piece0_ref), channel_id=1, source_target_pairs={{0,2},{1,3},{2,0},{3,1},{4,6},{5,7},{6,4},{7,5},{8,10},{9,11},{10,... | collective-permute-start | bytes 294920 | tf_op jit(solution)/shard_map/ppermute | solution.py:367
  35.2 5.2 %collective-permute-start.12 = (bf16[4,128,128]{2,1,0:T(8,128)(2,1)S(1)}, bf16[4,128,128]{2,1,0:T(8,128)(2,1)S(1)}, u32[]{:S(2)}, u32[]{:S(2)}) collective-permute-start(bf16[4,128,128]{2,1,0:T(8,128)(2,1)S(1)} %collective-permute-done.11.after_ref.two_own_ref), channel_id=1, source_target_pairs={{0,1},{1,0},{2,3},{3,2},{4,5},{5,4},{6,7},{7,6},{8,9},{9,8},{10,11... | collective-permute-start | bytes 393224 | tf_op jit(solution)/shard_map/ppermute | solution.py:367
  40.3 1.4 %collective-permute-start.16 = (bf16[1,4,128,128]{3,2,1,0:T(8,128)(2,1)S(1)}, bf16[1,4,128,128]{3,2,1,0:T(8,128)(2,1)S(1)}, u32[]{:S(2)}, u32[]{:S(2)}) collective-permute-start(bf16[1,4,128,128]{3,2,1,0:T(8,128)(2,1)S(1)} %shard_map.94.split_own_ref), channel_id=1, source_target_pairs={{0,8},{8,0},{16,24},{24,16},{1,9},{9,1},{17,25},{25,17},{2,10},{10... | collective-permute-start | bytes 393224 | tf_op jit(solution)/shard_map/ppermute | solution.py:371

commit v13 on v12

--- a/solution.py
+++ b/solution.py
@@ -483,24 +483,24 @@
                 row += size
         below = narrow(jnp.concatenate([parts[level] for level in range(NEAR, top)], axis=0))
         top_sent = narrow(parts[top])
-    one_sum = call(
-        one_sum_kernel,
-        [vmem] * 4 + [anywhere],
-        cells(head_count),
-        (lower_sent, lower_seen, rest, rest_seen, below),
-    )
     two_sum = call(
         two_sum_kernel, [vmem] * 2 + [anywhere], cells(half), (two_sum, swap(two_sum, 1), two_sum)
     )
     two_half = swap(two_sum, 2)
     two_rest = swap(two_half, 0)
-    one_done = swap(one_sum, 1)
     shares = call(
         pair_sum_kernel,
         [vmem] * 4 + [anywhere] * 2,
         cells(share_rows),
         (below, swap(below, 0), swap(top_sent, top), swap(top_sent, 0, top), two_sum, rest_seen),
     )
+    one_sum = call(
+        one_sum_kernel,
+        [vmem] * 4 + [anywhere],
+        cells(head_count),
+        (lower_sent, lower_seen, rest, rest_seen, shares),
+    )
+    one_done = swap(one_sum, 1)
     query_local, key_local, value_local = call(
         functools.partial(local_kernel, block_depth, head_size),
         [vmem] * 6 + [anywhere],

time: 44.7 us -> 45.9 us (1.027)
  waiting for transfers between devices: 11.2 us -> 12.9 us
  starting transfers between devices: 23.3 us -> 22.8 us
    ppermute x1, waiting for transfers between devices: 0.01 us -> 1.98 us  [swap(): lax.ppermute(block, ('gx', 'gy'), [(i, i ^ mask) for i in range(device_co...]
    ppermute x13, waiting for transfers between devices: 9.68 us -> 9.01 us  [swap(): return lax.ppermute(block, 'gy', [(i, i ^ mask) for i in range(inner_size)])]
    ppermute x13, starting transfers between devices: 20.8 us -> 20.3 us  [swap(): return lax.ppermute(block, 'gy', [(i, i ^ mask) for i in range(inner_size)])]
where the time goes in v13:
time: 45.9 us; the launch traced here: 45.8 us
  starting transfers between devices  22.8 us (50%)
  waiting for transfers between devices  12.9 us (28%)
  Pallas kernels  9.12 us (20%)
  between operations  0.79 us (2%)
    ppermute x13, starting transfers between devices, swap(): return lax.ppermute(block, 'gy', [(i, i ^ mask) for i in range(inner_size)])  20.3 us
    pallas_call x11, Pallas kernels, call(): pl.pallas_call(kernel, out_shape=outs, in_specs=in_specs, out_specs=out_s...  9.12 us
    ppermute x13, waiting for transfers between devices, swap(): return lax.ppermute(block, 'gy', [(i, i ^ mask) for i in range(inner_size)])  9.01 us
    ppermute x1, waiting for transfers between devices, swap(): lax.ppermute(block, ('gx', 'gy'), [(i, i ^ mask) for i in range(device_co...  1.98 us
    ppermute x3, waiting for transfers between devices, swap(): return lax.ppermute(block, 'gx', [(i, i ^ mask) for i in range(size)])  1.91 us
    ppermute x1, starting transfers between devices, swap(): lax.ppermute(block, ('gx', 'gy'), [(i, i ^ mask) for i in range(device_co...  1.49 us
    ppermute x3, starting transfers between devices, swap(): return lax.ppermute(block, 'gx', [(i, i ^ mask) for i in range(size)])  1.03 us
  transfers between devices with their start and end apart: 17, of which 7 were waited for; matrix products, arithmetic and copies ran while one was open for 0% of the time, Pallas kernels for 9%

profile of v13, /device:TPU:0, one launch (start us, length us, event | category | flops | bytes accessed | tf_op | source)
XLA Modules:
  0.0 45.8 jit_solution(4059795996715643111)
XLA Ops:
  0.7 0.0 copy-start.1
  0.7 2.3 %shard_map.85 = (bf16[12,128,128]{2,1,0:T(8,128)(2,1)S(1)}, bf16[4,128,128]{2,1,0:T(8,128)(2,1)S(1)}) custom-call(s32[5]{0:T(128)S(1)} %shift-right-arithmetic_and_fusion.flag_ref, s32[1,128]{1,0:T(1,128)} %bitcast.6, f32[20,8,32]{2,1,0:T(8,128)} %bitcast.2, bf16[128,1024]{1,0:T(8,128)(2,1)} %q_ref.3, bf16[128,1024]{1,0:T(8,128)(2,1)} %k_ref.5, ...), custom_call_target="tpu_custom_call" | custom-call | flops 67108864 | bytes 1069588 | tf_op jit(solution)/shard_map/pallas_call | solution.py:387
  3.0 0.5 %collective-permute-start = (bf16[12,128,128]{2,1,0:T(8,128)(2,1)S(1)}, bf16[12,128,128]{2,1,0:T(8,128)(2,1)S(1)}, u32[]{:S(2)}, u32[]{:S(2)}) collective-permute-start(bf16[12,128,128]{2,1,0:T(8,128)(2,1)S(1)} %get-tuple-element.17), channel_id=1, source_target_pairs={{0,8},{8,0},{16,24},{24,16},{1,9},{9,1},{17,25},{25,17},{2,10},{10... | collective-permute-start | bytes 1179656 | tf_op jit(solution)/shard_map/ppermute | solution.py:371
  3.5 0.1 copy-done.5
  3.6 1.2 %shard_map.86 = (bf16[4,128,128]{2,1,0:T(8,128)(2,1)S(1)}, bf16[8,128,128]{2,1,0:T(8,128)(2,1)S(1)}, bf16[12,128,128]{2,1,0:T(8,128)(2,1)S(1)}) custom-call(s32[5]{0:T(128)S(1)} %shift-right-arithmetic_and_fusion.flag_ref, s32[1,128]{1,0:T(1,128)S(1)} %bitcast.7, f32[20,8,32]{2,1,0:T(8,128)S(1)} %bitcast.3, bf16[128,1024]{1,0:T(8,128)(2,1)S(1)} %copy-done.3, ...), custom_call_target="tpu_custom_call" | custom-call | flops 100663296 | bytes 1200660 | tf_op jit(solution)/shard_map/pallas_call | solution.py:387
  4.8 3.0 %collective-permute-start.7 = (bf16[8,128,128]{2,1,0:T(8,128)(2,1)S(1)}, bf16[8,128,128]{2,1,0:T(8,128)(2,1)S(1)}, u32[]{:S(2)}, u32[]{:S(2)}) collective-permute-start(bf16[8,128,128]{2,1,0:T(8,128)(2,1)S(1)} %get-tuple-element.26.sent_ref), channel_id=1, source_target_pairs={{0,1},{1,0},{2,3},{3,2},{4,5},{5,4},{6,7},{7,6},{8,9},{9,8},{10,11... | collective-permute-start | bytes 786440 | tf_op jit(solution)/shard_map/ppermute | solution.py:367
  7.8 0.1 collective-permute-start.9
  7.9 0.6 %shard_map.87 = (bf16[3,128,128]{2,1,0:T(8,128)(2,1)S(1)}, bf16[3,128,128]{2,1,0:T(8,128)(2,1)S(1)}, bf16[3,128,128]{2,1,0:T(8,128)(2,1)S(1)}, bf16[3,128,128]{2,1,0:T(8,128)(2,1)S(1)}) custom-call(s32[5]{0:T(128)S(1)} %shift-right-arithmetic_and_fusion.flag_ref, bf16[12,128,128]{2,1,0:T(8,128)(2,1)S(1)} %collective-permute-done.seen_ref, ...), custom_call_target="tpu_custom_call" | custom-call | bytes 655380 | tf_op jit(solution)/shard_map/pallas_call | solution.py:387
  8.5 4.1 %collective-permute-start.1 = (bf16[3,128,128]{2,1,0:T(8,128)(2,1)S(1)}, bf16[3,128,128]{2,1,0:T(8,128)(2,1)S(1)}, u32[]{:S(2)}, u32[]{:S(2)}) collective-permute-start(bf16[3,128,128]{2,1,0:T(8,128)(2,1)S(1)} %get-tuple-element.21), channel_id=1, source_target_pairs={{0,6},{1,7},{2,4},{3,5},{4,2},{5,3},{6,0},{7,1},{8,14},{9,15},{10,... | collective-permute-start | bytes 294920 | tf_op jit(solution)/shard_map/ppermute | solution.py:367
  12.6 0.6 %collective-permute-start.3 = (bf16[3,128,128]{2,1,0:T(8,128)(2,1)S(1)}, bf16[3,128,128]{2,1,0:T(8,128)(2,1)S(1)}, u32[]{:S(2)}, u32[]{:S(2)}) collective-permute-start(bf16[3,128,128]{2,1,0:T(8,128)(2,1)S(1)} %get-tuple-element.23), channel_id=1, source_target_pairs={{0,2},{1,3},{2,0},{3,1},{4,6},{5,7},{6,4},{7,5},{8,10},{9,11},{10,... | collective-permute-start | bytes 294920 | tf_op jit(solution)/shard_map/ppermute | solution.py:367
  13.3 1.7 %collective-permute-done.7.seen_ref = bf16[8,128,128]{2,1,0:T(8,128)(2,1)S(1)} collective-permute-done((bf16[8,128,128]{2,1,0:T(8,128)(2,1)S(1)}, bf16[8,128,128]{2,1,0:T(8,128)(2,1)S(1)}, u32[]{:S(2)}, u32[]{:S(2)}) %collective-permute-start.7) | collective-permute-done | bytes 262176 | tf_op jit(solution)/shard_map/ppermute | solution.py:367
  15.0 2.2 %collective-permute-start.8 = (bf16[4,128,128]{2,1,0:T(8,128)(2,1)S(1)}, bf16[4,128,128]{2,1,0:T(8,128)(2,1)S(1)}, u32[]{:S(2)}, u32[]{:S(2)}) collective-permute-start(bf16[4,128,128]{2,1,0:T(8,128)(2,1)S(1)} %shard_map.89.own_ref.after_ref), channel_id=1, source_target_pairs={{0,2},{1,3},{2,0},{3,1},{4,6},{5,7},{6,4},{7,5},{8,10},{9,11},{10,... | collective-permute-start | bytes 393224 | tf_op jit(solution)/shard_map/ppermute | solution.py:367
  17.2 3.4 %collective-permute-done.2.refs_1_ = bf16[3,128,128]{2,1,0:T(8,128)(2,1)S(1)} collective-permute-done((bf16[3,128,128]{2,1,0:T(8,128)(2,1)S(1)}, bf16[3,128,128]{2,1,0:T(8,128)(2,1)S(1)}, u32[]{:S(2)}, u32[]{:S(2)}) %collective-permute-start.2) | collective-permute-done | bytes 98336 | tf_op jit(solution)/shard_map/ppermute | solution.py:367
  20.6 0.1 shard_map.88
  20.6 1.6 %collective-permute-start.4 = (bf16[2,128,128]{2,1,0:T(8,128)(2,1)S(1)}, bf16[2,128,128]{2,1,0:T(8,128)(2,1)S(1)}, u32[]{:S(2)}, u32[]{:S(2)}) collective-permute-start(bf16[2,128,128]{2,1,0:T(8,128)(2,1)S(1)} %get-tuple-element.24.below_ref), channel_id=1, source_target_pairs={{0,1},{1,0},{2,3},{3,2},{4,5},{5,4},{6,7},{7,6},{8,9},{9,8},{10,11... | collective-permute-start | bytes 196616 | tf_op jit(solution)/shard_map/ppermute | solution.py:367
  22.3 1.5 %collective-permute-start.6 = (bf16[1,128,128]{2,1,0:T(8,128)(2,1)S(1)}, bf16[1,128,128]{2,1,0:T(8,128)(2,1)S(1)}, u32[]{:S(2)}, u32[]{:S(2)}) collective-permute-start(bf16[1,128,128]{2,1,0:T(8,128)(2,1)S(1)} %get-tuple-element.25), channel_id=1, source_target_pairs={{0,17},{1,16},{2,19},{3,18},{4,21},{5,20},{6,23},{7,22},{8,25},{9,... | collective-permute-start | bytes 98312 | tf_op jit(solution)/shard_map/ppermute | solution.py:372
  23.8 0.4 collective-permute-start.5
  24.2 0.9 %collective-permute-start.11 = (bf16[4,128,128]{2,1,0:T(8,128)(2,1)S(1)}, bf16[4,128,128]{2,1,0:T(8,128)(2,1)S(1)}, u32[]{:S(2)}, u32[]{:S(2)}) collective-permute-start(bf16[4,128,128]{2,1,0:T(8,128)(2,1)S(1)} %shard_map.90.refs_0_), channel_id=1, source_target_pairs={{0,4},{1,5},{2,6},{3,7},{4,0},{5,1},{6,2},{7,3},{8,12},{9,13},{10,... | collective-permute-start | bytes 393224 | tf_op jit(solution)/shard_map/ppermute | solution.py:367
  25.1 2.0 %collective-permute-done.6.far_top_ref = bf16[1,128,128]{2,1,0:T(8,128)(2,1)S(1)} collective-permute-done((bf16[1,128,128]{2,1,0:T(8,128)(2,1)S(1)}, bf16[1,128,128]{2,1,0:T(8,128)(2,1)S(1)}, u32[]{:S(2)}, u32[]{:S(2)}) %collective-permute-start.6) | collective-permute-done | bytes 32800 | tf_op jit(solution)/shard_map/ppermute | solution.py:372
  27.1 0.6 %collective-permute-done.5.near_top_ref = bf16[1,128,128]{2,1,0:T(8,128)(2,1)S(1)} collective-permute-done((bf16[1,128,128]{2,1,0:T(8,128)(2,1)S(1)}, bf16[1,128,128]{2,1,0:T(8,128)(2,1)S(1)}, u32[]{:S(2)}, u32[]{:S(2)}) %collective-permute-start.5) | collective-permute-done | bytes 32800 | tf_op jit(solution)/shard_map/ppermute | solution.py:371
  27.7 0.1 shard_map.93
  27.8 1.8 %collective-permute-start.10 = (bf16[8,128,128]{2,1,0:T(8,128)(2,1)S(1)}, bf16[8,128,128]{2,1,0:T(8,128)(2,1)S(1)}, u32[]{:S(2)}, u32[]{:S(2)}) collective-permute-start(bf16[8,128,128]{2,1,0:T(8,128)(2,1)S(1)} %shard_map.93), channel_id=1, source_target_pairs={{0,2},{1,3},{2,0},{3,1},{4,6},{5,7},{6,4},{7,5},{8,10},{9,11},{10,... | collective-permute-start | bytes 786440 | tf_op jit(solution)/shard_map/ppermute | solution.py:367
  29.6 0.8 %collective-permute-start.15 = (bf16[3,128,128]{2,1,0:T(8,128)(2,1)S(1)}, bf16[3,128,128]{2,1,0:T(8,128)(2,1)S(1)}, u32[]{:S(2)}, u32[]{:S(2)}) collective-permute-start(bf16[3,128,128]{2,1,0:T(8,128)(2,1)S(1)} %shard_map.91.after_ref.piece0_ref), channel_id=1, source_target_pairs={{0,6},{1,7},{2,4},{3,5},{4,2},{5,3},{6,0},{7,1},{8,14},{9,15},{10,... | collective-permute-start | bytes 294920 | tf_op jit(solution)/shard_map/ppermute | solution.py:367
  30.4 0.9 %collective-permute-start.14 = (bf16[3,128,128]{2,1,0:T(8,128)(2,1)S(1)}, bf16[3,128,128]{2,1,0:T(8,128)(2,1)S(1)}, u32[]{:S(2)}, u32[]{:S(2)}) collective-permute-start(bf16[3,128,128]{2,1,0:T(8,128)(2,1)S(1)} %shard_map.91.after_ref.piece0_ref), channel_id=1, source_target_pairs={{0,4},{1,5},{2,6},{3,7},{4,0},{5,1},{6,2},{7,3},{8,12},{9,13},{10,... | collective-permute-start | bytes 294920 | tf_op jit(solution)/shard_map/ppermute | solution.py:367
  31.3 2.7 %collective-permute-start.13 = (bf16[3,128,128]{2,1,0:T(8,128)(2,1)S(1)}, bf16[3,128,128]{2,1,0:T(8,128)(2,1)S(1)}, u32[]{:S(2)}, u32[]{:S(2)}) collective-permute-start(bf16[3,128,128]{2,1,0:T(8,128)(2,1)S(1)} %shard_map.91.after_ref.piece0_ref), channel_id=1, source_target_pairs={{0,2},{1,3},{2,0},{3,1},{4,6},{5,7},{6,4},{7,5},{8,10},{9,11},{10,... | collective-permute-start | bytes 294920 | tf_op jit(solution)/shard_map/ppermute | solution.py:367
  34.0 2.0 %shard_map.92 = (f32[128,1024]{1,0:T(8,128)S(1)}, f32[128,1024]{1,0:T(8,128)S(1)}, f32[128,1024]{1,0:T(8,128)S(1)}) custom-call(s32[1,128]{1,0:T(1,128)S(1)} %bitcast.8, f32[20,8,32]{2,1,0:T(8,128)S(1)} %bitcast.4, bf16[128,1024]{1,0:T(8,128)(2,1)S(1)} %copy-done.3, bf16[128,1024]{1,0:T(8,128)(2,1)S(1)} %copy-done, bf16[128,1024]{1,0:T(8,128)(2,1)S(1)} %copy-done.1, ...), custom_call_target="tpu_custom_call" | custom-call | flops 167772160 | bytes 1167872 | tf_op jit(solution)/shard_map/pallas_call | solution.py:387
  36.0 1.6 %collective-permute-start.12 = (bf16[4,128,128]{2,1,0:T(8,128)(2,1)S(1)}, bf16[4,128,128]{2,1,0:T(8,128)(2,1)S(1)}, u32[]{:S(2)}, u32[]{:S(2)}) collective-permute-start(bf16[4,128,128]{2,1,0:T(8,128)(2,1)S(1)} %collective-permute-done.11.after_ref.two_own_ref), channel_id=1, source_target_pairs={{0,1},{1,0},{2,3},{3,2},{4,5},{5,4},{6,7},{7,6},{8,9},{9,8},{10,11... | collective-permute-start | bytes 393224 | tf_op jit(solution)/shard_map/ppermute | solution.py:367
  37.6 2.9 %collective-permute-done.15.piece3_ref = bf16[3,128,128]{2,1,0:T(8,128)(2,1)S(1)} collective-permute-done((bf16[3,128,128]{2,1,0:T(8,128)(2,1)S(1)}, bf16[3,128,128]{2,1,0:T(8,128)(2,1)S(1)}, u32[]{:S(2)}, u32[]{:S(2)}) %collective-permute-start.15) | collective-permute-done | bytes 98336 | tf_op jit(solution)/shard_map/ppermute | solution.py:367
  40.5 1.1 %collective-permute-done.13.piece1_ref = bf16[3,128,128]{2,1,0:T(8,128)(2,1)S(1)} collective-permute-done((bf16[3,128,128]{2,1,0:T(8,128)(2,1)S(1)}, bf16[3,128,128]{2,1,0:T(8,128)(2,1)S(1)}, u32[]{:S(2)}, u32[]{:S(2)}) %collective-permute-start.13) | collective-permute-done | bytes 98336 | tf_op jit(solution)/shard_map/ppermute | solution.py:367
  41.5 0.1 collective-permute-start.16
  41.6 1.3 %collective-permute-done.16.split_other_ref = bf16[1,4,128,128]{3,2,1,0:T(8,128)(2,1)S(1)} collective-permute-done((bf16[1,4,128,128]{3,2,1,0:T(8,128)(2,1)S(1)}, bf16[1,4,128,128]{3,2,1,0:T(8,128)(2,1)S(1)}, u32[]{:S(2)}, u32[]{:S(2)}) %collective-permute-start.16) | collective-permute-done | bytes 131104 | tf_op jit(solution)/shard_map/ppermute | solution.py:371
  43.0 2.8 %shard_map.95 = (bf16[128,1024]{1,0:T(8,128)(2,1)}, bf16[128,1024]{1,0:T(8,128)(2,1)}, bf16[128,1024]{1,0:T(8,128)(2,1)}) custom-call(s32[5]{0:T(128)S(1)} %shift-right-arithmetic_and_fusion.flag_ref, s32[1,128]{1,0:T(1,128)S(1)} %bitcast.9, f32[20,8,32]{2,1,0:T(8,128)S(1)} %bitcast.5, bf16[128,1024]{1,0:T(8,128)(2,1)S(1)} %copy-done, ...), custom_call_target="tpu_custom_call" | custom-call | flops 234881024 | bytes 3953172 | tf_op jit(solution)/shard_map/pallas_call | solution.py:387
  (26 shorter events, 0.2 us)
Async XLA Ops:
  0.6 2.9 %copy-start = (bf16[128,1024]{1,0:T(8,128)(2,1)S(1)}, bf16[128,1024]{1,0:T(8,128)(2,1)}, u32[]{:S(2)}) copy-start(bf16[128,1024]{1,0:T(8,128)(2,1)} %k_ref.5) | copy-start | bytes 786436
  0.7 2.9 %copy-start.1 = (bf16[128,1024]{1,0:T(8,128)(2,1)S(1)}, bf16[128,1024]{1,0:T(8,128)(2,1)}, u32[]{:S(2)}) copy-start(bf16[128,1024]{1,0:T(8,128)(2,1)} %v_ref.5) | copy-start | bytes 786436
  0.7 2.9 %copy-start.2 = (bf16[128,1024]{1,0:T(8,128)(2,1)S(1)}, bf16[128,1024]{1,0:T(8,128)(2,1)}, u32[]{:S(2)}) copy-start(bf16[128,1024]{1,0:T(8,128)(2,1)} %g_ref.5) | copy-start | bytes 786436
  0.7 2.8 %copy-start.3 = (bf16[128,1024]{1,0:T(8,128)(2,1)S(1)}, bf16[128,1024]{1,0:T(8,128)(2,1)}, u32[]{:S(2)}) copy-start(bf16[128,1024]{1,0:T(8,128)(2,1)} %q_ref.3) | copy-start | bytes 786436
  0.7 2.8 %copy-start.4 = (f32[32,20,8]{0,2,1:T(8,128)S(1)}, f32[32,20,8]{0,2,1:T(8,128)}, u32[]{:S(2)}) copy-start(f32[32,20,8]{0,2,1:T(8,128)} %param.11) | copy-start | bytes 61444
  3.0 0.7 %copy-start.5 = (s32[128]{0:T(128)S(1)}, s32[128]{0:T(128)}, u32[]{:S(2)}) copy-start(s32[128]{0:T(128)} %param.10) | copy-start | bytes 1540
  3.0 4.9 %collective-permute-start = (bf16[12,128,128]{2,1,0:T(8,128)(2,1)S(1)}, bf16[12,128,128]{2,1,0:T(8,128)(2,1)S(1)}, u32[]{:S(2)}, u32[]{:S(2)}) collective-permute-start(bf16[12,128,128]{2,1,0:T(8,128)(2,1)S(1)} %get-tuple-element.17), channel_id=1, source_target_pairs={{0,8},{8,0},{16,24},{24,16},{1,9},{9,1},{17,25},{25,17},{2,10},{10... | collective-permute-start | bytes 1179656 | tf_op jit(solution)/shard_map/ppermute | solution.py:371
  4.8 10.1 %collective-permute-start.7 = (bf16[8,128,128]{2,1,0:T(8,128)(2,1)S(1)}, bf16[8,128,128]{2,1,0:T(8,128)(2,1)S(1)}, u32[]{:S(2)}, u32[]{:S(2)}) collective-permute-start(bf16[8,128,128]{2,1,0:T(8,128)(2,1)S(1)} %get-tuple-element.26.sent_ref), channel_id=1, source_target_pairs={{0,1},{1,0},{2,3},{3,2},{4,5},{5,4},{6,7},{7,6},{8,9},{9,8},{10,11... | collective-permute-start | bytes 786440 | tf_op jit(solution)/shard_map/ppermute | solution.py:367
  7.8 17.3 %collective-permute-start.9 = (bf16[12,128,128]{2,1,0:T(8,128)(2,1)S(1)}, bf16[12,128,128]{2,1,0:T(8,128)(2,1)S(1)}, u32[]{:S(2)}, u32[]{:S(2)}) collective-permute-start(bf16[12,128,128]{2,1,0:T(8,128)(2,1)S(1)} %get-tuple-element.27.rest_ref), channel_id=1, source_target_pairs={{0,1},{1,0},{2,3},{3,2},{4,5},{5,4},{6,7},{7,6},{8,9},{9,8},{10,11... | collective-permute-start | bytes 1179656 | tf_op jit(solution)/shard_map/ppermute | solution.py:367
  8.5 8.7 %collective-permute-start.1 = (bf16[3,128,128]{2,1,0:T(8,128)(2,1)S(1)}, bf16[3,128,128]{2,1,0:T(8,128)(2,1)S(1)}, u32[]{:S(2)}, u32[]{:S(2)}) collective-permute-start(bf16[3,128,128]{2,1,0:T(8,128)(2,1)S(1)} %get-tuple-element.21), channel_id=1, source_target_pairs={{0,6},{1,7},{2,4},{3,5},{4,2},{5,3},{6,0},{7,1},{8,14},{9,15},{10,... | collective-permute-start | bytes 294920 | tf_op jit(solution)/shard_map/ppermute | solution.py:367
  12.6 7.9 %collective-permute-start.2 = (bf16[3,128,128]{2,1,0:T(8,128)(2,1)S(1)}, bf16[3,128,128]{2,1,0:T(8,128)(2,1)S(1)}, u32[]{:S(2)}, u32[]{:S(2)}) collective-permute-start(bf16[3,128,128]{2,1,0:T(8,128)(2,1)S(1)} %get-tuple-element.22), channel_id=1, source_target_pairs={{0,4},{1,5},{2,6},{3,7},{4,0},{5,1},{6,2},{7,3},{8,12},{9,13},{10,... | collective-permute-start | bytes 294920 | tf_op jit(solution)/shard_map/ppermute | solution.py:367
  12.6 7.9 %collective-permute-start.3 = (bf16[3,128,128]{2,1,0:T(8,128)(2,1)S(1)}, bf16[3,128,128]{2,1,0:T(8,128)(2,1)S(1)}, u32[]{:S(2)}, u32[]{:S(2)}) collective-permute-start(bf16[3,128,128]{2,1,0:T(8,128)(2,1)S(1)} %get-tuple-element.23), channel_id=1, source_target_pairs={{0,2},{1,3},{2,0},{3,1},{4,6},{5,7},{6,4},{7,5},{8,10},{9,11},{10,... | collective-permute-start | bytes 294920 | tf_op jit(solution)/shard_map/ppermute | solution.py:367
  15.0 9.2 %collective-permute-start.8 = (bf16[4,128,128]{2,1,0:T(8,128)(2,1)S(1)}, bf16[4,128,128]{2,1,0:T(8,128)(2,1)S(1)}, u32[]{:S(2)}, u32[]{:S(2)}) collective-permute-start(bf16[4,128,128]{2,1,0:T(8,128)(2,1)S(1)} %shard_map.89.own_ref.after_ref), channel_id=1, source_target_pairs={{0,2},{1,3},{2,0},{3,1},{4,6},{5,7},{6,4},{7,5},{8,10},{9,11},{10,... | collective-permute-start | bytes 393224 | tf_op jit(solution)/shard_map/ppermute | solution.py:367
  20.6 7.0 %collective-permute-start.4 = (bf16[2,128,128]{2,1,0:T(8,128)(2,1)S(1)}, bf16[2,128,128]{2,1,0:T(8,128)(2,1)S(1)}, u32[]{:S(2)}, u32[]{:S(2)}) collective-permute-start(bf16[2,128,128]{2,1,0:T(8,128)(2,1)S(1)} %get-tuple-element.24.below_ref), channel_id=1, source_target_pairs={{0,1},{1,0},{2,3},{3,2},{4,5},{5,4},{6,7},{7,6},{8,9},{9,8},{10,11... | collective-permute-start | bytes 196616 | tf_op jit(solution)/shard_map/ppermute | solution.py:367
  22.3 4.8 %collective-permute-start.6 = (bf16[1,128,128]{2,1,0:T(8,128)(2,1)S(1)}, bf16[1,128,128]{2,1,0:T(8,128)(2,1)S(1)}, u32[]{:S(2)}, u32[]{:S(2)}) collective-permute-start(bf16[1,128,128]{2,1,0:T(8,128)(2,1)S(1)} %get-tuple-element.25), channel_id=1, source_target_pairs={{0,17},{1,16},{2,19},{3,18},{4,21},{5,20},{6,23},{7,22},{8,25},{9,... | collective-permute-start | bytes 98312 | tf_op jit(solution)/shard_map/ppermute | solution.py:372
  23.8 3.9 %collective-permute-start.5 = (bf16[1,128,128]{2,1,0:T(8,128)(2,1)S(1)}, bf16[1,128,128]{2,1,0:T(8,128)(2,1)S(1)}, u32[]{:S(2)}, u32[]{:S(2)}) collective-permute-start(bf16[1,128,128]{2,1,0:T(8,128)(2,1)S(1)} %get-tuple-element.25), channel_id=1, source_target_pairs={{0,16},{8,24},{16,0},{24,8},{1,17},{9,25},{17,1},{25,9},{2,18},{10... | collective-permute-start | bytes 98312 | tf_op jit(solution)/shard_map/ppermute | solution.py:371
  24.2 11.8 %collective-permute-start.11 = (bf16[4,128,128]{2,1,0:T(8,128)(2,1)S(1)}, bf16[4,128,128]{2,1,0:T(8,128)(2,1)S(1)}, u32[]{:S(2)}, u32[]{:S(2)}) collective-permute-start(bf16[4,128,128]{2,1,0:T(8,128)(2,1)S(1)} %shard_map.90.refs_0_), channel_id=1, source_target_pairs={{0,4},{1,5},{2,6},{3,7},{4,0},{5,1},{6,2},{7,3},{8,12},{9,13},{10,... | collective-permute-start | bytes 393224 | tf_op jit(solution)/shard_map/ppermute | solution.py:367
  27.8 15.2 %collective-permute-start.10 = (bf16[8,128,128]{2,1,0:T(8,128)(2,1)S(1)}, bf16[8,128,128]{2,1,0:T(8,128)(2,1)S(1)}, u32[]{:S(2)}, u32[]{:S(2)}) collective-permute-start(bf16[8,128,128]{2,1,0:T(8,128)(2,1)S(1)} %shard_map.93), channel_id=1, source_target_pairs={{0,2},{1,3},{2,0},{3,1},{4,6},{5,7},{6,4},{7,5},{8,10},{9,11},{10,... | collective-permute-start | bytes 786440 | tf_op jit(solution)/shard_map/ppermute | solution.py:367
  29.6 10.9 %collective-permute-start.15 = (bf16[3,128,128]{2,1,0:T(8,128)(2,1)S(1)}, bf16[3,128,128]{2,1,0:T(8,128)(2,1)S(1)}, u32[]{:S(2)}, u32[]{:S(2)}) collective-permute-start(bf16[3,128,128]{2,1,0:T(8,128)(2,1)S(1)} %shard_map.91.after_ref.piece0_ref), channel_id=1, source_target_pairs={{0,6},{1,7},{2,4},{3,5},{4,2},{5,3},{6,0},{7,1},{8,14},{9,15},{10,... | collective-permute-start | bytes 294920 | tf_op jit(solution)/shard_map/ppermute | solution.py:367
  30.4 10.1 %collective-permute-start.14 = (bf16[3,128,128]{2,1,0:T(8,128)(2,1)S(1)}, bf16[3,128,128]{2,1,0:T(8,128)(2,1)S(1)}, u32[]{:S(2)}, u32[]{:S(2)}) collective-permute-start(bf16[3,128,128]{2,1,0:T(8,128)(2,1)S(1)} %shard_map.91.after_ref.piece0_ref), channel_id=1, source_target_pairs={{0,4},{1,5},{2,6},{3,7},{4,0},{5,1},{6,2},{7,3},{8,12},{9,13},{10,... | collective-permute-start | bytes 294920 | tf_op jit(solution)/shard_map/ppermute | solution.py:367
  31.3 10.2 %collective-permute-start.13 = (bf16[3,128,128]{2,1,0:T(8,128)(2,1)S(1)}, bf16[3,128,128]{2,1,0:T(8,128)(2,1)S(1)}, u32[]{:S(2)}, u32[]{:S(2)}) collective-permute-start(bf16[3,128,128]{2,1,0:T(8,128)(2,1)S(1)} %shard_map.91.after_ref.piece0_ref), channel_id=1, source_target_pairs={{0,2},{1,3},{2,0},{3,1},{4,6},{5,7},{6,4},{7,5},{8,10},{9,11},{10,... | collective-permute-start | bytes 294920 | tf_op jit(solution)/shard_map/ppermute | solution.py:367
  36.0 5.6 %collective-permute-start.12 = (bf16[4,128,128]{2,1,0:T(8,128)(2,1)S(1)}, bf16[4,128,128]{2,1,0:T(8,128)(2,1)S(1)}, u32[]{:S(2)}, u32[]{:S(2)}) collective-permute-start(bf16[4,128,128]{2,1,0:T(8,128)(2,1)S(1)} %collective-permute-done.11.after_ref.two_own_ref), channel_id=1, source_target_pairs={{0,1},{1,0},{2,3},{3,2},{4,5},{5,4},{6,7},{7,6},{8,9},{9,8},{10,11... | collective-permute-start | bytes 393224 | tf_op jit(solution)/shard_map/ppermute | solution.py:367
  41.5 1.4 %collective-permute-start.16 = (bf16[1,4,128,128]{3,2,1,0:T(8,128)(2,1)S(1)}, bf16[1,4,128,128]{3,2,1,0:T(8,128)(2,1)S(1)}, u32[]{:S(2)}, u32[]{:S(2)}) collective-permute-start(bf16[1,4,128,128]{3,2,1,0:T(8,128)(2,1)S(1)} %shard_map.94.split_own_ref), channel_id=1, source_target_pairs={{0,8},{8,0},{16,24},{24,16},{1,9},{9,1},{17,25},{25,17},{2,10},{10... | collective-permute-start | bytes 393224 | tf_op jit(solution)/shard_map/ppermute | solution.py:371

commit v14 on v12

--- a/solution.py
+++ b/solution.py
@@ -227,6 +227,8 @@
 def local_kernel(
     block_depth,
     head_size,
+    flag_ref,
+    zero_ref,
     class_ref,
     table_ref,
     q_ref,
@@ -240,7 +242,9 @@
 ):
     head_count = table_ref.shape[1]
     tokens = q_ref.shape[0]
-    gates = gate_lanes(class_ref, table_ref, 0, block_depth + 1)
+    gates = gate_lanes(class_ref, table_ref, 0, block_depth + 2)
+    outer = (gates[(block_depth + 1) * head_count :] * wide(flag_ref[0])).T
+    zero_first = zero_ref.shape[0] - head_count
     source = lax.broadcasted_iota(jnp.int32, (tokens, tokens), 0)
     target = lax.broadcasted_iota(jnp.int32, (tokens, tokens), 1)
     apart = jnp.bitwise_xor(source, target)
@@ -258,7 +262,10 @@
         weight = jnp.where(causal, weight, 0.0)
         weighted_scores = narrow(weight * product(key_here, query_here, 1, 1))
         weighted_grads = narrow(weight * product(value_here, grad_here, 1, 1))
-        qo_ref[:, columns] = product(weighted_grads, key_here, 0, 0)
+        outside = product(grad_here, zero_ref[zero_first + head], 1, 1)
+        qo_ref[:, columns] = (
+            product(weighted_grads, key_here, 0, 0) + outer[:, head : head + 1] * outside
+        )
         ko_ref[:, columns] = product(weighted_grads, query_here, 1, 0)
         vo_ref[:, columns] = product(weighted_scores, grad_here, 1, 0)
 
@@ -333,7 +340,8 @@
             term = product(grad_here, state, 1, 1)
             row = level * head_count + head
             on = wide(flag_ref[level])
-            query_total = query_total + (gates[:, row : row + 1] * on) * term
+            if level > 0:
+                query_total = query_total + (gates[:, row : row + 1] * on) * term
             state_grad = state_grad + wide(state) * (1.0 - on)
         grad_rounded = narrow(state_grad)
         qo_ref[:, columns] = narrow(query_total)
@@ -503,9 +511,9 @@
     )
     query_local, key_local, value_local = call(
         functools.partial(local_kernel, block_depth, head_size),
-        [vmem] * 6 + [anywhere],
+        [smem] + [vmem] * 7 + [anywhere],
         (big, big, big),
-        (class_lanes, table, query_rows, key_rows, value_rows, out_grad, shares),
+        (flag_bits, rest_seen, class_lanes, table, query_rows, key_rows, value_rows, out_grad, shares),
         flops=10 * row_count * width * row_count,
     )
     pieces = [shares] + [swap(shares, *z_bits(offs)) for offs in (1, 2, 3)]

time: 44.7 us -> 44.5 us (level)
  waiting for transfers between devices: 11.2 us -> 10.6 us
    ppermute x13, waiting for transfers between devices: 9.68 us -> 9.14 us  [swap(): return lax.ppermute(block, 'gy', [(i, i ^ mask) for i in range(inner_size)])]
  transfers between devices with their start and end apart: 17 -> 17, of which waited for: 7 -> 7; matrix products, arithmetic and copies ran while one was open for 0% -> 0% of each run, Pallas kernels for 9% -> 10%
where the time goes in v14:
time: 44.5 us; the launch traced here: 44.4 us
  starting transfers between devices  23.3 us (52%)
  waiting for transfers between devices  10.6 us (24%)
  Pallas kernels  9.47 us (21%)
  between operations  0.79 us (2%)
    ppermute x13, starting transfers between devices, swap(): return lax.ppermute(block, 'gy', [(i, i ^ mask) for i in range(inner_size)])  20.8 us
    pallas_call x11, Pallas kernels, call(): pl.pallas_call(kernel, out_shape=outs, in_specs=in_specs, out_specs=out_s...  9.47 us
    ppermute x13, waiting for transfers between devices, swap(): return lax.ppermute(block, 'gy', [(i, i ^ mask) for i in range(inner_size)])  9.14 us
    ppermute x1, starting transfers between devices, swap(): lax.ppermute(block, ('gx', 'gy'), [(i, i ^ mask) for i in range(device_co...  1.5 us
    ppermute x3, waiting for transfers between devices, swap(): return lax.ppermute(block, 'gx', [(i, i ^ mask) for i in range(size)])  1.47 us
    ppermute x3, starting transfers between devices, swap(): return lax.ppermute(block, 'gx', [(i, i ^ mask) for i in range(size)])  1.02 us
  transfers between devices with their start and end apart: 17, of which 7 were waited for; matrix products, arithmetic and copies ran while one was open for 0% of the time, Pallas kernels for 10%

profile of v14, /device:TPU:0, one launch (start us, length us, event | category | flops | bytes accessed | tf_op | source)
XLA Modules:
  0.0 44.4 jit_solution(9815348024608184588)
XLA Ops:
  0.7 0.0 copy-start.2
  0.7 2.3 %shard_map.85 = (bf16[12,128,128]{2,1,0:T(8,128)(2,1)S(1)}, bf16[4,128,128]{2,1,0:T(8,128)(2,1)S(1)}) custom-call(s32[5]{0:T(128)S(1)} %shift-right-arithmetic_and_fusion.flag_ref, s32[1,128]{1,0:T(1,128)} %bitcast.6, f32[20,8,32]{2,1,0:T(8,128)} %bitcast.2, bf16[128,1024]{1,0:T(8,128)(2,1)} %q_ref.3, bf16[128,1024]{1,0:T(8,128)(2,1)} %k_ref.5, ...), custom_call_target="tpu_custom_call" | custom-call | flops 67108864 | bytes 1069588 | tf_op jit(solution)/shard_map/pallas_call | solution.py:395
  3.0 0.5 %collective-permute-start.1 = (bf16[12,128,128]{2,1,0:T(8,128)(2,1)S(1)}, bf16[12,128,128]{2,1,0:T(8,128)(2,1)S(1)}, u32[]{:S(2)}, u32[]{:S(2)}) collective-permute-start(bf16[12,128,128]{2,1,0:T(8,128)(2,1)S(1)} %get-tuple-element.19), channel_id=1, source_target_pairs={{0,8},{8,0},{16,24},{24,16},{1,9},{9,1},{17,25},{25,17},{2,10},{10... | collective-permute-start | bytes 1179656 | tf_op jit(solution)/shard_map/ppermute | solution.py:379
  3.5 0.1 copy-done.5
  3.6 1.2 %shard_map.86 = (bf16[4,128,128]{2,1,0:T(8,128)(2,1)S(1)}, bf16[8,128,128]{2,1,0:T(8,128)(2,1)S(1)}, bf16[12,128,128]{2,1,0:T(8,128)(2,1)S(1)}) custom-call(s32[5]{0:T(128)S(1)} %shift-right-arithmetic_and_fusion.flag_ref, s32[1,128]{1,0:T(1,128)S(1)} %bitcast.7, f32[20,8,32]{2,1,0:T(8,128)S(1)} %bitcast.3, bf16[128,1024]{1,0:T(8,128)(2,1)S(1)} %copy-done.3, ...), custom_call_target="tpu_custom_call" | custom-call | flops 100663296 | bytes 1200660 | tf_op jit(solution)/shard_map/pallas_call | solution.py:395
  4.8 3.0 %collective-permute-start.8 = (bf16[8,128,128]{2,1,0:T(8,128)(2,1)S(1)}, bf16[8,128,128]{2,1,0:T(8,128)(2,1)S(1)}, u32[]{:S(2)}, u32[]{:S(2)}) collective-permute-start(bf16[8,128,128]{2,1,0:T(8,128)(2,1)S(1)} %get-tuple-element.27.sent_ref), channel_id=1, source_target_pairs={{0,1},{1,0},{2,3},{3,2},{4,5},{5,4},{6,7},{7,6},{8,9},{9,8},{10,11... | collective-permute-start | bytes 786440 | tf_op jit(solution)/shard_map/ppermute | solution.py:375
  7.8 0.1 collective-permute-start
  7.9 0.6 %shard_map.87 = (bf16[3,128,128]{2,1,0:T(8,128)(2,1)S(1)}, bf16[3,128,128]{2,1,0:T(8,128)(2,1)S(1)}, bf16[3,128,128]{2,1,0:T(8,128)(2,1)S(1)}, bf16[3,128,128]{2,1,0:T(8,128)(2,1)S(1)}) custom-call(s32[5]{0:T(128)S(1)} %shift-right-arithmetic_and_fusion.flag_ref, bf16[12,128,128]{2,1,0:T(8,128)(2,1)S(1)} %collective-permute-done.1.seen_ref, ...), custom_call_target="tpu_custom_call" | custom-call | bytes 655380 | tf_op jit(solution)/shard_map/pallas_call | solution.py:395
  8.5 4.1 %collective-permute-start.2 = (bf16[3,128,128]{2,1,0:T(8,128)(2,1)S(1)}, bf16[3,128,128]{2,1,0:T(8,128)(2,1)S(1)}, u32[]{:S(2)}, u32[]{:S(2)}) collective-permute-start(bf16[3,128,128]{2,1,0:T(8,128)(2,1)S(1)} %get-tuple-element.22), channel_id=1, source_target_pairs={{0,6},{1,7},{2,4},{3,5},{4,2},{5,3},{6,0},{7,1},{8,14},{9,15},{10,... | collective-permute-start | bytes 294920 | tf_op jit(solution)/shard_map/ppermute | solution.py:375
  12.6 0.6 %collective-permute-start.4 = (bf16[3,128,128]{2,1,0:T(8,128)(2,1)S(1)}, bf16[3,128,128]{2,1,0:T(8,128)(2,1)S(1)}, u32[]{:S(2)}, u32[]{:S(2)}) collective-permute-start(bf16[3,128,128]{2,1,0:T(8,128)(2,1)S(1)} %get-tuple-element.24), channel_id=1, source_target_pairs={{0,2},{1,3},{2,0},{3,1},{4,6},{5,7},{6,4},{7,5},{8,10},{9,11},{10,... | collective-permute-start | bytes 294920 | tf_op jit(solution)/shard_map/ppermute | solution.py:375
  13.3 1.7 %collective-permute-done.8.seen_ref = bf16[8,128,128]{2,1,0:T(8,128)(2,1)S(1)} collective-permute-done((bf16[8,128,128]{2,1,0:T(8,128)(2,1)S(1)}, bf16[8,128,128]{2,1,0:T(8,128)(2,1)S(1)}, u32[]{:S(2)}, u32[]{:S(2)}) %collective-permute-start.8) | collective-permute-done | bytes 262176 | tf_op jit(solution)/shard_map/ppermute | solution.py:375
  15.0 2.2 %collective-permute-start.9 = (bf16[4,128,128]{2,1,0:T(8,128)(2,1)S(1)}, bf16[4,128,128]{2,1,0:T(8,128)(2,1)S(1)}, u32[]{:S(2)}, u32[]{:S(2)}) collective-permute-start(bf16[4,128,128]{2,1,0:T(8,128)(2,1)S(1)} %shard_map.89.own_ref.after_ref), channel_id=1, source_target_pairs={{0,2},{1,3},{2,0},{3,1},{4,6},{5,7},{6,4},{7,5},{8,10},{9,11},{10,... | collective-permute-start | bytes 393224 | tf_op jit(solution)/shard_map/ppermute | solution.py:375
  17.2 3.4 %collective-permute-done.3.refs_1_ = bf16[3,128,128]{2,1,0:T(8,128)(2,1)S(1)} collective-permute-done((bf16[3,128,128]{2,1,0:T(8,128)(2,1)S(1)}, bf16[3,128,128]{2,1,0:T(8,128)(2,1)S(1)}, u32[]{:S(2)}, u32[]{:S(2)}) %collective-permute-start.3) | collective-permute-done | bytes 98336 | tf_op jit(solution)/shard_map/ppermute | solution.py:375
  20.6 0.1 shard_map.88
  20.6 1.6 %collective-permute-start.5 = (bf16[2,128,128]{2,1,0:T(8,128)(2,1)S(1)}, bf16[2,128,128]{2,1,0:T(8,128)(2,1)S(1)}, u32[]{:S(2)}, u32[]{:S(2)}) collective-permute-start(bf16[2,128,128]{2,1,0:T(8,128)(2,1)S(1)} %get-tuple-element.25.below_ref.after_ref), channel_id=1, source_target_pairs={{0,1},{1,0},{2,3},{3,2},{4,5},{5,4},{6,7},{7,6},{8,9},{9,8},{10,11... | collective-permute-start | bytes 196616 | tf_op jit(solution)/shard_map/ppermute | solution.py:375
  22.3 1.5 %collective-permute-start.7 = (bf16[1,128,128]{2,1,0:T(8,128)(2,1)S(1)}, bf16[1,128,128]{2,1,0:T(8,128)(2,1)S(1)}, u32[]{:S(2)}, u32[]{:S(2)}) collective-permute-start(bf16[1,128,128]{2,1,0:T(8,128)(2,1)S(1)} %get-tuple-element.26), channel_id=1, source_target_pairs={{0,17},{1,16},{2,19},{3,18},{4,21},{5,20},{6,23},{7,22},{8,25},{9,... | collective-permute-start | bytes 98312 | tf_op jit(solution)/shard_map/ppermute | solution.py:380
  23.8 0.4 collective-permute-start.6
  24.2 0.9 %collective-permute-start.11 = (bf16[4,128,128]{2,1,0:T(8,128)(2,1)S(1)}, bf16[4,128,128]{2,1,0:T(8,128)(2,1)S(1)}, u32[]{:S(2)}, u32[]{:S(2)}) collective-permute-start(bf16[4,128,128]{2,1,0:T(8,128)(2,1)S(1)} %shard_map.90.refs_0_), channel_id=1, source_target_pairs={{0,4},{1,5},{2,6},{3,7},{4,0},{5,1},{6,2},{7,3},{8,12},{9,13},{10,... | collective-permute-start | bytes 393224 | tf_op jit(solution)/shard_map/ppermute | solution.py:375
  25.1 0.1 shard_map.93
  25.2 2.3 %collective-permute-start.10 = (bf16[8,128,128]{2,1,0:T(8,128)(2,1)S(1)}, bf16[8,128,128]{2,1,0:T(8,128)(2,1)S(1)}, u32[]{:S(2)}, u32[]{:S(2)}) collective-permute-start(bf16[8,128,128]{2,1,0:T(8,128)(2,1)S(1)} %shard_map.93), channel_id=1, source_target_pairs={{0,2},{1,3},{2,0},{3,1},{4,6},{5,7},{6,4},{7,5},{8,10},{9,11},{10,... | collective-permute-start | bytes 786440 | tf_op jit(solution)/shard_map/ppermute | solution.py:375
  27.5 0.2 collective-permute-done.6.near_top_ref
  27.7 2.5 %collective-permute-start.15 = (bf16[3,128,128]{2,1,0:T(8,128)(2,1)S(1)}, bf16[3,128,128]{2,1,0:T(8,128)(2,1)S(1)}, u32[]{:S(2)}, u32[]{:S(2)}) collective-permute-start(bf16[3,128,128]{2,1,0:T(8,128)(2,1)S(1)} %shard_map.91.after_ref.piece0_ref), channel_id=1, source_target_pairs={{0,6},{1,7},{2,4},{3,5},{4,2},{5,3},{6,0},{7,1},{8,14},{9,15},{10,... | collective-permute-start | bytes 294920 | tf_op jit(solution)/shard_map/ppermute | solution.py:375
  30.2 0.8 %collective-permute-start.14 = (bf16[3,128,128]{2,1,0:T(8,128)(2,1)S(1)}, bf16[3,128,128]{2,1,0:T(8,128)(2,1)S(1)}, u32[]{:S(2)}, u32[]{:S(2)}) collective-permute-start(bf16[3,128,128]{2,1,0:T(8,128)(2,1)S(1)} %shard_map.91.after_ref.piece0_ref), channel_id=1, source_target_pairs={{0,4},{1,5},{2,6},{3,7},{4,0},{5,1},{6,2},{7,3},{8,12},{9,13},{10,... | collective-permute-start | bytes 294920 | tf_op jit(solution)/shard_map/ppermute | solution.py:375
  31.0 1.2 %collective-permute-start.13 = (bf16[3,128,128]{2,1,0:T(8,128)(2,1)S(1)}, bf16[3,128,128]{2,1,0:T(8,128)(2,1)S(1)}, u32[]{:S(2)}, u32[]{:S(2)}) collective-permute-start(bf16[3,128,128]{2,1,0:T(8,128)(2,1)S(1)} %shard_map.91.after_ref.piece0_ref), channel_id=1, source_target_pairs={{0,2},{1,3},{2,0},{3,1},{4,6},{5,7},{6,4},{7,5},{8,10},{9,11},{10,... | collective-permute-start | bytes 294920 | tf_op jit(solution)/shard_map/ppermute | solution.py:375
  32.2 2.6 %shard_map.92 = (f32[128,1024]{1,0:T(8,128)S(1)}, f32[128,1024]{1,0:T(8,128)S(1)}, f32[128,1024]{1,0:T(8,128)S(1)}) custom-call(s32[5]{0:T(128)S(1)} %shift-right-arithmetic_and_fusion.flag_ref, bf16[12,128,128]{2,1,0:T(8,128)(2,1)S(1)} %collective-permute-done.refs_1_.zero_ref.rest_seen_ref, s32[1,128]{1,0:T(1,128)S(1)} %bitcast.8, ...), custom_call_target="tpu_custom_call" | custom-call | flops 167772160 | bytes 1561108 | tf_op jit(solution)/shard_map/pallas_call | solution.py:395
  34.7 0.4 collective-permute-done.11.after_ref.two_own_ref
  35.2 1.5 %collective-permute-start.12 = (bf16[4,128,128]{2,1,0:T(8,128)(2,1)S(1)}, bf16[4,128,128]{2,1,0:T(8,128)(2,1)S(1)}, u32[]{:S(2)}, u32[]{:S(2)}) collective-permute-start(bf16[4,128,128]{2,1,0:T(8,128)(2,1)S(1)} %collective-permute-done.11.after_ref.two_own_ref), channel_id=1, source_target_pairs={{0,1},{1,0},{2,3},{3,2},{4,5},{5,4},{6,7},{7,6},{8,9},{9,8},{10,11... | collective-permute-start | bytes 393224 | tf_op jit(solution)/shard_map/ppermute | solution.py:375
  36.7 2.1 %collective-permute-done.15.piece3_ref = bf16[3,128,128]{2,1,0:T(8,128)(2,1)S(1)} collective-permute-done((bf16[3,128,128]{2,1,0:T(8,128)(2,1)S(1)}, bf16[3,128,128]{2,1,0:T(8,128)(2,1)S(1)}, u32[]{:S(2)}, u32[]{:S(2)}) %collective-permute-start.15) | collective-permute-done | bytes 98336 | tf_op jit(solution)/shard_map/ppermute | solution.py:375
  38.8 1.5 %collective-permute-done.13.piece1_ref = bf16[3,128,128]{2,1,0:T(8,128)(2,1)S(1)} collective-permute-done((bf16[3,128,128]{2,1,0:T(8,128)(2,1)S(1)}, bf16[3,128,128]{2,1,0:T(8,128)(2,1)S(1)}, u32[]{:S(2)}, u32[]{:S(2)}) %collective-permute-start.13) | collective-permute-done | bytes 98336 | tf_op jit(solution)/shard_map/ppermute | solution.py:375
  40.3 0.1 collective-permute-start.16
  40.4 1.3 %collective-permute-done.16.split_other_ref = bf16[1,4,128,128]{3,2,1,0:T(8,128)(2,1)S(1)} collective-permute-done((bf16[1,4,128,128]{3,2,1,0:T(8,128)(2,1)S(1)}, bf16[1,4,128,128]{3,2,1,0:T(8,128)(2,1)S(1)}, u32[]{:S(2)}, u32[]{:S(2)}) %collective-permute-start.16) | collective-permute-done | bytes 131104 | tf_op jit(solution)/shard_map/ppermute | solution.py:379
  41.7 2.6 %shard_map.95 = (bf16[128,1024]{1,0:T(8,128)(2,1)}, bf16[128,1024]{1,0:T(8,128)(2,1)}, bf16[128,1024]{1,0:T(8,128)(2,1)}) custom-call(s32[5]{0:T(128)S(1)} %shift-right-arithmetic_and_fusion.flag_ref, s32[1,128]{1,0:T(1,128)S(1)} %bitcast.9, f32[20,8,32]{2,1,0:T(8,128)S(1)} %bitcast.5, bf16[128,1024]{1,0:T(8,128)(2,1)S(1)} %copy-done, ...), custom_call_target="tpu_custom_call" | custom-call | flops 234881024 | bytes 3953172 | tf_op jit(solution)/shard_map/pallas_call | solution.py:395
  (26 shorter events, 0.2 us)
Async XLA Ops:
  0.6 2.9 %copy-start = (bf16[128,1024]{1,0:T(8,128)(2,1)S(1)}, bf16[128,1024]{1,0:T(8,128)(2,1)}, u32[]{:S(2)}) copy-start(bf16[128,1024]{1,0:T(8,128)(2,1)} %k_ref.5) | copy-start | bytes 786436
  0.7 2.9 %copy-start.1 = (bf16[128,1024]{1,0:T(8,128)(2,1)S(1)}, bf16[128,1024]{1,0:T(8,128)(2,1)}, u32[]{:S(2)}) copy-start(bf16[128,1024]{1,0:T(8,128)(2,1)} %v_ref.5) | copy-start | bytes 786436
  0.7 2.9 %copy-start.2 = (bf16[128,1024]{1,0:T(8,128)(2,1)S(1)}, bf16[128,1024]{1,0:T(8,128)(2,1)}, u32[]{:S(2)}) copy-start(bf16[128,1024]{1,0:T(8,128)(2,1)} %g_ref.5) | copy-start | bytes 786436
  0.7 2.8 %copy-start.3 = (bf16[128,1024]{1,0:T(8,128)(2,1)S(1)}, bf16[128,1024]{1,0:T(8,128)(2,1)}, u32[]{:S(2)}) copy-start(bf16[128,1024]{1,0:T(8,128)(2,1)} %q_ref.3) | copy-start | bytes 786436
  0.7 2.8 %copy-start.4 = (f32[32,20,8]{0,2,1:T(8,128)S(1)}, f32[32,20,8]{0,2,1:T(8,128)}, u32[]{:S(2)}) copy-start(f32[32,20,8]{0,2,1:T(8,128)} %param.11) | copy-start | bytes 61444
  3.0 0.7 %copy-start.5 = (s32[128]{0:T(128)S(1)}, s32[128]{0:T(128)}, u32[]{:S(2)}) copy-start(s32[128]{0:T(128)} %param.10) | copy-start | bytes 1540
  3.0 4.9 %collective-permute-start.1 = (bf16[12,128,128]{2,1,0:T(8,128)(2,1)S(1)}, bf16[12,128,128]{2,1,0:T(8,128)(2,1)S(1)}, u32[]{:S(2)}, u32[]{:S(2)}) collective-permute-start(bf16[12,128,128]{2,1,0:T(8,128)(2,1)S(1)} %get-tuple-element.19), channel_id=1, source_target_pairs={{0,8},{8,0},{16,24},{24,16},{1,9},{9,1},{17,25},{25,17},{2,10},{10... | collective-permute-start | bytes 1179656 | tf_op jit(solution)/shard_map/ppermute | solution.py:379
  4.8 10.1 %collective-permute-start.8 = (bf16[8,128,128]{2,1,0:T(8,128)(2,1)S(1)}, bf16[8,128,128]{2,1,0:T(8,128)(2,1)S(1)}, u32[]{:S(2)}, u32[]{:S(2)}) collective-permute-start(bf16[8,128,128]{2,1,0:T(8,128)(2,1)S(1)} %get-tuple-element.27.sent_ref), channel_id=1, source_target_pairs={{0,1},{1,0},{2,3},{3,2},{4,5},{5,4},{6,7},{7,6},{8,9},{9,8},{10,11... | collective-permute-start | bytes 786440 | tf_op jit(solution)/shard_map/ppermute | solution.py:375
  7.8 17.3 %collective-permute-start = (bf16[12,128,128]{2,1,0:T(8,128)(2,1)S(1)}, bf16[12,128,128]{2,1,0:T(8,128)(2,1)S(1)}, u32[]{:S(2)}, u32[]{:S(2)}) collective-permute-start(bf16[12,128,128]{2,1,0:T(8,128)(2,1)S(1)} %get-tuple-element.18.rest_ref), channel_id=1, source_target_pairs={{0,1},{1,0},{2,3},{3,2},{4,5},{5,4},{6,7},{7,6},{8,9},{9,8},{10,11... | collective-permute-start | bytes 1179656 | tf_op jit(solution)/shard_map/ppermute | solution.py:375
  8.5 8.7 %collective-permute-start.2 = (bf16[3,128,128]{2,1,0:T(8,128)(2,1)S(1)}, bf16[3,128,128]{2,1,0:T(8,128)(2,1)S(1)}, u32[]{:S(2)}, u32[]{:S(2)}) collective-permute-start(bf16[3,128,128]{2,1,0:T(8,128)(2,1)S(1)} %get-tuple-element.22), channel_id=1, source_target_pairs={{0,6},{1,7},{2,4},{3,5},{4,2},{5,3},{6,0},{7,1},{8,14},{9,15},{10,... | collective-permute-start | bytes 294920 | tf_op jit(solution)/shard_map/ppermute | solution.py:375
  12.6 7.9 %collective-permute-start.3 = (bf16[3,128,128]{2,1,0:T(8,128)(2,1)S(1)}, bf16[3,128,128]{2,1,0:T(8,128)(2,1)S(1)}, u32[]{:S(2)}, u32[]{:S(2)}) collective-permute-start(bf16[3,128,128]{2,1,0:T(8,128)(2,1)S(1)} %get-tuple-element.23), channel_id=1, source_target_pairs={{0,4},{1,5},{2,6},{3,7},{4,0},{5,1},{6,2},{7,3},{8,12},{9,13},{10,... | collective-permute-start | bytes 294920 | tf_op jit(solution)/shard_map/ppermute | solution.py:375
  12.6 7.9 %collective-permute-start.4 = (bf16[3,128,128]{2,1,0:T(8,128)(2,1)S(1)}, bf16[3,128,128]{2,1,0:T(8,128)(2,1)S(1)}, u32[]{:S(2)}, u32[]{:S(2)}) collective-permute-start(bf16[3,128,128]{2,1,0:T(8,128)(2,1)S(1)} %get-tuple-element.24), channel_id=1, source_target_pairs={{0,2},{1,3},{2,0},{3,1},{4,6},{5,7},{6,4},{7,5},{8,10},{9,11},{10,... | collective-permute-start | bytes 294920 | tf_op jit(solution)/shard_map/ppermute | solution.py:375
  15.0 9.2 %collective-permute-start.9 = (bf16[4,128,128]{2,1,0:T(8,128)(2,1)S(1)}, bf16[4,128,128]{2,1,0:T(8,128)(2,1)S(1)}, u32[]{:S(2)}, u32[]{:S(2)}) collective-permute-start(bf16[4,128,128]{2,1,0:T(8,128)(2,1)S(1)} %shard_map.89.own_ref.after_ref), channel_id=1, source_target_pairs={{0,2},{1,3},{2,0},{3,1},{4,6},{5,7},{6,4},{7,5},{8,10},{9,11},{10,... | collective-permute-start | bytes 393224 | tf_op jit(solution)/shard_map/ppermute | solution.py:375
  20.6 7.0 %collective-permute-start.5 = (bf16[2,128,128]{2,1,0:T(8,128)(2,1)S(1)}, bf16[2,128,128]{2,1,0:T(8,128)(2,1)S(1)}, u32[]{:S(2)}, u32[]{:S(2)}) collective-permute-start(bf16[2,128,128]{2,1,0:T(8,128)(2,1)S(1)} %get-tuple-element.25.below_ref.after_ref), channel_id=1, source_target_pairs={{0,1},{1,0},{2,3},{3,2},{4,5},{5,4},{6,7},{7,6},{8,9},{9,8},{10,11... | collective-permute-start | bytes 196616 | tf_op jit(solution)/shard_map/ppermute | solution.py:375
  22.3 5.3 %collective-permute-start.7 = (bf16[1,128,128]{2,1,0:T(8,128)(2,1)S(1)}, bf16[1,128,128]{2,1,0:T(8,128)(2,1)S(1)}, u32[]{:S(2)}, u32[]{:S(2)}) collective-permute-start(bf16[1,128,128]{2,1,0:T(8,128)(2,1)S(1)} %get-tuple-element.26), channel_id=1, source_target_pairs={{0,17},{1,16},{2,19},{3,18},{4,21},{5,20},{6,23},{7,22},{8,25},{9,... | collective-permute-start | bytes 98312 | tf_op jit(solution)/shard_map/ppermute | solution.py:380
  23.8 3.9 %collective-permute-start.6 = (bf16[1,128,128]{2,1,0:T(8,128)(2,1)S(1)}, bf16[1,128,128]{2,1,0:T(8,128)(2,1)S(1)}, u32[]{:S(2)}, u32[]{:S(2)}) collective-permute-start(bf16[1,128,128]{2,1,0:T(8,128)(2,1)S(1)} %get-tuple-element.26), channel_id=1, source_target_pairs={{0,16},{8,24},{16,0},{24,8},{1,17},{9,25},{17,1},{25,9},{2,18},{10... | collective-permute-start | bytes 98312 | tf_op jit(solution)/shard_map/ppermute | solution.py:379
  24.2 10.9 %collective-permute-start.11 = (bf16[4,128,128]{2,1,0:T(8,128)(2,1)S(1)}, bf16[4,128,128]{2,1,0:T(8,128)(2,1)S(1)}, u32[]{:S(2)}, u32[]{:S(2)}) collective-permute-start(bf16[4,128,128]{2,1,0:T(8,128)(2,1)S(1)} %shard_map.90.refs_0_), channel_id=1, source_target_pairs={{0,4},{1,5},{2,6},{3,7},{4,0},{5,1},{6,2},{7,3},{8,12},{9,13},{10,... | collective-permute-start | bytes 393224 | tf_op jit(solution)/shard_map/ppermute | solution.py:375
  25.2 15.2 %collective-permute-start.10 = (bf16[8,128,128]{2,1,0:T(8,128)(2,1)S(1)}, bf16[8,128,128]{2,1,0:T(8,128)(2,1)S(1)}, u32[]{:S(2)}, u32[]{:S(2)}) collective-permute-start(bf16[8,128,128]{2,1,0:T(8,128)(2,1)S(1)} %shard_map.93), channel_id=1, source_target_pairs={{0,2},{1,3},{2,0},{3,1},{4,6},{5,7},{6,4},{7,5},{8,10},{9,11},{10,... | collective-permute-start | bytes 786440 | tf_op jit(solution)/shard_map/ppermute | solution.py:375
  27.7 11.1 %collective-permute-start.15 = (bf16[3,128,128]{2,1,0:T(8,128)(2,1)S(1)}, bf16[3,128,128]{2,1,0:T(8,128)(2,1)S(1)}, u32[]{:S(2)}, u32[]{:S(2)}) collective-permute-start(bf16[3,128,128]{2,1,0:T(8,128)(2,1)S(1)} %shard_map.91.after_ref.piece0_ref), channel_id=1, source_target_pairs={{0,6},{1,7},{2,4},{3,5},{4,2},{5,3},{6,0},{7,1},{8,14},{9,15},{10,... | collective-permute-start | bytes 294920 | tf_op jit(solution)/shard_map/ppermute | solution.py:375
  30.2 8.6 %collective-permute-start.14 = (bf16[3,128,128]{2,1,0:T(8,128)(2,1)S(1)}, bf16[3,128,128]{2,1,0:T(8,128)(2,1)S(1)}, u32[]{:S(2)}, u32[]{:S(2)}) collective-permute-start(bf16[3,128,128]{2,1,0:T(8,128)(2,1)S(1)} %shard_map.91.after_ref.piece0_ref), channel_id=1, source_target_pairs={{0,4},{1,5},{2,6},{3,7},{4,0},{5,1},{6,2},{7,3},{8,12},{9,13},{10,... | collective-permute-start | bytes 294920 | tf_op jit(solution)/shard_map/ppermute | solution.py:375
  31.0 9.3 %collective-permute-start.13 = (bf16[3,128,128]{2,1,0:T(8,128)(2,1)S(1)}, bf16[3,128,128]{2,1,0:T(8,128)(2,1)S(1)}, u32[]{:S(2)}, u32[]{:S(2)}) collective-permute-start(bf16[3,128,128]{2,1,0:T(8,128)(2,1)S(1)} %shard_map.91.after_ref.piece0_ref), channel_id=1, source_target_pairs={{0,2},{1,3},{2,0},{3,1},{4,6},{5,7},{6,4},{7,5},{8,10},{9,11},{10,... | collective-permute-start | bytes 294920 | tf_op jit(solution)/shard_map/ppermute | solution.py:375
  35.2 5.2 %collective-permute-start.12 = (bf16[4,128,128]{2,1,0:T(8,128)(2,1)S(1)}, bf16[4,128,128]{2,1,0:T(8,128)(2,1)S(1)}, u32[]{:S(2)}, u32[]{:S(2)}) collective-permute-start(bf16[4,128,128]{2,1,0:T(8,128)(2,1)S(1)} %collective-permute-done.11.after_ref.two_own_ref), channel_id=1, source_target_pairs={{0,1},{1,0},{2,3},{3,2},{4,5},{5,4},{6,7},{7,6},{8,9},{9,8},{10,11... | collective-permute-start | bytes 393224 | tf_op jit(solution)/shard_map/ppermute | solution.py:375
  40.3 1.4 %collective-permute-start.16 = (bf16[1,4,128,128]{3,2,1,0:T(8,128)(2,1)S(1)}, bf16[1,4,128,128]{3,2,1,0:T(8,128)(2,1)S(1)}, u32[]{:S(2)}, u32[]{:S(2)}) collective-permute-start(bf16[1,4,128,128]{3,2,1,0:T(8,128)(2,1)S(1)} %shard_map.94.split_own_ref), channel_id=1, source_target_pairs={{0,8},{8,0},{16,24},{24,16},{1,9},{9,1},{17,25},{25,17},{2,10},{10... | collective-permute-start | bytes 393224 | tf_op jit(solution)/shard_map/ppermute | solution.py:379
